TPU v7x, 32 devices: a whole 2x2x4 slice. The times are simulated.
32 devices in a mesh: seq: 8 (over z, y), tensor: 4 (over x, core).
Axes of the slice: x: 2, y: 2, z: 4, core: 2. Of those that a mesh axis runs over, the one named last changes fastest.
Arguments:
- layer_input: bfloat16 [4, 2048, 2048], P(None, 'seq'), may hold values from -6 to 6
- attn_norm: bfloat16 [2048], replicated, may hold values from 0.5 to 1.5
- query_weight: bfloat16 [2048, 2048], P(None, 'tensor'), may hold values from -0.125 to 0.125
- key_weight: bfloat16 [2048, 2048], P(None, 'tensor'), may hold values from -0.125 to 0.125
- value_weight: bfloat16 [2048, 2048], P(None, 'tensor'), may hold values from -0.125 to 0.125
- gate_weight: bfloat16 [2048, 2048], P(None, 'tensor'), may hold values from -0.125 to 0.125
- rank_down: bfloat16 [2048, 16], replicated, may hold values from -0.125 to 0.125
- rank_up: bfloat16 [16, 2048], P(None, 'tensor'), may hold values from -1.5 to 1.5
- decay_bias: bfloat16 [2048], P('tensor')
- head_gain: bfloat16 [2048], P('tensor'), may hold values from 0.5 to 1.5
- out_weight: bfloat16 [2048, 2048], P('tensor'), may hold values from -0.1875 to 0.1875
- mlp_norm: bfloat16 [2048], replicated, may hold values from 0.5 to 1.5
- swish_weight: bfloat16 [2048, 5632], P(None, 'tensor'), may hold values from -0.125 to 0.125
- up_weight: bfloat16 [2048, 5632], P(None, 'tensor'), may hold values from -0.125 to 0.125
- down_weight: bfloat16 [5632, 2048], P('tensor'), may hold values from -0.109375 to 0.109375
- cotangent: bfloat16 [4, 2048, 2048], P(None, 'seq'), may hold values from -6 to 6
Outputs:
- layer_output: bfloat16 [4, 2048, 2048], P(None, 'seq')
- input_grad: bfloat16 [4, 2048, 2048], P(None, 'seq')
- attn_norm_grad: float32 [2048], P('seq')
- query_grad: float32 [2048, 2048], P('seq', 'tensor')
- key_grad: float32 [2048, 2048], P('seq', 'tensor')
- value_grad: float32 [2048, 2048], P('seq', 'tensor')
- gate_grad: float32 [2048, 2048], P('seq', 'tensor')
- rank_down_grad: float32 [2048, 16], P('seq')
- rank_up_grad: float32 [16, 2048], P(None, 'tensor')
- decay_bias_grad: float32 [2048], P('tensor')
- head_gain_grad: float32 [2048], P('tensor')
- out_grad: float32 [2048, 2048], P('tensor', 'seq')
- mlp_norm_grad: float32 [2048], P('seq')
- swish_grad: float32 [2048, 5632], P('seq', 'tensor')
- up_grad: float32 [2048, 5632], P('seq', 'tensor')
- down_grad: float32 [5632, 2048], P('tensor', 'seq')
All inputs are finite; a program needn't handle non-finite values.
Results may differ from a plain program's by a relative error of at most 0.025.
Values may be sent and summed in bfloat16 or wider, within the bound.
No kernel may reach another device: no remote copies, remote signals or barrier semaphores. Data moves between devices by JAX's collectives and lax.ppermute only.
A program may use at most 448 MiB of HBM per device.

v0:
```python
import jax
import jax.numpy as jnp
from jax import lax
from jax.sharding import PartitionSpec as P

DK = 512
BLOCK = 64


highest_precision = lax.Precision.HIGHEST
epsilon = 1e-06


def entering(x, axis, combine, identity, reverse):
    count, place = (lax.axis_size(axis), lax.axis_index(axis))
    everything = jax.tree.map(lambda part: lax.all_gather(part, axis), x)
    start = jax.tree.map(
        lambda part, zero: jnp.broadcast_to(jnp.asarray(zero, part.dtype), part.shape), x, identity
    )

    def turn(k, before):
        at = count - 1 - k if reverse else k
        reached = at > place if reverse else at < place
        new = combine(before, jax.tree.map(lambda part: part[at], everything))
        return jax.tree.map(lambda a, b: jnp.where(reached, a, b), new, before)

    return lax.fori_loop(0, count, turn, start)


def product(left_rows, right_rows):
    return jnp.dot(left_rows, right_rows, preferred_element_type=jnp.float32)


def across(left_rows, right_rows):
    return lax.dot_general(
        left_rows, right_rows, (((0,), (0,)), ((), ())), preferred_element_type=jnp.float32
    )


def against(left_rows, right_rows):
    return lax.dot_general(
        left_rows, right_rows, (((1,), (1,)), ((), ())), preferred_element_type=jnp.float32
    )


def block_step(state_matrix, pieces):
    query_rows, key_matrix, value_matrix, decays = pieces
    row_count = query_rows.shape[0]
    running_decay = jnp.cumsum(decays, axis=0)
    positions = jnp.arange(row_count)
    causal = (positions[None, :] <= positions[:, None]).astype(jnp.float32)
    center_decay = running_decay[row_count // 2]
    left_rows = query_rows * jnp.exp(running_decay - center_decay[None])
    right_rows = key_matrix * jnp.exp(center_decay[None] - running_decay)
    scores = (
        jnp.einsum("thk,shk->hts", left_rows, right_rows, precision=highest_precision)
        * causal[None]
    )
    inner_part = jnp.einsum("hts,shv->thv", scores, value_matrix, precision=highest_precision)
    carried_state = jnp.einsum(
        "xwn,wnl->xwl",
        query_rows * jnp.exp(running_decay),
        state_matrix,
        precision=highest_precision,
    )
    closing_decay = running_decay[-1]
    state_update = jnp.einsum(
        "awy,awq->wyq",
        key_matrix * jnp.exp(closing_decay[None] - running_decay),
        value_matrix,
        precision=highest_precision,
    )
    return (
        jnp.exp(closing_decay)[:, :, None] * state_matrix + state_update,
        inner_part + carried_state,
    )


def run_device(query_rows, key_matrix, value_matrix, decays, initial):
    seq_count, row_count, head_count, feature_count = query_rows.shape
    block_count = row_count // BLOCK

    def to_blocks(values):
        return jnp.moveaxis(
            values.reshape(seq_count, block_count, BLOCK, head_count, feature_count), 1, 0
        )

    stepper = jax.checkpoint(jax.vmap(block_step))
    final_state, mixed_rows = lax.scan(
        stepper,
        initial,
        (to_blocks(query_rows), to_blocks(key_matrix), to_blocks(value_matrix), to_blocks(decays)),
    )
    return (
        jnp.moveaxis(mixed_rows, 0, 1).reshape(seq_count, row_count, head_count, feature_count),
        final_state,
    )


def chain_combine(earlier, later):
    early_decay, early_state = earlier
    late_decay, late_state = later
    return (early_decay * late_decay, late_decay[..., None] * early_state + late_state)


def local(
    layer_input,
    attn_norm,
    query_weight,
    key_weight,
    value_weight,
    gate_weight,
    rank_down,
    rank_up,
    decay_bias,
    head_gain,
    out_weight,
    mlp_norm,
    swish_weight,
    up_weight,
    down_weight,
    cotangent,
):
    seq_count, seq_length, feature_count = layer_input.shape
    row_count = seq_count * seq_length
    local_width = query_weight.shape[1]
    local_heads = local_width // DK
    query_scale = DK ** (-0.5)
    flat_input = layer_input.reshape(row_count, feature_count).astype(jnp.float32)
    scale_one = lax.rsqrt(jnp.mean(flat_input * flat_input, axis=-1, keepdims=True) + epsilon)
    unit_one = flat_input * scale_one
    gain_one = attn_norm.astype(jnp.float32)
    first_norm = (unit_one * gain_one).astype(jnp.bfloat16)
    query_rows = product(first_norm, query_weight).astype(jnp.bfloat16)
    key_matrix = product(first_norm, key_weight).astype(jnp.bfloat16)
    value_matrix = product(first_norm, value_weight).astype(jnp.bfloat16)
    gate_rows = product(first_norm, gate_weight)
    rank_rows = product(first_norm, rank_down).astype(jnp.bfloat16)
    logits = product(rank_rows, rank_up) + decay_bias.astype(jnp.float32)
    decays = jax.nn.log_sigmoid(logits) / 16.0

    def heads_of(values):
        return values.astype(jnp.float32).reshape(seq_count, seq_length, local_heads, DK)

    query_heads = heads_of(query_rows) * query_scale
    key_heads = heads_of(key_matrix)
    value_heads = heads_of(value_matrix)
    decay_heads = heads_of(decays)
    running_decay = jnp.cumsum(decay_heads, axis=1)
    total_decay = running_decay[:, -1]
    carry_out = jnp.exp(total_decay)
    local_state = jnp.einsum(
        "bthk,bthv->bhkv",
        key_heads * jnp.exp(total_decay[:, None] - running_decay),
        value_heads,
        precision=highest_precision,
    )
    identity = (jnp.ones_like(carry_out), jnp.zeros_like(local_state))
    incoming = entering((carry_out, local_state), "seq", chain_combine, identity, False)[1]

    def device_mix(query_part, key_part, value_part, decay_part):
        return run_device(query_part, key_part, value_part, decay_part, incoming)

    mixed_rows, _ = device_mix(query_heads, key_heads, value_heads, decay_heads)
    head_scale = lax.rsqrt(jnp.mean(mixed_rows * mixed_rows, axis=-1, keepdims=True) + epsilon)
    unit_heads = mixed_rows * head_scale
    gain_heads = head_gain.astype(jnp.float32).reshape(local_heads, DK)
    shaped = (unit_heads * gain_heads).reshape(row_count, local_width)
    gate_sig = jax.nn.sigmoid(gate_rows)
    gate_act = gate_rows * gate_sig
    branch = (shaped * gate_act).astype(jnp.bfloat16)
    middle = flat_input + lax.psum(product(branch, out_weight), "tensor")
    scale_two = lax.rsqrt(jnp.mean(middle * middle, axis=-1, keepdims=True) + epsilon)
    unit_two = middle * scale_two
    gain_two = mlp_norm.astype(jnp.float32)
    second = (unit_two * gain_two).astype(jnp.bfloat16)
    swish_rows = product(second, swish_weight)
    up_rows = product(second, up_weight)
    swish_sig = jax.nn.sigmoid(swish_rows)
    swish_act = swish_rows * swish_sig
    inner_rows = (swish_act * up_rows).astype(jnp.bfloat16)
    result = middle + lax.psum(
        product(inner_rows, down_weight).astype(jnp.bfloat16), "tensor"
    ).astype(jnp.float32)
    layer_output = result.astype(jnp.bfloat16).reshape(seq_count, seq_length, feature_count)
    grad_rows = cotangent.reshape(row_count, feature_count)
    down_grad = across(inner_rows, grad_rows)
    inner_grad = against(grad_rows, down_weight)
    swish_back = (inner_grad * up_rows * swish_sig * (1.0 + swish_rows * (1.0 - swish_sig))).astype(
        jnp.bfloat16
    )
    up_back = (inner_grad * swish_act).astype(jnp.bfloat16)
    swish_grad = across(second, swish_back)
    up_grad = across(second, up_back)
    second_grad = lax.psum(
        against(swish_back, swish_weight) + against(up_back, up_weight), "tensor"
    )
    mlp_norm_grad = jnp.sum(second_grad * unit_two, axis=0)
    scaled_two = second_grad * gain_two
    middle_grad = grad_rows.astype(jnp.float32) + scale_two * (
        scaled_two - unit_two * jnp.mean(scaled_two * unit_two, axis=-1, keepdims=True)
    )
    branch_rows = middle_grad.astype(jnp.bfloat16)
    out_grad = across(branch, branch_rows)
    branch_grad = against(branch_rows, out_weight)
    shaped_grad = branch_grad * gate_act
    gate_back = (branch_grad * shaped * gate_sig * (1.0 + gate_rows * (1.0 - gate_sig))).astype(
        jnp.bfloat16
    )
    shaped_heads = shaped_grad.reshape(seq_count, seq_length, local_heads, DK)
    head_gain_grad = jnp.sum(shaped_heads * unit_heads, axis=(0, 1)).reshape(local_width)
    unit_grad = shaped_heads * gain_heads
    mixed_grad = head_scale * (
        unit_grad - unit_heads * jnp.mean(unit_grad * unit_heads, axis=-1, keepdims=True)
    )
    local_back = jnp.einsum(
        "bthk,bthv->bhkv",
        query_heads * jnp.exp(running_decay),
        mixed_grad,
        precision=highest_precision,
    )
    outgoing = entering((carry_out, local_back), "seq", chain_combine, identity, True)[1]
    _, pullback = jax.vjp(device_mix, query_heads, key_heads, value_heads, decay_heads)
    query_back, key_back, value_back, decay_back = pullback((mixed_grad, outgoing))

    def rows_of(values):
        return values.reshape(row_count, local_width)

    query_rows_back = (rows_of(query_back) * query_scale).astype(jnp.bfloat16)
    key_rows_back = rows_of(key_back).astype(jnp.bfloat16)
    value_rows_back = rows_of(value_back).astype(jnp.bfloat16)
    logit_back = (rows_of(decay_back) * jax.nn.sigmoid(-logits) / 16.0).astype(jnp.bfloat16)
    decay_bias_grad = jnp.sum(logit_back.astype(jnp.float32), axis=0)
    rank_up_grad = across(rank_rows, logit_back)
    logit_whole, rank_up_whole = (
        lax.all_gather(logit_back, "tensor", axis=1, tiled=True),
        lax.all_gather(rank_up, "tensor", axis=1, tiled=True),
    )
    rank_back = against(logit_whole, rank_up_whole).astype(jnp.bfloat16)
    first_part = (
        against(query_rows_back, query_weight)
        + against(key_rows_back, key_weight)
        + against(value_rows_back, value_weight)
        + against(gate_back, gate_weight)
    )
    first_grad = lax.psum(first_part.astype(jnp.bfloat16), "tensor").astype(jnp.float32) + against(
        rank_back, rank_down
    )
    rank_down_grad = across(first_norm, rank_back)
    query_grad = across(first_norm, query_rows_back)
    key_grad = across(first_norm, key_rows_back)
    value_grad = across(first_norm, value_rows_back)
    gate_grad = across(first_norm, gate_back)
    attn_norm_grad = jnp.sum(first_grad * unit_one, axis=0)
    scaled_one = first_grad * gain_one
    input_rows = middle_grad + scale_one * (
        scaled_one - unit_one * jnp.mean(scaled_one * unit_one, axis=-1, keepdims=True)
    )
    input_grad = input_rows.astype(jnp.bfloat16).reshape(seq_count, seq_length, feature_count)
    rank_up_share, decay_bias_share, head_gain_share = (
        lax.psum(rank_up_grad.astype(jnp.bfloat16), "seq").astype(jnp.float32),
        lax.psum(decay_bias_grad.astype(jnp.bfloat16), "seq").astype(jnp.float32),
        lax.psum(head_gain_grad.astype(jnp.bfloat16), "seq").astype(jnp.float32),
    )
    (
        attn_norm_share,
        query_share,
        key_share,
        value_share,
        gate_share,
        rank_down_share,
        out_share,
        mlp_norm_share,
        swish_share,
        up_share,
        down_share,
    ) = (
        lax.psum_scatter(
            attn_norm_grad.astype(jnp.bfloat16), "seq", scatter_dimension=0, tiled=True
        ).astype(jnp.float32),
        lax.psum_scatter(
            query_grad.astype(jnp.bfloat16), "seq", scatter_dimension=0, tiled=True
        ).astype(jnp.float32),
        lax.psum_scatter(
            key_grad.astype(jnp.bfloat16), "seq", scatter_dimension=0, tiled=True
        ).astype(jnp.float32),
        lax.psum_scatter(
            value_grad.astype(jnp.bfloat16), "seq", scatter_dimension=0, tiled=True
        ).astype(jnp.float32),
        lax.psum_scatter(
            gate_grad.astype(jnp.bfloat16), "seq", scatter_dimension=0, tiled=True
        ).astype(jnp.float32),
        lax.psum_scatter(
            rank_down_grad.astype(jnp.bfloat16), "seq", scatter_dimension=0, tiled=True
        ).astype(jnp.float32),
        lax.psum_scatter(
            out_grad.astype(jnp.bfloat16), "seq", scatter_dimension=1, tiled=True
        ).astype(jnp.float32),
        lax.psum_scatter(
            mlp_norm_grad.astype(jnp.bfloat16), "seq", scatter_dimension=0, tiled=True
        ).astype(jnp.float32),
        lax.psum_scatter(
            swish_grad.astype(jnp.bfloat16), "seq", scatter_dimension=0, tiled=True
        ).astype(jnp.float32),
        lax.psum_scatter(
            up_grad.astype(jnp.bfloat16), "seq", scatter_dimension=0, tiled=True
        ).astype(jnp.float32),
        lax.psum_scatter(
            down_grad.astype(jnp.bfloat16), "seq", scatter_dimension=1, tiled=True
        ).astype(jnp.float32),
    )
    return (
        layer_output,
        input_grad,
        attn_norm_share,
        query_share,
        key_share,
        value_share,
        gate_share,
        rank_down_share,
        rank_up_share,
        decay_bias_share,
        head_gain_share,
        out_share,
        mlp_norm_share,
        swish_share,
        up_share,
        down_share,
    )


def solution(mesh):
    return jax.shard_map(
        local,
        mesh=mesh,
        in_specs=(
            P(None, "seq", None),
            P(),
            P(None, "tensor"),
            P(None, "tensor"),
            P(None, "tensor"),
            P(None, "tensor"),
            P(),
            P(None, "tensor"),
            P("tensor"),
            P("tensor"),
            P("tensor", None),
            P(),
            P(None, "tensor"),
            P(None, "tensor"),
            P("tensor", None),
            P(None, "seq", None),
        ),
        out_specs=(
            P(None, "seq", None),
            P(None, "seq", None),
            P("seq"),
            P("seq", "tensor"),
            P("seq", "tensor"),
            P("seq", "tensor"),
            P("seq", "tensor"),
            P("seq", None),
            P(None, "tensor"),
            P("tensor"),
            P("tensor"),
            P("tensor", "seq"),
            P("seq"),
            P("seq", "tensor"),
            P("seq", "tensor"),
            P("tensor", "seq"),
        ),
        check_vma=False,
    )
```

profile of v0, /device:TPU:0, one launch (start us, length us, event | category | flops | bytes accessed | tf_op | source)
XLA Modules:
  0.0 2829.9 jit_solution(13785965646688666933)
XLA Ops:
  40.9 74.7 %all-gather = f32[32,1,1,512]{3,2,1,0:T(1,128)S(1)} all-gather(f32[4,1,1,512]{3,2,1,0:T(1,128)S(1)} %copy.181), channel_id=2, replica_groups=mesh['seq'=8,'tensor'=4] {'seq'}, dimensions={0}, use_global_device_ids=true | all-gather | bytes 73728 | tf_op jit(solution)/shard_map/all_gather | solution.py:16
  125.0 557.4 %all-gather.9.cloned.1.call-done = f32[32,512,512]{2,1,0:T(8,128)} async-done(((f32[4,512,512]{2,1,0:T(8,128)}), f32[32,512,512]{2,1,0:T(8,128)}) %all-gather.9.cloned.1.call-update) | async-done | bytes 33554448 | tf_op jit(solution)/shard_map/all_gather | solution.py:16
  682.4 47.6 %while.79 = (s32[]{:T(128)}, f32[4,1,512,512]{3,2,1,0:T(8,128)}, s32[]{:T(128)}, f32[8,4,1,512]{3,1,2,0:T(4,128)S(1)}, f32[8,4,1,512,512]{4,3,1,2,0:T(8,128)}, /*index=5*/s32[]{:T(128)}, s32[]{:T(128)}) while((s32[]{:T(128)}, f32[4,1,512,512]{3,2,1,0:T(8,128)}, s32[]{:T(128)}, f32[8,4,1,512]{3,1,2,0:T(4,128)S(1)}, ...), condition=%wide.region_4.5_spmd.clone, body=%wide.region_3.4_spmd.clone.sunk | while | flops 4194308 | bytes 12607593 | solution.py:27
  736.2 76.4 %while.76 = (s32[]{:T(128)}, f32[4,1,512,512]{3,2,0,1:T(8,128)}, f32[4,4,64,1,512]{4,2,0,1,3:T(8,128)}, f32[4,4,64,1,512]{4,3,2,1,0:T(1,128)}, f32[4,4,64,1,512]...) while((s32[]{:T(128)}, f32[4,1,512,512]{3,2,0,1:T(8,128)}, ...), condition=%wide.region_7.8_spmd, body=%wide.region_5.7_spmd.sunk | while | flops 1823367168 | bytes 20746324 | solution.py:89
  829.2 152.2 %all-reduce.10.cloned.1.call-done = f32[1024,2048]{1,0:T(8,128)} async-done(((f32[1024,2048]{1,0:T(8,128)}), f32[1024,2048]{1,0:T(8,128)}) %all-reduce.10.cloned.1.call-update) | async-done | bytes 8388624 | tf_op jit(solution)/shard_map/psum | solution.py:172
  990.4 11.7 fusion.195
  1002.2 10.4 fusion.196
  1012.6 14.6 multiply_convert_fusion.1
  1027.2 10.6 fusion.197
  1037.9 10.9 convolution_add_fusion
  1048.9 153.0 %all-reduce.12.cloned.1.call-done = f32[1024,2048]{1,0:T(8,128)} async-done(((f32[1024,2048]{1,0:T(8,128)}), f32[1024,2048]{1,0:T(8,128)}) %all-reduce.12.cloned.1.call-update) | async-done | bytes 8388624 | tf_op jit(solution)/shard_map/psum | solution.py:195
  1223.5 10.0 fusion.165
  1248.4 11.0 convolution_convert_fusion.2
  1259.5 11.0 convolution_convert_fusion.1
  1277.4 57.2 %while.77 = (s32[]{:T(128)}, f32[4,1,512,512]{3,2,0,1:T(8,128)}, f32[4,4,1,512,512]{4,3,1,2,0:T(8,128)}, f32[4,4,64,1,512]{4,3,2,1,0:T(1,128)}, f32[4,4,64,1,512...) while((s32[]{:T(128)}, f32[4,1,512,512]{3,2,0,1:T(8,128)}, ...), condition=%wide.region_19.20_spmd, body=%wide.region_17.19_spmd.sunk | while | flops 815923200 | bytes 19466316 | solution.py:89
  1297.8 8.2 bitcast_add_fusion.13
  1334.6 10.5 convolution_convert_fusion
  1350.0 521.6 %all-gather.11.cloned.1.call-done = f32[32,512,512]{2,1,0:T(8,128)} async-done(((f32[4,512,512]{2,1,0:T(8,128)}), f32[32,512,512]{2,1,0:T(8,128)}) %all-gather.11.cloned.1.call-update) | async-done | bytes 33554448 | tf_op jit(solution)/shard_map/all_gather | solution.py:16
  1871.6 53.3 %while.80 = (s32[]{:T(128)}, f32[4,1,512,512]{3,2,1,0:T(8,128)}, s32[]{:T(128)}, f32[8,4,1,512]{3,1,2,0:T(4,128)}, f32[8,4,1,512,512]{4,3,1,2,0:T(8,128)}, /*index=5*/s32[]{:T(128)}, s32[]{:T(128)}, s32[]{:T(128)}, s32[]{:T(128)}) while((s32[]{:T(128)}, f32[4,1,512,512]{3,2,1,0:T(8,128)}, s32[]{:T(128)}, ...), condition=%wide.region_16.17_spmd.clone, body=%wide.region_15.16_spmd.clone.sunk | while | flops 4194312 | bytes 12607655 | solution.py:27
  1934.8 213.1 %while.78 = (s32[]{:T(128)}, f32[4,1,512,512]{2,3,0,1:T(8,128)}, f32[4,4,64,1,512]{4,2,0,1,3:T(8,128)}, bf16[4,4,64,1,512]{4,2,0,1,3:T(8,128)(2,1)}, bf16[4,4,64...) while((s32[]{:T(128)}, f32[4,1,512,512]{2,3,0,1:T(8,128)}, ...), condition=%wide.region_27.28_spmd, body=%wide.region_20.27_spmd.sunk | while | flops 3751976960 | bytes 111886648 | solution.py:89
  2168.1 11.2 convolution_convert_fusion.3
  2193.0 11.5 add_convert_fusion
  2221.2 18.1 reduce-scatter.24.cloned.1.call-done
  2241.6 111.6 %reduce-scatter.26.cloned.1.call-done = bf16[1408,256]{1,0:T(8,128)(2,1)} async-done(((bf16[1408,2048]{1,0:T(8,128)(2,1)}), bf16[1408,256]{1,0:T(8,128)(2,1)}) %reduce-scatter.26.cloned.1.call-update) | async-done | bytes 720912 | tf_op jit(solution)/shard_map/reduce_scatter | solution.py:308
  2355.8 68.3 %reduce-scatter.10.cloned.1.call-done = bf16[256,512]{1,0:T(8,128)(2,1)} async-done(((bf16[2048,512]{1,0:T(8,128)(2,1)}), bf16[256,512]{1,0:T(8,128)(2,1)}) %reduce-scatter.10.cloned.1.call-update) | async-done | bytes 262160 | tf_op jit(solution)/shard_map/reduce_scatter | solution.py:281
  2425.9 68.5 %reduce-scatter.12.cloned.1.call-done = bf16[256,512]{1,0:T(8,128)(2,1)} async-done(((bf16[2048,512]{1,0:T(8,128)(2,1)}), bf16[256,512]{1,0:T(8,128)(2,1)}) %reduce-scatter.12.cloned.1.call-update) | async-done | bytes 262160 | tf_op jit(solution)/shard_map/reduce_scatter | solution.py:284
  2496.2 68.2 %reduce-scatter.14.cloned.1.call-done = bf16[256,512]{1,0:T(8,128)(2,1)} async-done(((bf16[2048,512]{1,0:T(8,128)(2,1)}), bf16[256,512]{1,0:T(8,128)(2,1)}) %reduce-scatter.14.cloned.1.call-update) | async-done | bytes 262160 | tf_op jit(solution)/shard_map/reduce_scatter | solution.py:287
  2566.1 153.6 %all-reduce.14.cloned.1.call-done = (bf16[1024,2048]{1,0:T(8,128)(2,1)}, bf16[1024,2048]{1,0:T(8,128)(2,1)}) async-done(((bf16[1024,2048]{1,0:T(8,128)(2,1)}, bf16[1024,2048]{1,0:T(8,128)(2,1)}), (bf16[1024,2048]{1,0:T(8,128)(2,1)}, bf16[1024,2048]{1,0:T(8,128)(2,1)})) %all-reduce.14.cloned.1.call-update) | async-done | bytes 8388624 | tf_op jit(solution)/shard_map/psum | solution.py:182
  2719.7 8.3 add_convert_fusion.1
  2728.0 27.8 all-gather.7.cloned.1.call-done
  2768.0 10.4 fusion.150
  2778.3 37.1 %all-reduce.4 = (bf16[2048]{0:T(1024)(128)(2,1)S(1)}, bf16[16,512]{1,0:T(8,128)(2,1)S(1)}, bf16[512]{0:T(512)(128)(2,1)S(1)}, bf16[512]{0:T(512)(128)(2,1)S(1)}, bf16[2048]{0:T(1024)(128)(2,1)S(1)}) all-reduce(bf16[2048]{0:T(1024)(128)(2,1)S(1)} %get-tuple-element.781, ...), channel_id=5, replica_groups=mesh['seq'=8,'tensor'=4] {'seq'}, use_global_device_ids=true, to_apply=%region_31.32.clone | all-reduce | flops 13312 | bytes 53248
  (491 shorter events, 650.1 us)
Async XLA Ops:
  7.2 815.7 %copy-start = (bf16[512,2048]{1,0:T(8,128)(2,1)S(1)}, bf16[512,2048]{1,0:T(8,128)(2,1)}, u32[]{:S(2)}) copy-start(bf16[512,2048]{1,0:T(8,128)(2,1)} %param.36) | copy-start | bytes 6291460
  7.2 675.2 %all-gather.9.cloned.1.call-start = ((), (), s32[]{:S(2)}) async-start(), calls=%async_computation.21 | async-start | bytes 37748736 | tf_op jit(solution)/shard_map/all_gather | solution.py:16
  40.8 940.6 %all-reduce.10.cloned.1.call-start = ((), (), s32[]{:S(2)}) async-start(), calls=%async_computation.9 | async-start | bytes 16777216 | tf_op jit(solution)/shard_map/psum | solution.py:172
  828.5 373.4 %all-reduce.12.cloned.1.call-start = ((), (), s32[]{:S(2)}) async-start(), calls=%async_computation.10 | async-start | bytes 16777216 | tf_op jit(solution)/shard_map/psum | solution.py:195
  990.4 11.8 copy-start.22
  1002.2 10.4 copy-start.20
  1027.2 10.7 copy-start.63
  1048.8 822.8 %all-gather.11.cloned.1.call-start = ((), (), s32[]{:S(2)}) async-start(), calls=%async_computation.22 | async-start | bytes 37748736 | tf_op jit(solution)/shard_map/all_gather | solution.py:16
  1202.0 8.2 copy-start.9
  1202.0 9.4 copy-start.21
  1216.1 7.4 copy-start.5
  1223.5 18.4 copy-start.29
  1233.5 981.7 %reduce-scatter.20.cloned.1.call-start = ((), (), s32[]{:S(2)}) async-start(), calls=%async_computation.17 | async-start | bytes 2359296 | tf_op jit(solution)/shard_map/reduce_scatter | solution.py:296
  1241.9 975.2 %reduce-scatter.16.cloned.1.call-start = ((), (), s32[]{:S(2)}) async-start(), calls=%async_computation.15 | async-start | bytes 2359296 | tf_op jit(solution)/shard_map/reduce_scatter | solution.py:290
  1248.3 970.6 %reduce-scatter.22.cloned.1.call-start = ((), (), s32[]{:S(2)}) async-start(), calls=%async_computation.18 | async-start | bytes 6488064 | tf_op jit(solution)/shard_map/reduce_scatter | solution.py:302
  1259.4 979.9 %reduce-scatter.24.cloned.1.call-start = ((), (), s32[]{:S(2)}) async-start(), calls=%async_computation.19 | async-start | bytes 6488064 | tf_op jit(solution)/shard_map/reduce_scatter | solution.py:305
  1270.5 1082.7 %reduce-scatter.26.cloned.1.call-start = ((), (), s32[]{:S(2)}) async-start(), calls=%async_computation.20 | async-start | bytes 6488064 | tf_op jit(solution)/shard_map/reduce_scatter | solution.py:308
  1345.1 1079.0 %reduce-scatter.10.cloned.1.call-start = ((), (), s32[]{:S(2)}) async-start(), calls=%async_computation.12 | async-start | bytes 2359296 | tf_op jit(solution)/shard_map/reduce_scatter | solution.py:281
  2155.9 338.5 %reduce-scatter.12.cloned.1.call-start = ((), (), s32[]{:S(2)}) async-start(), calls=%async_computation.13 | async-start | bytes 2359296 | tf_op jit(solution)/shard_map/reduce_scatter | solution.py:284
  2162.1 402.2 %reduce-scatter.14.cloned.1.call-start = ((), (), s32[]{:S(2)}) async-start(), calls=%async_computation.14 | async-start | bytes 2359296 | tf_op jit(solution)/shard_map/reduce_scatter | solution.py:287
  2168.1 551.6 %all-reduce.14.cloned.1.call-start = ((), (), s32[]{:S(2)}) async-start(), calls=%async_computation.23 | async-start | bytes 16777216 | tf_op jit(solution)/shard_map/psum | solution.py:182
  2168.1 11.2 copy-start.57
  2204.5 551.3 %all-gather.7.cloned.1.call-start = ((), (), s32[]{:S(2)}) async-start(), calls=%async_computation.11 | async-start | bytes 5242880 | tf_op jit(solution)/shard_map/all_gather | solution.py:236
  2208.5 147.0 %copy-start.12 = (bf16[1024,512]{1,0:T(8,128)(2,1)S(1)}, bf16[1024,512]{1,0:T(8,128)(2,1)}, u32[]{:S(2)}) copy-start(bf16[1024,512]{1,0:T(8,128)(2,1)} %get-tuple-element.863) | copy-start | bytes 3145732
  2208.5 147.0 %copy-start.38 = (bf16[1024,16]{0,1:T(8,128)(2,1)S(1)}, bf16[1024,16]{0,1:T(8,128)(2,1)}, u32[]{:S(2)}) copy-start(bf16[1024,16]{0,1:T(8,128)(2,1)} %copy-done.37) | copy-start | bytes 98308
  2208.5 613.3 %reduce-scatter.18.cloned.1.call-start = ((), (), s32[]{:S(2)}) async-start(), calls=%async_computation.16 | async-start | bytes 73728 | tf_op jit(solution)/shard_map/reduce_scatter | solution.py:293
  2728.0 32.6 %copy-start.41 = (f32[2048]{0:T(1024)S(1)}, f32[2048]{0:T(1024)}, u32[]{:S(2)}) copy-start(f32[2048]{0:T(1024)} %copy-done.39) | copy-start | bytes 24580
  2728.0 32.6 %copy-start.43 = (bf16[2048,16]{0,1:T(8,128)(2,1)S(1)}, bf16[2048,16]{0,1:T(8,128)(2,1)}, u32[]{:S(2)}) copy-start(bf16[2048,16]{0,1:T(8,128)(2,1)} %param.32) | copy-start | bytes 196612
  2728.0 32.6 %copy-start.45 = (f32[1,2,4,128]{3,1,2,0:T(2,128)S(1)}, f32[1,2,4,128]{3,1,2,0:T(2,128)}, u32[]{:S(2)}) copy-start(f32[1,2,4,128]{3,1,2,0:T(2,128)} %copy-done.44) | copy-start | bytes 12292
  2767.9 10.4 copy-start.49
  2767.9 10.4 copy-start.56
  2768.0 55.1 %copy-start.1 = (bf16[512,2048]{1,0:T(8,128)(2,1)S(1)}, bf16[512,2048]{1,0:T(8,128)(2,1)}, u32[]{:S(2)}) copy-start(bf16[512,2048]{1,0:T(8,128)(2,1)} %param.36) | copy-start | bytes 6291460
  (62 other events, 239.5 us)
Sparse Core Ops, SparseCore 0:
  40.9 641.4 all-gather.8
  828.6 152.7 all-reduce.9
  1048.9 153.0 all-reduce.11
  1233.7 637.8 all-gather.10
  1875.0 68.0 reduce-scatter.19
  1946.5 66.8 reduce-scatter.15
  2017.0 108.8 reduce-scatter.21
  2129.5 109.7 reduce-scatter.23
  2243.0 110.1 reduce-scatter.25
  2356.6 67.4 reduce-scatter.9
  2427.6 66.6 reduce-scatter.11
  2497.7 66.5 reduce-scatter.13
  2567.5 152.1 all-reduce.13
  2721.1 34.5 all-gather.6
  2768.1 53.6 reduce-scatter.17
where the time goes:
time: 2840 us; the launch traced here: 2830 us
  waiting for transfers between devices  1900 us (67%)
  matrix products  433 us (15%)
  other arithmetic  231 us (8%)
  local copies, waits for them, and re-layouts  125 us (4%)
  blocking collectives  117 us (4%)
    all_gather x2, waiting for transfers between devices, entering(): everything = jax.tree.map(lambda part: lax.all_gather(part, axis), x)  1080 us
    psum x1, waiting for transfers between devices, local(): lax.psum(product(inner_rows, down_weight).astype(jnp.bfloat16), 'tensor')  154 us
    psum x1, waiting for transfers between devices, local(): lax.psum(against(swish_back, swish_weight) + against(up_back, up_weight),...  153 us
    psum x1, waiting for transfers between devices, local(): middle = flat_input + lax.psum(product(branch, out_weight), 'tensor')  152 us
    reduce_scatter x1, waiting for transfers between devices, local(): lax.psum_scatter(down_grad.astype(jnp.bfloat16), 'seq', scatter_dimension...  112 us
    dot_general x16, matrix products, block_step(): jnp.einsum('awy,awq->wyq', key_matrix * jnp.exp(closing_decay[None] - run...  111 us
    select_n x16, other arithmetic, turn(): return jax.tree.map(lambda a, b: jnp.where(reached, a, b), new, before)  95 us
    dot_general x10, matrix products, against(): lax.dot_general(left_rows, right_rows, (((1,), (1,)), ((), ())), preferre...  79.4 us
  transfers between devices with their start and end apart: 15, of which 12 were waited for; matrix products, arithmetic and copies ran while one was open for 17% of the time, Pallas kernels for 0%

commit v1 on v0

v1 whole, which is shorter than its diff:
```python
import functools

import jax
import jax.numpy as jnp
from jax import lax
from jax.experimental import pallas as pl
from jax.experimental.pallas import tpu as pltpu
from jax.sharding import PartitionSpec as P

DK = 512
BLOCK = 64
VMEM = 48 * 1024 * 1024

bf16 = jnp.bfloat16
f32 = jnp.float32
highest_precision = lax.Precision.HIGHEST
epsilon = 1e-06


def contract(left, right, left_dim, right_dim, precision=None):
    return lax.dot_general(
        left,
        right,
        (((left_dim,), (right_dim,)), ((), ())),
        preferred_element_type=f32,
        precision=precision,
    )


def product(left, right):
    return contract(left, right, 1, 0)


def across(left, right):
    return contract(left, right, 0, 0)


def against(left, right):
    return contract(left, right, 1, 1)


def forget_logits(rank_ref, up_ref, bias_ref):
    return product(rank_ref[...], up_ref[...]) + bias_ref[...].astype(f32)


def positions(count):
    rows = lax.broadcasted_iota(jnp.int32, (count, count), 0)
    cols = lax.broadcasted_iota(jnp.int32, (count, count), 1)
    return rows, cols


def spread(pieces, size):
    width = pieces[0].shape[1]
    return jnp.concatenate([jnp.broadcast_to(piece, (size, width)) for piece in pieces], axis=0)


def scaled_pair(level, query_scaled, key_rows, run):
    count = run.shape[0]
    if level == 0:
        starts = range(0, count, BLOCK)
        center = spread([run[s + BLOCK // 2 : s + BLOCK // 2 + 1] for s in starts], BLOCK)
        query_factor = jnp.exp(run - center)
        key_factor = jnp.exp(center - run)
        return query_scaled * query_factor, key_rows * key_factor, query_factor, key_factor
    group = BLOCK << level
    half = group // 2
    center = spread([run[s + half - 1 : s + half] for s in range(0, count, group)], group)
    place = lax.broadcasted_iota(jnp.int32, run.shape, 0)
    right = (place % group) >= half
    gap = run - center
    query_factor = jnp.where(right, jnp.exp(jnp.where(right, gap, 0.0)), 0.0)
    key_factor = jnp.where(right, 0.0, jnp.exp(jnp.where(right, 0.0, -gap)))
    return query_scaled * query_factor, key_rows * key_factor, query_factor, key_factor


def level_mask(level, rows, cols):
    if level == 0:
        return (rows // BLOCK == cols // BLOCK) & (cols <= rows)
    group = BLOCK << level
    half = group // 2
    return (rows // group == cols // group) & (rows % group >= half) & (cols % group < half)


def level_count(count):
    levels = 1
    while (BLOCK << (levels - 1)) < count:
        levels += 1
    return levels


def state_kernel(rank_ref, up_ref, bias_ref, key_ref, value_ref, run_ref, state_ref):
    logits = forget_logits(rank_ref, up_ref, bias_ref)
    decays = (jnp.minimum(logits, 0.0) - jnp.log1p(jnp.exp(-jnp.abs(logits)))) * (1.0 / 16.0)
    rows, cols = positions(decays.shape[0])
    run = contract((cols <= rows).astype(f32), decays, 1, 0, highest_precision)
    run_ref[...] = run
    count = run.shape[0]
    left = (key_ref[...].astype(f32) * jnp.exp(run[count - 1 : count] - run)).astype(bf16)
    state_ref[0] = across(value_ref[...], left).astype(bf16)


def score_kernel(query_ref, key_ref, run_ref, score_ref):
    run = run_ref[...]
    query_scaled = query_ref[...].astype(f32) * DK ** (-0.5)
    key_rows = key_ref[...].astype(f32)
    rows, cols = positions(run.shape[0])
    scores = jnp.zeros(rows.shape, f32)
    for level in range(level_count(run.shape[0])):
        left, right, _, _ = scaled_pair(level, query_scaled, key_rows, run)
        scores = jnp.where(
            level_mask(level, rows, cols), against(left.astype(bf16), right.astype(bf16)), scores
        )
    score_ref[0] = scores.astype(bf16)


def whole_state(ref):
    return ref[...].reshape(DK, DK)


def mix_kernel(query_ref, value_ref, run_ref, score_ref, state_ref, gate_ref, gain_ref, mixed_ref, branch_ref):
    faded = (query_ref[...].astype(f32) * DK ** (-0.5) * jnp.exp(run_ref[...])).astype(bf16)
    mixed = product(score_ref[0], value_ref[...]) + against(faded, whole_state(state_ref))
    mixed_ref[...] = mixed
    scale = lax.rsqrt(jnp.mean(mixed * mixed, axis=-1, keepdims=True) + epsilon)
    gate = gate_ref[...]
    branch_ref[...] = (
        mixed * scale * gain_ref[...].astype(f32) * (gate * jax.nn.sigmoid(gate))
    ).astype(bf16)


def branch_back_kernel(
    rows_ref, weight_ref, mixed_ref, gate_ref, gain_ref, query_ref, run_ref,
    gate_back_ref, mixed_back_ref, gain_back_ref, state_back_ref,
):
    branch_grad = against(rows_ref[...], weight_ref[...])
    mixed = mixed_ref[...]
    scale = lax.rsqrt(jnp.mean(mixed * mixed, axis=-1, keepdims=True) + epsilon)
    unit = mixed * scale
    gate = gate_ref[...]
    gain = gain_ref[...].astype(f32)
    sig = jax.nn.sigmoid(gate)
    gate_back_ref[...] = (branch_grad * unit * gain * sig * (1.0 + gate * (1.0 - sig))).astype(bf16)
    shaped_grad = branch_grad * (gate * sig)
    gain_back_ref[0] = jnp.sum(shaped_grad * unit, axis=0, keepdims=True)
    unit_grad = shaped_grad * gain
    mixed_grad = scale * (unit_grad - unit * jnp.mean(unit_grad * unit, axis=-1, keepdims=True))
    mixed_back = mixed_grad.astype(bf16)
    mixed_back_ref[...] = mixed_back
    faded = (query_ref[...].astype(f32) * DK ** (-0.5) * jnp.exp(run_ref[...])).astype(bf16)
    state_back_ref[0] = across(mixed_back, faded).astype(bf16)


def ordered_sum(mask, values):
    high = values.astype(bf16)
    low = (values - high.astype(f32)).astype(bf16)
    ones = mask.astype(f32).astype(bf16)
    return product(ones, high) + product(ones, low)


def mix_back_kernel(
    query_ref, key_ref, value_ref, grad_ref, run_ref, score_ref, state_ref, state_back_ref,
    rank_ref, up_ref, bias_ref,
    query_back_ref, key_back_ref, value_back_ref, logit_back_ref, rank_back_ref, up_back_ref, bias_back_ref,
):
    run = run_ref[...]
    count = run.shape[0]
    query_scaled = query_ref[...].astype(f32) * DK ** (-0.5)
    key_rows = key_ref[...].astype(f32)
    values = value_ref[...]
    grads = grad_ref[...]
    state = whole_state(state_ref)
    state_back = whole_state(state_back_ref)
    rows, cols = positions(count)
    pairs = against(grads, values)

    closing = run[count - 1 : count]
    fade_in = jnp.exp(run)
    fade_out = jnp.exp(closing - run)
    kept = (key_rows * fade_out).astype(bf16)
    value_back_ref[...] = (across(score_ref[0], grads) + against(kept, state_back)).astype(bf16)

    from_state = product(grads, state)
    to_state = product(values, state_back)
    query_back = fade_in * from_state
    key_back = fade_out * to_state
    decay_back = jnp.exp(closing) * jnp.sum(
        state.astype(f32) * state_back.astype(f32), axis=0, keepdims=True
    )
    decay_back = decay_back + ordered_sum(cols >= rows, query_scaled * fade_in * from_state)
    decay_back = decay_back + ordered_sum(cols < rows, key_rows * fade_out * to_state)
    for level in range(level_count(count)):
        left, right, query_factor, key_factor = scaled_pair(level, query_scaled, key_rows, run)
        left, right = left.astype(bf16), right.astype(bf16)
        here = jnp.where(level_mask(level, rows, cols), pairs, 0.0).astype(bf16)
        to_query = product(here, right)
        to_key = across(here, left)
        query_back = query_back + query_factor * to_query
        key_back = key_back + key_factor * to_key
        left_part = left.astype(f32) * to_query
        right_part = right.astype(f32) * to_key
        if level == 0:
            mask = (rows // BLOCK == cols // BLOCK) & (cols >= rows)
            decay_back = decay_back + ordered_sum(mask, left_part - right_part)
        else:
            group = BLOCK << level
            half = group // 2
            same = rows // group == cols // group
            late = same & (rows % group >= half) & (cols >= rows)
            early = same & (rows % group < half) & (cols < rows)
            decay_back = decay_back + ordered_sum(late | early, left_part + right_part)
    query_back_ref[...] = (query_back * DK ** (-0.5)).astype(bf16)
    key_back_ref[...] = key_back.astype(bf16)
    logits = forget_logits(rank_ref, up_ref, bias_ref)
    logit_back = (decay_back * jax.nn.sigmoid(-logits) * (1.0 / 16.0)).astype(bf16)
    logit_back_ref[...] = logit_back
    rank_back_ref[0] = against(up_ref[...], logit_back)
    up_back_ref[0] = across(rank_ref[...], logit_back)
    bias_back_ref[0] = jnp.sum(logit_back.astype(f32), axis=0, keepdims=True)


def prefix_kernel(reverse, totals_ref, parts_ref, out_ref):
    count = parts_ref.shape[0]
    carry = jnp.zeros(parts_ref.shape[2:], f32)
    for step in range(count):
        at = count - 1 - step if reverse else step
        out_ref[at, 0] = carry.astype(bf16)
        carry = carry * jnp.exp(totals_ref[at, 0]) + parts_ref[at, 0].astype(f32)


def grid_call(kernel, grid, in_specs, out_specs, out_shape, flops, moved, *args):
    return pl.pallas_call(
        kernel,
        grid=grid,
        in_specs=in_specs,
        out_specs=out_specs,
        out_shape=out_shape,
        compiler_params=pltpu.CompilerParams(vmem_limit_bytes=VMEM),
        cost_estimate=pl.CostEstimate(flops=flops, bytes_accessed=moved, transcendentals=0),
    )(*args)


def struct(shape, dtype):
    return jax.ShapeDtypeStruct(shape, dtype)


def swap(values, axis, distance):
    count = lax.axis_size(axis)
    return lax.ppermute(values, axis, [(i, i ^ distance) for i in range(count)])


def bits_of(count):
    return [1 << k for k in range(count.bit_length() - 1)]


def spread_totals(values, axis):
    return lax.all_gather(values, axis)


def entering(local_state, totals, reverse):
    count = lax.axis_size("seq")
    seq_count = local_state.shape[0]
    rows = DK // count
    pieces = jnp.moveaxis(local_state.reshape(seq_count, count, rows, DK), 1, 0)
    pieces = lax.all_to_all(pieces, "seq", 0, 0)
    block = pl.BlockSpec((count, 1, rows, DK), lambda b: (0, b, 0, 0))
    carried = grid_call(
        functools.partial(prefix_kernel, reverse),
        (seq_count,),
        [pl.BlockSpec((count, 1, 1, DK), lambda b: (0, b, 0, 0)), block],
        block,
        struct(pieces.shape, bf16),
        2 * pieces.size,
        4 * pieces.size,
        totals,
        pieces,
    )
    return lax.all_to_all(carried, "seq", 0, 0)


def tensor_reduce(near, far):
    third = swap(far[1].astype(bf16), "tensor", 1)
    second = (far[0] + third.astype(f32)).astype(bf16)
    first = swap(near[1].astype(bf16), "tensor", 1)
    return near[0] + first.astype(f32) + swap(second, "tensor", 2).astype(f32)


def tensor_gather(own):
    first = swap(own, "tensor", 1)
    second = swap(own, "tensor", 2)
    third = swap(second, "tensor", 1)
    return jnp.stack([own, first]), jnp.stack([second, third])


def in_order(near, far):
    place = lax.axis_index("tensor")
    blocks = jnp.concatenate([near, far], axis=0)
    return jnp.concatenate(
        [lax.dynamic_index_in_dim(blocks, k ^ place, 0, keepdims=True) for k in range(4)], axis=0
    )


def scatter_grad(left, right, scatter_left, order):
    count = lax.axis_size("seq")
    me = lax.axis_index("seq")
    bits = bits_of(count)
    names = list(reversed(bits))
    rows = left.shape[0]
    cut = left if scatter_left else right
    share = cut.shape[1] // count
    cut = cut.reshape([rows] + [2] * len(bits) + [share])
    remaining = list(names)

    def choose(values, bit, first_axis, mine):
        at = remaining.index(bit) + first_axis
        here = (me // bit) % 2
        return lax.dynamic_index_in_dim(values, here if mine else 1 - here, at, keepdims=False)

    def grad(part):
        part = part.reshape(rows, -1)
        return across(part, right) if scatter_left else across(left, part)

    bit = order[0]
    away = grad(choose(cut, bit, 1, False)).astype(bf16)
    came = swap(away, "seq", bit)
    total = grad(choose(cut, bit, 1, True)) + came.astype(f32)
    remaining.remove(bit)
    for bit in order[1:]:
        total = total.astype(bf16)
        if scatter_left:
            view = total.reshape([2] * len(remaining) + [share, right.shape[1]])
            first_axis = 0
        else:
            view = total.reshape([left.shape[1]] + [2] * len(remaining) + [share])
            first_axis = 1
        came = swap(choose(view, bit, first_axis, False), "seq", bit)
        total = choose(view, bit, first_axis, True).astype(f32) + came.astype(f32)
        remaining.remove(bit)
    return total.reshape((share, right.shape[1]) if scatter_left else (left.shape[1], share))


def sum_over(values, axis):
    for bit in bits_of(lax.axis_size(axis)):
        values = values + swap(values, axis, bit)
    return values


def scatter_sum(values):
    count = lax.axis_size("seq")
    me = lax.axis_index("seq")
    share = values.shape[1] // count
    values = values.reshape(values.shape[0], count, share)
    for bit in reversed(bits_of(count)):
        view = values.reshape(values.shape[0], 2, -1, share)
        here = (me // bit) % 2
        came = swap(lax.dynamic_index_in_dim(view, 1 - here, 1, keepdims=False), "seq", bit)
        values = lax.dynamic_index_in_dim(view, here, 1, keepdims=False) + came
    return values.reshape(values.shape[0], share)


def local(
    layer_input,
    attn_norm,
    query_weight,
    key_weight,
    value_weight,
    gate_weight,
    rank_down,
    rank_up,
    decay_bias,
    head_gain,
    out_weight,
    mlp_norm,
    swish_weight,
    up_weight,
    down_weight,
    cotangent,
):
    seq_count, length, width = layer_input.shape
    place = lax.axis_index("tensor")
    devices = lax.axis_size("seq")
    bits = bits_of(devices)

    def arranged(values):
        return [lax.dynamic_index_in_dim(values, k ^ place, 0, keepdims=False) for k in range(4)]

    input_blocks = arranged(layer_input)
    grad_blocks = arranged(cotangent)
    grad_rows = jnp.concatenate(grad_blocks, axis=0)
    gain_one = attn_norm.astype(f32)
    gain_two = mlp_norm.astype(f32)
    bias = decay_bias.reshape(1, DK)
    gain = head_gain.reshape(1, DK)

    def normed(rows):
        scale = lax.rsqrt(jnp.mean(rows * rows, axis=-1, keepdims=True) + epsilon)
        return rows * scale, scale

    flat = jnp.concatenate(input_blocks, axis=0).astype(f32)
    first_norm = (normed(flat)[0] * gain_one).astype(bf16)
    own_input = input_blocks[0].astype(f32)

    key_rows = product(first_norm, key_weight).astype(bf16)
    value_rows = product(first_norm, value_weight).astype(bf16)
    rank_rows = product(first_norm, rank_down).astype(bf16)
    rank = rank_rows.shape[1]

    def row_spec(width, first=0):
        return pl.BlockSpec((length, width), lambda b: (b + first, 0))

    def fixed(shape):
        return pl.BlockSpec(shape, lambda b: (0,) * len(shape))

    def square(size, first=0):
        return pl.BlockSpec((1, size, size), lambda b: (b + first, 0, 0))

    def chunked(first=0):
        return pl.BlockSpec((devices, 1, DK // devices, DK), lambda b: (0, b + first, 0, 0))

    def line(rows, width, first=0):
        return pl.BlockSpec((1, rows, width), lambda b: (b + first, 0, 0))

    all_rows = seq_count * length
    run, local_state = grid_call(
        state_kernel,
        (seq_count,),
        [row_spec(rank), fixed((rank, DK)), fixed((1, DK)), row_spec(DK), row_spec(DK)],
        [row_spec(DK), square(DK)],
        [struct((all_rows, DK), f32), struct((seq_count, DK, DK), bf16)],
        2 * all_rows * DK * (DK + 6 * length),
        all_rows * DK * 8 + seq_count * DK * DK * 2,
        rank_rows, rank_up, bias, key_rows, value_rows,
    )
    totals = run.reshape(seq_count, length, DK)[:, length - 1 :]
    totals = spread_totals(totals, "seq")
    incoming = entering(local_state, totals, False)

    query_rows = product(first_norm, query_weight).astype(bf16)
    gate_rows = product(first_norm, gate_weight)
    scores = grid_call(
        score_kernel,
        (seq_count,),
        [row_spec(DK), row_spec(DK), row_spec(DK)],
        square(length),
        struct((seq_count, length, length), bf16),
        2 * all_rows * DK * length * 3,
        all_rows * DK * 8 + seq_count * length * length * 2,
        query_rows, key_rows, run,
    )

    half = 2
    half_rows = half * length

    def mix(first):
        return grid_call(
            mix_kernel,
            (half,),
            [
                row_spec(DK, first), row_spec(DK, first), row_spec(DK, first), square(length, first),
                chunked(first), row_spec(DK, first), fixed((1, DK)),
            ],
            [row_spec(DK), row_spec(DK)],
            [struct((half_rows, DK), f32), struct((half_rows, DK), bf16)],
            2 * half_rows * DK * (DK + length),
            half_rows * DK * 18 + half * DK * DK * 2,
            query_rows, value_rows, run, scores, incoming, gate_rows, gain,
        )

    def blocks(values):
        return values.reshape(half, length, values.shape[-1])

    mixed_far, branch_far = mix(half)
    out_far = product(branch_far, out_weight)
    mixed_near, branch_near = mix(0)
    out_near = product(branch_near, out_weight)
    middle = own_input + tensor_reduce(blocks(out_near), blocks(out_far))
    unit_two, scale_two = normed(middle)
    second_own = (unit_two * gain_two).astype(bf16)
    second_near, second_far = tensor_gather(second_own)

    def feed(second, grads):
        second = second.reshape(half_rows, width)
        swish_rows = product(second, swish_weight)
        up_rows = product(second, up_weight)
        sig = jax.nn.sigmoid(swish_rows)
        act = swish_rows * sig
        inner = (act * up_rows).astype(bf16)
        inner_grad = against(grads, down_weight)
        swish_back = (inner_grad * up_rows * sig * (1.0 + swish_rows * (1.0 - sig))).astype(bf16)
        up_back = (inner_grad * act).astype(bf16)
        down = product(inner, down_weight)
        second_grad = against(swish_back, swish_weight) + against(up_back, up_weight)
        return inner, swish_back, up_back, down, second_grad

    inner_near, swish_back_near, up_back_near, down_near, second_grad_near = feed(
        second_near, grad_rows[:half_rows]
    )
    inner_far, swish_back_far, up_back_far, down_far, second_grad_far = feed(
        second_far, grad_rows[half_rows:]
    )
    second_grad = tensor_reduce(blocks(second_grad_near), blocks(second_grad_far))

    join = lambda near, far: jnp.concatenate(
        [near.reshape(half_rows, near.shape[-1]), far.reshape(half_rows, far.shape[-1])], axis=0
    )
    second = join(second_near, second_far)
    down_share = scatter_grad(join(inner_near, inner_far), grad_rows, False, list(reversed(bits)))
    swish_share = scatter_grad(second, join(swish_back_near, swish_back_far), True, bits)
    up_share = scatter_grad(second, join(up_back_near, up_back_far), True, bits)

    mlp_norm_part = jnp.sum(second_grad * unit_two, axis=0, keepdims=True)
    scaled_two = second_grad * gain_two
    middle_grad = grad_blocks[0].astype(f32) + scale_two * (
        scaled_two - unit_two * jnp.mean(scaled_two * unit_two, axis=-1, keepdims=True)
    )
    rows_near, rows_far = tensor_gather(middle_grad.astype(bf16))

    def branch_back(branch_rows, mixed, first):
        return grid_call(
            branch_back_kernel,
            (half,),
            [
                row_spec(width), fixed((DK, width)), row_spec(DK), row_spec(DK, first), fixed((1, DK)),
                row_spec(DK, first), row_spec(DK, first),
            ],
            [row_spec(DK), row_spec(DK), line(1, DK), square(DK)],
            [
                struct((half_rows, DK), bf16), struct((half_rows, DK), bf16),
                struct((half, 1, DK), f32), struct((half, DK, DK), bf16),
            ],
            2 * half_rows * DK * (DK + width),
            half_rows * (width * 2 + DK * 18) + DK * width * 2 + half * DK * DK * 2,
            branch_rows.reshape(half_rows, width), out_weight, mixed, gate_rows, gain, query_rows, run,
        )

    gate_back_near, mixed_back_near, gain_back_near, state_back_near = branch_back(rows_near, mixed_near, 0)
    gate_back_far, mixed_back_far, gain_back_far, state_back_far = branch_back(rows_far, mixed_far, half)
    outgoing = entering(jnp.concatenate([state_back_near, state_back_far], axis=0), totals, True)

    branch = join(branch_near, branch_far)
    branch_rows = join(rows_near, rows_far)
    gate_back = join(gate_back_near, gate_back_far)
    mixed_back = join(mixed_back_near, mixed_back_far)
    out_share = scatter_grad(branch, branch_rows, False, bits)
    gate_share = scatter_grad(first_norm, gate_back, True, bits)

    query_back, key_back, value_back, logit_back, rank_part, up_part, bias_part = grid_call(
        mix_back_kernel,
        (seq_count,),
        [row_spec(DK)] * 5
        + [square(length), chunked(), chunked(), row_spec(rank), fixed((rank, DK)), fixed((1, DK))],
        [row_spec(DK)] * 4 + [line(rank, length), line(rank, DK), line(1, DK)],
        [struct((all_rows, DK), bf16)] * 4
        + [
            struct((seq_count, rank, length), f32),
            struct((seq_count, rank, DK), f32),
            struct((seq_count, 1, DK), f32),
        ],
        2 * all_rows * DK * (3 * DK + 20 * length),
        all_rows * DK * 20 + seq_count * DK * DK * 4,
        query_rows, key_rows, value_rows, mixed_back, run, scores, incoming, outgoing,
        rank_rows, rank_up, bias,
    )

    rank_part = rank_part + swap(rank_part, "tensor", 1)[jnp.array([1, 0, 3, 2])]
    rank_part = rank_part + swap(rank_part, "tensor", 2)[jnp.array([2, 3, 0, 1])]
    rank_back = rank_part.astype(bf16)

    def first_part(rows):
        return (
            against(query_back[rows], query_weight)
            + against(key_back[rows], key_weight)
            + against(value_back[rows], value_weight)
            + against(gate_back[rows], gate_weight)
        )

    first_far = first_part(slice(half_rows, all_rows))
    first_near = first_part(slice(0, half_rows))
    first_grad = tensor_reduce(blocks(first_near), blocks(first_far))
    first_grad = first_grad + contract(rank_back[0], rank_down, 0, 1)
    query_share = scatter_grad(first_norm, query_back, True, bits)
    key_share = scatter_grad(first_norm, key_back, True, bits)
    value_share = scatter_grad(first_norm, value_back, True, list(reversed(bits)))

    unit_one, scale_one = normed(own_input)
    attn_norm_part = jnp.sum(first_grad * unit_one, axis=0, keepdims=True)
    scaled_one = first_grad * gain_one
    input_rows = middle_grad + scale_one * (
        scaled_one - unit_one * jnp.mean(scaled_one * unit_one, axis=-1, keepdims=True)
    )
    input_grad = in_order(*tensor_gather(input_rows.astype(bf16)))

    down_sum = tensor_reduce(blocks(down_near), blocks(down_far))
    layer_output = in_order(*tensor_gather((middle + down_sum).astype(bf16)))

    rank_down_part = sum(
        contract(rank_back[k], first_norm[k * length : (k + 1) * length], 1, 0) for k in range(seq_count)
    )
    mlp_norm_part = sum_over(mlp_norm_part, "tensor")
    early = scatter_sum(jnp.concatenate([rank_down_part, mlp_norm_part], axis=0))
    attn_norm_share = scatter_sum(sum_over(attn_norm_part, "tensor")).reshape(-1)
    gain_back = sum(gain_back_near) + sum(gain_back_far)
    sums = jnp.concatenate([sum(up_part), sum(bias_part), gain_back], axis=0)
    sums = sum_over(sums, "seq")
    return (
        layer_output,
        input_grad,
        attn_norm_share,
        query_share,
        key_share,
        value_share,
        gate_share,
        early[:rank].T,
        sums[:rank],
        sums[rank],
        sums[rank + 1],
        out_share,
        early[rank],
        swish_share,
        up_share,
        down_share,
    )


def solution(mesh):
    return jax.shard_map(
        local,
        mesh=mesh,
        in_specs=(
            P(None, "seq", None),
            P(),
            P(None, "tensor"),
            P(None, "tensor"),
            P(None, "tensor"),
            P(None, "tensor"),
            P(),
            P(None, "tensor"),
            P("tensor"),
            P("tensor"),
            P("tensor", None),
            P(),
            P(None, "tensor"),
            P(None, "tensor"),
            P("tensor", None),
            P(None, "seq", None),
        ),
        out_specs=(
            P(None, "seq", None),
            P(None, "seq", None),
            P("seq"),
            P("seq", "tensor"),
            P("seq", "tensor"),
            P("seq", "tensor"),
            P("seq", "tensor"),
            P("seq", None),
            P(None, "tensor"),
            P("tensor"),
            P("tensor"),
            P("tensor", "seq"),
            P("seq"),
            P("seq", "tensor"),
            P("seq", "tensor"),
            P("tensor", "seq"),
        ),
        check_vma=False,
    )
```

time: 2840 us -> 1100 us (0.39)
  waiting for transfers between devices: 1900 us -> 487 us
  matrix products: 433 us -> 182 us
  other arithmetic: 231 us -> 66.6 us
  starting transfers between devices: 1.3 us -> 83.8 us
  blocking collectives: 117 us -> 67.5 us
  Pallas kernels: 0 us -> 43.6 us
    all_gather x3 -> x0, waiting for transfers between devices: 1110 us -> none  [the longest x2 1080 us: entering(): everything = jax.tree.map(lambda part: lax.all_gather(part, axis), x)]
    psum x3 -> x0, waiting for transfers between devices: 459 us -> none  [the longest x1 154 us: local(): lax.psum(product(inner_rows, down_weight).astype(jnp.bfloat16), 'tensor')]
    ppermute x0 -> x63, waiting for transfers between devices: none -> 455 us  [swap(): return lax.ppermute(values, axis, [(i, i ^ distance) for i in range(count)])]
    reduce_scatter x9 -> x0, waiting for transfers between devices: 338 us -> none  [the longest x1 112 us: local(): lax.psum_scatter(down_grad.astype(jnp.bfloat16), 'seq', scatter_dimension...]
    dot_general x88 -> x48, matrix products: 433 us -> 182 us  [contract(): lax.dot_general(left, right, (((left_dim,), (right_dim,)), ((), ())), pre...]
    select_n x16 -> x0, other arithmetic: 95 us -> none  [turn(): return jax.tree.map(lambda a, b: jnp.where(reached, a, b), new, before)]
    ppermute x0 -> x63, starting transfers between devices: none -> 62.4 us  [swap(): return lax.ppermute(values, axis, [(i, i ^ distance) for i in range(count)])]
    concatenate x0 -> x15, local copies, waits for them, and re-layouts: none -> 56.4 us  [the longest x10 44.3 us: local(): jnp.concatenate([near.reshape(half_rows, near.shape[-1]), far.reshape(hal...]
  transfers between devices with their start and end apart: 15 -> 67, of which waited for: 12 -> 22; matrix products, arithmetic and copies ran while one was open for 17% -> 31% of each run, Pallas kernels for 0% -> 2%
where the time goes in v1:
time: 1100 us; the launch traced here: 1090 us
  waiting for transfers between devices  487 us (44%)
  matrix products  182 us (17%)
  local copies, waits for them, and re-layouts  153 us (14%)
  starting transfers between devices  83.8 us (8%)
  blocking collectives  67.5 us (6%)
  other arithmetic  66.6 us (6%)
  Pallas kernels  43.6 us (4%)
    ppermute x63, waiting for transfers between devices, swap(): return lax.ppermute(values, axis, [(i, i ^ distance) for i in range(count)])  455 us
    dot_general x48, matrix products, contract(): lax.dot_general(left, right, (((left_dim,), (right_dim,)), ((), ())), pre...  182 us
    all_gather x1, blocking collectives, spread_totals(): return lax.all_gather(values, axis)  67.5 us
    ppermute x63, starting transfers between devices, swap(): return lax.ppermute(values, axis, [(i, i ^ distance) for i in range(count)])  62.4 us
    concatenate x10, local copies, waits for them, and re-layouts, local(): jnp.concatenate([near.reshape(half_rows, near.shape[-1]), far.reshape(hal...  44.3 us
    pallas_call x9, Pallas kernels, grid_call(): pl.pallas_call(kernel, grid=grid, in_specs=in_specs, out_specs=out_specs,...  43.6 us
    unnamed x292, local copies, waits for them, and re-layouts  40.2 us
    all_to_all x2, waiting for transfers between devices, entering(): return lax.all_to_all(carried, 'seq', 0, 0)  31.7 us
  transfers between devices with their start and end apart: 67, of which 22 were waited for; matrix products, arithmetic and copies ran while one was open for 31% of the time, Pallas kernels for 2%

profile of v1, /device:TPU:0, one launch (start us, length us, event | category | flops | bytes accessed | tf_op | source)
XLA Modules:
  0.0 1087.1 jit_solution(13854568871229690212)
XLA Ops:
  7.0 7.3 fusion.2
  21.2 6.6 shard_map.297
  31.6 7.3 all-to-all-start
  39.8 67.5 %all-gather = f32[32,1,512]{2,1,0:T(1,128)S(1)} all-gather(f32[4,1,512]{2,1,0:T(1,128)S(1)} %slice.182), channel_id=2, replica_groups=mesh['seq'=8,'tensor'=4] {'seq'}, dimensions={0}, use_global_device_ids=true | all-gather | bytes 73728 | tf_op jit(solution)/shard_map/all_gather | solution.py:256
  127.6 31.7 %all-to-all-done.1.state_ref = bf16[8,4,64,512]{3,2,1,0:T(8,128)(2,1)} async-done(((bf16[8,4,64,512]{3,2,1,0:T(8,128)(2,1)}), bf16[8,4,64,512]{3,2,1,0:T(8,128)(2,1)}, u32[]{:S(2)}, u32[]{:S(2)}) %all-to-all-start.1) | async-done | bytes 2097184 | tf_op jit(solution)/shard_map/all_to_all | solution.py:277
  209.3 7.1 constant_dynamic-slice_fusion.3
  220.9 6.7 fusion.33
  237.2 8.1 fusion.37
  260.1 9.6 collective-permute-done.5
  281.0 8.7 fusion.90
  289.7 6.5 multiply_convert_fusion.1
  301.2 7.4 convolution_add_fusion
  316.1 6.3 convolution_convert_fusion
  327.8 20.9 %collective-permute-done.14 = bf16[256,2048]{1,0:T(8,128)(2,1)S(1)} collective-permute-done((bf16[256,2048]{1,0:T(8,128)(2,1)S(1)}, bf16[256,2048]{1,0:T(8,128)(2,1)S(1)}, u32[]{:S(2)}, u32[]{:S(2)}) %collective-permute-start.14) | collective-permute-done | bytes 1048608 | tf_op jit(solution)/shard_map/ppermute | solution.py:248
  349.6 21.1 %collective-permute-done.8 = bf16[256,2048]{1,0:T(8,128)(2,1)S(1)} collective-permute-done((bf16[256,2048]{1,0:T(8,128)(2,1)S(1)}, bf16[256,2048]{1,0:T(8,128)(2,1)S(1)}, u32[]{:S(2)}, u32[]{:S(2)}) %collective-permute-start.8) | collective-permute-done | bytes 1048608 | tf_op jit(solution)/shard_map/ppermute | solution.py:248
  396.3 6.1 copy.117
  406.9 6.3 copy.118
  415.5 34.2 %collective-permute-done.60 = bf16[1408,1024]{0,1:T(8,128)(2,1)} collective-permute-done((bf16[1408,1024]{0,1:T(8,128)(2,1)}, bf16[1408,1024]{0,1:T(8,128)(2,1)}, u32[]{:S(2)}, u32[]{:S(2)}) %collective-permute-start.60) | collective-permute-done | bytes 2883616 | tf_op jit(solution)/shard_map/ppermute | solution.py:248
  449.6 6.8 add_convert_fusion
  470.9 6.1 copy.113
  493.5 6.1 copy.114
  548.7 87.1 %collective-permute-done.62 = bf16[1408,256]{1,0:T(8,128)(2,1)S(1)} collective-permute-done((bf16[1408,256]{1,0:T(8,128)(2,1)S(1)}, bf16[1408,256]{1,0:T(8,128)(2,1)S(1)}, u32[]{:S(2)}, u32[]{:S(2)}) %collective-permute-start.62) | collective-permute-done | bytes 720928 | tf_op jit(solution)/shard_map/ppermute | solution.py:248
  647.0 72.7 %collective-permute-done.40 = bf16[1024,512]{1,0:T(8,128)(2,1)} collective-permute-done((bf16[1024,512]{1,0:T(8,128)(2,1)}, bf16[1024,512]{1,0:T(8,128)(2,1)}, u32[]{:S(2)}, u32[]{:S(2)}) %collective-permute-start.40) | collective-permute-done | bytes 1048608 | tf_op jit(solution)/shard_map/ppermute | solution.py:248
  755.8 83.2 %collective-permute-done.53 = bf16[512,256]{1,0:T(8,128)(2,1)S(1)} collective-permute-done((bf16[512,256]{1,0:T(8,128)(2,1)S(1)}, bf16[512,256]{1,0:T(8,128)(2,1)S(1)}, u32[]{:S(2)}, u32[]{:S(2)}) %collective-permute-start.53) | collective-permute-done | bytes 262176 | tf_op jit(solution)/shard_map/ppermute | solution.py:248
  846.8 45.1 %collective-permute-done.59 = bf16[256,1408]{1,0:T(8,128)(2,1)S(1)} collective-permute-done((bf16[256,1408]{1,0:T(8,128)(2,1)S(1)}, bf16[256,1408]{1,0:T(8,128)(2,1)S(1)}, u32[]{:S(2)}, u32[]{:S(2)}) %collective-permute-start.59) | collective-permute-done | bytes 720928 | tf_op jit(solution)/shard_map/ppermute | solution.py:248
  893.2 14.1 %collective-permute-done.56 = bf16[256,1408]{1,0:T(8,128)(2,1)S(1)} collective-permute-done((bf16[256,1408]{1,0:T(8,128)(2,1)S(1)}, bf16[256,1408]{1,0:T(8,128)(2,1)S(1)}, u32[]{:S(2)}, u32[]{:S(2)}) %collective-permute-start.56) | collective-permute-done | bytes 720928 | tf_op jit(solution)/shard_map/ppermute | solution.py:248
  908.5 13.1 %shard_map.305 = (bf16[1024,512]{1,0:T(8,128)(2,1)S(1)}, bf16[1024,512]{1,0:T(8,128)(2,1)S(1)}, bf16[1024,512]{1,0:T(8,128)(2,1)S(1)}, bf16[1024,512]{1,0:T(8,12...) custom-call(bf16[1024,512]{1,0:T(8,128)(2,1)} %copy-done.3, ...), custom_call_target="tpu_custom_call" | custom-call | flops 6979321856 | bytes 14680064 | tf_op jit(solution)/shard_map/pallas_call | solution.py:231
  967.3 23.1 %collective-permute-done.45 = f32[17,4,256]{2,1,0:T(4,128)S(1)} collective-permute-done((f32[17,4,256]{2,1,0:T(4,128)S(1)}, f32[17,4,256]{2,1,0:T(4,128)S(1)}, u32[]{:S(2)}, u32[]{:S(2)}) %collective-permute-start.45) | collective-permute-done | bytes 69664 | tf_op jit(solution)/shard_map/ppermute | solution.py:248
  990.6 7.1 add_add_fusion
  1023.0 8.9 collective-permute-done.35
  1040.4 8.2 collective-permute-done.32
  1051.5 13.2 %collective-permute-done.27 = f32[1,2048]{1,0:T(1,128)S(1)} collective-permute-done((f32[1,2048]{1,0:T(1,128)S(1)}, f32[1,2048]{1,0:T(1,128)S(1)}, u32[]{:S(2)}, u32[]{:S(2)}) %collective-permute-start.27) | collective-permute-done | bytes 8224 | tf_op jit(solution)/shard_map/ppermute | solution.py:248
  (598 shorter events, 419.9 us)
Async XLA Ops:
  31.6 75.6 %all-to-all-start = ((bf16[8,4,64,512]{3,2,1,0:T(8,128)(2,1)}), bf16[8,4,64,512]{3,2,1,0:T(8,128)(2,1)}, u32[]{:S(2)}, u32[]{:S(2)}) async-start(bf16[8,4,64,512]{3,2,1,0:T(8,128)(2,1)} %bitcast.308), calls=%async_computation | async-start | bytes 4194304 | tf_op jit(solution)/shard_map/all_to_all | solution.py:264
  111.3 48.1 %all-to-all-start.1 = ((bf16[8,4,64,512]{3,2,1,0:T(8,128)(2,1)}), bf16[8,4,64,512]{3,2,1,0:T(8,128)(2,1)}, u32[]{:S(2)}, u32[]{:S(2)}) async-start(bf16[8,4,64,512]{3,2,1,0:T(8,128)(2,1)} %copy-done.5), calls=%async_computation.1 | async-start | bytes 4194304 | tf_op jit(solution)/shard_map/all_to_all | solution.py:277
  273.3 54.5 %collective-permute-start.12 = (bf16[256,2048]{1,0:T(8,128)(2,1)S(1)}, bf16[256,2048]{1,0:T(8,128)(2,1)S(1)}, u32[]{:S(2)}, u32[]{:S(2)}) collective-permute-start(bf16[256,2048]{1,0:T(8,128)(2,1)S(1)} %slice.293), channel_id=1, source_target_pairs={{0,1},{1,0},{2,3},{3,2},{4,5},{5,4},{6,7},{7,6},{8,9},{9,8},{10,11... | collective-permute-start | bytes 3145736 | tf_op jit(solution)/shard_map/ppermute | solution.py:248
  280.2 69.4 %collective-permute-start.4 = (bf16[256,2048]{1,0:T(8,128)(2,1)S(1)}, bf16[256,2048]{1,0:T(8,128)(2,1)}, u32[]{:S(2)}, u32[]{:S(2)}) collective-permute-start(bf16[256,2048]{1,0:T(8,128)(2,1)S(1)} %slice.295), channel_id=1, source_target_pairs={{0,1},{1,0},{2,3},{3,2},{4,5},{5,4},{6,7},{7,6},{8,9},{9,8},{10,11... | collective-permute-start | bytes 3145736 | tf_op jit(solution)/shard_map/ppermute | solution.py:248
  322.3 127.3 %collective-permute-start.60 = (bf16[1408,1024]{0,1:T(8,128)(2,1)}, bf16[1408,1024]{0,1:T(8,128)(2,1)}, u32[]{:S(2)}, u32[]{:S(2)}) collective-permute-start(bf16[1408,1024]{0,1:T(8,128)(2,1)} %convolution_convert_fusion), channel_id=1, source_target_pairs={{0,16},{4,20},{8,24},{12,28},{16,0},{20,4},{24,8},{28,12},{1,17},{... | collective-permute-start | bytes 8650760 | tf_op jit(solution)/shard_map/ppermute | solution.py:248
  324.6 46.2 %collective-permute-start.8 = (bf16[256,2048]{1,0:T(8,128)(2,1)S(1)}, bf16[256,2048]{1,0:T(8,128)(2,1)S(1)}, u32[]{:S(2)}, u32[]{:S(2)}) collective-permute-start(bf16[256,2048]{1,0:T(8,128)(2,1)S(1)} %fusion.27), channel_id=1, source_target_pairs={{0,2},{1,3},{2,0},{3,1},{4,6},{5,7},{6,4},{7,5},{8,10},{9,11},{10,... | collective-permute-start | bytes 3145736 | tf_op jit(solution)/shard_map/ppermute | solution.py:248
  375.3 39.8 %collective-permute-start.16 = (bf16[256,2048]{1,0:T(8,128)(2,1)}, bf16[256,2048]{1,0:T(8,128)(2,1)}, u32[]{:S(2)}, u32[]{:S(2)}) collective-permute-start(bf16[256,2048]{1,0:T(8,128)(2,1)} %get-tuple-element.62), channel_id=1, source_target_pairs={{0,2},{1,3},{2,0},{3,1},{4,6},{5,7},{6,4},{7,5},{8,10},{9,11},{10,... | collective-permute-start | bytes 3145736 | tf_op jit(solution)/shard_map/ppermute | solution.py:248
  413.2 50.1 %collective-permute-start.15 = (bf16[256,2048]{1,0:T(8,128)(2,1)}, bf16[256,2048]{1,0:T(8,128)(2,1)}, u32[]{:S(2)}, u32[]{:S(2)}) collective-permute-start(bf16[256,2048]{1,0:T(8,128)(2,1)} %get-tuple-element.62), channel_id=1, source_target_pairs={{0,1},{1,0},{2,3},{3,2},{4,5},{5,4},{6,7},{7,6},{8,9},{9,8},{10,11... | collective-permute-start | bytes 3145736 | tf_op jit(solution)/shard_map/ppermute | solution.py:248
  413.3 63.8 %collective-permute-start.10 = (bf16[256,2048]{1,0:T(8,128)(2,1)}, bf16[256,2048]{1,0:T(8,128)(2,1)}, u32[]{:S(2)}, u32[]{:S(2)}) collective-permute-start(bf16[256,2048]{1,0:T(8,128)(2,1)} %get-tuple-element.99), channel_id=1, source_target_pairs={{0,2},{1,3},{2,0},{3,1},{4,6},{5,7},{6,4},{7,5},{8,10},{9,11},{10,... | collective-permute-start | bytes 3145736 | tf_op jit(solution)/shard_map/ppermute | solution.py:248
  414.9 128.2 %collective-permute-start.9 = (bf16[256,2048]{1,0:T(8,128)(2,1)}, bf16[256,2048]{1,0:T(8,128)(2,1)}, u32[]{:S(2)}, u32[]{:S(2)}) collective-permute-start(bf16[256,2048]{1,0:T(8,128)(2,1)} %get-tuple-element.99), channel_id=1, source_target_pairs={{0,1},{1,0},{2,3},{3,2},{4,5},{5,4},{6,7},{7,6},{8,9},{9,8},{10,11... | collective-permute-start | bytes 3145736 | tf_op jit(solution)/shard_map/ppermute | solution.py:248
  415.1 70.9 %collective-permute-start.17 = (bf16[256,2048]{1,0:T(8,128)(2,1)}, bf16[256,2048]{1,0:T(8,128)(2,1)}, u32[]{:S(2)}, u32[]{:S(2)}) collective-permute-start(bf16[256,2048]{1,0:T(8,128)(2,1)} %collective-permute-done.16), channel_id=1, source_target_pairs={{0,1},{1,0},{2,3},{3,2},{4,5},{5,4},{6,7},{7,6},{8,9},{9,8},{10,11... | collective-permute-start | bytes 3145736 | tf_op jit(solution)/shard_map/ppermute | solution.py:248
  460.8 77.2 %collective-permute-start.61 = (bf16[1408,2,256]{2,0,1:T(8,128)(2,1)}, bf16[1408,2,256]{2,0,1:T(8,128)(2,1)}, u32[]{:S(2)}, u32[]{:S(2)}) collective-permute-start(bf16[1408,2,256]{2,0,1:T(8,128)(2,1)} %bitcast.339), channel_id=1, source_target_pairs={{0,8},{4,12},{8,0},{12,4},{16,24},{20,28},{24,16},{28,20},{1,9},{5... | collective-permute-start | bytes 4325384 | tf_op jit(solution)/shard_map/ppermute | solution.py:248
  477.1 66.0 %collective-permute-start.11 = (bf16[256,2048]{1,0:T(8,128)(2,1)}, bf16[256,2048]{1,0:T(8,128)(2,1)}, u32[]{:S(2)}, u32[]{:S(2)}) collective-permute-start(bf16[256,2048]{1,0:T(8,128)(2,1)} %collective-permute-done.10), channel_id=1, source_target_pairs={{0,1},{1,0},{2,3},{3,2},{4,5},{5,4},{6,7},{7,6},{8,9},{9,8},{10,11... | collective-permute-start | bytes 3145736 | tf_op jit(solution)/shard_map/ppermute | solution.py:248
  509.9 215.5 %collective-permute-start.57 = (bf16[1024,1408]{1,0:T(8,128)(2,1)}, bf16[1024,1408]{1,0:T(8,128)(2,1)}, u32[]{:S(2)}, u32[]{:S(2)}) collective-permute-start(bf16[1024,1408]{1,0:T(8,128)(2,1)} %convolution_convert_fusion.1), channel_id=1, source_target_pairs={{0,4},{4,0},{8,12},{12,8},{16,20},{20,16},{24,28},{28,24},{1,5},{5... | collective-permute-start | bytes 8650760 | tf_op jit(solution)/shard_map/ppermute | solution.py:248
  514.1 122.9 %collective-permute-start.51 = (bf16[512,1024]{1,0:T(8,128)(2,1)}, bf16[512,1024]{1,0:T(8,128)(2,1)}, u32[]{:S(2)}, u32[]{:S(2)}) collective-permute-start(bf16[512,1024]{1,0:T(8,128)(2,1)} %convolution_convert_fusion.3), channel_id=1, source_target_pairs={{0,4},{4,0},{8,12},{12,8},{16,20},{20,16},{24,28},{28,24},{1,5},{5... | collective-permute-start | bytes 3145736 | tf_op jit(solution)/shard_map/ppermute | solution.py:248
  523.3 217.1 %all-to-all-start.2 = ((bf16[8,4,64,512]{3,2,1,0:T(8,128)(2,1)}), bf16[8,4,64,512]{3,2,1,0:T(8,128)(2,1)}, u32[]{:S(2)}, u32[]{:S(2)}) async-start(bf16[8,4,64,512]{3,2,1,0:T(8,128)(2,1)} %bitcast.307), calls=%async_computation.2 | async-start | bytes 4194304 | tf_op jit(solution)/shard_map/all_to_all | solution.py:264
  539.9 95.8 %collective-permute-start.62 = (bf16[1408,256]{1,0:T(8,128)(2,1)S(1)}, bf16[1408,256]{1,0:T(8,128)(2,1)S(1)}, u32[]{:S(2)}, u32[]{:S(2)}) collective-permute-start(bf16[1408,256]{1,0:T(8,128)(2,1)S(1)} %dynamic-slice_bitcast_fusion.2), channel_id=1, source_target_pairs={{0,4},{4,0},{8,12},{12,8},{16,20},{20,16},{24,28},{28,24},{1,5},{5... | collective-permute-start | bytes 2162696 | tf_op jit(solution)/shard_map/ppermute | solution.py:248
  543.0 191.3 %collective-permute-start.54 = (bf16[1024,1408]{1,0:T(8,128)(2,1)}, bf16[1024,1408]{1,0:T(8,128)(2,1)}, u32[]{:S(2)}, u32[]{:S(2)}) collective-permute-start(bf16[1024,1408]{1,0:T(8,128)(2,1)} %convolution_convert_fusion.2), channel_id=1, source_target_pairs={{0,4},{4,0},{8,12},{12,8},{16,20},{20,16},{24,28},{28,24},{1,5},{5... | collective-permute-start | bytes 8650760 | tf_op jit(solution)/shard_map/ppermute | solution.py:248
  543.1 176.6 %collective-permute-start.40 = (bf16[1024,512]{1,0:T(8,128)(2,1)}, bf16[1024,512]{1,0:T(8,128)(2,1)}, u32[]{:S(2)}, u32[]{:S(2)}) collective-permute-start(bf16[1024,512]{1,0:T(8,128)(2,1)} %convolution_convert_fusion.4), channel_id=1, source_target_pairs={{0,4},{4,0},{8,12},{12,8},{16,20},{20,16},{24,28},{28,24},{1,5},{5... | collective-permute-start | bytes 3145736 | tf_op jit(solution)/shard_map/ppermute | solution.py:248
  645.0 80.2 %collective-permute-start.52 = (bf16[512,2,256]{2,0,1:T(8,128)(2,1)S(1)}, bf16[512,2,256]{2,0,1:T(8,128)(2,1)S(1)}, u32[]{:S(2)}, u32[]{:S(2)}) collective-permute-start(bf16[512,2,256]{2,0,1:T(8,128)(2,1)S(1)} %bitcast.352), channel_id=1, source_target_pairs={{0,8},{4,12},{8,0},{12,4},{16,24},{20,28},{24,16},{28,20},{1,9},{5... | collective-permute-start | bytes 1572872 | tf_op jit(solution)/shard_map/ppermute | solution.py:248
  733.2 106.7 %collective-permute-start.58 = (bf16[2,256,1408]{2,1,0:T(8,128)(2,1)}, bf16[2,256,1408]{2,1,0:T(8,128)(2,1)}, u32[]{:S(2)}, u32[]{:S(2)}) collective-permute-start(bf16[2,256,1408]{2,1,0:T(8,128)(2,1)} %dynamic-slice_bitcast_fusion), channel_id=1, source_target_pairs={{0,8},{4,12},{8,0},{12,4},{16,24},{20,28},{24,16},{28,20},{1,9},{5... | collective-permute-start | bytes 4325384 | tf_op jit(solution)/shard_map/ppermute | solution.py:248
  744.4 164.1 %all-to-all-start.3 = ((bf16[8,4,64,512]{3,2,1,0:T(8,128)(2,1)}), bf16[8,4,64,512]{3,2,1,0:T(8,128)(2,1)}, u32[]{:S(2)}, u32[]{:S(2)}) async-start(bf16[8,4,64,512]{3,2,1,0:T(8,128)(2,1)} %copy-done.4), calls=%async_computation.3 | async-start | bytes 4194304 | tf_op jit(solution)/shard_map/all_to_all | solution.py:277
  750.5 94.7 %collective-permute-start.55 = (bf16[2,256,1408]{2,1,0:T(8,128)(2,1)S(1)}, bf16[2,256,1408]{2,1,0:T(8,128)(2,1)S(1)}, u32[]{:S(2)}, u32[]{:S(2)}) collective-permute-start(bf16[2,256,1408]{2,1,0:T(8,128)(2,1)S(1)} %dynamic-slice_bitcast_fusion.1), channel_id=1, source_target_pairs={{0,8},{4,12},{8,0},{12,4},{16,24},{20,28},{24,16},{28,20},{1,9},{5... | collective-permute-start | bytes 4325384 | tf_op jit(solution)/shard_map/ppermute | solution.py:248
  752.6 86.4 %collective-permute-start.53 = (bf16[512,256]{1,0:T(8,128)(2,1)S(1)}, bf16[512,256]{1,0:T(8,128)(2,1)S(1)}, u32[]{:S(2)}, u32[]{:S(2)}) collective-permute-start(bf16[512,256]{1,0:T(8,128)(2,1)S(1)} %dynamic-slice_bitcast_fusion.9), channel_id=1, source_target_pairs={{0,16},{4,20},{8,24},{12,28},{16,0},{20,4},{24,8},{28,12},{1,17},{... | collective-permute-start | bytes 786440 | tf_op jit(solution)/shard_map/ppermute | solution.py:248
  755.2 90.7 %collective-permute-start.42 = (bf16[256,512]{1,0:T(8,128)(2,1)S(1)}, bf16[256,512]{1,0:T(8,128)(2,1)S(1)}, u32[]{:S(2)}, u32[]{:S(2)}) collective-permute-start(bf16[256,512]{1,0:T(8,128)(2,1)S(1)} %dynamic-slice_bitcast_fusion.10), channel_id=1, source_target_pairs={{0,16},{4,20},{8,24},{12,28},{16,0},{20,4},{24,8},{28,12},{1,17},{... | collective-permute-start | bytes 786440 | tf_op jit(solution)/shard_map/ppermute | solution.py:248
  841.8 50.1 %collective-permute-start.59 = (bf16[256,1408]{1,0:T(8,128)(2,1)S(1)}, bf16[256,1408]{1,0:T(8,128)(2,1)S(1)}, u32[]{:S(2)}, u32[]{:S(2)}) collective-permute-start(bf16[256,1408]{1,0:T(8,128)(2,1)S(1)} %dynamic-slice_bitcast_fusion.3), channel_id=1, source_target_pairs={{0,16},{4,20},{8,24},{12,28},{16,0},{20,4},{24,8},{28,12},{1,17},{... | collective-permute-start | bytes 2162696 | tf_op jit(solution)/shard_map/ppermute | solution.py:248
  845.7 61.6 %collective-permute-start.56 = (bf16[256,1408]{1,0:T(8,128)(2,1)S(1)}, bf16[256,1408]{1,0:T(8,128)(2,1)S(1)}, u32[]{:S(2)}, u32[]{:S(2)}) collective-permute-start(bf16[256,1408]{1,0:T(8,128)(2,1)S(1)} %dynamic-slice_bitcast_fusion.4), channel_id=1, source_target_pairs={{0,16},{4,20},{8,24},{12,28},{16,0},{20,4},{24,8},{28,12},{1,17},{... | collective-permute-start | bytes 2162696 | tf_op jit(solution)/shard_map/ppermute | solution.py:248
  938.3 65.0 %collective-permute-start.37 = (bf16[1024,512]{1,0:T(8,128)(2,1)}, bf16[1024,512]{1,0:T(8,128)(2,1)}, u32[]{:S(2)}, u32[]{:S(2)}) collective-permute-start(bf16[1024,512]{1,0:T(8,128)(2,1)} %convolution_convert_fusion.5), channel_id=1, source_target_pairs={{0,16},{4,20},{8,24},{12,28},{16,0},{20,4},{24,8},{28,12},{1,17},{... | collective-permute-start | bytes 3145736 | tf_op jit(solution)/shard_map/ppermute | solution.py:248
  938.3 69.6 %collective-permute-start.34 = (bf16[1024,512]{1,0:T(8,128)(2,1)}, bf16[1024,512]{1,0:T(8,128)(2,1)}, u32[]{:S(2)}, u32[]{:S(2)}) collective-permute-start(bf16[1024,512]{1,0:T(8,128)(2,1)} %convolution_convert_fusion.6), channel_id=1, source_target_pairs={{0,4},{4,0},{8,12},{12,8},{16,20},{20,16},{24,28},{28,24},{1,5},{5... | collective-permute-start | bytes 3145736 | tf_op jit(solution)/shard_map/ppermute | solution.py:248
  939.0 73.6 %collective-permute-start.31 = (bf16[1024,512]{1,0:T(8,128)(2,1)}, bf16[1024,512]{1,0:T(8,128)(2,1)}, u32[]{:S(2)}, u32[]{:S(2)}) collective-permute-start(bf16[1024,512]{1,0:T(8,128)(2,1)} %convolution_convert_fusion.7), channel_id=1, source_target_pairs={{0,4},{4,0},{8,12},{12,8},{16,20},{20,16},{24,28},{28,24},{1,5},{5... | collective-permute-start | bytes 3145736 | tf_op jit(solution)/shard_map/ppermute | solution.py:248
  1021.7 45.6 %collective-permute-start.39 = (bf16[256,512]{1,0:T(8,128)(2,1)}, bf16[256,512]{1,0:T(8,128)(2,1)}, u32[]{:S(2)}, u32[]{:S(2)}) collective-permute-start(bf16[256,512]{1,0:T(8,128)(2,1)} %dynamic-slice_bitcast_fusion.11), channel_id=1, source_target_pairs={{0,4},{4,0},{8,12},{12,8},{16,20},{20,16},{24,28},{28,24},{1,5},{5... | collective-permute-start | bytes 786440 | tf_op jit(solution)/shard_map/ppermute | solution.py:248
  1032.2 39.0 %collective-permute-start.36 = (bf16[256,512]{1,0:T(8,128)(2,1)S(1)}, bf16[256,512]{1,0:T(8,128)(2,1)}, u32[]{:S(2)}, u32[]{:S(2)}) collective-permute-start(bf16[256,512]{1,0:T(8,128)(2,1)S(1)} %dynamic-slice_bitcast_fusion.12), channel_id=1, source_target_pairs={{0,16},{4,20},{8,24},{12,28},{16,0},{20,4},{24,8},{28,12},{1,17},{... | collective-permute-start | bytes 786440 | tf_op jit(solution)/shard_map/ppermute | solution.py:248
  (176 other events, 2214.2 us)

commit v2 on v1

v2 whole, which is shorter than its diff:
```python
import functools

import jax
import jax.numpy as jnp
from jax import lax
from jax.experimental import pallas as pl
from jax.experimental.pallas import tpu as pltpu
from jax.sharding import PartitionSpec as P

DK = 512
BLOCK = 64
EXTRA = 16
ROWS = 256
COST = 1024
VMEM = 48 * 1024 * 1024

bf16 = jnp.bfloat16
f32 = jnp.float32
highest_precision = lax.Precision.HIGHEST
epsilon = 1e-06


def contract(left, right, left_dim, right_dim, precision=None):
    return lax.dot_general(
        left,
        right,
        (((left_dim,), (right_dim,)), ((), ())),
        preferred_element_type=f32,
        precision=precision,
    )


def product(left, right):
    return contract(left, right, 1, 0)


def across(left, right):
    return contract(left, right, 0, 0)


def against(left, right):
    return contract(left, right, 1, 1)


def forget_logits(rank_ref, up_ref, bias_ref):
    return product(rank_ref[...], up_ref[...]) + bias_ref[...].astype(f32)


def positions(count):
    rows = lax.broadcasted_iota(jnp.int32, (count, count), 0)
    cols = lax.broadcasted_iota(jnp.int32, (count, count), 1)
    return rows, cols


def spread(pieces, size):
    width = pieces[0].shape[1]
    return jnp.concatenate([jnp.broadcast_to(piece, (size, width)) for piece in pieces], axis=0)


def scaled_pair(level, query_scaled, key_rows, run):
    count = run.shape[0]
    if level == 0:
        starts = range(0, count, BLOCK)
        center = spread([run[s + BLOCK // 2 : s + BLOCK // 2 + 1] for s in starts], BLOCK)
        query_factor = jnp.exp(run - center)
        key_factor = jnp.exp(center - run)
        return query_scaled * query_factor, key_rows * key_factor, query_factor, key_factor
    group = BLOCK << level
    half = group // 2
    center = spread([run[s + half - 1 : s + half] for s in range(0, count, group)], group)
    place = lax.broadcasted_iota(jnp.int32, run.shape, 0)
    right = (place % group) >= half
    gap = run - center
    query_factor = jnp.where(right, jnp.exp(jnp.where(right, gap, 0.0)), 0.0)
    key_factor = jnp.where(right, 0.0, jnp.exp(jnp.where(right, 0.0, -gap)))
    return query_scaled * query_factor, key_rows * key_factor, query_factor, key_factor


def level_mask(level, rows, cols):
    if level == 0:
        return (rows // BLOCK == cols // BLOCK) & (cols <= rows)
    group = BLOCK << level
    half = group // 2
    return (rows // group == cols // group) & (rows % group >= half) & (cols % group < half)


def level_count(count):
    levels = 1
    while (BLOCK << (levels - 1)) < count:
        levels += 1
    return levels


def norm_kernel(order_ref, input_ref, grad_ref, gain_ref, norm_ref, rows_ref):
    values = input_ref[0].astype(f32)
    scale = lax.rsqrt(jnp.mean(values * values, axis=-1, keepdims=True) + epsilon)
    norm_ref[...] = (values * scale * gain_ref[...].astype(f32)).astype(bf16)
    rows_ref[...] = grad_ref[0]


def decay_kernel(rank_ref, up_ref, bias_ref, run_ref):
    logits = forget_logits(rank_ref, up_ref, bias_ref)
    decays = (jnp.minimum(logits, 0.0) - jnp.log1p(jnp.exp(-jnp.abs(logits)))) * (1.0 / 16.0)
    rows, cols = positions(decays.shape[0])
    run_ref[...] = contract((cols <= rows).astype(f32), decays, 1, 0, highest_precision)


def state_kernel(key_ref, value_ref, run_ref, state_ref):
    run = run_ref[...]
    count = run.shape[0]
    total = run[count - 1 : count]
    left = (key_ref[...].astype(f32) * jnp.exp(total - run)).astype(bf16)
    devices, _, rows, _ = state_ref.shape
    state = across(value_ref[...], left).astype(bf16).reshape(devices, rows - EXTRA, DK)
    high = total.astype(bf16)
    rest = total - high.astype(f32)
    middle = rest.astype(bf16)
    low = (rest - middle.astype(f32)).astype(bf16)
    place = lax.broadcasted_iota(jnp.int32, (EXTRA, DK), 0)
    lines = jnp.zeros((EXTRA, DK), f32)
    for at, line in enumerate((high, middle, low)):
        lines = jnp.where(place == at, line.astype(f32), lines)
    lines = lines.astype(bf16)
    for at in range(devices):
        state_ref[at, 0, : rows - EXTRA] = state[at]
        state_ref[at, 0, rows - EXTRA :] = lines


def score_kernel(query_ref, key_ref, run_ref, score_ref):
    run = run_ref[...]
    query_scaled = query_ref[...].astype(f32) * DK ** (-0.5)
    key_rows = key_ref[...].astype(f32)
    rows, cols = positions(run.shape[0])
    scores = jnp.zeros(rows.shape, f32)
    for level in range(level_count(run.shape[0])):
        left, right, _, _ = scaled_pair(level, query_scaled, key_rows, run)
        scores = jnp.where(
            level_mask(level, rows, cols), against(left.astype(bf16), right.astype(bf16)), scores
        )
    score_ref[0] = scores.astype(bf16)


def whole_state(ref):
    return ref[...].reshape(DK, DK)


def faded_queries(query_ref, run_ref):
    return (query_ref[...].astype(f32) * DK ** (-0.5) * jnp.exp(run_ref[...])).astype(bf16)


def mix_kernel(query_ref, value_ref, run_ref, score_ref, state_ref, gate_ref, gain_ref, mixed_ref, branch_ref):
    faded = faded_queries(query_ref, run_ref)
    mixed = product(score_ref[0], value_ref[...]) + against(faded, whole_state(state_ref))
    mixed_ref[...] = mixed
    scale = lax.rsqrt(jnp.mean(mixed * mixed, axis=-1, keepdims=True) + epsilon)
    gate = gate_ref[...]
    branch_ref[...] = (
        mixed * scale * gain_ref[...].astype(f32) * (gate * jax.nn.sigmoid(gate))
    ).astype(bf16)


def branch_back_kernel(
    first_ref, second_ref, weight_ref, mixed_ref, gate_ref, gain_ref, query_ref, run_ref,
    gate_back_ref, mixed_back_ref, gain_back_ref, state_back_ref,
):
    branch_grad = against(either(first_ref, second_ref), weight_ref[...])
    mixed = mixed_ref[...]
    scale = lax.rsqrt(jnp.mean(mixed * mixed, axis=-1, keepdims=True) + epsilon)
    unit = mixed * scale
    gate = gate_ref[...]
    gain = gain_ref[...].astype(f32)
    sig = jax.nn.sigmoid(gate)
    gate_back_ref[...] = (branch_grad * unit * gain * sig * (1.0 + gate * (1.0 - sig))).astype(bf16)
    shaped_grad = branch_grad * (gate * sig)
    gain_back_ref[0] = jnp.sum(shaped_grad * unit, axis=0, keepdims=True)
    unit_grad = shaped_grad * gain
    mixed_grad = scale * (unit_grad - unit * jnp.mean(unit_grad * unit, axis=-1, keepdims=True))
    mixed_back = mixed_grad.astype(bf16)
    mixed_back_ref[...] = mixed_back
    faded = faded_queries(query_ref, run_ref)
    state_back_ref[...] = across(mixed_back, faded).astype(bf16).reshape(state_back_ref.shape)


def ordered_sum(mask, values):
    high = values.astype(bf16)
    low = (values - high.astype(f32)).astype(bf16)
    ones = mask.astype(f32).astype(bf16)
    return product(ones, high) + product(ones, low)


def mix_back_kernel(
    query_ref, key_ref, value_ref, grad_ref, run_ref, score_ref, state_ref, state_back_ref,
    rank_ref, up_ref, bias_ref,
    query_back_ref, key_back_ref, value_back_ref, rank_back_ref, up_back_ref, bias_back_ref,
):
    run = run_ref[...]
    count = run.shape[0]
    query_scaled = query_ref[...].astype(f32) * DK ** (-0.5)
    key_rows = key_ref[...].astype(f32)
    values = value_ref[...]
    grads = grad_ref[...]
    state = whole_state(state_ref)
    state_back = whole_state(state_back_ref)
    rows, cols = positions(count)
    pairs = against(grads, values)

    closing = run[count - 1 : count]
    fade_in = jnp.exp(run)
    fade_out = jnp.exp(closing - run)
    kept = (key_rows * fade_out).astype(bf16)
    value_back_ref[...] = (across(score_ref[0], grads) + against(kept, state_back)).astype(bf16)

    from_state = product(grads, state)
    to_state = product(values, state_back)
    query_back = fade_in * from_state
    key_back = fade_out * to_state
    decay_back = jnp.exp(closing) * jnp.sum(
        state.astype(f32) * state_back.astype(f32), axis=0, keepdims=True
    )
    decay_back = decay_back + ordered_sum(cols >= rows, query_scaled * fade_in * from_state)
    decay_back = decay_back + ordered_sum(cols < rows, key_rows * fade_out * to_state)
    for level in range(level_count(count)):
        left, right, query_factor, key_factor = scaled_pair(level, query_scaled, key_rows, run)
        left, right = left.astype(bf16), right.astype(bf16)
        here = jnp.where(level_mask(level, rows, cols), pairs, 0.0).astype(bf16)
        to_query = product(here, right)
        to_key = across(here, left)
        query_back = query_back + query_factor * to_query
        key_back = key_back + key_factor * to_key
        left_part = left.astype(f32) * to_query
        right_part = right.astype(f32) * to_key
        if level == 0:
            mask = (rows // BLOCK == cols // BLOCK) & (cols >= rows)
            decay_back = decay_back + ordered_sum(mask, left_part - right_part)
        else:
            group = BLOCK << level
            half = group // 2
            same = rows // group == cols // group
            late = same & (rows % group >= half) & (cols >= rows)
            early = same & (rows % group < half) & (cols < rows)
            decay_back = decay_back + ordered_sum(late | early, left_part + right_part)
    query_back_ref[...] = (query_back * DK ** (-0.5)).astype(bf16)
    key_back_ref[...] = key_back.astype(bf16)
    logits = forget_logits(rank_ref, up_ref, bias_ref)
    logit_back = (decay_back * jax.nn.sigmoid(-logits) * (1.0 / 16.0)).astype(bf16)
    rank_back_ref[0] = against(up_ref[...], logit_back)
    up_back_ref[0] = across(rank_ref[...], logit_back)
    bias_back_ref[0] = jnp.sum(logit_back.astype(f32), axis=0, keepdims=True)


def prefix_kernel(reverse, lines_ref, parts_ref, out_ref):
    count = parts_ref.shape[0]
    rows = out_ref.shape[2]
    carry = jnp.zeros(out_ref.shape[2:], f32)
    for step in range(count):
        at = count - 1 - step if reverse else step
        out_ref[at, 0] = carry.astype(bf16)
        lines = lines_ref[at, 0].astype(f32)
        total = lines[0:1] + lines[1:2] + lines[2:3]
        carry = carry * jnp.exp(total) + parts_ref[at, 0, :rows].astype(f32)


def hold_kernel(values_ref, out_ref):
    out_ref[...] = values_ref[...]


def either(first_ref, second_ref):
    return jnp.where(pl.program_id(0) == 0, first_ref[...], second_ref[...])


def middle_kernel(place_ref, input_ref, own_ref, first_ref, last_ref, gain_ref, middle_ref, second_ref):
    middle = input_ref[0].astype(f32) + (
        own_ref[...].astype(f32) + first_ref[...].astype(f32) + last_ref[...].astype(f32)
    )
    middle_ref[...] = middle
    scale = lax.rsqrt(jnp.mean(middle * middle, axis=-1, keepdims=True) + epsilon)
    second_ref[...] = (middle * scale * gain_ref[...].astype(f32)).astype(bf16)


def norm_back(values, grad, gain):
    scale = lax.rsqrt(jnp.mean(values * values, axis=-1, keepdims=True) + epsilon)
    unit = values * scale
    scaled = grad * gain
    back = scale * (scaled - unit * jnp.mean(scaled * unit, axis=-1, keepdims=True))
    return back, jnp.sum(grad * unit, axis=0, keepdims=True)


def add_part(out_ref, part):
    @pl.when(pl.program_id(0) == 0)
    def _():
        out_ref[...] = part

    @pl.when(pl.program_id(0) != 0)
    def _():
        out_ref[...] += part


def middle_back_kernel(
    place_ref, grad_ref, own_ref, first_ref, last_ref, middle_ref, gain_ref, back_ref, rows_ref, part_ref
):
    grad = own_ref[...].astype(f32) + first_ref[...].astype(f32) + last_ref[...].astype(f32)
    back, part = norm_back(middle_ref[...], grad, gain_ref[...].astype(f32))
    back = grad_ref[0].astype(f32) + back
    back_ref[...] = back
    rows_ref[...] = back.astype(bf16)
    add_part(part_ref, part)


def input_back_kernel(
    place_ref, input_ref, own_ref, first_ref, last_ref, rank_ref, down_ref, middle_ref, gain_ref, rows_ref, part_ref
):
    grad = own_ref[...].astype(f32) + first_ref[...].astype(f32) + last_ref[...].astype(f32)
    grad = grad + contract(rank_ref[...], down_ref[...], 0, 1)
    back, part = norm_back(input_ref[0].astype(f32), grad, gain_ref[...].astype(f32))
    rows_ref[...] = (middle_ref[...] + back).astype(bf16)
    add_part(part_ref, part)


def feed_kernel(
    first_ref, second_ref, grads_ref, swish_ref, up_ref, down_ref,
    inner_ref, swish_back_ref, up_back_ref, second_back_ref, out_ref,
    swish_held, up_held, down_held, semaphores,
):
    copies = [
        pltpu.make_async_copy(swish_ref, swish_held, semaphores.at[0]),
        pltpu.make_async_copy(up_ref, up_held, semaphores.at[1]),
        pltpu.make_async_copy(down_ref, down_held, semaphores.at[2]),
    ]
    start = pl.program_id(0) == 0

    @pl.when(start)
    def _():
        for copy in copies:
            copy.start()

    rows = either(first_ref, second_ref)

    @pl.when(start)
    def _():
        copies[0].wait()

    swish = product(rows, swish_held[...])

    @pl.when(start)
    def _():
        copies[1].wait()

    up = product(rows, up_held[...])
    sig = jax.nn.sigmoid(swish)
    act = swish * sig
    inner = (act * up).astype(bf16)
    inner_ref[...] = inner

    @pl.when(start)
    def _():
        copies[2].wait()

    inner_grad = against(grads_ref[...], down_held[...])
    swish_back = (inner_grad * up * sig * (1.0 + swish * (1.0 - sig))).astype(bf16)
    up_back = (inner_grad * act).astype(bf16)
    swish_back_ref[...] = swish_back
    up_back_ref[...] = up_back
    second_back_ref[...] = (against(swish_back, swish_held[...]) + against(up_back, up_held[...])).astype(bf16)
    out_ref[...] = product(inner, down_held[...]).astype(bf16)


def place_kernel(order_ref, *refs):
    out_ref = refs[-1]
    step = pl.program_id(0)
    for k in range(4):

        @pl.when(step == k)
        def _():
            out_ref[0] = refs[k][...]


def sum_kernel(count, *refs):
    out_ref = refs[-1]
    total = against(refs[0][...], refs[count][...])
    for k in range(1, count):
        total = total + against(refs[k][...], refs[count + k][...])
    out_ref[...] = total.astype(out_ref.dtype)


def grad_kernel(parts, groups, turned, pick_ref, *refs):
    cuts, refs = refs[:parts], refs[parts:]
    others, refs = refs[: parts * groups], refs[parts * groups :]
    arrived, out_ref = refs[:-1], refs[-1]
    for group in range(groups):
        total = None
        members = others[group * parts : (group + 1) * parts]
        width = members[0].shape[1]
        columns = slice(group * width, (group + 1) * width)
        for cut, other in zip(cuts, members):
            part = across(cut[...], other[...])
            total = part if total is None else total + part
        for ref in arrived:
            total = total + ref[0, :, columns].astype(f32)
        if turned:
            out_ref[...] = total.T
        else:
            out_ref[0, :, columns] = total.astype(out_ref.dtype)


def struct(shape, dtype):
    return jax.ShapeDtypeStruct(shape, dtype)


def grid_call(kernel, grid, in_specs, out_specs, out_shape, args, prefetch=0, after=(), scratch=(), into=None):
    first, last = len(args), len(args) + len(after)
    aliases = {}
    if into is not None:
        aliases = {last: into[1]}
        after = (*after, into[0])
        last += 1

    def run(*refs):
        kernel(*refs[:first], *refs[last:])

    return pl.pallas_call(
        run,
        grid_spec=pltpu.PrefetchScalarGridSpec(
            num_scalar_prefetch=prefetch,
            grid=grid,
            in_specs=list(in_specs) + [pl.BlockSpec(memory_space=pl.ANY)] * len(after),
            out_specs=out_specs,
            scratch_shapes=list(scratch),
        ),
        out_shape=out_shape,
        input_output_aliases=aliases,
        compiler_params=pltpu.CompilerParams(vmem_limit_bytes=VMEM),
        cost_estimate=pl.CostEstimate(flops=COST, bytes_accessed=COST, transcendentals=0),
    )(*args, *after)


def swap(values, axis, distance):
    count = lax.axis_size(axis)
    return lax.ppermute(values, axis, [(i, i ^ distance) for i in range(count)])


def region(function, *args):
    shapes = jax.eval_shape(function, *args)

    def never(*_):
        return jax.tree.map(lambda a: jnp.zeros(a.shape, a.dtype), shapes)

    return lax.cond(lax.axis_index("seq") >= 0, function, never, *args)


def bits_of(count):
    return [1 << k for k in range(count.bit_length() - 1)]


def hold(values, after):
    spec = pl.BlockSpec(values.shape, lambda: (0,) * values.ndim)
    return grid_call(hold_kernel, (), [spec], spec, struct(values.shape, values.dtype), [values], after=after)


def chunk_spec(count, extra=0, first=0):
    return pl.BlockSpec((count, 1, DK // count + extra, DK), lambda b, *_: (0, b + first, 0, 0))


def carried(pieces, lines, reverse, after=()):
    count, seq_count, rows, _ = pieces.shape
    share = DK // count
    return grid_call(
        functools.partial(prefix_kernel, reverse),
        (seq_count,),
        [
            pl.BlockSpec((count, 1, EXTRA, DK), lambda b: (0, b, share // EXTRA, 0)),
            chunk_spec(count, rows - share),
        ],
        chunk_spec(count),
        struct((count, seq_count, share, DK), bf16),
        [lines, pieces],
        after=after,
    )


def deal(pieces):
    return lax.all_to_all(pieces, "seq", 0, 0)


def tensor_reduce(near, far):
    third = swap(far[1], "tensor", 1)
    second = (far[0].astype(f32) + third.astype(f32)).astype(bf16)
    first = swap(near[1], "tensor", 1)
    return (near[0], first, swap(second, "tensor", 2)), second


def tensor_gather(own):
    first = swap(own, "tensor", 1)
    second = swap(own, "tensor", 2)

    def third(after):
        return swap(hold(second, after) if after else second, "tensor", 1)

    return own, first, second, third


def in_order(blocks, order, after=()):
    length, width = blocks[0].shape
    whole = pl.BlockSpec((length, width), lambda k, order: (0, 0))
    return grid_call(
        place_kernel,
        (4,),
        [whole] * 4,
        pl.BlockSpec((1, length, width), lambda k, order: (order[k], 0, 0)),
        struct((4, length, width), blocks[0].dtype),
        [order, *blocks],
        prefetch=1,
        after=after,
    )


def grad_part(cuts, groups, picks, arrived, dtype, turned=False, after=()):
    rows = ROWS
    width = groups[0][0][0].shape[1]
    whole = width * len(groups)
    share = cuts[0][0].shape[1] // lax.axis_size("seq")
    chunks = len(picks)
    me = lax.axis_index("seq")
    index = jnp.stack([me ^ r for r in picks]).astype(jnp.int32)
    others = [block for group in groups for block in group]
    in_specs = [pl.BlockSpec((rows, share), lambda k, pick, at=at: (at, pick[k])) for _, at in cuts]
    in_specs += [pl.BlockSpec((rows, width), lambda k, pick, at=at: (at, 0)) for _, at in others]
    for _, first in arrived:
        in_specs.append(pl.BlockSpec((1, share, whole), lambda k, pick, first=first: (k + first, 0, 0)))
    if turned:
        out_spec = pl.BlockSpec((whole, share), lambda k, pick: (0, 0))
        shape = (whole, share)
    else:
        out_spec = pl.BlockSpec((1, share, whole), lambda k, pick: (k, 0, 0))
        shape = (chunks, share, whole)
    return grid_call(
        functools.partial(grad_kernel, len(cuts), len(groups), turned),
        (chunks,),
        in_specs,
        out_spec,
        struct(shape, dtype),
        [index, *[a for a, _ in cuts], *[a for a, _ in others], *[a for a, _ in arrived]],
        prefetch=1,
        after=after,
    )


class Scatter:
    def __init__(self, cuts, groups, order, turned=False):
        self.cuts, self.groups, self.order, self.turned = cuts, groups, order, turned
        self.split = lax.axis_size("seq") == 8

    def part(self, picks, arrived, dtype, turned=False, after=()):
        return grad_part(self.cuts, self.groups, picks, arrived, dtype, turned, after)

    def send(self, after=()):
        if not self.split:
            total = jnp.concatenate(
                [
                    sum(
                        across(a[i * ROWS : (i + 1) * ROWS], b[j * ROWS : (j + 1) * ROWS])
                        for (a, i), (b, j) in zip(self.cuts, group)
                    ).astype(bf16)
                    for group in self.groups
                ],
                axis=1,
            )
            self.total = lax.psum_scatter(total, "seq", scatter_dimension=0, tiled=True).astype(f32)
            return self.total
        a, b, c = self.order
        away = self.part([a ^ b, a ^ b ^ c, a ^ c, a], [], bf16, after=after)
        self.came = swap(away, "seq", a)
        return away

    def step_one(self, after=()):
        if not self.split:
            return self.total
        a, b, c = self.order
        first = self.part([b, b ^ c], [(self.came, 0)], bf16, after=after)
        self.came_first = swap(first, "seq", b)
        return first

    def step_two(self, after=()):
        if not self.split:
            return self.total
        a, b, c = self.order
        second = self.part([c], [(self.came, 2), (self.came_first, 1)], bf16, after=after)
        self.came_second = swap(second, "seq", c)
        return second

    def last(self, after=()):
        if not self.split:
            return self.total.T if self.turned else self.total
        total = self.part(
            [0],
            [(self.came, 3), (self.came_first, 0), (self.came_second, 0)],
            f32,
            self.turned,
            after=after,
        )
        return total if self.turned else total[0]


def product_sum(pairs, dtype, after=()):
    rows = pairs[0][0].shape[0]
    width = pairs[0][1].shape[0]
    tile = 512
    in_specs = [pl.BlockSpec((rows, p[0].shape[1]), lambda j: (0, 0)) for p in pairs]
    in_specs += [pl.BlockSpec((tile, p[1].shape[1]), lambda j: (j, 0)) for p in pairs]
    return grid_call(
        functools.partial(sum_kernel, len(pairs)),
        (width // tile,),
        in_specs,
        pl.BlockSpec((rows, tile), lambda j: (0, j)),
        struct((rows, width), dtype),
        [p[0] for p in pairs] + [p[1] for p in pairs],
        after=after,
    )


def sum_over(values, axis):
    for bit in bits_of(lax.axis_size(axis)):
        values = values + swap(values, axis, bit)
    return values


def spread_sum(values):
    return jnp.sum(lax.all_to_all(values, "seq", 0, 0), axis=0)


def local(
    layer_input,
    attn_norm,
    query_weight,
    key_weight,
    value_weight,
    gate_weight,
    rank_down,
    rank_up,
    decay_bias,
    head_gain,
    out_weight,
    mlp_norm,
    swish_weight,
    up_weight,
    down_weight,
    cotangent,
):
    seq_count, length, width = layer_input.shape
    place = lax.axis_index("tensor")
    devices = lax.axis_size("seq")
    half = seq_count // 2
    half_rows = half * length
    rank = rank_down.shape[1]
    bias = decay_bias.reshape(1, DK)
    gain = head_gain.reshape(1, DK)
    share = DK // devices

    def row_spec(size):
        return pl.BlockSpec((length, size), lambda b, *_: (b, 0))

    def fixed(shape):
        return pl.BlockSpec(shape, lambda b, *_: (0,) * len(shape))

    def square(size):
        return pl.BlockSpec((1, size, size), lambda b, *_: (b, 0, 0))

    def line(rows, size):
        return pl.BlockSpec((1, rows, size), lambda b, *_: (b, 0, 0))

    def rows_of(size, dtype):
        return struct((half_rows, size), dtype)

    chunks = struct((devices, seq_count, share, DK), bf16)
    whole_block = pl.BlockSpec((length, width), lambda b, *_: (0, 0))

    def blocks(near, far):
        return [(near, 0), (near, 1), (far, 0), (far, 1)]

    def halves(values):
        return values[:length], values[length:]

    def first_rows(order, after=()):
        spec = pl.BlockSpec((1, length, width), lambda b, order: (order[b], 0, 0))
        return grid_call(
            norm_kernel,
            (half,),
            [spec, spec, fixed((1, width))],
            [row_spec(width), row_spec(width)],
            [rows_of(width, bf16), rows_of(width, bf16)],
            [order, layer_input, cotangent, attn_norm.reshape(1, width)],
            prefetch=1,
            after=after,
        )

    def decays(norm):
        rank_rows = product(norm, rank_down).astype(bf16)
        run = grid_call(
            decay_kernel,
            (half,),
            [row_spec(rank), fixed((rank, DK)), fixed((1, DK))],
            row_spec(DK),
            rows_of(DK, f32),
            [rank_rows, rank_up, bias],
        )
        return rank_rows, run

    def states(norm, run, at, into=None):
        keys = product(norm, key_weight).astype(bf16)
        values = product(norm, value_weight).astype(bf16)
        state = grid_call(
            state_kernel,
            (half,),
            [row_spec(DK)] * 3,
            chunk_spec(devices, EXTRA, at),
            struct((devices, seq_count, share + EXTRA, DK), bf16),
            [keys, values, run],
            into=None if into is None else (into, 0),
        )
        return keys, values, state

    def scored(norm, keys, run, after=()):
        queries = product(norm, query_weight).astype(bf16)
        gates = product(norm, gate_weight)
        scores = grid_call(
            score_kernel,
            (half,),
            [row_spec(DK)] * 3,
            square(length),
            struct((half, length, length), bf16),
            [queries, keys, run],
            after=after,
        )
        return queries, gates, scores

    def mix(queries, values, run, scores, incoming, at, gates, after=()):
        return grid_call(
            mix_kernel,
            (half,),
            [row_spec(DK)] * 3
            + [square(length), chunk_spec(devices, 0, at), row_spec(DK), fixed((1, DK))],
            [row_spec(DK), row_spec(DK)],
            [rows_of(DK, f32), rows_of(DK, bf16)],
            [queries, values, run, scores, incoming, gates, gain],
            after=after,
        )

    order = jnp.arange(seq_count, dtype=jnp.int32) ^ place
    place_index = order[:1]
    norm_far, grads_far = first_rows(order[half:])
    rank_far, run_far = decays(norm_far)
    keys_far, values_far, state = states(norm_far, run_far, 0)
    norm_near, grads_near = first_rows(order[:half])
    rank_near, run_near = decays(norm_near)
    keys_near, values_near, state = states(norm_near, run_near, half, state)
    queries_far, gates_far, scores_far = scored(norm_far, keys_far, run_far, [state])
    queries_near, gates_near, scores_near = scored(norm_near, keys_near, run_near, [scores_far])
    lines = deal(state)
    incoming = deal(carried(lines, lines, False, [scores_far, gates_far, scores_near, gates_near]))

    mixed_far, branch_far = mix(queries_far, values_far, run_far, scores_far, incoming, 0, gates_far)
    out_far = product(branch_far, out_weight).astype(bf16)
    out_third = swap(out_far[length:], "tensor", 1)
    out_second = (out_far[:length].astype(f32) + out_third.astype(f32)).astype(bf16)
    out_last = swap(out_second, "tensor", 2)
    mixed_near, branch_near = mix(
        queries_near, values_near, run_near, scores_near, incoming, half, gates_near, [out_second]
    )
    out_near = product(branch_near, out_weight).astype(bf16)
    out_parts = (out_near[:length], swap(out_near[length:], "tensor", 1), out_last)

    tile = 128
    tiles = (length // tile,)
    tile_spec = pl.BlockSpec((tile, width), lambda b, *_: (b, 0))
    own_spec = pl.BlockSpec((1, tile, width), lambda b, place: (place[0], b, 0))
    gain_two = mlp_norm.reshape(1, width)
    middle, second_own = grid_call(
        middle_kernel,
        tiles,
        [own_spec] + [tile_spec] * 3 + [fixed((1, width))],
        [tile_spec] * 2,
        [struct((length, width), f32), struct((length, width), bf16)],
        [place_index, layer_input, *out_parts, gain_two],
        prefetch=1,
    )
    *seconds, second_third = tensor_gather(second_own)

    hidden = swish_weight.shape[1]
    anywhere = pl.BlockSpec(memory_space=pl.ANY)

    def feed(rows, grads, at, after=()):
        count = len(rows)
        return grid_call(
            feed_kernel,
            (count,),
            [whole_block] * 2
            + [pl.BlockSpec((length, width), lambda b: (b + at, 0))]
            + [anywhere] * 3,
            [row_spec(hidden)] * 3 + [row_spec(width)] * 2,
            [struct((count * length, hidden), bf16)] * 3 + [struct((count * length, width), bf16)] * 2,
            [rows[0], rows[-1], grads, swish_weight, up_weight, down_weight],
            scratch=[
                pltpu.VMEM((width, hidden), bf16),
                pltpu.VMEM((width, hidden), bf16),
                pltpu.VMEM((hidden, width), bf16),
                pltpu.SemaphoreType.DMA((3,)),
            ],
            after=after,
        )

    feed_near = feed(seconds[:2], grads_near, 0)
    seconds.append(second_third([feed_near[4]]))
    feed_two = feed(seconds[2:3], grads_far, 0, [feed_near[4]])
    feed_three = feed(seconds[3:4], grads_far, 1, [feed_two[4]])
    inner, swish_back, up_back = (
        [(feed_near[k], 0), (feed_near[k], 1), (feed_two[k], 0), (feed_three[k], 0)] for k in range(3)
    )
    second_parts, second_sent = tensor_reduce(halves(feed_near[3]), (feed_two[3], feed_three[3]))
    down_near, down_far = halves(feed_near[4]), (feed_two[4], feed_three[4])

    bits = bits_of(devices)
    late_bits = [bits[1], bits[0], *bits[2:]]
    second_blocks = [(values, 0) for values in seconds]
    swish_grad = Scatter(second_blocks, [swish_back], bits)
    up_grad = Scatter(second_blocks, [up_back], bits)
    down_grad = Scatter(blocks(grads_near, grads_far), [inner], late_bits, True)
    swish_away = swish_grad.send()
    down_away = down_grad.send([second_sent, swish_away])
    up_away = up_grad.send([down_away])

    middle_grad, own_rows, mlp_norm_part = grid_call(
        middle_back_kernel,
        tiles,
        [own_spec] + [tile_spec] * 4 + [fixed((1, width))],
        [tile_spec, tile_spec, fixed((1, width))],
        [struct((length, width), f32), struct((length, width), bf16), struct((1, width), f32)],
        [place_index, cotangent, *second_parts, middle, gain_two],
        prefetch=1,
        after=[up_away],
    )

    def branch_back(first, second, mixed, gates, queries, run, at, into=None):
        return grid_call(
            branch_back_kernel,
            (half,),
            [
                whole_block, whole_block, fixed((DK, width)), row_spec(DK), row_spec(DK), fixed((1, DK)),
                row_spec(DK), row_spec(DK),
            ],
            [row_spec(DK), row_spec(DK), line(1, DK), chunk_spec(devices, 0, at)],
            [rows_of(DK, bf16), rows_of(DK, bf16), struct((half, 1, DK), f32), chunks],
            [first, second, out_weight, mixed, gates, gain, queries, run],
            into=None if into is None else (into, 3),
        )

    def gather_back(own_rows):
        *rows, rows_third = tensor_gather(own_rows)
        *near, state_back = branch_back(
            rows[0], rows[1], mixed_near, gates_near, queries_near, run_near, half
        )
        rows.append(rows_third([near[0]]))
        *far, state_back = branch_back(
            rows[2], rows[3], mixed_far, gates_far, queries_far, run_far, 0, state_back
        )
        return rows[1:], near, far, state_back

    others, near, far, state_back = region(gather_back, own_rows)
    rows = [own_rows, *others]
    gate_back_near, mixed_back_near, gain_back_near = near
    gate_back_far, mixed_back_far, gain_back_far = far
    norms = blocks(norm_near, norm_far)
    out_grad = Scatter([(values, 0) for values in rows], [blocks(branch_near, branch_far)], bits, True)
    out_away = out_grad.send([state_back])

    def states_back(state_back):
        came = deal(state_back)
        down_parts, _ = tensor_reduce(down_near, down_far)
        return came, down_parts[1:]

    came, down_parts = region(states_back, state_back)
    swish_one = swish_grad.step_one([came])
    down_one = down_grad.step_one([swish_one])

    def states_out(came, down_parts):
        outgoing = deal(carried(came, lines, True, [swish_one, down_one]))
        own = sum((part.astype(f32) for part in (down_near[0], *down_parts)), middle).astype(bf16)
        *blocks, third = tensor_gather(own)
        return outgoing, [*blocks, third([])]

    outgoing, output_blocks = region(states_out, came, down_parts)

    def mix_back(queries, keys, values, mixed_back, run, scores, at, rank_rows, after):
        return grid_call(
            mix_back_kernel,
            (half,),
            [row_spec(DK)] * 5
            + [square(length)]
            + [chunk_spec(devices, 0, at)] * 2
            + [row_spec(rank), fixed((rank, DK)), fixed((1, DK))],
            [row_spec(DK)] * 3 + [line(rank, length), line(rank, DK), line(1, DK)],
            [rows_of(DK, bf16)] * 3
            + [
                struct((half, rank, length), f32),
                struct((half, rank, DK), f32),
                struct((half, 1, DK), f32),
            ],
            [
                queries, keys, values, mixed_back, run, scores, incoming, outgoing,
                rank_rows, rank_up, bias,
            ],
            after=after,
        )

    query_back_near, key_back_near, value_back_near, rank_part_near, up_part_near, bias_part_near = (
        mix_back(
            queries_near, keys_near, values_near, mixed_back_near, run_near, scores_near,
            half, rank_near, [],
        )
    )
    query_back_far, key_back_far, value_back_far, rank_part_far, up_part_far, bias_part_far = mix_back(
        queries_far, keys_far, values_far, mixed_back_far, run_far, scores_far,
        0, rank_far, [bias_part_near],
    )
    up_one = up_grad.step_one([bias_part_far])

    query_gate_grad = Scatter(
        norms, [blocks(query_back_near, query_back_far), blocks(gate_back_near, gate_back_far)], bits
    )
    key_value_grad = Scatter(
        norms, [blocks(key_back_near, key_back_far), blocks(value_back_near, value_back_far)], late_bits
    )
    query_gate_away = query_gate_grad.send([up_one])
    key_value_away = key_value_grad.send([query_gate_away])

    def first_part(query_back, key_back, value_back, gate_back, after):
        return product_sum(
            [
                (query_back, query_weight),
                (key_back, key_weight),
                (value_back, value_weight),
                (gate_back, gate_weight),
            ],
            bf16,
            after,
        )

    first_far = first_part(query_back_far, key_back_far, value_back_far, gate_back_far, [key_value_away])
    first_near = first_part(query_back_near, key_back_near, value_back_near, gate_back_near, [first_far])
    first_parts, first_sent = tensor_reduce(halves(first_near), halves(first_far))

    rank_part = jnp.concatenate([rank_part_near, rank_part_far], axis=0)
    rank_part = rank_part + swap(rank_part, "tensor", 1)[jnp.array([1, 0, 3, 2])]
    rank_part = rank_part + swap(rank_part, "tensor", 2)[jnp.array([2, 3, 0, 1])]
    rank_back = rank_part.astype(bf16)

    swish_two = swish_grad.step_two([first_near, first_sent])
    down_two = down_grad.step_two([swish_two])
    out_one = out_grad.step_one([down_two])
    up_two = up_grad.step_two([out_one])

    input_rows, attn_norm_part = grid_call(
        input_back_kernel,
        tiles,
        [own_spec] + [tile_spec] * 3
        + [
            pl.BlockSpec((rank, tile), lambda b, *_: (0, b)), fixed((width, rank)), tile_spec,
            fixed((1, width)),
        ],
        [tile_spec, fixed((1, width))],
        [struct((length, width), bf16), struct((1, width), f32)],
        [
            place_index, layer_input, *first_parts, rank_back[0], rank_down, middle_grad,
            attn_norm.reshape(1, width),
        ],
        prefetch=1,
        after=[up_two],
    )
    *input_blocks, input_third = tensor_gather(input_rows)
    input_blocks.append(input_third([]))
    query_gate_one = query_gate_grad.step_one([input_rows])
    key_value_one = key_value_grad.step_one([query_gate_one])
    out_two = out_grad.step_two([key_value_one])
    swish_share = swish_grad.last([out_two])
    down_share = down_grad.last([swish_share])
    up_share = up_grad.last([down_share])
    query_gate_two = query_gate_grad.step_two([up_share])
    key_value_two = key_value_grad.step_two([query_gate_two])
    layer_output = in_order(output_blocks, order, [key_value_two])
    out_share = out_grad.last([layer_output])
    input_grad = in_order(input_blocks, order, [out_share])
    query_gate_share = query_gate_grad.last([out_share])
    key_value_share = key_value_grad.last([query_gate_share])

    rank_down_part = sum(
        contract(rank_back[k], array[at * length : (at + 1) * length], 1, 0)
        for k, (array, at) in enumerate(norms)
    )
    own_part = jnp.concatenate([rank_down_part, mlp_norm_part, attn_norm_part], axis=0)
    shared = jnp.concatenate(
        [
            sum(up_part_near) + sum(up_part_far),
            sum(bias_part_near) + sum(bias_part_far),
            sum(gain_back_near) + sum(gain_back_far),
        ],
        axis=0,
    )
    column = width // devices
    own_part = jnp.moveaxis(own_part.reshape(rank + 2, devices, column), 1, 0)
    own_size = (rank + 2) * column
    mail = jnp.concatenate(
        [
            own_part.reshape(devices, own_size),
            jnp.broadcast_to(shared.reshape(1, -1), (devices, shared.size)),
        ],
        axis=1,
    )
    mail = spread_sum(mail.reshape(devices, 1, -1)).reshape(-1)
    own_part = mail[:own_size].reshape(rank + 2, column)
    shared = mail[own_size:].reshape(rank + 2, DK)
    norm_parts = sum_over(own_part[rank:], "tensor")
    return (
        layer_output,
        input_grad,
        norm_parts[1],
        query_gate_share[:, :DK],
        key_value_share[:, :DK],
        key_value_share[:, DK:],
        query_gate_share[:, DK:],
        own_part[:rank].T,
        shared[:rank],
        shared[rank],
        shared[rank + 1],
        out_share,
        norm_parts[0],
        swish_share,
        up_share,
        down_share,
    )


def solution(mesh):
    return jax.shard_map(
        local,
        mesh=mesh,
        in_specs=(
            P(None, "seq", None),
            P(),
            P(None, "tensor"),
            P(None, "tensor"),
            P(None, "tensor"),
            P(None, "tensor"),
            P(),
            P(None, "tensor"),
            P("tensor"),
            P("tensor"),
            P("tensor", None),
            P(),
            P(None, "tensor"),
            P(None, "tensor"),
            P("tensor", None),
            P(None, "seq", None),
        ),
        out_specs=(
            P(None, "seq", None),
            P(None, "seq", None),
            P("seq"),
            P("seq", "tensor"),
            P("seq", "tensor"),
            P("seq", "tensor"),
            P("seq", "tensor"),
            P("seq", None),
            P(None, "tensor"),
            P("tensor"),
            P("tensor"),
            P("tensor", "seq"),
            P("seq"),
            P("seq", "tensor"),
            P("seq", "tensor"),
            P("tensor", "seq"),
        ),
        check_vma=False,
    )
```

time: 1100 us -> 820 us (0.75)
  Pallas kernels: 43.6 us -> 246 us
  matrix products: 182 us -> 17.7 us
  waiting for transfers between devices: 487 us -> 392 us
  local copies, waits for them, and re-layouts: 153 us -> 67.1 us
  blocking collectives: 67.5 us -> 0 us
  other arithmetic: 66.6 us -> 17.2 us
  starting transfers between devices: 83.8 us -> 68.2 us
    pallas_call x9 -> x52, Pallas kernels: 43.6 us -> 246 us  [grid_call(): pl.pallas_call(run, grid_spec=pltpu.PrefetchScalarGridSpec(num_scalar_pre...]
    ppermute x63 -> x46, waiting for transfers between devices: 455 us -> 261 us  [swap(): return lax.ppermute(values, axis, [(i, i ^ distance) for i in range(count)])]
    dot_general x48 -> x16, matrix products: 182 us -> 17.7 us  [contract(): lax.dot_general(left, right, (((left_dim,), (right_dim,)), ((), ())), pre...]
    all_to_all x4 -> x5, waiting for transfers between devices: 31.7 us -> 131 us  [the longest x4 131 us: deal(): return lax.all_to_all(pieces, 'seq', 0, 0)]
    all_gather x1 -> x0, blocking collectives: 67.5 us -> none  [spread_totals(): return lax.all_gather(values, axis)]
    concatenate x15 -> x2, local copies, waits for them, and re-layouts: 56.4 us -> 0.62 us  [the longest x1 0.62 us: local(): jnp.concatenate([own_part.reshape(devices, own_size), jnp.broadcast_to(sh...]
    dynamic_slice x12 -> x0, local copies, waits for them, and re-layouts: 27.3 us -> none  [the longest x7 21 us: choose(): lax.dynamic_index_in_dim(values, here if mine else 1 - here, at, keepdims...]
    ppermute x63 -> x46, starting transfers between devices: 62.4 us -> 43.8 us  [swap(): return lax.ppermute(values, axis, [(i, i ^ distance) for i in range(count)])]
  transfers between devices with their start and end apart: 67 -> 51, of which waited for: 22 -> 26; matrix products, arithmetic and copies ran while one was open for 31% -> 5% of each run, Pallas kernels for 2% -> 25%
where the time goes in v2:
time: 820 us; the launch traced here: 812 us
  waiting for transfers between devices  392 us (48%)
  Pallas kernels  246 us (30%)
  starting transfers between devices  68.2 us (8%)
  local copies, waits for them, and re-layouts  67.1 us (8%)
  matrix products  17.7 us (2%)
  other arithmetic  17.2 us (2%)
    ppermute x46, waiting for transfers between devices, swap(): return lax.ppermute(values, axis, [(i, i ^ distance) for i in range(count)])  261 us
    pallas_call x52, Pallas kernels, grid_call(): pl.pallas_call(run, grid_spec=pltpu.PrefetchScalarGridSpec(num_scalar_pre...  246 us
    all_to_all x4, waiting for transfers between devices, deal(): return lax.all_to_all(pieces, 'seq', 0, 0)  131 us
    unnamed x403, local copies, waits for them, and re-layouts  50.7 us
    ppermute x46, starting transfers between devices, swap(): return lax.ppermute(values, axis, [(i, i ^ distance) for i in range(count)])  43.8 us
    all_to_all x4, starting transfers between devices, deal(): return lax.all_to_all(pieces, 'seq', 0, 0)  20 us
    dot_general x16, matrix products, contract(): lax.dot_general(left, right, (((left_dim,), (right_dim,)), ((), ())), pre...  17.7 us
  transfers between devices with their start and end apart: 51, of which 26 were waited for; matrix products, arithmetic and copies ran while one was open for 5% of the time, Pallas kernels for 25%

profile of v2, /device:TPU:0, one launch (start us, length us, event | category | flops | bytes accessed | tf_op | source)
XLA Modules:
  0.0 811.5 jit_solution(11365560214210865996)
XLA Ops:
  25.8 7.5 all-to-all-start.2
  45.3 47.6 %all-to-all-done.2.refs_0_.refs_1_ = bf16[8,4,80,512]{3,2,1,0:T(8,128)(2,1)} async-done(((bf16[8,4,80,512]{3,2,1,0:T(8,128)(2,1)}), bf16[8,4,80,512]{3,2,1,0:T(8,128)(2,1)}, u32[]{:S(2)}, u32[]{:S(2)}) %all-to-all-start.2) | async-done | bytes 2621472 | tf_op jit(solution)/shard_map/all_to_all | solution.py:481
  103.2 47.2 %all-to-all-done.3.refs_4_.refs_6_ = bf16[8,4,64,512]{3,2,1,0:T(8,128)(2,1)S(1)} async-done(((bf16[8,4,64,512]{3,2,1,0:T(8,128)(2,1)}), bf16[8,4,64,512]{3,2,1,0:T(8,128)(2,1)S(1)}, u32[]{:S(2)}, u32[]{:S(2)}) %all-to-all-start.3) | async-done | bytes 2097184 | tf_op jit(solution)/shard_map/all_to_all | solution.py:481
  164.3 19.8 %collective-permute-done.11.refs_4_ = bf16[256,2048]{1,0:T(8,128)(2,1)S(1)} collective-permute-done((bf16[256,2048]{1,0:T(8,128)(2,1)S(1)}, bf16[256,2048]{1,0:T(8,128)(2,1)S(1)}, u32[]{:S(2)}, u32[]{:S(2)}) %collective-permute-start.11) | collective-permute-done | bytes 1048608 | tf_op jit(solution)/shard_map/ppermute | solution.py:438
  189.8 25.9 %shard_map.309 = (bf16[512,1408]{1,0:T(8,128)(2,1)S(1)}, bf16[512,1408]{1,0:T(8,128)(2,1)S(1)}, bf16[512,1408]{1,0:T(8,128)(2,1)}, bf16[512,2048]{1,0:T(8,128)(2,1)}, bf16[512,2048]{1,0:T(8,128)(2,1)S(1)}) custom-call(bf16[256,2048]{1,0:T(8,128)(2,1)S(1)} %get-tuple-element.159.refs_0_.refs_1_, ...), custom_call_target="tpu_custom_call" | custom-call | flops 1024 | bytes 1024 | tf_op jit(solution)/shard_map/pallas_call | solution.py:420
  217.4 14.5 %shard_map.310 = (bf16[256,1408]{1,0:T(8,128)(2,1)S(1)}, bf16[256,1408]{1,0:T(8,128)(2,1)S(1)}, bf16[256,1408]{1,0:T(8,128)(2,1)S(1)}, bf16[256,2048]{1,0:T(8,128)(2,1)S(1)}, bf16[256,2048]{1,0:T(8,128)(2,1)S(1)}) custom-call(bf16[256,2048]{1,0:T(8,128)(2,1)S(1)} %collective-permute-done.14.refs_0_.refs_1_.refs_3_, ...), custom_call_target="tpu_custom_call" | custom-call | flops 1024 | bytes 1024 | tf_op jit(solution)/shard_map/pallas_call | solution.py:420
  235.6 16.6 %shard_map.312 = (bf16[256,1408]{1,0:T(8,128)(2,1)S(1)}, bf16[256,1408]{1,0:T(8,128)(2,1)S(1)}, bf16[256,1408]{1,0:T(8,128)(2,1)S(1)}, bf16[256,2048]{1,0:T(8,128)(2,1)}, bf16[256,2048]{1,0:T(8,128)(2,1)}) custom-call(bf16[256,2048]{1,0:T(8,128)(2,1)S(1)} %collective-permute-done.15.refs_0_.refs_1_.refs_4_, ...), custom_call_target="tpu_custom_call" | custom-call | flops 1024 | bytes 1024 | tf_op jit(solution)/shard_map/pallas_call | solution.py:420
  258.8 7.5 shard_map.313.refs_10_
  270.5 7.1 shard_map.314.refs_9_
  277.7 7.2 shard_map.315.refs_7_
  294.4 18.8 %collective-permute-done.17.refs_4_ = bf16[256,2048]{1,0:T(8,128)(2,1)} collective-permute-done((bf16[256,2048]{1,0:T(8,128)(2,1)}, bf16[256,2048]{1,0:T(8,128)(2,1)}, u32[]{:S(2)}, u32[]{:S(2)}) %collective-permute-start.17) | collective-permute-done | bytes 1048608 | tf_op jit(solution)/shard_map/ppermute | solution.py:438
  321.5 35.2 %conditional.3 = (bf16[256,2048]{1,0:T(8,128)(2,1)}, bf16[256,2048]{1,0:T(8,128)(2,1)}, bf16[256,2048]{1,0:T(8,128)(2,1)}, bf16[512,512]{1,0:T(8,128)(2,1)}, bf1...) conditional(s32[]{:T(128)} %convert_element_type.86, () %tuple.34, ...), branch_computations={%region_0.0_spmd, %region_1.0_spmd} | conditional | flops 3072 | bytes 18877696 | solution.py:447
  329.3 17.8 %collective-permute-done.1.refs_0_ = bf16[256,2048]{1,0:T(8,128)(2,1)} collective-permute-done((bf16[256,2048]{1,0:T(8,128)(2,1)S(1)}, bf16[256,2048]{1,0:T(8,128)(2,1)}, u32[]{:S(2)}, u32[]{:S(2)}) %collective-permute-start.1) | collective-permute-done | bytes 1048608 | tf_op jit(solution)/shard_map/cond/branch_1_fun/ppermute | solution.py:438
  351.3 5.4 branch_1_fun.6
  364.7 53.2 %conditional.4 = (bf16[8,4,64,512]{3,2,1,0:T(8,128)(2,1)}, bf16[256,2048]{1,0:T(8,128)(2,1)}, bf16[256,2048]{1,0:T(8,128)(2,1)}) conditional(s32[]{:T(128)} %convert_element_type.86, () %tuple.33, (bf16[8,4,64,512]{3,2,1,0:T(8,128)(2,1)}, bf16[512,2048]{1,0:T(8,128)(2,1)}, bf16[256,2048]{1,0:T(8,128)(2,1)}, bf16[256,2048]{1,0:T(8,128)(2,1)}) %tuple.65), branch_computations={%region_2.0_spmd, %region_3.0_spmd} | conditional | flops 2097152 | bytes 28311756 | solution.py:447
  374.0 23.8 %collective-permute-done.5 = bf16[256,2048]{1,0:T(8,128)(2,1)} collective-permute-done((bf16[256,2048]{1,0:T(8,128)(2,1)S(1)}, bf16[256,2048]{1,0:T(8,128)(2,1)}, u32[]{:S(2)}, u32[]{:S(2)}) %collective-permute-start.5) | collective-permute-done | bytes 1048608 | tf_op jit(solution)/shard_map/cond/branch_1_fun/ppermute | solution.py:438
  397.8 20.1 %all-to-all-done = bf16[8,4,64,512]{3,2,1,0:T(8,128)(2,1)} async-done(((bf16[8,4,64,512]{3,2,1,0:T(8,128)(2,1)}), bf16[8,4,64,512]{3,2,1,0:T(8,128)(2,1)}, u32[]{:S(2)}, u32[]{:S(2)}) %all-to-all-start) | async-done | bytes 2097184 | tf_op jit(solution)/shard_map/cond/branch_1_fun/all_to_all | solution.py:481
  427.2 5.3 shard_map.317.refs_10_
  437.4 56.4 %conditional.5 = (bf16[8,4,64,512]{3,2,1,0:T(8,128)(2,1)}, bf16[256,2048]{1,0:T(8,128)(2,1)}, bf16[256,2048]{1,0:T(8,128)(2,1)}, bf16[256,2048]{1,0:T(8,128)(2,1)}, bf16[256,2048]{1,0:T(8,128)(2,1)}) conditional(s32[]{:T(128)} %convert_element_type.86, () %tuple.32, (bf16[8,4,80,512]{3,2,1,0:T(8,128)(2,1)}, bf16[8,4,64,512]{3,2,1,0:T(8,128)(2,1)}, ...), branch_computations={%region_4.0_spmd, %region_5.0_spmd} | conditional | flops 3671040 | bytes 33555676 | solution.py:447
  451.7 22.9 %collective-permute-done.7 = bf16[256,2048]{1,0:T(8,128)(2,1)} collective-permute-done((bf16[256,2048]{1,0:T(8,128)(2,1)}, bf16[256,2048]{1,0:T(8,128)(2,1)}, u32[]{:S(2)}, u32[]{:S(2)}) %collective-permute-start.7) | collective-permute-done | bytes 1048608 | tf_op jit(solution)/shard_map/cond/branch_1_fun/ppermute | solution.py:438
  477.6 16.2 %all-to-all-done.1 = bf16[8,4,64,512]{3,2,1,0:T(8,128)(2,1)} async-done(((bf16[8,4,64,512]{3,2,1,0:T(8,128)(2,1)}), bf16[8,4,64,512]{3,2,1,0:T(8,128)(2,1)}, u32[]{:S(2)}, u32[]{:S(2)}) %all-to-all-start.1) | async-done | bytes 2097184 | tf_op jit(solution)/shard_map/cond/branch_1_fun/all_to_all | solution.py:481
  498.5 6.9 shard_map.319
  505.6 7.2 shard_map.320
  518.1 5.4 shard_map.322.refs_13_
  531.3 6.7 shard_map.324.refs_8_
  541.4 7.4 shard_map.325.refs_11_
  566.2 30.9 %collective-permute-done.28.refs_10_ = bf16[2,256,1408]{2,1,0:T(8,128)(2,1)} collective-permute-done((bf16[2,256,1408]{2,1,0:T(8,128)(2,1)}, bf16[2,256,1408]{2,1,0:T(8,128)(2,1)}, u32[]{:S(2)}, u32[]{:S(2)}) %collective-permute-start.28) | collective-permute-done | bytes 1441824 | tf_op jit(solution)/shard_map/ppermute | solution.py:438
  625.8 5.7 collective-permute-done.22.refs_13_
  637.4 35.5 %collective-permute-done.21.refs_13_ = bf16[4,256,1024]{2,1,0:T(8,128)(2,1)} collective-permute-done((bf16[4,256,1024]{2,1,0:T(8,128)(2,1)}, bf16[4,256,1024]{2,1,0:T(8,128)(2,1)}, u32[]{:S(2)}, u32[]{:S(2)}) %collective-permute-start.21) | collective-permute-done | bytes 2097184 | tf_op jit(solution)/shard_map/ppermute | solution.py:438
  698.3 26.6 %collective-permute-done.34.refs_11_ = bf16[1,256,1408]{2,1,0:T(8,128)(2,1)S(1)} collective-permute-done((bf16[1,256,1408]{2,1,0:T(8,128)(2,1)}, bf16[1,256,1408]{2,1,0:T(8,128)(2,1)S(1)}, u32[]{:S(2)}, u32[]{:S(2)}) %collective-permute-start.34) | collective-permute-done | bytes 720928 | tf_op jit(solution)/shard_map/ppermute | solution.py:438
  752.9 5.2 shard_map.340.refs_12_
  758.1 37.8 %collective-permute-done.41.refs_11_ = bf16[1,256,512]{2,1,0:T(8,128)(2,1)S(1)} collective-permute-done((bf16[1,256,512]{2,1,0:T(8,128)(2,1)S(1)}, bf16[1,256,512]{2,1,0:T(8,128)(2,1)S(1)}, u32[]{:S(2)}, u32[]{:S(2)}) %collective-permute-start.41) | collective-permute-done | bytes 262176 | tf_op jit(solution)/shard_map/ppermute | solution.py:438
  (603 shorter events, 301.5 us)
Async XLA Ops:
  25.8 67.1 %all-to-all-start.2 = ((bf16[8,4,80,512]{3,2,1,0:T(8,128)(2,1)}), bf16[8,4,80,512]{3,2,1,0:T(8,128)(2,1)}, u32[]{:S(2)}, u32[]{:S(2)}) async-start(bf16[8,4,80,512]{3,2,1,0:T(8,128)(2,1)} %copy-done.57), calls=%async_computation.2 | async-start | bytes 5242880 | tf_op jit(solution)/shard_map/all_to_all | solution.py:481
  98.2 52.2 %all-to-all-start.3 = ((bf16[8,4,64,512]{3,2,1,0:T(8,128)(2,1)}), bf16[8,4,64,512]{3,2,1,0:T(8,128)(2,1)S(1)}, u32[]{:S(2)}, u32[]{:S(2)}) async-start(bf16[8,4,64,512]{3,2,1,0:T(8,128)(2,1)} %copy-done.103), calls=%async_computation.3 | async-start | bytes 4194304 | tf_op jit(solution)/shard_map/all_to_all | solution.py:481
  158.8 25.3 %collective-permute-start.11 = (bf16[256,2048]{1,0:T(8,128)(2,1)S(1)}, bf16[256,2048]{1,0:T(8,128)(2,1)S(1)}, u32[]{:S(2)}, u32[]{:S(2)}) collective-permute-start(bf16[256,2048]{1,0:T(8,128)(2,1)S(1)} %add_convert_fusion.4.refs_7_), channel_id=1, source_target_pairs={{0,2},{1,3},{2,0},{3,1},{4,6},{5,7},{6,4},{7,5},{8,10},{9,11},{10,... | collective-permute-start | bytes 3145736 | tf_op jit(solution)/shard_map/ppermute | solution.py:438
  187.1 28.6 %collective-permute-start.14 = (bf16[256,2048]{1,0:T(8,128)(2,1)S(1)}, bf16[256,2048]{1,0:T(8,128)(2,1)S(1)}, u32[]{:S(2)}, u32[]{:S(2)}) collective-permute-start(bf16[256,2048]{1,0:T(8,128)(2,1)S(1)} %get-tuple-element.159.refs_0_.refs_1_), channel_id=1, source_target_pairs={{0,2},{1,3},{2,0},{3,1},{4,6},{5,7},{6,4},{7,5},{8,10},{9,11},{10,... | collective-permute-start | bytes 3145736 | tf_op jit(solution)/shard_map/ppermute | solution.py:438
  266.3 154.4 %collective-permute-start.18 = (bf16[4,256,1408]{2,1,0:T(8,128)(2,1)}, bf16[4,256,1408]{2,1,0:T(8,128)(2,1)}, u32[]{:S(2)}, u32[]{:S(2)}) collective-permute-start(bf16[4,256,1408]{2,1,0:T(8,128)(2,1)} %shard_map.313.refs_10_), channel_id=1, source_target_pairs={{0,4},{4,0},{8,12},{12,8},{16,20},{20,16},{24,28},{28,24},{1,5},{5... | collective-permute-start | bytes 8650760 | tf_op jit(solution)/shard_map/ppermute | solution.py:438
  277.6 154.9 %collective-permute-start.19 = (bf16[4,256,1408]{2,1,0:T(8,128)(2,1)}, bf16[4,256,1408]{2,1,0:T(8,128)(2,1)}, u32[]{:S(2)}, u32[]{:S(2)}) collective-permute-start(bf16[4,256,1408]{2,1,0:T(8,128)(2,1)} %shard_map.314.refs_9_), channel_id=1, source_target_pairs={{0,8},{4,12},{8,0},{12,4},{16,24},{20,28},{24,16},{28,20},{1,9},{5... | collective-permute-start | bytes 8650760 | tf_op jit(solution)/shard_map/ppermute | solution.py:438
  284.9 227.9 %collective-permute-start.20 = (bf16[4,256,1408]{2,1,0:T(8,128)(2,1)}, bf16[4,256,1408]{2,1,0:T(8,128)(2,1)}, u32[]{:S(2)}, u32[]{:S(2)}) collective-permute-start(bf16[4,256,1408]{2,1,0:T(8,128)(2,1)} %shard_map.315.refs_7_), channel_id=1, source_target_pairs={{0,4},{4,0},{8,12},{12,8},{16,20},{20,16},{24,28},{28,24},{1,5},{5... | collective-permute-start | bytes 8650760 | tf_op jit(solution)/shard_map/ppermute | solution.py:438
  287.3 25.9 %collective-permute-start.17 = (bf16[256,2048]{1,0:T(8,128)(2,1)}, bf16[256,2048]{1,0:T(8,128)(2,1)}, u32[]{:S(2)}, u32[]{:S(2)}) collective-permute-start(bf16[256,2048]{1,0:T(8,128)(2,1)} %add_convert_fusion.3.refs_9_), channel_id=1, source_target_pairs={{0,2},{1,3},{2,0},{3,1},{4,6},{5,7},{6,4},{7,5},{8,10},{9,11},{10,... | collective-permute-start | bytes 3145736 | tf_op jit(solution)/shard_map/ppermute | solution.py:438
  321.5 25.7 %collective-permute-start.1 = (bf16[256,2048]{1,0:T(8,128)(2,1)S(1)}, bf16[256,2048]{1,0:T(8,128)(2,1)}, u32[]{:S(2)}, u32[]{:S(2)}) collective-permute-start(bf16[256,2048]{1,0:T(8,128)(2,1)S(1)} %get-tuple-element.48.refs_0_), channel_id=1, source_target_pairs={{0,2},{1,3},{2,0},{3,1},{4,6},{5,7},{6,4},{7,5},{8,10},{9,11},{10,... | collective-permute-start | bytes 3145736 | tf_op jit(solution)/shard_map/cond/branch_1_fun/ppermute | solution.py:438
  364.7 53.2 %all-to-all-start = ((bf16[8,4,64,512]{3,2,1,0:T(8,128)(2,1)}), bf16[8,4,64,512]{3,2,1,0:T(8,128)(2,1)}, u32[]{:S(2)}, u32[]{:S(2)}) async-start(bf16[8,4,64,512]{3,2,1,0:T(8,128)(2,1)} %get-tuple-element.67), calls=%async_computation | async-start | bytes 4194304 | tf_op jit(solution)/shard_map/cond/branch_1_fun/all_to_all | solution.py:481
  372.4 25.4 %collective-permute-start.5 = (bf16[256,2048]{1,0:T(8,128)(2,1)S(1)}, bf16[256,2048]{1,0:T(8,128)(2,1)}, u32[]{:S(2)}, u32[]{:S(2)}) collective-permute-start(bf16[256,2048]{1,0:T(8,128)(2,1)S(1)} %add_convert_fusion), channel_id=1, source_target_pairs={{0,2},{1,3},{2,0},{3,1},{4,6},{5,7},{6,4},{7,5},{8,10},{9,11},{10,... | collective-permute-start | bytes 3145736 | tf_op jit(solution)/shard_map/cond/branch_1_fun/ppermute | solution.py:438
  417.9 136.7 %collective-permute-start.29 = (bf16[4,256,512]{2,1,0:T(8,128)(2,1)}, bf16[4,256,512]{2,1,0:T(8,128)(2,1)}, u32[]{:S(2)}, u32[]{:S(2)}) collective-permute-start(bf16[4,256,512]{2,1,0:T(8,128)(2,1)} %copy-done.128), channel_id=1, source_target_pairs={{0,4},{4,0},{8,12},{12,8},{16,20},{20,16},{24,28},{28,24},{1,5},{5... | collective-permute-start | bytes 3145736 | tf_op jit(solution)/shard_map/ppermute | solution.py:438
  441.8 52.1 %all-to-all-start.1 = ((bf16[8,4,64,512]{3,2,1,0:T(8,128)(2,1)}), bf16[8,4,64,512]{3,2,1,0:T(8,128)(2,1)}, u32[]{:S(2)}, u32[]{:S(2)}) async-start(bf16[8,4,64,512]{3,2,1,0:T(8,128)(2,1)} %copy-done.102), calls=%async_computation.1 | async-start | bytes 4194304 | tf_op jit(solution)/shard_map/cond/branch_1_fun/all_to_all | solution.py:481
  531.3 34.8 %collective-permute-start.31 = (bf16[2,256,1408]{2,1,0:T(8,128)(2,1)}, bf16[2,256,1408]{2,1,0:T(8,128)(2,1)}, u32[]{:S(2)}, u32[]{:S(2)}) collective-permute-start(bf16[2,256,1408]{2,1,0:T(8,128)(2,1)} %shard_map.317.refs_10_), channel_id=1, source_target_pairs={{0,8},{4,12},{8,0},{12,4},{16,24},{20,28},{24,16},{28,20},{1,9},{5... | collective-permute-start | bytes 4325384 | tf_op jit(solution)/shard_map/ppermute | solution.py:438
  539.4 57.7 %collective-permute-start.28 = (bf16[2,256,1408]{2,1,0:T(8,128)(2,1)}, bf16[2,256,1408]{2,1,0:T(8,128)(2,1)}, u32[]{:S(2)}, u32[]{:S(2)}) collective-permute-start(bf16[2,256,1408]{2,1,0:T(8,128)(2,1)} %shard_map.321.refs_13_), channel_id=1, source_target_pairs={{0,8},{4,12},{8,0},{12,4},{16,24},{20,28},{24,16},{28,20},{1,9},{5... | collective-permute-start | bytes 4325384 | tf_op jit(solution)/shard_map/ppermute | solution.py:438
  552.4 49.7 %collective-permute-start.30 = (bf16[2,256,1408]{2,1,0:T(8,128)(2,1)}, bf16[2,256,1408]{2,1,0:T(8,128)(2,1)}, u32[]{:S(2)}, u32[]{:S(2)}) collective-permute-start(bf16[2,256,1408]{2,1,0:T(8,128)(2,1)} %shard_map.318), channel_id=1, source_target_pairs={{0,4},{4,0},{8,12},{12,8},{16,20},{20,16},{24,28},{28,24},{1,5},{5... | collective-permute-start | bytes 4325384 | tf_op jit(solution)/shard_map/ppermute | solution.py:438
  559.0 113.9 %collective-permute-start.21 = (bf16[4,256,1024]{2,1,0:T(8,128)(2,1)}, bf16[4,256,1024]{2,1,0:T(8,128)(2,1)}, u32[]{:S(2)}, u32[]{:S(2)}) collective-permute-start(bf16[4,256,1024]{2,1,0:T(8,128)(2,1)} %copy-done.100), channel_id=1, source_target_pairs={{0,8},{4,12},{8,0},{12,4},{16,24},{20,28},{24,16},{28,20},{1,9},{5... | collective-permute-start | bytes 6291464 | tf_op jit(solution)/shard_map/ppermute | solution.py:438
  559.0 72.5 %collective-permute-start.22 = (bf16[4,256,1024]{2,1,0:T(8,128)(2,1)}, bf16[4,256,1024]{2,1,0:T(8,128)(2,1)}, u32[]{:S(2)}, u32[]{:S(2)}) collective-permute-start(bf16[4,256,1024]{2,1,0:T(8,128)(2,1)} %copy-done.101), channel_id=1, source_target_pairs={{0,4},{4,0},{8,12},{12,8},{16,20},{20,16},{24,28},{28,24},{1,5},{5... | collective-permute-start | bytes 6291464 | tf_op jit(solution)/shard_map/ppermute | solution.py:438
  566.2 47.2 %collective-permute-start.23 = (bf16[256,2048]{1,0:T(8,128)(2,1)}, bf16[256,2048]{1,0:T(8,128)(2,1)S(1)}, u32[]{:S(2)}, u32[]{:S(2)}) collective-permute-start(bf16[256,2048]{1,0:T(8,128)(2,1)} %get-tuple-element.215), channel_id=1, source_target_pairs={{0,1},{1,0},{2,3},{3,2},{4,5},{5,4},{6,7},{7,6},{8,9},{9,8},{10,11... | collective-permute-start | bytes 3145736 | tf_op jit(solution)/shard_map/ppermute | solution.py:438
  602.1 75.2 %collective-permute-start.36 = (bf16[1,256,1408]{2,1,0:T(8,128)(2,1)S(1)}, bf16[1,256,1408]{2,1,0:T(8,128)(2,1)}, u32[]{:S(2)}, u32[]{:S(2)}) collective-permute-start(bf16[1,256,1408]{2,1,0:T(8,128)(2,1)S(1)} %shard_map.327.refs_11_), channel_id=1, source_target_pairs={{0,16},{4,20},{8,24},{12,28},{16,0},{20,4},{24,8},{28,12},{1,17},{... | collective-permute-start | bytes 2162696 | tf_op jit(solution)/shard_map/ppermute | solution.py:438
  613.3 71.1 %collective-permute-start.37 = (bf16[2,256,512]{2,1,0:T(8,128)(2,1)}, bf16[2,256,512]{2,1,0:T(8,128)(2,1)}, u32[]{:S(2)}, u32[]{:S(2)}) collective-permute-start(bf16[2,256,512]{2,1,0:T(8,128)(2,1)} %shard_map.329.refs_11_), channel_id=1, source_target_pairs={{0,8},{4,12},{8,0},{12,4},{16,24},{20,28},{24,16},{28,20},{1,9},{5... | collective-permute-start | bytes 1572872 | tf_op jit(solution)/shard_map/ppermute | solution.py:438
  616.7 70.7 %collective-permute-start.35 = (bf16[1,256,1408]{2,1,0:T(8,128)(2,1)}, bf16[1,256,1408]{2,1,0:T(8,128)(2,1)}, u32[]{:S(2)}, u32[]{:S(2)}) collective-permute-start(bf16[1,256,1408]{2,1,0:T(8,128)(2,1)} %shard_map.328.refs_10_), channel_id=1, source_target_pairs={{0,16},{4,20},{8,24},{12,28},{16,0},{20,4},{24,8},{28,12},{1,17},{... | collective-permute-start | bytes 2162696 | tf_op jit(solution)/shard_map/ppermute | solution.py:438
  631.5 55.8 %collective-permute-start.39 = (bf16[256,2048]{1,0:T(8,128)(2,1)}, bf16[256,2048]{1,0:T(8,128)(2,1)}, u32[]{:S(2)}, u32[]{:S(2)}) collective-permute-start(bf16[256,2048]{1,0:T(8,128)(2,1)} %get-tuple-element.208.refs_14_.refs_1_), channel_id=1, source_target_pairs={{0,2},{1,3},{2,0},{3,1},{4,6},{5,7},{6,4},{7,5},{8,10},{9,11},{10,... | collective-permute-start | bytes 3145736 | tf_op jit(solution)/shard_map/ppermute | solution.py:438
  672.9 57.4 %collective-permute-start.33 = (bf16[2,256,1024]{2,1,0:T(8,128)(2,1)}, bf16[2,256,1024]{2,1,0:T(8,128)(2,1)}, u32[]{:S(2)}, u32[]{:S(2)}) collective-permute-start(bf16[2,256,1024]{2,1,0:T(8,128)(2,1)} %shard_map.332.refs_14_), channel_id=1, source_target_pairs={{0,8},{4,12},{8,0},{12,4},{16,24},{20,28},{24,16},{28,20},{1,9},{5... | collective-permute-start | bytes 3145736 | tf_op jit(solution)/shard_map/ppermute | solution.py:438
  677.3 63.1 %collective-permute-start.32 = (bf16[2,256,1024]{2,1,0:T(8,128)(2,1)}, bf16[2,256,1024]{2,1,0:T(8,128)(2,1)}, u32[]{:S(2)}, u32[]{:S(2)}) collective-permute-start(bf16[2,256,1024]{2,1,0:T(8,128)(2,1)} %shard_map.333.refs_11_), channel_id=1, source_target_pairs={{0,4},{4,0},{8,12},{12,8},{16,20},{20,16},{24,28},{28,24},{1,5},{5... | collective-permute-start | bytes 3145736 | tf_op jit(solution)/shard_map/ppermute | solution.py:438
  680.0 49.0 %all-to-all-start.4 = ((f32[8,1,13824]{2,1,0:T(1,128)}), f32[8,1,13824]{2,1,0:T(1,128)}, u32[]{:S(2)}, u32[]{:S(2)}) async-start(f32[8,1,13824]{2,1,0:T(1,128)} %reshape.175), calls=%async_computation.4 | async-start | bytes 884736 | tf_op jit(solution)/shard_map/all_to_all | solution.py:627
  684.4 40.5 %collective-permute-start.34 = (bf16[1,256,1408]{2,1,0:T(8,128)(2,1)}, bf16[1,256,1408]{2,1,0:T(8,128)(2,1)S(1)}, u32[]{:S(2)}, u32[]{:S(2)}) collective-permute-start(bf16[1,256,1408]{2,1,0:T(8,128)(2,1)} %copy-done.123), channel_id=1, source_target_pairs={{0,16},{4,20},{8,24},{12,28},{16,0},{20,4},{24,8},{28,12},{1,17},{... | collective-permute-start | bytes 2162696 | tf_op jit(solution)/shard_map/ppermute | solution.py:438
  687.3 118.6 %collective-permute-start.38 = (bf16[256,2048]{1,0:T(8,128)(2,1)}, bf16[256,2048]{1,0:T(8,128)(2,1)}, u32[]{:S(2)}, u32[]{:S(2)}) collective-permute-start(bf16[256,2048]{1,0:T(8,128)(2,1)} %get-tuple-element.208.refs_14_.refs_1_), channel_id=1, source_target_pairs={{0,1},{1,0},{2,3},{3,2},{4,5},{5,4},{6,7},{7,6},{8,9},{9,8},{10,11... | collective-permute-start | bytes 3145736 | tf_op jit(solution)/shard_map/ppermute | solution.py:438
  687.3 118.6 %collective-permute-start.40 = (bf16[256,2048]{1,0:T(8,128)(2,1)}, bf16[256,2048]{1,0:T(8,128)(2,1)}, u32[]{:S(2)}, u32[]{:S(2)}) collective-permute-start(bf16[256,2048]{1,0:T(8,128)(2,1)} %collective-permute-done.39.refs_3_), channel_id=1, source_target_pairs={{0,1},{1,0},{2,3},{3,2},{4,5},{5,4},{6,7},{7,6},{8,9},{9,8},{10,11... | collective-permute-start | bytes 3145736 | tf_op jit(solution)/shard_map/ppermute | solution.py:438
  737.1 61.5 %collective-permute-start.44 = (bf16[1,256,1024]{2,1,0:T(8,128)(2,1)}, bf16[1,256,1024]{2,1,0:T(8,128)(2,1)S(1)}, u32[]{:S(2)}, u32[]{:S(2)}) collective-permute-start(bf16[1,256,1024]{2,1,0:T(8,128)(2,1)} %shard_map.338.refs_15_), channel_id=1, source_target_pairs={{0,16},{4,20},{8,24},{12,28},{16,0},{20,4},{24,8},{28,12},{1,17},{... | collective-permute-start | bytes 1572872 | tf_op jit(solution)/shard_map/ppermute | solution.py:438
  742.7 59.5 %collective-permute-start.45 = (bf16[1,256,1024]{2,1,0:T(8,128)(2,1)S(1)}, bf16[1,256,1024]{2,1,0:T(8,128)(2,1)S(1)}, u32[]{:S(2)}, u32[]{:S(2)}) collective-permute-start(bf16[1,256,1024]{2,1,0:T(8,128)(2,1)S(1)} %shard_map.339.refs_5_), channel_id=1, source_target_pairs={{0,16},{4,20},{8,24},{12,28},{16,0},{20,4},{24,8},{28,12},{1,17},{... | collective-permute-start | bytes 1572872 | tf_op jit(solution)/shard_map/ppermute | solution.py:438
  748.2 47.8 %collective-permute-start.41 = (bf16[1,256,512]{2,1,0:T(8,128)(2,1)S(1)}, bf16[1,256,512]{2,1,0:T(8,128)(2,1)S(1)}, u32[]{:S(2)}, u32[]{:S(2)}) collective-permute-start(bf16[1,256,512]{2,1,0:T(8,128)(2,1)S(1)} %copy-done.127), channel_id=1, source_target_pairs={{0,16},{4,20},{8,24},{12,28},{16,0},{20,4},{24,8},{28,12},{1,17},{... | collective-permute-start | bytes 786440 | tf_op jit(solution)/shard_map/ppermute | solution.py:438
  (223 other events, 2531.6 us)

commit v3 on v2

--- a/solution.py
+++ b/solution.py
@@ -105,13 +105,11 @@
     run_ref[...] = contract((cols <= rows).astype(f32), decays, 1, 0, highest_precision)
 
 
-def state_kernel(key_ref, value_ref, run_ref, state_ref):
-    run = run_ref[...]
-    count = run.shape[0]
-    total = run[count - 1 : count]
-    left = (key_ref[...].astype(f32) * jnp.exp(total - run)).astype(bf16)
-    devices, _, rows, _ = state_ref.shape
-    state = across(value_ref[...], left).astype(bf16).reshape(devices, rows - EXTRA, DK)
+def total_lines(run):
+    return as_lines(run[run.shape[0] - 1 :])
+
+
+def as_lines(total):
     high = total.astype(bf16)
     rest = total - high.astype(f32)
     middle = rest.astype(bf16)
@@ -120,10 +118,81 @@
     lines = jnp.zeros((EXTRA, DK), f32)
     for at, line in enumerate((high, middle, low)):
         lines = jnp.where(place == at, line.astype(f32), lines)
-    lines = lines.astype(bf16)
-    for at in range(devices):
-        state_ref[at, 0, : rows - EXTRA] = state[at]
-        state_ref[at, 0, rows - EXTRA :] = lines
+    return lines.astype(bf16)
+
+
+def from_lines(lines):
+    lines = lines.astype(f32)
+    return lines[0:1] + lines[1:2] + lines[2:3]
+
+
+def state_of(key_ref, value_ref, run):
+    left = (key_ref[...].astype(f32) * jnp.exp(run[run.shape[0] - 1 :] - run)).astype(bf16)
+    return across(value_ref[...], left).astype(bf16)
+
+
+def state_kernel(key_ref, value_ref, run_ref, state_ref, lines_ref):
+    run = run_ref[...]
+    state_ref[0] = state_of(key_ref, value_ref, run)
+    lines_ref[0] = total_lines(run)
+
+
+def cut_state_kernel(me_ref, key_ref, value_ref, run_ref, keep_ref, send_ref, lines_ref, held):
+    run = run_ref[...]
+    held[...] = state_of(key_ref, value_ref, run).reshape(held.shape)
+    lines = total_lines(run)
+    y, z = me_ref[0] % 2, me_ref[0] // 2
+    for at in range(4):
+        keep_ref[0, at] = held[y * 4 + (z ^ at)]
+        send_ref[0, at] = held[(1 - y) * 4 + (z ^ at)]
+    lines_ref[0] = lines
+    send_ref[0, 4, :EXTRA] = lines
+
+
+def pair_kernel(me_ref, keep_ref, lines_ref, came_ref, first_ref, *part_refs):
+    lead = me_ref[0] % 2 == 0
+    own, other = from_lines(lines_ref[0]), from_lines(came_ref[0, 4, :EXTRA])
+    later = jnp.exp(jnp.where(lead, other, own))
+    lines = as_lines(own + other)
+    for at, part_ref in enumerate(part_refs):
+        mine, came = keep_ref[0, at].astype(f32), came_ref[0, at].astype(f32)
+        first = jnp.where(lead, mine, came)
+        first_ref[0, at] = first.astype(bf16)
+        rows = first.shape[0]
+        part_ref[0, :rows] = (first * later + jnp.where(lead, came, mine)).astype(bf16)
+        part_ref[0, rows:] = lines
+
+
+def chain_kernel(me_ref, *refs):
+    part_refs, out_refs = refs[:4], refs[4:8]
+    held, lines, entered = refs[8:]
+    z = me_ref[0] // 2
+    rows = held.shape[1]
+    for at in range(4):
+        held[z ^ at] = part_refs[at][0, :rows]
+        lines[z ^ at] = part_refs[at][0, rows:]
+    carry = jnp.zeros(held.shape[1:], f32)
+    for at in range(4):
+        entered[at] = carry.astype(bf16)
+        carry = carry * jnp.exp(from_lines(lines[at])) + held[at].astype(f32)
+    for at in range(4):
+        out_refs[at][0] = entered[z ^ at]
+
+
+def enter_kernel(me_ref, lines_ref, came_ref, first_ref, *refs):
+    *part_refs, whole_ref, send_ref = refs
+    y, z = me_ref[0] % 2, me_ref[0] // 2
+    lead = y == 0
+    earlier = jnp.exp(jnp.where(lead, from_lines(lines_ref[0]), from_lines(came_ref[0, 0, :EXTRA])))
+    for at in range(4):
+        pair = part_refs[at][0].astype(f32)
+        inner = pair * earlier + first_ref[0, at].astype(f32)
+        whole_ref[0, 0, z ^ at] = jnp.where(lead, pair, inner).astype(bf16)
+        send_ref[0, z ^ at] = jnp.where(lead, inner, pair).astype(bf16)
+
+
+def join_kernel(me_ref, came_ref, whole_ref):
+    whole_ref[0, 0] = came_ref[0]
 
 
 def score_kernel(query_ref, key_ref, run_ref, score_ref):
@@ -255,9 +324,8 @@
     for step in range(count):
         at = count - 1 - step if reverse else step
         out_ref[at, 0] = carry.astype(bf16)
-        lines = lines_ref[at, 0].astype(f32)
-        total = lines[0:1] + lines[1:2] + lines[2:3]
-        carry = carry * jnp.exp(total) + parts_ref[at, 0, :rows].astype(f32)
+        total = from_lines(lines_ref[at, 0])
+        carry = carry * jnp.exp(total) + parts_ref[at, 0].astype(f32)
 
 
 def hold_kernel(values_ref, out_ref):
@@ -307,10 +375,9 @@
 
 
 def input_back_kernel(
-    place_ref, input_ref, own_ref, first_ref, last_ref, rank_ref, down_ref, middle_ref, gain_ref, rows_ref, part_ref
+    place_ref, input_ref, sum_ref, rank_ref, down_ref, middle_ref, gain_ref, rows_ref, part_ref
 ):
-    grad = own_ref[...].astype(f32) + first_ref[...].astype(f32) + last_ref[...].astype(f32)
-    grad = grad + contract(rank_ref[...], down_ref[...], 0, 1)
+    grad = sum_ref[0].astype(f32) + contract(rank_ref[...], down_ref[...], 0, 1)
     back, part = norm_back(input_ref[0].astype(f32), grad, gain_ref[...].astype(f32))
     rows_ref[...] = (middle_ref[...] + back).astype(bf16)
     add_part(part_ref, part)
@@ -374,16 +441,41 @@
             out_ref[0] = refs[k][...]
 
 
-def sum_kernel(count, *refs):
+def output_kernel(order_ref, middle_ref, *refs):
     out_ref = refs[-1]
-    total = against(refs[0][...], refs[count][...])
-    for k in range(1, count):
-        total = total + against(refs[k][...], refs[count + k][...])
-    out_ref[...] = total.astype(out_ref.dtype)
-
-
-def grad_kernel(parts, groups, turned, pick_ref, *refs):
-    cuts, refs = refs[:parts], refs[parts:]
+    step = pl.program_id(0)
+
+    @pl.when(step == 0)
+    def _():
+        out_ref[0] = (refs[0][...].astype(f32) + middle_ref[...]).astype(bf16)
+
+    for k in range(1, 4):
+
+        @pl.when(step == k)
+        def _():
+            out_ref[0] = refs[k][...]
+
+
+def sum_kernel(order_ref, *refs):
+    *refs, out_ref, held = refs
+    count = (len(refs)) // 2
+    rows = out_ref.shape[1]
+
+    @pl.when(pl.program_id(1) == 0)
+    def _():
+        total = against(refs[0][...], refs[count][...])
+        for k in range(1, count):
+            total = total + against(refs[k][...], refs[count + k][...])
+        held[...] = total.astype(bf16)
+        out_ref[0] = held[:rows]
+
+    @pl.when(pl.program_id(1) == 1)
+    def _():
+        out_ref[0] = held[rows:]
+
+
+def grad_kernel(parts, groups, cut_groups, turned, pick_ref, *refs):
+    cuts, refs = refs[: parts * cut_groups], refs[parts * cut_groups :]
     others, refs = refs[: parts * groups], refs[parts * groups :]
     arrived, out_ref = refs[:-1], refs[-1]
     for group in range(groups):
@@ -391,7 +483,8 @@
         members = others[group * parts : (group + 1) * parts]
         width = members[0].shape[1]
         columns = slice(group * width, (group + 1) * width)
-        for cut, other in zip(cuts, members):
+        first = group * parts if cut_groups > 1 else 0
+        for cut, other in zip(cuts[first : first + parts], members):
             part = across(cut[...], other[...])
             total = part if total is None else total + part
         for ref in arrived:
@@ -406,12 +499,12 @@
     return jax.ShapeDtypeStruct(shape, dtype)
 
 
-def grid_call(kernel, grid, in_specs, out_specs, out_shape, args, prefetch=0, after=(), scratch=(), into=None):
+def grid_call(kernel, grid, in_specs, out_specs, out_shape, args, prefetch=0, after=(), scratch=(), into=()):
     first, last = len(args), len(args) + len(after)
     aliases = {}
-    if into is not None:
-        aliases = {last: into[1]}
-        after = (*after, into[0])
+    for array, at in into:
+        aliases[last] = at
+        after = (*after, array)
         last += 1
 
     def run(*refs):
@@ -456,20 +549,16 @@
     return grid_call(hold_kernel, (), [spec], spec, struct(values.shape, values.dtype), [values], after=after)
 
 
-def chunk_spec(count, extra=0, first=0):
-    return pl.BlockSpec((count, 1, DK // count + extra, DK), lambda b, *_: (0, b + first, 0, 0))
+def chunk_spec(count, first=0):
+    return pl.BlockSpec((count, 1, DK // count, DK), lambda b, *_: (0, b + first, 0, 0))
 
 
 def carried(pieces, lines, reverse, after=()):
-    count, seq_count, rows, _ = pieces.shape
-    share = DK // count
+    count, seq_count, share, _ = pieces.shape
     return grid_call(
         functools.partial(prefix_kernel, reverse),
         (seq_count,),
-        [
-            pl.BlockSpec((count, 1, EXTRA, DK), lambda b: (0, b, share // EXTRA, 0)),
-            chunk_spec(count, rows - share),
-        ],
+        [pl.BlockSpec((count, 1, EXTRA, DK), lambda b: (0, b, 0, 0)), chunk_spec(count)],
         chunk_spec(count),
         struct((count, seq_count, share, DK), bf16),
         [lines, pieces],
@@ -498,25 +587,13 @@
     return own, first, second, third
 
 
-def in_order(blocks, order, after=()):
-    length, width = blocks[0].shape
-    whole = pl.BlockSpec((length, width), lambda k, order: (0, 0))
-    return grid_call(
-        place_kernel,
-        (4,),
-        [whole] * 4,
-        pl.BlockSpec((1, length, width), lambda k, order: (order[k], 0, 0)),
-        struct((4, length, width), blocks[0].dtype),
-        [order, *blocks],
-        prefetch=1,
-        after=after,
-    )
-
-
 def grad_part(cuts, groups, picks, arrived, dtype, turned=False, after=()):
     rows = ROWS
     width = groups[0][0][0].shape[1]
     whole = width * len(groups)
+    parts = len(groups[0])
+    cut_groups = len(cuts)
+    cuts = [block for group in cuts for block in group]
     share = cuts[0][0].shape[1] // lax.axis_size("seq")
     chunks = len(picks)
     me = lax.axis_index("seq")
@@ -533,7 +610,7 @@
         out_spec = pl.BlockSpec((1, share, whole), lambda k, pick: (k, 0, 0))
         shape = (chunks, share, whole)
     return grid_call(
-        functools.partial(grad_kernel, len(cuts), len(groups), turned),
+        functools.partial(grad_kernel, parts, len(groups), cut_groups, turned),
         (chunks,),
         in_specs,
         out_spec,
@@ -546,85 +623,61 @@
 
 class Scatter:
     def __init__(self, cuts, groups, order, turned=False):
+        cuts = cuts if isinstance(cuts[0], list) else [cuts]
         self.cuts, self.groups, self.order, self.turned = cuts, groups, order, turned
         self.split = lax.axis_size("seq") == 8
+        self.came = [None] * 3
 
     def part(self, picks, arrived, dtype, turned=False, after=()):
         return grad_part(self.cuts, self.groups, picks, arrived, dtype, turned, after)
 
-    def send(self, after=()):
+    def hop(self, at, part):
+        if self.split:
+            return swap(part, "seq", self.order[at])
+        return part if at else lax.psum_scatter(part, "seq", scatter_dimension=0, tiled=True)
+
+    def away(self, after=()):
         if not self.split:
-            total = jnp.concatenate(
+            return jnp.concatenate(
                 [
                     sum(
                         across(a[i * ROWS : (i + 1) * ROWS], b[j * ROWS : (j + 1) * ROWS])
-                        for (a, i), (b, j) in zip(self.cuts, group)
+                        for (a, i), (b, j) in zip(cuts, group)
                     ).astype(bf16)
-                    for group in self.groups
+                    for cuts, group in zip(
+                        self.cuts if len(self.cuts) > 1 else self.cuts * len(self.groups), self.groups
+                    )
                 ],
                 axis=1,
             )
-            self.total = lax.psum_scatter(total, "seq", scatter_dimension=0, tiled=True).astype(f32)
-            return self.total
         a, b, c = self.order
-        away = self.part([a ^ b, a ^ b ^ c, a ^ c, a], [], bf16, after=after)
-        self.came = swap(away, "seq", a)
-        return away
-
-    def step_one(self, after=()):
+        return self.part([a ^ b, a ^ b ^ c, a ^ c, a], [], bf16, after=after)
+
+    def one(self, after=()):
         if not self.split:
-            return self.total
+            return self.came[0]
         a, b, c = self.order
-        first = self.part([b, b ^ c], [(self.came, 0)], bf16, after=after)
-        self.came_first = swap(first, "seq", b)
-        return first
-
-    def step_two(self, after=()):
+        return self.part([b, b ^ c], [(self.came[0], 0)], bf16, after=after)
+
+    def two(self, after=()):
         if not self.split:
-            return self.total
-        a, b, c = self.order
-        second = self.part([c], [(self.came, 2), (self.came_first, 1)], bf16, after=after)
-        self.came_second = swap(second, "seq", c)
-        return second
+            return self.came[0]
+        c = self.order[2]
+        return self.part([c], [(self.came[0], 2), (self.came[1], 1)], bf16, after=after)
 
     def last(self, after=()):
         if not self.split:
-            return self.total.T if self.turned else self.total
-        total = self.part(
-            [0],
-            [(self.came, 3), (self.came_first, 0), (self.came_second, 0)],
-            f32,
-            self.turned,
-            after=after,
-        )
+            total = self.came[0].astype(f32)
+            return total.T if self.turned else total
+        arrived = [(self.came[0], 3), (self.came[1], 0), (self.came[2], 0)]
+        total = self.part([0], arrived, f32, self.turned, after=after)
         return total if self.turned else total[0]
-
-
-def product_sum(pairs, dtype, after=()):
-    rows = pairs[0][0].shape[0]
-    width = pairs[0][1].shape[0]
-    tile = 512
-    in_specs = [pl.BlockSpec((rows, p[0].shape[1]), lambda j: (0, 0)) for p in pairs]
-    in_specs += [pl.BlockSpec((tile, p[1].shape[1]), lambda j: (j, 0)) for p in pairs]
-    return grid_call(
-        functools.partial(sum_kernel, len(pairs)),
-        (width // tile,),
-        in_specs,
-        pl.BlockSpec((rows, tile), lambda j: (0, j)),
-        struct((rows, width), dtype),
-        [p[0] for p in pairs] + [p[1] for p in pairs],
-        after=after,
-    )
 
 
 def sum_over(values, axis):
     for bit in bits_of(lax.axis_size(axis)):
         values = values + swap(values, axis, bit)
     return values
-
-
-def spread_sum(values):
-    return jnp.sum(lax.all_to_all(values, "seq", 0, 0), axis=0)
 
 
 def local(
@@ -704,19 +757,97 @@
         )
         return rank_rows, run
 
-    def states(norm, run, at, into=None):
+    quarter = DK // 8
+    me = lax.axis_index("seq").astype(jnp.int32).reshape(1)
+
+    def quarters(count, size=quarter):
+        return pl.BlockSpec((1, count, size, DK), lambda b, *_: (b, 0, 0, 0))
+
+    def states(norm, run, after=()):
         keys = product(norm, key_weight).astype(bf16)
         values = product(norm, value_weight).astype(bf16)
-        state = grid_call(
-            state_kernel,
+        lines = struct((half, EXTRA, DK), bf16)
+        if devices != 8:
+            parts = grid_call(
+                state_kernel,
+                (half,),
+                [row_spec(DK)] * 3,
+                [square(DK), line(EXTRA, DK)],
+                [struct((half, DK, DK), bf16), lines],
+                [keys, values, run],
+                after=after,
+            )
+        else:
+            parts = grid_call(
+                cut_state_kernel,
+                (half,),
+                [row_spec(DK)] * 3,
+                [quarters(4), quarters(5), line(EXTRA, DK)],
+                [struct((half, 4, quarter, DK), bf16), struct((half, 5, quarter, DK), bf16), lines],
+                [me, keys, values, run],
+                prefetch=1,
+                after=after,
+                scratch=[pltpu.VMEM((8, quarter, DK), bf16)],
+            )
+        return keys, values, parts
+
+    def pairs(parts, came, after=()):
+        keep, _, lines = parts
+        return grid_call(
+            pair_kernel,
             (half,),
-            [row_spec(DK)] * 3,
-            chunk_spec(devices, EXTRA, at),
-            struct((devices, seq_count, share + EXTRA, DK), bf16),
-            [keys, values, run],
-            into=None if into is None else (into, 0),
-        )
-        return keys, values, state
+            [quarters(4), line(EXTRA, DK), quarters(5)],
+            [quarters(4)] + [line(quarter + EXTRA, DK)] * 4,
+            [struct((half, 4, quarter, DK), bf16)] + [struct((half, quarter + EXTRA, DK), bf16)] * 4,
+            [me, keep, lines, came],
+            prefetch=1,
+            after=after,
+        )
+
+    def chain(own, came, after=()):
+        return grid_call(
+            chain_kernel,
+            (half,),
+            [line(quarter + EXTRA, DK)] * 4,
+            [line(quarter, DK)] * 4,
+            [struct((half, quarter, DK), bf16)] * 4,
+            [me, own, *came],
+            prefetch=1,
+            after=after,
+            scratch=[
+                pltpu.VMEM((4, quarter, DK), bf16),
+                pltpu.VMEM((4, EXTRA, DK), bf16),
+                pltpu.VMEM((4, quarter, DK), bf16),
+            ],
+        )
+
+    def enter(parts, came, first, own, others, after=()):
+        return grid_call(
+            enter_kernel,
+            (half,),
+            [line(EXTRA, DK), pl.BlockSpec((1, 1, quarter, DK), lambda b, *_: (b, 4, 0, 0)), quarters(4)]
+            + [line(quarter, DK)] * 4,
+            [pl.BlockSpec((1, 1, 4, quarter, DK), lambda b, me: (me[0] % 2, b, 0, 0, 0)), quarters(4)],
+            [struct((2, half, 4, quarter, DK), bf16), struct((half, 4, quarter, DK), bf16)],
+            [me, parts[2], came, first, own, *others],
+            prefetch=1,
+            after=after,
+        )
+
+    def join(whole, came):
+        return grid_call(
+            join_kernel,
+            (half,),
+            [quarters(4)],
+            pl.BlockSpec((1, 1, 4, quarter, DK), lambda b, me: (1 - me[0] % 2, b, 0, 0, 0)),
+            struct(whole.shape, bf16),
+            [me, came],
+            prefetch=1,
+            into=[(whole, 0)],
+        )
+
+    def along(parts):
+        return [swap(part, "seq", 2 * at) for at, part in enumerate(parts, 1)]
 
     def scored(norm, keys, run, after=()):
         queries = product(norm, query_weight).astype(bf16)
@@ -737,7 +868,7 @@
             mix_kernel,
             (half,),
             [row_spec(DK)] * 3
-            + [square(length), chunk_spec(devices, 0, at), row_spec(DK), fixed((1, DK))],
+            + [square(length), state_specs[at], row_spec(DK), fixed((1, DK))],
             [row_spec(DK), row_spec(DK)],
             [rows_of(DK, f32), rows_of(DK, bf16)],
             [queries, values, run, scores, incoming, gates, gain],
@@ -748,22 +879,53 @@
     place_index = order[:1]
     norm_far, grads_far = first_rows(order[half:])
     rank_far, run_far = decays(norm_far)
-    keys_far, values_far, state = states(norm_far, run_far, 0)
-    norm_near, grads_near = first_rows(order[:half])
+    keys_far, values_far, parts_far = states(norm_far, run_far)
+    norm_near, grads_near = first_rows(order[:half], [parts_far[1]])
     rank_near, run_near = decays(norm_near)
-    keys_near, values_near, state = states(norm_near, run_near, half, state)
-    queries_far, gates_far, scores_far = scored(norm_far, keys_far, run_far, [state])
-    queries_near, gates_near, scores_near = scored(norm_near, keys_near, run_near, [scores_far])
-    lines = deal(state)
-    incoming = deal(carried(lines, lines, False, [scores_far, gates_far, scores_near, gates_near]))
-
-    mixed_far, branch_far = mix(queries_far, values_far, run_far, scores_far, incoming, 0, gates_far)
+    keys_near, values_near, parts_near = states(norm_near, run_near)
+    queries_far, gates_far, scores_far = scored(norm_far, keys_far, run_far, [parts_near[1]])
+    if devices != 8:
+        queries_near, gates_near, scores_near = scored(norm_near, keys_near, run_near, [scores_far])
+        state = jnp.concatenate([parts_far[0], parts_near[0]], axis=0)
+        state = jnp.moveaxis(state.reshape(seq_count, devices, share, DK), 1, 0)
+        every_line = jnp.concatenate([parts_far[1], parts_near[1]], axis=0)
+        lines = deal(jnp.broadcast_to(every_line[None], (devices, *every_line.shape)))
+        incoming = deal(carried(deal(state), lines, False))
+        incoming_far = incoming_near = incoming
+        state_specs = [chunk_spec(devices, at) for at in (0, half)]
+    else:
+        came_far = swap(parts_far[1], "seq", 1)
+        came_near = swap(parts_near[1], "seq", 1)
+        first_far, *pair_far = pairs(parts_far, came_far, [parts_near[1]])
+        others_far = along(pair_far[1:])
+        first_near, *pair_near = pairs(parts_near, came_near, [pair_far[0], scores_far])
+        others_near = along(pair_near[1:])
+        chain_far = chain(pair_far[0], others_far, [pair_near[0]])
+        back_far = along(chain_far[1:])
+        queries_near, gates_near, scores_near = scored(norm_near, keys_near, run_near, [chain_far[0]])
+        chain_near = chain(pair_near[0], others_near, [chain_far[0]])
+        back_near = along(chain_near[1:])
+        whole_far, send_far = enter(parts_far, came_far, first_far, chain_far[0], back_far, [chain_near[0]])
+        half_far = swap(send_far, "seq", 1)
+        whole_near, send_near = enter(
+            parts_near, came_near, first_near, chain_near[0], back_near, [send_far, scores_near]
+        )
+        half_near = swap(send_near, "seq", 1)
+        incoming_far = join(whole_far, half_far)
+        incoming_near = join(whole_near, half_near)
+        every_line = jnp.concatenate([parts_far[2], parts_near[2]], axis=0)
+        lines = deal(jnp.broadcast_to(every_line[None], (devices, *every_line.shape)))
+        state_specs = [
+            pl.BlockSpec((2, 1, 4, quarter, DK), lambda b, *_: (0, b, 0, 0, 0)) for at in range(2)
+        ]
+
+    mixed_far, branch_far = mix(queries_far, values_far, run_far, scores_far, incoming_far, 0, gates_far)
     out_far = product(branch_far, out_weight).astype(bf16)
     out_third = swap(out_far[length:], "tensor", 1)
     out_second = (out_far[:length].astype(f32) + out_third.astype(f32)).astype(bf16)
     out_last = swap(out_second, "tensor", 2)
     mixed_near, branch_near = mix(
-        queries_near, values_near, run_near, scores_near, incoming, half, gates_near, [out_second]
+        queries_near, values_near, run_near, scores_near, incoming_near, 1, gates_near, [out_second]
     )
     out_near = product(branch_near, out_weight).astype(bf16)
     out_parts = (out_near[:length], swap(out_near[length:], "tensor", 1), out_last)
@@ -814,8 +976,6 @@
     inner, swish_back, up_back = (
         [(feed_near[k], 0), (feed_near[k], 1), (feed_two[k], 0), (feed_three[k], 0)] for k in range(3)
     )
-    second_parts, second_sent = tensor_reduce(halves(feed_near[3]), (feed_two[3], feed_three[3]))
-    down_near, down_far = halves(feed_near[4]), (feed_two[4], feed_three[4])
 
     bits = bits_of(devices)
     late_bits = [bits[1], bits[0], *bits[2:]]
@@ -823,9 +983,20 @@
     swish_grad = Scatter(second_blocks, [swish_back], bits)
     up_grad = Scatter(second_blocks, [up_back], bits)
     down_grad = Scatter(blocks(grads_near, grads_far), [inner], late_bits, True)
-    swish_away = swish_grad.send()
-    down_away = down_grad.send([second_sent, swish_away])
-    up_away = up_grad.send([down_away])
+    swish_away = swish_grad.away([lines])
+    swish_grad.came[0] = swish_grad.hop(0, swish_away)
+
+    def second_sum(near, far):
+        parts, _ = tensor_reduce(near, far)
+        down_away = down_grad.away([swish_away])
+        return parts[1:], down_away, up_grad.away([down_away])
+
+    second_parts, down_away, up_away = region(
+        second_sum, halves(feed_near[3]), (feed_two[3], feed_three[3])
+    )
+    second_parts = (feed_near[3], *second_parts)
+    down_grad.came[0] = down_grad.hop(0, down_away)
+    up_grad.came[0] = up_grad.hop(0, up_away)
 
     middle_grad, own_rows, mlp_norm_part = grid_call(
         middle_back_kernel,
@@ -835,7 +1006,6 @@
         [struct((length, width), f32), struct((length, width), bf16), struct((1, width), f32)],
         [place_index, cotangent, *second_parts, middle, gain_two],
         prefetch=1,
-        after=[up_away],
     )
 
     def branch_back(first, second, mixed, gates, queries, run, at, into=None):
@@ -846,55 +1016,73 @@
                 whole_block, whole_block, fixed((DK, width)), row_spec(DK), row_spec(DK), fixed((1, DK)),
                 row_spec(DK), row_spec(DK),
             ],
-            [row_spec(DK), row_spec(DK), line(1, DK), chunk_spec(devices, 0, at)],
+            [row_spec(DK), row_spec(DK), line(1, DK), chunk_spec(devices, at)],
             [rows_of(DK, bf16), rows_of(DK, bf16), struct((half, 1, DK), f32), chunks],
             [first, second, out_weight, mixed, gates, gain, queries, run],
-            into=None if into is None else (into, 3),
-        )
-
-    def gather_back(own_rows):
-        *rows, rows_third = tensor_gather(own_rows)
+            into=() if into is None else [(into, 3)],
+        )
+
+    first_row = swap(own_rows, "tensor", 1)
+
+    def gather_back(own_rows, first_row):
+        second_row = swap(own_rows, "tensor", 2)
         *near, state_back = branch_back(
-            rows[0], rows[1], mixed_near, gates_near, queries_near, run_near, half
-        )
-        rows.append(rows_third([near[0]]))
+            own_rows, first_row, mixed_near, gates_near, queries_near, run_near, half
+        )
+        third_row = swap(second_row, "tensor", 1)
         *far, state_back = branch_back(
-            rows[2], rows[3], mixed_far, gates_far, queries_far, run_far, 0, state_back
-        )
-        return rows[1:], near, far, state_back
-
-    others, near, far, state_back = region(gather_back, own_rows)
-    rows = [own_rows, *others]
+            second_row, third_row, mixed_far, gates_far, queries_far, run_far, 0, state_back
+        )
+        return second_row, third_row, near, far, state_back
+
+    second_row, third_row, near, far, state_back = region(gather_back, own_rows, first_row)
+    rows = [(values, 0) for values in (own_rows, first_row, second_row, third_row)]
     gate_back_near, mixed_back_near, gain_back_near = near
     gate_back_far, mixed_back_far, gain_back_far = far
     norms = blocks(norm_near, norm_far)
-    out_grad = Scatter([(values, 0) for values in rows], [blocks(branch_near, branch_far)], bits, True)
-    out_away = out_grad.send([state_back])
+
+    def ordered_output():
+        return grid_call(
+            output_kernel,
+            (4,),
+            [whole_block]
+            + [pl.BlockSpec((length, width), lambda k, order, at=at: (at, 0)) for at in (0, 1, 0, 0)],
+            pl.BlockSpec((1, length, width), lambda k, order: (order[k], 0, 0)),
+            struct((seq_count, length, width), bf16),
+            [order, middle, feed_near[4], feed_near[4], feed_two[4], feed_three[4]],
+            prefetch=1,
+        )
+
+    out_grad = Scatter(rows, [blocks(branch_near, branch_far)], bits, True)
+    gate_grad = Scatter(norms, [blocks(gate_back_near, gate_back_far)], bits)
 
     def states_back(state_back):
-        came = deal(state_back)
-        down_parts, _ = tensor_reduce(down_near, down_far)
-        return came, down_parts[1:]
-
-    came, down_parts = region(states_back, state_back)
-    swish_one = swish_grad.step_one([came])
-    down_one = down_grad.step_one([swish_one])
-
-    def states_out(came, down_parts):
-        outgoing = deal(carried(came, lines, True, [swish_one, down_one]))
-        own = sum((part.astype(f32) for part in (down_near[0], *down_parts)), middle).astype(bf16)
-        *blocks, third = tensor_gather(own)
-        return outgoing, [*blocks, third([])]
-
-    outgoing, output_blocks = region(states_out, came, down_parts)
-
-    def mix_back(queries, keys, values, mixed_back, run, scores, at, rank_rows, after):
+        swish_one = swish_grad.one([state_back])
+        gate_away = gate_grad.away([swish_one])
+        return deal(state_back), swish_one, gate_away, out_grad.away([gate_away]), ordered_output()
+
+    came, swish_one, gate_away, out_away, output = region(states_back, state_back)
+    layer_output = lax.psum(output, "tensor")
+
+    def states_out(came, swish_one, out_away):
+        up_one = up_grad.one([came])
+        return (
+            deal(carried(came, lines, True)), swish_grad.hop(1, swish_one), out_grad.hop(0, out_away),
+            up_one, down_grad.one([up_one]),
+        )
+
+    outgoing, swish_grad.came[1], out_grad.came[0], up_one, down_one = region(
+        states_out, came, swish_one, out_away
+    )
+    swish_two = swish_grad.two([outgoing])
+
+    def mix_back(queries, keys, values, mixed_back, run, scores, incoming, at, rank_rows, after):
         return grid_call(
             mix_back_kernel,
             (half,),
             [row_spec(DK)] * 5
             + [square(length)]
-            + [chunk_spec(devices, 0, at)] * 2
+            + [state_specs[1 if at else 0], chunk_spec(devices, at)]
             + [row_spec(rank), fixed((rank, DK)), fixed((1, DK))],
             [row_spec(DK)] * 3 + [line(rank, length), line(rank, DK), line(1, DK)],
             [rows_of(DK, bf16)] * 3
@@ -910,57 +1098,92 @@
             after=after,
         )
 
-    query_back_near, key_back_near, value_back_near, rank_part_near, up_part_near, bias_part_near = (
-        mix_back(
+    def first_part(query_back, key_back, value_back, gate_back, first, into=()):
+        tile = 512
+        pairs = [
+            (query_back, query_weight),
+            (key_back, key_weight),
+            (value_back, value_weight),
+            (gate_back, gate_weight),
+        ]
+        return grid_call(
+            sum_kernel,
+            (width // tile, half),
+            [pl.BlockSpec((half_rows, DK), lambda j, r, order: (0, 0))] * 4
+            + [pl.BlockSpec((tile, DK), lambda j, r, order: (j, 0))] * 4,
+            pl.BlockSpec((1, length, tile), lambda j, r, order: (order[first + r], 0, j)),
+            struct((seq_count, length, width), bf16),
+            [order, *[p[0] for p in pairs], *[p[1] for p in pairs]],
+            prefetch=1,
+            into=into,
+            scratch=[pltpu.VMEM((half_rows, tile), bf16)],
+        )
+
+    def mixed_pair(near, far):
+        query_key = Scatter(norms, [blocks(near[0], far[0]), blocks(near[1], far[1])], bits)
+        return query_key, Scatter(norms, [blocks(near[2], far[2])], late_bits)
+
+    def mixes_back(up_one, swish_two, down_one, gate_away):
+        near = mix_back(
             queries_near, keys_near, values_near, mixed_back_near, run_near, scores_near,
-            half, rank_near, [],
-        )
-    )
-    query_back_far, key_back_far, value_back_far, rank_part_far, up_part_far, bias_part_far = mix_back(
-        queries_far, keys_far, values_far, mixed_back_far, run_far, scores_far,
-        0, rank_far, [bias_part_near],
-    )
-    up_one = up_grad.step_one([bias_part_far])
-
-    query_gate_grad = Scatter(
-        norms, [blocks(query_back_near, query_back_far), blocks(gate_back_near, gate_back_far)], bits
-    )
-    key_value_grad = Scatter(
-        norms, [blocks(key_back_near, key_back_far), blocks(value_back_near, value_back_far)], late_bits
-    )
-    query_gate_away = query_gate_grad.send([up_one])
-    key_value_away = key_value_grad.send([query_gate_away])
-
-    def first_part(query_back, key_back, value_back, gate_back, after):
-        return product_sum(
-            [
-                (query_back, query_weight),
-                (key_back, key_weight),
-                (value_back, value_weight),
-                (gate_back, gate_weight),
-            ],
-            bf16,
-            after,
-        )
-
-    first_far = first_part(query_back_far, key_back_far, value_back_far, gate_back_far, [key_value_away])
-    first_near = first_part(query_back_near, key_back_near, value_back_near, gate_back_near, [first_far])
-    first_parts, first_sent = tensor_reduce(halves(first_near), halves(first_far))
-
-    rank_part = jnp.concatenate([rank_part_near, rank_part_far], axis=0)
-    rank_part = rank_part + swap(rank_part, "tensor", 1)[jnp.array([1, 0, 3, 2])]
-    rank_part = rank_part + swap(rank_part, "tensor", 2)[jnp.array([2, 3, 0, 1])]
-    rank_back = rank_part.astype(bf16)
-
-    swish_two = swish_grad.step_two([first_near, first_sent])
-    down_two = down_grad.step_two([swish_two])
-    out_one = out_grad.step_one([down_two])
-    up_two = up_grad.step_two([out_one])
+            incoming_near, half, rank_near, [swish_two],
+        )
+        far = mix_back(
+            queries_far, keys_far, values_far, mixed_back_far, run_far, scores_far,
+            incoming_far, 0, rank_far, [near[5]],
+        )
+        query_key, value = mixed_pair(near, far)
+        query_key_away = query_key.away([far[5]])
+        value_away = value.away([query_key_away])
+        first_sum = first_part(*far[:3], gate_back_far, half)
+        first_sum = first_part(*near[:3], gate_back_near, 0, [(first_sum, 0)])
+        return (
+            up_grad.hop(1, up_one), swish_grad.hop(2, swish_two), down_grad.hop(1, down_one),
+            gate_grad.hop(0, gate_away), near, far, query_key_away, value_away, first_sum, out_grad.one([first_sum]),
+        )
+
+    (
+        up_grad.came[1], swish_grad.came[2], down_grad.came[1], gate_grad.came[0], near, far, query_key_away,
+        value_away, first_sum, out_one,
+    ) = region(mixes_back, up_one, swish_two, down_one, gate_away)
+    gate_one = gate_grad.one([first_sum])
+    down_two = down_grad.two([gate_one])
+    rank_part_near, up_part_near, bias_part_near = near[3:]
+    rank_part_far, up_part_far, bias_part_far = far[3:]
+    query_key_grad, value_grad = mixed_pair(near, far)
+    first_grad = lax.psum_scatter(first_sum, "tensor", scatter_dimension=0, tiled=True)
+
+    def third_window(query_key_away, value_away, gate_one, down_two):
+        rank_part = jnp.concatenate([rank_part_near, rank_part_far], axis=0)
+        rank_part = lax.all_to_all(jnp.take(rank_part, order, axis=0), "tensor", 0, 0)
+        return (
+            query_key_grad.hop(0, query_key_away), value_grad.hop(0, value_away),
+            gate_grad.hop(1, gate_one), down_grad.hop(2, down_two), up_grad.two(),
+            swish_grad.last(), jnp.sum(rank_part, axis=0).astype(bf16),
+        )
+
+    (
+        query_key_grad.came[0], value_grad.came[0], gate_grad.came[1], down_grad.came[2], up_two,
+        swish_share, rank_back,
+    ) = region(third_window, query_key_away, value_away, gate_one, down_two)
+    query_key_one = query_key_grad.one()
+    value_one = value_grad.one([query_key_one])
+
+    def fourth_window(query_key_one, value_one, up_two, out_one, layer_output):
+        return (
+            query_key_grad.hop(1, query_key_one), value_grad.hop(1, value_one), up_grad.hop(2, up_two),
+            out_grad.hop(1, out_one), gate_grad.two(), down_grad.last(), layer_output,
+        )
+
+    (
+        query_key_grad.came[1], value_grad.came[1], up_grad.came[2], out_grad.came[1], gate_two, down_share,
+        layer_output,
+    ) = region(fourth_window, query_key_one, value_one, up_two, out_one, layer_output)
 
     input_rows, attn_norm_part = grid_call(
         input_back_kernel,
         tiles,
-        [own_spec] + [tile_spec] * 3
+        [own_spec, pl.BlockSpec((1, tile, width), lambda b, *_: (0, b, 0))]
         + [
             pl.BlockSpec((rank, tile), lambda b, *_: (0, b)), fixed((width, rank)), tile_spec,
             fixed((1, width)),
@@ -968,32 +1191,17 @@
         [tile_spec, fixed((1, width))],
         [struct((length, width), bf16), struct((1, width), f32)],
         [
-            place_index, layer_input, *first_parts, rank_back[0], rank_down, middle_grad,
+            place_index, layer_input, first_grad, rank_back, rank_down, middle_grad,
             attn_norm.reshape(1, width),
         ],
         prefetch=1,
-        after=[up_two],
-    )
-    *input_blocks, input_third = tensor_gather(input_rows)
-    input_blocks.append(input_third([]))
-    query_gate_one = query_gate_grad.step_one([input_rows])
-    key_value_one = key_value_grad.step_one([query_gate_one])
-    out_two = out_grad.step_two([key_value_one])
-    swish_share = swish_grad.last([out_two])
-    down_share = down_grad.last([swish_share])
-    up_share = up_grad.last([down_share])
-    query_gate_two = query_gate_grad.step_two([up_share])
-    key_value_two = key_value_grad.step_two([query_gate_two])
-    layer_output = in_order(output_blocks, order, [key_value_two])
-    out_share = out_grad.last([layer_output])
-    input_grad = in_order(input_blocks, order, [out_share])
-    query_gate_share = query_gate_grad.last([out_share])
-    key_value_share = key_value_grad.last([query_gate_share])
-
-    rank_down_part = sum(
-        contract(rank_back[k], array[at * length : (at + 1) * length], 1, 0)
-        for k, (array, at) in enumerate(norms)
-    )
+        after=[gate_two],
+    )
+    out_two = out_grad.two([input_rows])
+    query_key_two = query_key_grad.two([out_two])
+    value_two = value_grad.two([query_key_two])
+
+    rank_down_part = contract(rank_back, norm_near[:length], 1, 0)
     own_part = jnp.concatenate([rank_down_part, mlp_norm_part, attn_norm_part], axis=0)
     shared = jnp.concatenate(
         [
@@ -1013,24 +1221,58 @@
         ],
         axis=1,
     )
-    mail = spread_sum(mail.reshape(devices, 1, -1)).reshape(-1)
+
+    def fifth_window(input_rows, query_key_two, value_two, gate_two, out_two, mail):
+        mail = lax.all_to_all(mail, "seq", 0, 0)
+        return (
+            swap(input_rows, "tensor", 2), query_key_grad.hop(2, query_key_two),
+            value_grad.hop(2, value_two), gate_grad.hop(2, gate_two),
+            jnp.sum(mail.astype(f32), axis=0), up_grad.last(), out_grad.hop(2, out_two),
+        )
+
+    (
+        second_rows, query_key_grad.came[2], value_grad.came[2], gate_grad.came[2], mail, up_share,
+        out_grad.came[2],
+    ) = region(
+        fifth_window, input_rows, query_key_two, value_two, gate_two, out_two,
+        mail.reshape(devices, 1, -1).astype(bf16),
+    )
+
+    def sixth_window(input_rows, second_rows):
+        pair = swap(jnp.stack([input_rows, second_rows]), "tensor", 1)
+        whole = pl.BlockSpec((length, width), lambda k, order: (0, 0))
+        input_grad = grid_call(
+            place_kernel,
+            (4,),
+            [whole] * 4,
+            pl.BlockSpec((1, length, width), lambda k, order: (order[k], 0, 0)),
+            struct((seq_count, length, width), bf16),
+            [order, input_rows, pair[0], second_rows, pair[1]],
+            prefetch=1,
+        )
+        return input_grad, query_key_grad.last(), value_grad.last(), gate_grad.last(), out_grad.last()
+
+    input_grad, query_key_share, value_share, gate_share, out_share = region(
+        sixth_window, input_rows, second_rows
+    )
+    mail = mail.reshape(-1)
     own_part = mail[:own_size].reshape(rank + 2, column)
     shared = mail[own_size:].reshape(rank + 2, DK)
-    norm_parts = sum_over(own_part[rank:], "tensor")
+    own_part = sum_over(own_part, "tensor")
     return (
         layer_output,
         input_grad,
-        norm_parts[1],
-        query_gate_share[:, :DK],
-        key_value_share[:, :DK],
-        key_value_share[:, DK:],
-        query_gate_share[:, DK:],
+        own_part[rank + 1],
+        query_key_share[:, :DK],
+        query_key_share[:, DK:],
+        value_share,
+        gate_share,
         own_part[:rank].T,
         shared[:rank],
         shared[rank],
         shared[rank + 1],
         out_share,
-        norm_parts[0],
+        own_part[rank],
         swish_share,
         up_share,
         down_share,

time: 820 us -> 782 us (0.954)
  waiting for transfers between devices: 392 us -> 320 us
  local copies, waits for them, and re-layouts: 67.1 us -> 39.7 us
  starting transfers between devices: 68.2 us -> 94.8 us
  Pallas kernels: 246 us -> 269 us
  between operations: 3.33 us -> 15.9 us
    all_to_all x4 -> x3, waiting for transfers between devices: 131 us -> 47.7 us  [deal(): return lax.all_to_all(pieces, 'seq', 0, 0)]
    unnamed x403 -> x204, local copies, waits for them, and re-layouts: 50.7 us -> 18.8 us
    ppermute x46 -> x53, starting transfers between devices: 43.8 us -> 70.9 us  [swap(): return lax.ppermute(values, axis, [(i, i ^ distance) for i in range(count)])]
    all_to_all x1 -> x2, waiting for transfers between devices: 0.01 us -> 25.5 us  [the longest x1 25.5 us: fifth_window(): mail = lax.all_to_all(mail, 'seq', 0, 0)]
    pallas_call x52 -> x62, Pallas kernels: 246 us -> 269 us  [grid_call(): pl.pallas_call(run, grid_spec=pltpu.PrefetchScalarGridSpec(num_scalar_pre...]
    ppermute x46 -> x53, waiting for transfers between devices: 261 us -> 247 us  [swap(): return lax.ppermute(values, axis, [(i, i ^ distance) for i in range(count)])]
    all_to_all x4 -> x3, starting transfers between devices: 20 us -> 16.9 us  [deal(): return lax.all_to_all(pieces, 'seq', 0, 0)]
    dot_general x16 -> x13, matrix products: 17.7 us -> 15.3 us  [contract(): lax.dot_general(left, right, (((left_dim,), (right_dim,)), ((), ())), pre...]
  transfers between devices with their start and end apart: 51 -> 60, of which waited for: 26 -> 24; matrix products, arithmetic and copies ran while one was open for 5% -> 4% of each run, Pallas kernels for 25% -> 31%
where the time goes in v3:
time: 782 us; the launch traced here: 771 us
  waiting for transfers between devices  320 us (41%)
  Pallas kernels  269 us (34%)
  starting transfers between devices  94.8 us (12%)
  local copies, waits for them, and re-layouts  39.7 us (5%)
  between operations  15.9 us (2%)
  other arithmetic  15.4 us (2%)
  matrix products  15.3 us (2%)
    pallas_call x62, Pallas kernels, grid_call(): pl.pallas_call(run, grid_spec=pltpu.PrefetchScalarGridSpec(num_scalar_pre...  269 us
    ppermute x53, waiting for transfers between devices, swap(): return lax.ppermute(values, axis, [(i, i ^ distance) for i in range(count)])  247 us
    ppermute x53, starting transfers between devices, swap(): return lax.ppermute(values, axis, [(i, i ^ distance) for i in range(count)])  70.9 us
    all_to_all x3, waiting for transfers between devices, deal(): return lax.all_to_all(pieces, 'seq', 0, 0)  47.7 us
    all_to_all x1, waiting for transfers between devices, fifth_window(): mail = lax.all_to_all(mail, 'seq', 0, 0)  25.5 us
    unnamed x204, local copies, waits for them, and re-layouts  18.8 us
    all_to_all x3, starting transfers between devices, deal(): return lax.all_to_all(pieces, 'seq', 0, 0)  16.9 us
  transfers between devices with their start and end apart: 60, of which 24 were waited for; matrix products, arithmetic and copies ran while one was open for 4% of the time, Pallas kernels for 31%

profile of v3, /device:TPU:0, one launch (start us, length us, event | category | flops | bytes accessed | tf_op | source)
XLA Modules:
  0.0 770.8 jit_solution(6479577361513645820)
XLA Ops:
  48.0 7.4 collective-permute-done.29.refs_3_.refs_2_
  60.6 7.7 collective-permute-start.36
  88.7 8.6 %collective-permute-done.40.refs_1_ = bf16[2,4,64,512]{3,2,1,0:T(8,128)(2,1)S(1)} collective-permute-done((bf16[2,4,64,512]{3,2,1,0:T(8,128)(2,1)S(1)}, bf16[2,4,64,512]{3,2,1,0:T(8,128)(2,1)S(1)}, u32[]{:S(2)}, u32[]{:S(2)}) %collective-permute-start.40) | collective-permute-done | bytes 524320 | tf_op jit(solution)/shard_map/ppermute | solution.py:531
  121.2 10.2 %collective-permute-done.39.refs_1_ = bf16[2,4,64,512]{3,2,1,0:T(8,128)(2,1)S(1)} collective-permute-done((bf16[2,4,64,512]{3,2,1,0:T(8,128)(2,1)S(1)}, bf16[2,4,64,512]{3,2,1,0:T(8,128)(2,1)S(1)}, u32[]{:S(2)}, u32[]{:S(2)}) %collective-permute-start.39) | collective-permute-done | bytes 524320 | tf_op jit(solution)/shard_map/ppermute | solution.py:531
  139.8 22.9 %collective-permute-done.43.refs_4_ = bf16[256,2048]{1,0:T(8,128)(2,1)S(1)} collective-permute-done((bf16[256,2048]{1,0:T(8,128)(2,1)S(1)}, bf16[256,2048]{1,0:T(8,128)(2,1)S(1)}, u32[]{:S(2)}, u32[]{:S(2)}) %collective-permute-start.43) | collective-permute-done | bytes 1048608 | tf_op jit(solution)/shard_map/ppermute | solution.py:531
  168.6 23.1 %shard_map.298 = (bf16[512,1408]{1,0:T(8,128)(2,1)}, bf16[512,1408]{1,0:T(8,128)(2,1)}, bf16[512,1408]{1,0:T(8,128)(2,1)}, bf16[512,2048]{1,0:T(8,128)(2,1)}, bf16[512,2048]{1,0:T(8,128)(2,1)S(1)}) custom-call(bf16[256,2048]{1,0:T(8,128)(2,1)S(1)} %get-tuple-element.801.refs_0_.refs_1_, bf16[256,2048]{1,0:T(8,128)(2,1)S(1)} %collective-permute-done.44.refs_1_.refs_2_, ...), custom_call_target="tpu_custom_call" | custom-call | flops 1024 | bytes 1024 | tf_op jit(solution)/shard_map/pallas_call | solution.py:513
  203.3 13.3 %shard_map.299 = (bf16[256,1408]{1,0:T(8,128)(2,1)}, bf16[256,1408]{1,0:T(8,128)(2,1)}, bf16[256,1408]{1,0:T(8,128)(2,1)}, bf16[256,2048]{1,0:T(8,128)(2,1)}, bf16[256,2048]{1,0:T(8,128)(2,1)S(1)}) custom-call(bf16[256,2048]{1,0:T(8,128)(2,1)S(1)} %collective-permute-done.45.refs_0_.refs_1_.refs_3_, ...), custom_call_target="tpu_custom_call" | custom-call | flops 1024 | bytes 1024 | tf_op jit(solution)/shard_map/pallas_call | solution.py:513
  217.6 14.7 %shard_map.301 = (bf16[256,1408]{1,0:T(8,128)(2,1)}, bf16[256,1408]{1,0:T(8,128)(2,1)}, bf16[256,1408]{1,0:T(8,128)(2,1)}, bf16[256,2048]{1,0:T(8,128)(2,1)}, bf16[256,2048]{1,0:T(8,128)(2,1)}) custom-call(bf16[256,2048]{1,0:T(8,128)(2,1)} %collective-permute-done.46.refs_0_.refs_1_.refs_4_, ...), custom_call_target="tpu_custom_call" | custom-call | flops 1024 | bytes 1024 | tf_op jit(solution)/shard_map/pallas_call | solution.py:513
  232.3 7.5 shard_map.302
  241.8 29.8 %conditional.9 = (bf16[256,2048]{1,0:T(8,128)(2,1)}, bf16[256,2048]{1,0:T(8,128)(2,1)}, bf16[4,256,1408]{2,1,0:T(8,128)(2,1)}, bf16[4,256,1408]{2,1,0:T(8,128)(2,1)}) conditional(s32[]{:T(128)} %convert_element_type.74, () %tuple.89, (bf16[512,2048]{1,0:T(8,128)(2,1)}, bf16[256,2048]{1,0:T(8,128)(2,1)}, bf16[256,2048]{1,0:T(8,128)(2,1)}, ...), branch_computations={%region_0.0_spmd, %region_1.0_spmd} | conditional | flops 2099229 | bytes 41945568 | solution.py:540
  247.6 8.3 %branch_1_fun.28.refs_9_ = bf16[4,256,1408]{2,1,0:T(8,128)(2,1)} custom-call(s32[4]{0:T(128)S(1)} %get-tuple-element.904.refs_0_, bf16[512,2048]{1,0:T(8,128)(2,1)} %get-tuple-element.408.refs_1_.refs_2_, bf16[512,2048]{1,0:T(8,128)(2,1)} %get-tuple-element.408.refs_1_.refs_2_, bf16[512,2048]{1,0:T(8,128)(2,1)} %get-tuple-element.409.refs_3_.refs_4_, ...), custom_call_target="tpu_custom_call" | custom-call | flops 1024 | bytes 1024 | tf_op jit(solution)/shard_map/cond/branch_1_fun/pallas_call | solution.py:513
  262.7 8.9 %collective-permute-done.8 = bf16[256,2048]{1,0:T(8,128)(2,1)} collective-permute-done((bf16[256,2048]{1,0:T(8,128)(2,1)}, bf16[256,2048]{1,0:T(8,128)(2,1)}, u32[]{:S(2)}, u32[]{:S(2)}) %collective-permute-start.8) | collective-permute-done | bytes 1048608 | tf_op jit(solution)/shard_map/cond/branch_1_fun/ppermute | solution.py:531
  279.9 34.0 %conditional.10 = (bf16[256,2048]{1,0:T(8,128)(2,1)}, bf16[256,2048]{1,0:T(8,128)(2,1)}, bf16[512,512]{1,0:T(8,128)(2,1)}, bf16[512,512]{1,0:T(8,128)(2,1)}, f32...) conditional(s32[]{:T(128)} %convert_element_type.74, () %tuple.88, ...), branch_computations={%region_2.0_spmd, %region_3.0_spmd} | conditional | flops 2048 | bytes 8390808 | solution.py:540
  281.4 23.8 %collective-permute-done.refs_0_ = bf16[256,2048]{1,0:T(8,128)(2,1)} collective-permute-done((bf16[256,2048]{1,0:T(8,128)(2,1)S(1)}, bf16[256,2048]{1,0:T(8,128)(2,1)}, u32[]{:S(2)}, u32[]{:S(2)}) %collective-permute-start) | collective-permute-done | bytes 1048608 | tf_op jit(solution)/shard_map/cond/branch_1_fun/ppermute | solution.py:531
  314.0 74.9 %conditional.11 = (bf16[8,4,64,512]{3,2,1,0:T(8,128)(2,1)}, bf16[2,256,1408]{2,1,0:T(8,128)(2,1)}, bf16[4,256,512]{2,1,0:T(8,128)(2,1)}, bf16[4,256,512]{2,1,0:T(8,128)(2,1)}, bf16[4,256,2048]{2,1,0:T(8,128)(2,1)}) conditional(s32[]{:T(128)} %convert_element_type.74, () %tuple.87, (bf16[8,4,64,512]{3,2,1,0:T(8,128)(2,1)}, ...), branch_computations={%region_4.0_spmd, %region_5.0_spmd} | conditional | flops 4119 | bytes 18878800 | solution.py:540
  341.2 47.7 %all-to-all-done = bf16[8,4,64,512]{3,2,1,0:T(8,128)(2,1)} async-done(((bf16[8,4,64,512]{3,2,1,0:T(8,128)(2,1)}), bf16[8,4,64,512]{3,2,1,0:T(8,128)(2,1)}, u32[]{:S(2)}, u32[]{:S(2)}) %all-to-all-start) | async-done | bytes 2097184 | tf_op jit(solution)/shard_map/cond/branch_1_fun/all_to_all | solution.py:570
  388.9 76.2 %conditional.12 = (bf16[8,4,64,512]{3,2,1,0:T(8,128)(2,1)}, bf16[2,256,1408]{2,1,0:T(8,128)(2,1)}, bf16[4,256,512]{2,1,0:T(8,128)(2,1)}, bf16[2,256,1408]{2,1,0:T(8,128)(2,1)}, bf16[2,256,1408]{2,1,0:T(8,128)(2,1)}) conditional(s32[]{:T(128)} %convert_element_type.74, () %tuple.86, (bf16[8,4,16,512]{3,2,1,0:T(8,128)(2,1)}, ...), branch_computations={%region_6.0_spmd, %region_7.0_spmd} | conditional | flops 3083 | bytes 16256264 | solution.py:540
  414.5 30.9 %collective-permute-done.10 = bf16[4,256,512]{2,1,0:T(8,128)(2,1)} collective-permute-done((bf16[4,256,512]{2,1,0:T(8,128)(2,1)}, bf16[4,256,512]{2,1,0:T(8,128)(2,1)}, u32[]{:S(2)}, u32[]{:S(2)}) %collective-permute-start.10) | collective-permute-done | bytes 1048608 | tf_op jit(solution)/shard_map/cond/branch_1_fun/ppermute | solution.py:531
  445.4 19.7 %collective-permute-done.9 = bf16[2,256,1408]{2,1,0:T(8,128)(2,1)} collective-permute-done((bf16[2,256,1408]{2,1,0:T(8,128)(2,1)}, bf16[2,256,1408]{2,1,0:T(8,128)(2,1)}, u32[]{:S(2)}, u32[]{:S(2)}) %collective-permute-start.9) | collective-permute-done | bytes 1441824 | tf_op jit(solution)/shard_map/cond/branch_1_fun/ppermute | solution.py:531
  471.7 56.1 %conditional.13 = (bf16[2,256,1408]{2,1,0:T(8,128)(2,1)}, bf16[1,256,1408]{2,1,0:T(8,128)(2,1)}, bf16[2,256,1408]{2,1,0:T(8,128)(2,1)}, bf16[4,256,512]{2,1,0:T(...) conditional(s32[]{:T(128)} %convert_element_type.74, () %tuple.85, ...), branch_computations={%region_8.0_spmd, %region_9.0_spmd} | conditional | flops 7199 | bytes 54452060 | solution.py:540
  476.4 7.4 branch_1_fun.39
  483.9 8.1 %branch_1_fun.40 = (bf16[512,512]{1,0:T(8,128)(2,1)}, bf16[512,512]{1,0:T(8,128)(2,1)}, bf16[512,512]{1,0:T(8,128)(2,1)}, f32[2,16,256]{2,1,0:T(8,128)}, f32[2,1...) custom-call(bf16[512,512]{1,0:T(8,128)(2,1)} %get-tuple-element.504.refs_0_, bf16[512,512]{1,0:T(8,128)(2,1)} %get-tuple-element.505.refs_1_, ...), custom_call_target="tpu_custom_call" | custom-call | flops 1024 | bytes 1024 | tf_op jit(solution)/shard_map/cond/branch_1_fun/pallas_call | solution.py:513
  492.0 10.3 %branch_1_fun.43.refs_9_ = bf16[4,256,2048]{2,1,0:T(8,128)(2,1)} custom-call(s32[4]{0:T(128)S(1)} %get-tuple-element.520.refs_0_, bf16[512,512]{1,0:T(8,128)(2,1)} %get-tuple-element.1000.refs_7_.refs_8_.refs_1_, bf16[512,512]{1,0:T(8,128)(2,1)} %get-tuple-element.1001.refs_11_.refs_12_.refs_2_, ...), custom_call_target="tpu_custom_call" | custom-call | flops 1024 | bytes 1024 | tf_op jit(solution)/shard_map/cond/branch_1_fun/pallas_call | solution.py:513
  502.2 10.0 %branch_1_fun.44.refs_10_ = bf16[4,256,2048]{2,1,0:T(8,128)(2,1)} custom-call(s32[4]{0:T(128)S(1)} %get-tuple-element.520.refs_0_, bf16[512,512]{1,0:T(8,128)(2,1)S(1)} %get-tuple-element.994.refs_5_.refs_6_.refs_1_, bf16[512,512]{1,0:T(8,128)(2,1)S(1)} %get-tuple-element.995.refs_9_.refs_10_.refs_2_, ...), custom_call_target="tpu_custom_call", output_to_operand_aliasing={{}: (9, {})} | custom-call | flops 1024 | bytes 1024 | tf_op jit(solution)/shard_map/cond/branch_1_fun/pallas_call | solution.py:513
  538.3 50.9 %conditional.14 = (bf16[4,256,1024]{2,1,0:T(8,128)(2,1)}, bf16[4,256,512]{2,1,0:T(8,128)(2,1)}, bf16[2,256,512]{2,1,0:T(8,128)(2,1)}, bf16[1,256,1408]{2,1,0:T(8...) conditional(s32[]{:T(128)} %convert_element_type.74, () %tuple.95, ...), branch_computations={%region_10.0_spmd, %region_11.13_spmd} | conditional | flops 48168 | bytes 42351144 | solution.py:540
  555.9 33.2 %collective-permute-done.17 = bf16[2,256,512]{2,1,0:T(8,128)(2,1)} collective-permute-done((bf16[2,256,512]{2,1,0:T(8,128)(2,1)}, bf16[2,256,512]{2,1,0:T(8,128)(2,1)}, u32[]{:S(2)}, u32[]{:S(2)}) %collective-permute-start.17) | collective-permute-done | bytes 524320 | tf_op jit(solution)/shard_map/cond/branch_1_fun/ppermute | solution.py:531
  598.9 51.1 %conditional.15 = (bf16[2,256,1024]{2,1,0:T(8,128)(2,1)}, bf16[2,256,512]{2,1,0:T(8,128)(2,1)}, bf16[1,256,1408]{2,1,0:T(8,128)(2,1)}, bf16[2,256,512]{2,1,0:T(8...) conditional(s32[]{:T(128)} %convert_element_type.74, () %tuple.84, ...), branch_computations={%region_14.0_spmd, %region_15.16_spmd} | conditional | flops 2052 | bytes 64752044 | solution.py:540
  614.7 35.3 %collective-permute-done.5 = bf16[2,256,512]{2,1,0:T(8,128)(2,1)} collective-permute-done((bf16[2,256,512]{2,1,0:T(8,128)(2,1)}, bf16[2,256,512]{2,1,0:T(8,128)(2,1)}, u32[]{:S(2)}, u32[]{:S(2)}) %collective-permute-start.5) | collective-permute-done | bytes 524320 | tf_op jit(solution)/shard_map/cond/branch_1_fun/ppermute | solution.py:531
  664.5 71.4 %conditional.16 = (bf16[256,2048]{1,0:T(8,128)(2,1)}, bf16[1,256,1024]{2,1,0:T(8,128)(2,1)}, bf16[1,256,512]{2,1,0:T(8,128)(2,1)}, bf16[1,256,512]{2,1,0:T(8,128...) conditional(s32[]{:T(128)} %convert_element_type.74, () %tuple.99, ...), branch_computations={%region_17.18_spmd, %region_18.20_spmd} | conditional | flops 221187 | bytes 17830318 | solution.py:540
  683.8 25.5 %all-to-all-done.3 = bf16[8,2,6912]{2,1,0:T(2,128)(2,1)S(1)} async-done(((bf16[8,2,6912]{2,1,0:T(2,128)(2,1)}), bf16[8,2,6912]{2,1,0:T(2,128)(2,1)S(1)}, u32[]{:S(2)}, u32[]{:S(2)}) %all-to-all-start.3) | async-done | bytes 221216 | tf_op jit(solution)/shard_map/cond/branch_1_fun/all_to_all | solution.py:1226
  716.0 10.2 %collective-permute-done.22 = bf16[1,256,512]{2,1,0:T(8,128)(2,1)} collective-permute-done((bf16[1,256,512]{2,1,0:T(8,128)(2,1)}, bf16[1,256,512]{2,1,0:T(8,128)(2,1)}, u32[]{:S(2)}, u32[]{:S(2)}) %collective-permute-start.22) | collective-permute-done | bytes 262176 | tf_op jit(solution)/shard_map/cond/branch_1_fun/ppermute | solution.py:531
  738.4 23.9 %conditional.17 = (bf16[4,256,2048]{2,1,0:T(8,128)(2,1)}, f32[256,1024]{1,0:T(8,128)}, f32[256,512]{1,0:T(8,128)}, f32[256,512]{1,0:T(8,128)}, f32[512,256]{1,0:...) conditional(s32[]{:T(128)} %convert_element_type.74, () %tuple.98, (bf16[256,2048]{1,0:T(8,128)(2,1)}, ...), branch_computations={%region_20.21_spmd, %region_21.22_spmd} | conditional | flops 1053699 | bytes 52434272 | solution.py:540
  (531 shorter events, 359.8 us)
Async XLA Ops:
  102.0 29.5 %collective-permute-start.41 = (bf16[256,2048]{1,0:T(8,128)(2,1)}, bf16[256,2048]{1,0:T(8,128)(2,1)}, u32[]{:S(2)}, u32[]{:S(2)}) collective-permute-start(bf16[256,2048]{1,0:T(8,128)(2,1)} %slice.114), channel_id=1, source_target_pairs={{0,1},{1,0},{2,3},{3,2},{4,5},{5,4},{6,7},{7,6},{8,9},{9,8},{10,11... | collective-permute-start | bytes 3145736 | tf_op jit(solution)/shard_map/ppermute | solution.py:531
  137.2 25.6 %collective-permute-start.43 = (bf16[256,2048]{1,0:T(8,128)(2,1)S(1)}, bf16[256,2048]{1,0:T(8,128)(2,1)S(1)}, u32[]{:S(2)}, u32[]{:S(2)}) collective-permute-start(bf16[256,2048]{1,0:T(8,128)(2,1)S(1)} %add_convert_fusion.1.refs_7_), channel_id=1, source_target_pairs={{0,2},{1,3},{2,0},{3,1},{4,6},{5,7},{6,4},{7,5},{8,10},{9,11},{10,... | collective-permute-start | bytes 3145736 | tf_op jit(solution)/shard_map/ppermute | solution.py:531
  165.9 25.8 %collective-permute-start.45 = (bf16[256,2048]{1,0:T(8,128)(2,1)S(1)}, bf16[256,2048]{1,0:T(8,128)(2,1)S(1)}, u32[]{:S(2)}, u32[]{:S(2)}) collective-permute-start(bf16[256,2048]{1,0:T(8,128)(2,1)S(1)} %get-tuple-element.801.refs_0_.refs_1_), channel_id=1, source_target_pairs={{0,2},{1,3},{2,0},{3,1},{4,6},{5,7},{6,4},{7,5},{8,10},{9,11},{10,... | collective-permute-start | bytes 3145736 | tf_op jit(solution)/shard_map/ppermute | solution.py:531
  194.0 38.3 %all-to-all-start.4 = ((bf16[8,4,16,512]{3,2,1,0:T(8,128)(2,1)}), bf16[8,4,16,512]{3,2,1,0:T(8,128)(2,1)S(1)}, u32[]{:S(2)}, u32[]{:S(2)}) async-start(bf16[8,4,16,512]{3,2,1,0:T(8,128)(2,1)} %broadcast_in_dim.25), calls=%async_computation.4 | async-start | bytes 1048576 | tf_op jit(solution)/shard_map/all_to_all | solution.py:570
  200.5 398.4 %all-reduce.2.cloned.1.call-start = ((), (), s32[]{:S(2)}) async-start(), calls=%async_computation.6 | async-start | bytes 8388608 | tf_op jit(solution)/shard_map/psum | solution.py:1065
  239.8 74.2 %collective-permute-start.48 = (bf16[4,256,1408]{2,1,0:T(8,128)(2,1)}, bf16[4,256,1408]{2,1,0:T(8,128)(2,1)}, u32[]{:S(2)}, u32[]{:S(2)}) collective-permute-start(bf16[4,256,1408]{2,1,0:T(8,128)(2,1)} %shard_map.302), channel_id=1, source_target_pairs={{0,4},{4,0},{8,12},{12,8},{16,20},{20,16},{24,28},{28,24},{1,5},{5... | collective-permute-start | bytes 8650760 | tf_op jit(solution)/shard_map/ppermute | solution.py:531
  246.0 25.5 %collective-permute-start.8 = (bf16[256,2048]{1,0:T(8,128)(2,1)}, bf16[256,2048]{1,0:T(8,128)(2,1)}, u32[]{:S(2)}, u32[]{:S(2)}) collective-permute-start(bf16[256,2048]{1,0:T(8,128)(2,1)} %add_convert_fusion), channel_id=1, source_target_pairs={{0,2},{1,3},{2,0},{3,1},{4,6},{5,7},{6,4},{7,5},{8,10},{9,11},{10,... | collective-permute-start | bytes 3145736 | tf_op jit(solution)/shard_map/cond/branch_1_fun/ppermute | solution.py:531
  276.3 112.6 %collective-permute-start.49 = (bf16[4,256,1408]{2,1,0:T(8,128)(2,1)}, bf16[4,256,1408]{2,1,0:T(8,128)(2,1)}, u32[]{:S(2)}, u32[]{:S(2)}) collective-permute-start(bf16[4,256,1408]{2,1,0:T(8,128)(2,1)} %get-tuple-element.833), channel_id=1, source_target_pairs={{0,4},{4,0},{8,12},{12,8},{16,20},{20,16},{24,28},{28,24},{1,5},{5... | collective-permute-start | bytes 8650760 | tf_op jit(solution)/shard_map/ppermute | solution.py:531
  276.5 112.5 %collective-permute-start.50 = (bf16[4,256,1408]{2,1,0:T(8,128)(2,1)}, bf16[4,256,1408]{2,1,0:T(8,128)(2,1)}, u32[]{:S(2)}, u32[]{:S(2)}) collective-permute-start(bf16[4,256,1408]{2,1,0:T(8,128)(2,1)} %get-tuple-element.834), channel_id=1, source_target_pairs={{0,8},{4,12},{8,0},{12,4},{16,24},{20,28},{24,16},{28,20},{1,9},{5... | collective-permute-start | bytes 8650760 | tf_op jit(solution)/shard_map/ppermute | solution.py:531
  279.9 25.3 %collective-permute-start = (bf16[256,2048]{1,0:T(8,128)(2,1)S(1)}, bf16[256,2048]{1,0:T(8,128)(2,1)}, u32[]{:S(2)}, u32[]{:S(2)}) collective-permute-start(bf16[256,2048]{1,0:T(8,128)(2,1)S(1)} %get-tuple-element.421.refs_0_), channel_id=1, source_target_pairs={{0,2},{1,3},{2,0},{3,1},{4,6},{5,7},{6,4},{7,5},{8,10},{9,11},{10,... | collective-permute-start | bytes 3145736 | tf_op jit(solution)/shard_map/cond/branch_1_fun/ppermute | solution.py:531
  314.0 74.9 %all-to-all-start = ((bf16[8,4,64,512]{3,2,1,0:T(8,128)(2,1)}), bf16[8,4,64,512]{3,2,1,0:T(8,128)(2,1)}, u32[]{:S(2)}, u32[]{:S(2)}) async-start(bf16[8,4,64,512]{3,2,1,0:T(8,128)(2,1)} %get-tuple-element.441.refs_10_), calls=%async_computation | async-start | bytes 4194304 | tf_op jit(solution)/shard_map/cond/branch_1_fun/all_to_all | solution.py:570
  388.9 261.2 %reduce-scatter.2.cloned.1.call-start = ((), (), s32[]{:S(2)}) async-start(), calls=%async_computation.7 | async-start | bytes 5242880 | tf_op jit(solution)/shard_map/reduce_scatter | solution.py:1154
  393.1 72.0 %all-to-all-start.1 = ((bf16[8,4,64,512]{3,2,1,0:T(8,128)(2,1)}), bf16[8,4,64,512]{3,2,1,0:T(8,128)(2,1)}, u32[]{:S(2)}, u32[]{:S(2)}) async-start(bf16[8,4,64,512]{3,2,1,0:T(8,128)(2,1)} %branch_1_fun.36), calls=%async_computation.1 | async-start | bytes 4194304 | tf_op jit(solution)/shard_map/cond/branch_1_fun/all_to_all | solution.py:570
  399.0 66.1 %collective-permute-start.9 = (bf16[2,256,1408]{2,1,0:T(8,128)(2,1)}, bf16[2,256,1408]{2,1,0:T(8,128)(2,1)}, u32[]{:S(2)}, u32[]{:S(2)}) collective-permute-start(bf16[2,256,1408]{2,1,0:T(8,128)(2,1)} %get-tuple-element.467), channel_id=1, source_target_pairs={{0,8},{4,12},{8,0},{12,4},{16,24},{20,28},{24,16},{28,20},{1,9},{5... | collective-permute-start | bytes 4325384 | tf_op jit(solution)/shard_map/cond/branch_1_fun/ppermute | solution.py:531
  401.1 44.3 %collective-permute-start.10 = (bf16[4,256,512]{2,1,0:T(8,128)(2,1)}, bf16[4,256,512]{2,1,0:T(8,128)(2,1)}, u32[]{:S(2)}, u32[]{:S(2)}) collective-permute-start(bf16[4,256,512]{2,1,0:T(8,128)(2,1)} %get-tuple-element.468), channel_id=1, source_target_pairs={{0,4},{4,0},{8,12},{12,8},{16,20},{20,16},{24,28},{28,24},{1,5},{5... | collective-permute-start | bytes 3145736 | tf_op jit(solution)/shard_map/cond/branch_1_fun/ppermute | solution.py:531
  471.7 56.1 %collective-permute-start.11 = (bf16[2,256,1408]{2,1,0:T(8,128)(2,1)}, bf16[2,256,1408]{2,1,0:T(8,128)(2,1)}, u32[]{:S(2)}, u32[]{:S(2)}) collective-permute-start(bf16[2,256,1408]{2,1,0:T(8,128)(2,1)} %get-tuple-element.483), channel_id=1, source_target_pairs={{0,8},{4,12},{8,0},{12,4},{16,24},{20,28},{24,16},{28,20},{1,9},{5... | collective-permute-start | bytes 4325384 | tf_op jit(solution)/shard_map/cond/branch_1_fun/ppermute | solution.py:531
  472.2 55.6 %collective-permute-start.13 = (bf16[2,256,1408]{2,1,0:T(8,128)(2,1)}, bf16[2,256,1408]{2,1,0:T(8,128)(2,1)}, u32[]{:S(2)}, u32[]{:S(2)}) collective-permute-start(bf16[2,256,1408]{2,1,0:T(8,128)(2,1)} %get-tuple-element.485), channel_id=1, source_target_pairs={{0,4},{4,0},{8,12},{12,8},{16,20},{20,16},{24,28},{28,24},{1,5},{5... | collective-permute-start | bytes 4325384 | tf_op jit(solution)/shard_map/cond/branch_1_fun/ppermute | solution.py:531
  473.8 54.0 %collective-permute-start.14 = (bf16[4,256,512]{2,1,0:T(8,128)(2,1)}, bf16[4,256,512]{2,1,0:T(8,128)(2,1)}, u32[]{:S(2)}, u32[]{:S(2)}) collective-permute-start(bf16[4,256,512]{2,1,0:T(8,128)(2,1)} %get-tuple-element.486), channel_id=1, source_target_pairs={{0,4},{4,0},{8,12},{12,8},{16,20},{20,16},{24,28},{28,24},{1,5},{5... | collective-permute-start | bytes 3145736 | tf_op jit(solution)/shard_map/cond/branch_1_fun/ppermute | solution.py:531
  474.2 53.5 %collective-permute-start.12 = (bf16[1,256,1408]{2,1,0:T(8,128)(2,1)}, bf16[1,256,1408]{2,1,0:T(8,128)(2,1)}, u32[]{:S(2)}, u32[]{:S(2)}) collective-permute-start(bf16[1,256,1408]{2,1,0:T(8,128)(2,1)} %get-tuple-element.484.refs_11_), channel_id=1, source_target_pairs={{0,16},{4,20},{8,24},{12,28},{16,0},{20,4},{24,8},{28,12},{1,17},{... | collective-permute-start | bytes 2162696 | tf_op jit(solution)/shard_map/cond/branch_1_fun/ppermute | solution.py:531
  538.3 50.9 %collective-permute-start.15 = (bf16[4,256,1024]{2,1,0:T(8,128)(2,1)}, bf16[4,256,1024]{2,1,0:T(8,128)(2,1)}, u32[]{:S(2)}, u32[]{:S(2)}) collective-permute-start(bf16[4,256,1024]{2,1,0:T(8,128)(2,1)} %get-tuple-element.534), channel_id=1, source_target_pairs={{0,4},{4,0},{8,12},{12,8},{16,20},{20,16},{24,28},{28,24},{1,5},{5... | collective-permute-start | bytes 6291464 | tf_op jit(solution)/shard_map/cond/branch_1_fun/ppermute | solution.py:531
  540.0 49.2 %collective-permute-start.16 = (bf16[4,256,512]{2,1,0:T(8,128)(2,1)}, bf16[4,256,512]{2,1,0:T(8,128)(2,1)}, u32[]{:S(2)}, u32[]{:S(2)}) collective-permute-start(bf16[4,256,512]{2,1,0:T(8,128)(2,1)} %get-tuple-element.535), channel_id=1, source_target_pairs={{0,8},{4,12},{8,0},{12,4},{16,24},{20,28},{24,16},{28,20},{1,9},{5... | collective-permute-start | bytes 3145736 | tf_op jit(solution)/shard_map/cond/branch_1_fun/ppermute | solution.py:531
  541.4 47.7 %collective-permute-start.18 = (bf16[1,256,1408]{2,1,0:T(8,128)(2,1)}, bf16[1,256,1408]{2,1,0:T(8,128)(2,1)}, u32[]{:S(2)}, u32[]{:S(2)}) collective-permute-start(bf16[1,256,1408]{2,1,0:T(8,128)(2,1)} %get-tuple-element.537), channel_id=1, source_target_pairs={{0,16},{4,20},{8,24},{12,28},{16,0},{20,4},{24,8},{28,12},{1,17},{... | collective-permute-start | bytes 2162696 | tf_op jit(solution)/shard_map/cond/branch_1_fun/ppermute | solution.py:531
  541.6 47.6 %collective-permute-start.17 = (bf16[2,256,512]{2,1,0:T(8,128)(2,1)}, bf16[2,256,512]{2,1,0:T(8,128)(2,1)}, u32[]{:S(2)}, u32[]{:S(2)}) collective-permute-start(bf16[2,256,512]{2,1,0:T(8,128)(2,1)} %get-tuple-element.536), channel_id=1, source_target_pairs={{0,8},{4,12},{8,0},{12,4},{16,24},{20,28},{24,16},{28,20},{1,9},{5... | collective-permute-start | bytes 1572872 | tf_op jit(solution)/shard_map/cond/branch_1_fun/ppermute | solution.py:531
  598.9 51.1 %collective-permute-start.2 = (bf16[2,256,1024]{2,1,0:T(8,128)(2,1)}, bf16[2,256,1024]{2,1,0:T(8,128)(2,1)}, u32[]{:S(2)}, u32[]{:S(2)}) collective-permute-start(bf16[2,256,1024]{2,1,0:T(8,128)(2,1)} %get-tuple-element.556), channel_id=1, source_target_pairs={{0,8},{4,12},{8,0},{12,4},{16,24},{20,28},{24,16},{28,20},{1,9},{5... | collective-permute-start | bytes 3145736 | tf_op jit(solution)/shard_map/cond/branch_1_fun/ppermute | solution.py:531
  599.3 50.7 %collective-permute-start.4 = (bf16[1,256,1408]{2,1,0:T(8,128)(2,1)}, bf16[1,256,1408]{2,1,0:T(8,128)(2,1)}, u32[]{:S(2)}, u32[]{:S(2)}) collective-permute-start(bf16[1,256,1408]{2,1,0:T(8,128)(2,1)} %get-tuple-element.558), channel_id=1, source_target_pairs={{0,16},{4,20},{8,24},{12,28},{16,0},{20,4},{24,8},{28,12},{1,17},{... | collective-permute-start | bytes 2162696 | tf_op jit(solution)/shard_map/cond/branch_1_fun/ppermute | solution.py:531
  603.2 46.8 %collective-permute-start.5 = (bf16[2,256,512]{2,1,0:T(8,128)(2,1)}, bf16[2,256,512]{2,1,0:T(8,128)(2,1)}, u32[]{:S(2)}, u32[]{:S(2)}) collective-permute-start(bf16[2,256,512]{2,1,0:T(8,128)(2,1)} %get-tuple-element.559), channel_id=1, source_target_pairs={{0,8},{4,12},{8,0},{12,4},{16,24},{20,28},{24,16},{28,20},{1,9},{5... | collective-permute-start | bytes 1572872 | tf_op jit(solution)/shard_map/cond/branch_1_fun/ppermute | solution.py:531
  668.6 40.6 %all-to-all-start.3 = ((bf16[8,2,6912]{2,1,0:T(2,128)(2,1)}), bf16[8,2,6912]{2,1,0:T(2,128)(2,1)S(1)}, u32[]{:S(2)}, u32[]{:S(2)}) async-start(bf16[8,2,6912]{2,1,0:T(2,128)(2,1)} %reshape.254), calls=%async_computation.3 | async-start | bytes 442368 | tf_op jit(solution)/shard_map/cond/branch_1_fun/all_to_all | solution.py:1226
  672.3 63.6 %collective-permute-start.20 = (bf16[256,2048]{1,0:T(8,128)(2,1)}, bf16[256,2048]{1,0:T(8,128)(2,1)}, u32[]{:S(2)}, u32[]{:S(2)}) collective-permute-start(bf16[256,2048]{1,0:T(8,128)(2,1)} %get-tuple-element.575), channel_id=1, source_target_pairs={{0,2},{1,3},{2,0},{3,1},{4,6},{5,7},{6,4},{7,5},{8,10},{9,11},{10,... | collective-permute-start | bytes 3145736 | tf_op jit(solution)/shard_map/cond/branch_1_fun/ppermute | solution.py:531
  673.6 62.3 %collective-permute-start.21 = (bf16[1,256,1024]{2,1,0:T(8,128)(2,1)}, bf16[1,256,1024]{2,1,0:T(8,128)(2,1)}, u32[]{:S(2)}, u32[]{:S(2)}) collective-permute-start(bf16[1,256,1024]{2,1,0:T(8,128)(2,1)} %get-tuple-element.576), channel_id=1, source_target_pairs={{0,16},{4,20},{8,24},{12,28},{16,0},{20,4},{24,8},{28,12},{1,17},{... | collective-permute-start | bytes 1572872 | tf_op jit(solution)/shard_map/cond/branch_1_fun/ppermute | solution.py:531
  676.5 49.7 %collective-permute-start.22 = (bf16[1,256,512]{2,1,0:T(8,128)(2,1)}, bf16[1,256,512]{2,1,0:T(8,128)(2,1)}, u32[]{:S(2)}, u32[]{:S(2)}) collective-permute-start(bf16[1,256,512]{2,1,0:T(8,128)(2,1)} %get-tuple-element.577), channel_id=1, source_target_pairs={{0,16},{4,20},{8,24},{12,28},{16,0},{20,4},{24,8},{28,12},{1,17},{... | collective-permute-start | bytes 786440 | tf_op jit(solution)/shard_map/cond/branch_1_fun/ppermute | solution.py:531
  676.5 55.3 %collective-permute-start.23 = (bf16[1,256,512]{2,1,0:T(8,128)(2,1)}, bf16[1,256,512]{2,1,0:T(8,128)(2,1)}, u32[]{:S(2)}, u32[]{:S(2)}) collective-permute-start(bf16[1,256,512]{2,1,0:T(8,128)(2,1)} %get-tuple-element.578), channel_id=1, source_target_pairs={{0,16},{4,20},{8,24},{12,28},{16,0},{20,4},{24,8},{28,12},{1,17},{... | collective-permute-start | bytes 786440 | tf_op jit(solution)/shard_map/cond/branch_1_fun/ppermute | solution.py:531
  679.4 56.5 %collective-permute-start.24 = (bf16[1,256,512]{2,1,0:T(8,128)(2,1)S(1)}, bf16[1,256,512]{2,1,0:T(8,128)(2,1)}, u32[]{:S(2)}, u32[]{:S(2)}) collective-permute-start(bf16[1,256,512]{2,1,0:T(8,128)(2,1)S(1)} %get-tuple-element.590), channel_id=1, source_target_pairs={{0,16},{4,20},{8,24},{12,28},{16,0},{20,4},{24,8},{28,12},{1,17},{... | collective-permute-start | bytes 786440 | tf_op jit(solution)/shard_map/cond/branch_1_fun/ppermute | solution.py:531
  (173 other events, 2025.1 us)
Sparse Core Ops, SparseCore 0:
  389.0 86.5 all-reduce.1
  528.0 44.5 reduce-scatter.1

commit v4 on v3

--- a/solution.py
+++ b/solution.py
@@ -109,20 +109,21 @@
     return as_lines(run[run.shape[0] - 1 :])
 
 
-def as_lines(total):
-    high = total.astype(bf16)
-    rest = total - high.astype(f32)
-    middle = rest.astype(bf16)
-    low = (rest - middle.astype(f32)).astype(bf16)
+def as_lines(*totals):
     place = lax.broadcasted_iota(jnp.int32, (EXTRA, DK), 0)
     lines = jnp.zeros((EXTRA, DK), f32)
-    for at, line in enumerate((high, middle, low)):
-        lines = jnp.where(place == at, line.astype(f32), lines)
+    for first, total in enumerate(totals):
+        high = total.astype(bf16)
+        rest = total - high.astype(f32)
+        middle = rest.astype(bf16)
+        low = (rest - middle.astype(f32)).astype(bf16)
+        for at, line in enumerate((high, middle, low)):
+            lines = jnp.where(place == 3 * first + at, line.astype(f32), lines)
     return lines.astype(bf16)
 
 
-def from_lines(lines):
-    lines = lines.astype(f32)
+def from_lines(lines, first=0):
+    lines = lines.astype(f32)[3 * first : 3 * first + 3]
     return lines[0:1] + lines[1:2] + lines[2:3]
 
 
@@ -153,7 +154,7 @@
     lead = me_ref[0] % 2 == 0
     own, other = from_lines(lines_ref[0]), from_lines(came_ref[0, 4, :EXTRA])
     later = jnp.exp(jnp.where(lead, other, own))
-    lines = as_lines(own + other)
+    lines = as_lines(jnp.where(lead, own, other), jnp.where(lead, other, own))
     for at, part_ref in enumerate(part_refs):
         mine, came = keep_ref[0, at].astype(f32), came_ref[0, at].astype(f32)
         first = jnp.where(lead, mine, came)
@@ -164,8 +165,8 @@
 
 
 def chain_kernel(me_ref, *refs):
-    part_refs, out_refs = refs[:4], refs[4:8]
-    held, lines, entered = refs[8:]
+    part_refs, out_refs, every_ref = refs[:4], refs[4:8], refs[8]
+    held, lines, entered = refs[9:]
     z = me_ref[0] // 2
     rows = held.shape[1]
     for at in range(4):
@@ -174,7 +175,10 @@
     carry = jnp.zeros(held.shape[1:], f32)
     for at in range(4):
         entered[at] = carry.astype(bf16)
-        carry = carry * jnp.exp(from_lines(lines[at])) + held[at].astype(f32)
+        totals = from_lines(lines[at]), from_lines(lines[at], 1)
+        for y in range(2):
+            every_ref[2 * at + y, 0] = as_lines(totals[y])
+        carry = carry * jnp.exp(totals[0] + totals[1]) + held[at].astype(f32)
     for at in range(4):
         out_refs[at][0] = entered[z ^ at]
 
@@ -375,9 +379,10 @@
 
 
 def input_back_kernel(
-    place_ref, input_ref, sum_ref, rank_ref, down_ref, middle_ref, gain_ref, rows_ref, part_ref
+    place_ref, input_ref, own_ref, first_ref, last_ref, rank_ref, down_ref, middle_ref, gain_ref, rows_ref, part_ref
 ):
-    grad = sum_ref[0].astype(f32) + contract(rank_ref[...], down_ref[...], 0, 1)
+    grad = own_ref[0].astype(f32) + first_ref[0].astype(f32) + last_ref[...].astype(f32)
+    grad = grad + contract(rank_ref[...], down_ref[...], 0, 1)
     back, part = norm_back(input_ref[0].astype(f32), grad, gain_ref[...].astype(f32))
     rows_ref[...] = (middle_ref[...] + back).astype(bf16)
     add_part(part_ref, part)
@@ -441,37 +446,16 @@
             out_ref[0] = refs[k][...]
 
 
-def output_kernel(order_ref, middle_ref, *refs):
-    out_ref = refs[-1]
-    step = pl.program_id(0)
-
-    @pl.when(step == 0)
-    def _():
-        out_ref[0] = (refs[0][...].astype(f32) + middle_ref[...]).astype(bf16)
-
-    for k in range(1, 4):
-
-        @pl.when(step == k)
-        def _():
-            out_ref[0] = refs[k][...]
-
-
-def sum_kernel(order_ref, *refs):
-    *refs, out_ref, held = refs
-    count = (len(refs)) // 2
-    rows = out_ref.shape[1]
-
-    @pl.when(pl.program_id(1) == 0)
-    def _():
-        total = against(refs[0][...], refs[count][...])
-        for k in range(1, count):
-            total = total + against(refs[k][...], refs[count + k][...])
-        held[...] = total.astype(bf16)
-        out_ref[0] = held[:rows]
-
-    @pl.when(pl.program_id(1) == 1)
-    def _():
-        out_ref[0] = held[rows:]
+def sum_kernel(*refs):
+    *refs, keep_ref, send_ref = refs
+    count = len(refs) // 2
+    rows = keep_ref.shape[1]
+    total = against(refs[0][...], refs[count][...])
+    for k in range(1, count):
+        total = total + against(refs[k][...], refs[count + k][...])
+    total = total.astype(bf16)
+    keep_ref[0] = total[:rows]
+    send_ref[0] = total[rows:]
 
 
 def grad_kernel(parts, groups, cut_groups, turned, pick_ref, *refs):
@@ -804,16 +788,18 @@
             after=after,
         )
 
-    def chain(own, came, after=()):
+    def chain(own, came, first, after=(), into=()):
         return grid_call(
             chain_kernel,
             (half,),
             [line(quarter + EXTRA, DK)] * 4,
-            [line(quarter, DK)] * 4,
-            [struct((half, quarter, DK), bf16)] * 4,
+            [line(quarter, DK)] * 4
+            + [pl.BlockSpec((8, 1, EXTRA, DK), lambda b, *_: (0, b + first, 0, 0))],
+            [struct((half, quarter, DK), bf16)] * 4 + [struct((8, seq_count, EXTRA, DK), bf16)],
             [me, own, *came],
             prefetch=1,
             after=after,
+            into=into,
             scratch=[
                 pltpu.VMEM((4, quarter, DK), bf16),
                 pltpu.VMEM((4, EXTRA, DK), bf16),
@@ -900,10 +886,10 @@
         others_far = along(pair_far[1:])
         first_near, *pair_near = pairs(parts_near, came_near, [pair_far[0], scores_far])
         others_near = along(pair_near[1:])
-        chain_far = chain(pair_far[0], others_far, [pair_near[0]])
+        *chain_far, lines = chain(pair_far[0], others_far, 0, [pair_near[0]])
         back_far = along(chain_far[1:])
         queries_near, gates_near, scores_near = scored(norm_near, keys_near, run_near, [chain_far[0]])
-        chain_near = chain(pair_near[0], others_near, [chain_far[0]])
+        *chain_near, lines = chain(pair_near[0], others_near, half, [chain_far[0]], [(lines, 4)])
         back_near = along(chain_near[1:])
         whole_far, send_far = enter(parts_far, came_far, first_far, chain_far[0], back_far, [chain_near[0]])
         half_far = swap(send_far, "seq", 1)
@@ -913,8 +899,6 @@
         half_near = swap(send_near, "seq", 1)
         incoming_far = join(whole_far, half_far)
         incoming_near = join(whole_near, half_near)
-        every_line = jnp.concatenate([parts_far[2], parts_near[2]], axis=0)
-        lines = deal(jnp.broadcast_to(every_line[None], (devices, *every_line.shape)))
         state_specs = [
             pl.BlockSpec((2, 1, 4, quarter, DK), lambda b, *_: (0, b, 0, 0, 0)) for at in range(2)
         ]
@@ -928,7 +912,8 @@
         queries_near, values_near, run_near, scores_near, incoming_near, 1, gates_near, [out_second]
     )
     out_near = product(branch_near, out_weight).astype(bf16)
-    out_parts = (out_near[:length], swap(out_near[length:], "tensor", 1), out_last)
+    out_first = region(lambda values: swap(values[length:], "tensor", 1), out_near)
+    out_parts = (out_near[:length], out_first, out_last)
 
     tile = 128
     tiles = (length // tile,)
@@ -983,7 +968,7 @@
     swish_grad = Scatter(second_blocks, [swish_back], bits)
     up_grad = Scatter(second_blocks, [up_back], bits)
     down_grad = Scatter(blocks(grads_near, grads_far), [inner], late_bits, True)
-    swish_away = swish_grad.away([lines])
+    swish_away = swish_grad.away()
     swish_grad.came[0] = swish_grad.hop(0, swish_away)
 
     def second_sum(near, far):
@@ -1029,7 +1014,7 @@
         *near, state_back = branch_back(
             own_rows, first_row, mixed_near, gates_near, queries_near, run_near, half
         )
-        third_row = swap(second_row, "tensor", 1)
+        third_row = swap(hold(second_row, [near[0]]), "tensor", 1)
         *far, state_back = branch_back(
             second_row, third_row, mixed_far, gates_far, queries_far, run_far, 0, state_back
         )
@@ -1041,39 +1026,31 @@
     gate_back_far, mixed_back_far, gain_back_far = far
     norms = blocks(norm_near, norm_far)
 
-    def ordered_output():
-        return grid_call(
-            output_kernel,
-            (4,),
-            [whole_block]
-            + [pl.BlockSpec((length, width), lambda k, order, at=at: (at, 0)) for at in (0, 1, 0, 0)],
-            pl.BlockSpec((1, length, width), lambda k, order: (order[k], 0, 0)),
-            struct((seq_count, length, width), bf16),
-            [order, middle, feed_near[4], feed_near[4], feed_two[4], feed_three[4]],
-            prefetch=1,
-        )
-
     out_grad = Scatter(rows, [blocks(branch_near, branch_far)], bits, True)
     gate_grad = Scatter(norms, [blocks(gate_back_near, gate_back_far)], bits)
 
     def states_back(state_back):
         swish_one = swish_grad.one([state_back])
         gate_away = gate_grad.away([swish_one])
-        return deal(state_back), swish_one, gate_away, out_grad.away([gate_away]), ordered_output()
-
-    came, swish_one, gate_away, out_away, output = region(states_back, state_back)
-    layer_output = lax.psum(output, "tensor")
-
-    def states_out(came, swish_one, out_away):
+        return (
+            deal(state_back), swish_one, gate_away, out_grad.away([gate_away]),
+            tensor_reduce(halves(feed_near[4]), (feed_two[4], feed_three[4]))[0],
+        )
+
+    came, swish_one, gate_away, out_away, output_parts = region(states_back, state_back)
+
+    def states_out(came, swish_one, out_away, gate_away, output_parts):
         up_one = up_grad.one([came])
+        own = sum((part.astype(f32) for part in output_parts), middle).astype(bf16)
         return (
             deal(carried(came, lines, True)), swish_grad.hop(1, swish_one), out_grad.hop(0, out_away),
-            up_one, down_grad.one([up_one]),
-        )
-
-    outgoing, swish_grad.came[1], out_grad.came[0], up_one, down_one = region(
-        states_out, came, swish_one, out_away
-    )
+            up_one, down_grad.one([up_one]), own, swap(own, "tensor", 2), gate_grad.hop(0, gate_away),
+        )
+
+    (
+        outgoing, swish_grad.came[1], out_grad.came[0], up_one, down_one, output_own, output_second,
+        gate_grad.came[0],
+    ) = region(states_out, came, swish_one, out_away, gate_away, output_parts)
     swish_two = swish_grad.two([outgoing])
 
     def mix_back(queries, keys, values, mixed_back, run, scores, incoming, at, rank_rows, after):
@@ -1098,7 +1075,7 @@
             after=after,
         )
 
-    def first_part(query_back, key_back, value_back, gate_back, first, into=()):
+    def first_part(query_back, key_back, value_back, gate_back, at, into=()):
         tile = 512
         pairs = [
             (query_back, query_weight),
@@ -1108,22 +1085,35 @@
         ]
         return grid_call(
             sum_kernel,
-            (width // tile, half),
-            [pl.BlockSpec((half_rows, DK), lambda j, r, order: (0, 0))] * 4
-            + [pl.BlockSpec((tile, DK), lambda j, r, order: (j, 0))] * 4,
-            pl.BlockSpec((1, length, tile), lambda j, r, order: (order[first + r], 0, j)),
+            (width // tile,),
+            [pl.BlockSpec((half_rows, DK), lambda j: (0, 0))] * 4
+            + [pl.BlockSpec((tile, DK), lambda j: (j, 0))] * 4,
+            [pl.BlockSpec((1, length, tile), lambda j: (at, 0, j))] * 2,
+            [struct((half, length, width), bf16)] * 2,
+            [*[p[0] for p in pairs], *[p[1] for p in pairs]],
+            into=into,
+        )
+
+    def in_order(blocks, after=()):
+        whole = pl.BlockSpec((length, width), lambda k, order: (0, 0))
+        return grid_call(
+            place_kernel,
+            (4,),
+            [whole] * 4,
+            pl.BlockSpec((1, length, width), lambda k, order: (order[k], 0, 0)),
             struct((seq_count, length, width), bf16),
-            [order, *[p[0] for p in pairs], *[p[1] for p in pairs]],
+            [order, *blocks],
             prefetch=1,
-            into=into,
-            scratch=[pltpu.VMEM((half_rows, tile), bf16)],
+            after=after,
         )
 
     def mixed_pair(near, far):
         query_key = Scatter(norms, [blocks(near[0], far[0]), blocks(near[1], far[1])], bits)
         return query_key, Scatter(norms, [blocks(near[2], far[2])], late_bits)
 
-    def mixes_back(up_one, swish_two, down_one, gate_away):
+    def mixes_back(up_one, swish_two, down_one, output_own, output_second):
+        gate_one = gate_grad.one([swish_two])
+        output_pair = swap(jnp.stack([output_own, output_second]), "tensor", 1)
         near = mix_back(
             queries_near, keys_near, values_near, mixed_back_near, run_near, scores_near,
             incoming_near, half, rank_near, [swish_two],
@@ -1133,76 +1123,51 @@
             incoming_far, 0, rank_far, [near[5]],
         )
         query_key, value = mixed_pair(near, far)
-        query_key_away = query_key.away([far[5]])
+        keep, send = first_part(*far[:3], gate_back_far, 1)
+        keep, send = first_part(*near[:3], gate_back_near, 0, [(keep, 0), (send, 1)])
+        query_key_away = query_key.away([send])
         value_away = value.away([query_key_away])
-        first_sum = first_part(*far[:3], gate_back_far, half)
-        first_sum = first_part(*near[:3], gate_back_near, 0, [(first_sum, 0)])
         return (
             up_grad.hop(1, up_one), swish_grad.hop(2, swish_two), down_grad.hop(1, down_one),
-            gate_grad.hop(0, gate_away), near, far, query_key_away, value_away, first_sum, out_grad.one([first_sum]),
+            gate_grad.hop(1, gate_one), near, far, query_key_away, value_away,
+            keep, send, out_grad.one([value_away]), output_pair,
         )
 
     (
-        up_grad.came[1], swish_grad.came[2], down_grad.came[1], gate_grad.came[0], near, far, query_key_away,
-        value_away, first_sum, out_one,
-    ) = region(mixes_back, up_one, swish_two, down_one, gate_away)
-    gate_one = gate_grad.one([first_sum])
-    down_two = down_grad.two([gate_one])
+        up_grad.came[1], swish_grad.came[2], down_grad.came[1], gate_grad.came[1], near, far, query_key_away,
+        value_away, first_keep, first_send, out_one, output_pair,
+    ) = region(mixes_back, up_one, swish_two, down_one, output_own, output_second)
+
+    def first_sum(keep, send):
+        came = swap(send, "tensor", 1)
+        gate_two = gate_grad.two([send])
+        down_two = down_grad.two([gate_two])
+        return came, (keep[1].astype(f32) + came[1].astype(f32)).astype(bf16), gate_two, down_two
+
+    first_came, first_second, gate_two, down_two = region(first_sum, first_keep, first_send)
     rank_part_near, up_part_near, bias_part_near = near[3:]
     rank_part_far, up_part_far, bias_part_far = far[3:]
     query_key_grad, value_grad = mixed_pair(near, far)
-    first_grad = lax.psum_scatter(first_sum, "tensor", scatter_dimension=0, tiled=True)
-
-    def third_window(query_key_away, value_away, gate_one, down_two):
+
+    def third_window(query_key_away, value_away, gate_two, down_two, first_second):
         rank_part = jnp.concatenate([rank_part_near, rank_part_far], axis=0)
         rank_part = lax.all_to_all(jnp.take(rank_part, order, axis=0), "tensor", 0, 0)
         return (
             query_key_grad.hop(0, query_key_away), value_grad.hop(0, value_away),
-            gate_grad.hop(1, gate_one), down_grad.hop(2, down_two), up_grad.two(),
-            swish_grad.last(), jnp.sum(rank_part, axis=0).astype(bf16),
+            gate_grad.hop(2, gate_two), down_grad.hop(2, down_two), up_grad.two(),
+            swish_grad.last(), jnp.sum(rank_part, axis=0).astype(bf16), swap(first_second, "tensor", 2),
+            in_order([output_own, output_pair[0], output_second, output_pair[1]], [down_two]),
         )
 
     (
-        query_key_grad.came[0], value_grad.came[0], gate_grad.came[1], down_grad.came[2], up_two,
-        swish_share, rank_back,
-    ) = region(third_window, query_key_away, value_away, gate_one, down_two)
+        query_key_grad.came[0], value_grad.came[0], gate_grad.came[2], down_grad.came[2], up_two,
+        swish_share, rank_back, first_last, layer_output,
+    ) = region(third_window, query_key_away, value_away, gate_two, down_two, first_second)
     query_key_one = query_key_grad.one()
     value_one = value_grad.one([query_key_one])
 
-    def fourth_window(query_key_one, value_one, up_two, out_one, layer_output):
-        return (
-            query_key_grad.hop(1, query_key_one), value_grad.hop(1, value_one), up_grad.hop(2, up_two),
-            out_grad.hop(1, out_one), gate_grad.two(), down_grad.last(), layer_output,
-        )
-
-    (
-        query_key_grad.came[1], value_grad.came[1], up_grad.came[2], out_grad.came[1], gate_two, down_share,
-        layer_output,
-    ) = region(fourth_window, query_key_one, value_one, up_two, out_one, layer_output)
-
-    input_rows, attn_norm_part = grid_call(
-        input_back_kernel,
-        tiles,
-        [own_spec, pl.BlockSpec((1, tile, width), lambda b, *_: (0, b, 0))]
-        + [
-            pl.BlockSpec((rank, tile), lambda b, *_: (0, b)), fixed((width, rank)), tile_spec,
-            fixed((1, width)),
-        ],
-        [tile_spec, fixed((1, width))],
-        [struct((length, width), bf16), struct((1, width), f32)],
-        [
-            place_index, layer_input, first_grad, rank_back, rank_down, middle_grad,
-            attn_norm.reshape(1, width),
-        ],
-        prefetch=1,
-        after=[gate_two],
-    )
-    out_two = out_grad.two([input_rows])
-    query_key_two = query_key_grad.two([out_two])
-    value_two = value_grad.two([query_key_two])
-
     rank_down_part = contract(rank_back, norm_near[:length], 1, 0)
-    own_part = jnp.concatenate([rank_down_part, mlp_norm_part, attn_norm_part], axis=0)
+    own_part = jnp.concatenate([rank_down_part, mlp_norm_part], axis=0)
     shared = jnp.concatenate(
         [
             sum(up_part_near) + sum(up_part_far),
@@ -1212,8 +1177,8 @@
         axis=0,
     )
     column = width // devices
-    own_part = jnp.moveaxis(own_part.reshape(rank + 2, devices, column), 1, 0)
-    own_size = (rank + 2) * column
+    own_part = jnp.moveaxis(own_part.reshape(rank + 1, devices, column), 1, 0)
+    own_size = (rank + 1) * column
     mail = jnp.concatenate(
         [
             own_part.reshape(devices, own_size),
@@ -1222,43 +1187,70 @@
         axis=1,
     )
 
-    def fifth_window(input_rows, query_key_two, value_two, gate_two, out_two, mail):
-        mail = lax.all_to_all(mail, "seq", 0, 0)
+    def summed(mail):
+        mail = mail.reshape(devices, 1, -1).astype(bf16)
+        return jnp.sum(lax.all_to_all(mail, "seq", 0, 0).astype(f32), axis=0)
+
+    def fourth_window(query_key_one, value_one, up_two, out_one, mail):
+        return (
+            query_key_grad.hop(1, query_key_one), value_grad.hop(1, value_one), up_grad.hop(2, up_two),
+            out_grad.hop(1, out_one), gate_grad.last(), down_grad.last(), summed(mail),
+        )
+
+    (
+        query_key_grad.came[1], value_grad.came[1], up_grad.came[2], out_grad.came[1], gate_share, down_share,
+        mail,
+    ) = region(fourth_window, query_key_one, value_one, up_two, out_one, mail)
+
+    input_rows, attn_norm_part = grid_call(
+        input_back_kernel,
+        tiles,
+        [own_spec]
+        + [pl.BlockSpec((1, tile, width), lambda b, *_: (0, b, 0))] * 2
+        + [
+            tile_spec,
+            pl.BlockSpec((rank, tile), lambda b, *_: (0, b)), fixed((width, rank)), tile_spec,
+            fixed((1, width)),
+        ],
+        [tile_spec, fixed((1, width))],
+        [struct((length, width), bf16), struct((1, width), f32)],
+        [
+            place_index, layer_input, first_keep, first_came, first_last, rank_back, rank_down, middle_grad,
+            attn_norm.reshape(1, width),
+        ],
+        prefetch=1,
+        after=[gate_share],
+    )
+    out_two = out_grad.two([input_rows])
+    query_key_two = query_key_grad.two([out_two])
+    value_two = value_grad.two([query_key_two])
+
+    def fifth_window(input_rows, query_key_two, value_two, out_two, attn_norm_part):
         return (
             swap(input_rows, "tensor", 2), query_key_grad.hop(2, query_key_two),
-            value_grad.hop(2, value_two), gate_grad.hop(2, gate_two),
-            jnp.sum(mail.astype(f32), axis=0), up_grad.last(), out_grad.hop(2, out_two),
+            value_grad.hop(2, value_two), out_grad.hop(2, out_two),
+            summed(attn_norm_part), up_grad.last(),
         )
 
     (
-        second_rows, query_key_grad.came[2], value_grad.came[2], gate_grad.came[2], mail, up_share,
-        out_grad.came[2],
-    ) = region(
-        fifth_window, input_rows, query_key_two, value_two, gate_two, out_two,
-        mail.reshape(devices, 1, -1).astype(bf16),
-    )
-
-    def sixth_window(input_rows, second_rows):
-        pair = swap(jnp.stack([input_rows, second_rows]), "tensor", 1)
-        whole = pl.BlockSpec((length, width), lambda k, order: (0, 0))
-        input_grad = grid_call(
-            place_kernel,
-            (4,),
-            [whole] * 4,
-            pl.BlockSpec((1, length, width), lambda k, order: (order[k], 0, 0)),
-            struct((seq_count, length, width), bf16),
-            [order, input_rows, pair[0], second_rows, pair[1]],
-            prefetch=1,
-        )
-        return input_grad, query_key_grad.last(), value_grad.last(), gate_grad.last(), out_grad.last()
-
-    input_grad, query_key_share, value_share, gate_share, out_share = region(
-        sixth_window, input_rows, second_rows
-    )
-    mail = mail.reshape(-1)
-    own_part = mail[:own_size].reshape(rank + 2, column)
-    shared = mail[own_size:].reshape(rank + 2, DK)
-    own_part = sum_over(own_part, "tensor")
+        second_rows, query_key_grad.came[2], value_grad.came[2], out_grad.came[2],
+        attn_norm_part, up_share,
+    ) = region(fifth_window, input_rows, query_key_two, value_two, out_two, attn_norm_part)
+
+    def sixth_window(input_rows, second_rows, mail, attn_norm_part):
+        first_rows = swap(input_rows, "tensor", 1)
+        third_rows = swap(second_rows, "tensor", 1)
+        parts = jnp.concatenate([mail.reshape(-1)[:own_size], attn_norm_part.reshape(-1)])
+        return (
+            in_order([input_rows, first_rows, second_rows, third_rows]), query_key_grad.last(),
+            value_grad.last(), out_grad.last(),
+            sum_over(parts.reshape(rank + 2, column), "tensor"),
+        )
+
+    input_grad, query_key_share, value_share, out_share, own_part = region(
+        sixth_window, input_rows, second_rows, mail, attn_norm_part
+    )
+    shared = mail.reshape(-1)[own_size:].reshape(rank + 2, DK)
     return (
         layer_output,
         input_grad,

time: 782 us -> 731 us (0.935)
  waiting for transfers between devices: 320 us -> 260 us
  matrix products: 15.3 us -> 32.8 us
  between operations: 15.9 us -> 1.95 us
  starting transfers between devices: 94.8 us -> 104 us
  local copies, waits for them, and re-layouts: 39.7 us -> 31.6 us
    ppermute x53 -> x61, waiting for transfers between devices: 247 us -> 162 us  [swap(): return lax.ppermute(values, axis, [(i, i ^ distance) for i in range(count)])]
    all_to_all x1 -> x2, waiting for transfers between devices: 25.5 us -> 58.2 us  [summed(): return jnp.sum(lax.all_to_all(mail, 'seq', 0, 0).astype(f32), axis=0)]
    dot_general x13, matrix products: 15.3 us -> 32.8 us  [contract(): lax.dot_general(left, right, (((left_dim,), (right_dim,)), ((), ())), pre...]
    ppermute x53 -> x61, starting transfers between devices: 70.9 us -> 83.3 us  [swap(): return lax.ppermute(values, axis, [(i, i ^ distance) for i in range(count)])]
    all_to_all x3 -> x2, waiting for transfers between devices: 47.7 us -> 36 us  [deal(): return lax.all_to_all(pieces, 'seq', 0, 0)]
    convert_element_type x0 -> x5, other arithmetic: none -> 9.21 us  [the longest x1 4.13 us: states_out(): own = sum((part.astype(f32) for part in output_parts), middle).astype(bf16)]
    all_to_all x3 -> x2, starting transfers between devices: 16.9 us -> 10.3 us  [deal(): return lax.all_to_all(pieces, 'seq', 0, 0)]
    unnamed x204 -> x130, local copies, waits for them, and re-layouts: 18.8 us -> 12.6 us
  transfers between devices with their start and end apart: 60 -> 66, of which waited for: 24 -> 25; matrix products, arithmetic and copies ran while one was open for 4% -> 6% of each run, Pallas kernels for 31% -> 28%
where the time goes in v4:
time: 731 us; the launch traced here: 720 us
  Pallas kernels  271 us (37%)
  waiting for transfers between devices  260 us (36%)
  starting transfers between devices  104 us (14%)
  matrix products  32.8 us (4%)
  local copies, waits for them, and re-layouts  31.6 us (4%)
  other arithmetic  18.6 us (3%)
    pallas_call x63, Pallas kernels, grid_call(): pl.pallas_call(run, grid_spec=pltpu.PrefetchScalarGridSpec(num_scalar_pre...  271 us
    ppermute x61, waiting for transfers between devices, swap(): return lax.ppermute(values, axis, [(i, i ^ distance) for i in range(count)])  162 us
    ppermute x61, starting transfers between devices, swap(): return lax.ppermute(values, axis, [(i, i ^ distance) for i in range(count)])  83.3 us
    all_to_all x2, waiting for transfers between devices, summed(): return jnp.sum(lax.all_to_all(mail, 'seq', 0, 0).astype(f32), axis=0)  58.2 us
    all_to_all x2, waiting for transfers between devices, deal(): return lax.all_to_all(pieces, 'seq', 0, 0)  36 us
    dot_general x13, matrix products, contract(): lax.dot_general(left, right, (((left_dim,), (right_dim,)), ((), ())), pre...  32.8 us
  transfers between devices with their start and end apart: 66, of which 25 were waited for; matrix products, arithmetic and copies ran while one was open for 6% of the time, Pallas kernels for 28%

profile of v4, /device:TPU:0, one launch (start us, length us, event | category | flops | bytes accessed | tf_op | source)
XLA Modules:
  0.0 720.2 jit_solution(366748338782102243)
XLA Ops:
  62.5 9.6 %collective-permute-start.47 = (bf16[2,64,512]{2,1,0:T(8,128)(2,1)S(1)}, bf16[2,64,512]{2,1,0:T(8,128)(2,1)S(1)}, u32[]{:S(2)}, u32[]{:S(2)}) collective-permute-start(bf16[2,64,512]{2,1,0:T(8,128)(2,1)S(1)} %get-tuple-element.865), channel_id=1, source_target_pairs={{0,8},{4,12},{8,0},{12,4},{16,24},{20,28},{24,16},{28,20},{1,9},{5... | collective-permute-start | bytes 393224 | tf_op jit(solution)/shard_map/ppermute | solution.py:515
  79.1 7.9 %collective-permute-done.48.refs_6_ = bf16[2,64,512]{2,1,0:T(8,128)(2,1)S(1)} collective-permute-done((bf16[2,64,512]{2,1,0:T(8,128)(2,1)S(1)}, bf16[2,64,512]{2,1,0:T(8,128)(2,1)S(1)}, u32[]{:S(2)}, u32[]{:S(2)}) %collective-permute-start.48) | collective-permute-done | bytes 131104 | tf_op jit(solution)/shard_map/ppermute | solution.py:515
  91.8 9.3 %collective-permute-done.51.refs_1_ = bf16[2,4,64,512]{3,2,1,0:T(8,128)(2,1)S(1)} collective-permute-done((bf16[2,4,64,512]{3,2,1,0:T(8,128)(2,1)S(1)}, bf16[2,4,64,512]{3,2,1,0:T(8,128)(2,1)S(1)}, u32[]{:S(2)}, u32[]{:S(2)}) %collective-permute-start.51) | collective-permute-done | bytes 524320 | tf_op jit(solution)/shard_map/ppermute | solution.py:515
  127.2 7.5 %collective-permute-done.50.refs_1_ = bf16[2,4,64,512]{3,2,1,0:T(8,128)(2,1)S(1)} collective-permute-done((bf16[2,4,64,512]{3,2,1,0:T(8,128)(2,1)S(1)}, bf16[2,4,64,512]{3,2,1,0:T(8,128)(2,1)S(1)}, u32[]{:S(2)}, u32[]{:S(2)}) %collective-permute-start.50) | collective-permute-done | bytes 524320 | tf_op jit(solution)/shard_map/ppermute | solution.py:515
  151.1 22.9 %shard_map.298 = (bf16[512,1408]{1,0:T(8,128)(2,1)}, bf16[512,1408]{1,0:T(8,128)(2,1)}, bf16[512,1408]{1,0:T(8,128)(2,1)}, bf16[512,2048]{1,0:T(8,128)(2,1)}, bf16[512,2048]{1,0:T(8,128)(2,1)S(1)}) custom-call(bf16[256,2048]{1,0:T(8,128)(2,1)S(1)} %get-tuple-element.874.refs_0_.refs_1_, bf16[256,2048]{1,0:T(8,128)(2,1)S(1)} %collective-permute-done.54.refs_1_.refs_2_, ...), custom_call_target="tpu_custom_call" | custom-call | flops 1024 | bytes 1024 | tf_op jit(solution)/shard_map/pallas_call | solution.py:497
  178.1 13.6 %shard_map.299 = (bf16[256,1408]{1,0:T(8,128)(2,1)}, bf16[256,1408]{1,0:T(8,128)(2,1)S(1)}, bf16[256,1408]{1,0:T(8,128)(2,1)}, bf16[256,2048]{1,0:T(8,128)(2,1)}, bf16[256,2048]{1,0:T(8,128)(2,1)S(1)}) custom-call(bf16[256,2048]{1,0:T(8,128)(2,1)S(1)} %collective-permute-done.55.refs_0_.refs_1_.refs_3_, ...), custom_call_target="tpu_custom_call" | custom-call | flops 1024 | bytes 1024 | tf_op jit(solution)/shard_map/pallas_call | solution.py:497
  191.8 15.5 %shard_map.301 = (bf16[256,1408]{1,0:T(8,128)(2,1)}, bf16[256,1408]{1,0:T(8,128)(2,1)S(1)}, bf16[256,1408]{1,0:T(8,128)(2,1)}, bf16[256,2048]{1,0:T(8,128)(2,1)}, bf16[256,2048]{1,0:T(8,128)(2,1)}) custom-call(bf16[256,2048]{1,0:T(8,128)(2,1)} %collective-permute-done.56.refs_0_.refs_1_.refs_4_, ...), custom_call_target="tpu_custom_call" | custom-call | flops 1024 | bytes 1024 | tf_op jit(solution)/shard_map/pallas_call | solution.py:497
  215.9 29.9 %conditional.12 = (bf16[256,2048]{1,0:T(8,128)(2,1)}, bf16[256,2048]{1,0:T(8,128)(2,1)}, bf16[4,256,1408]{2,1,0:T(8,128)(2,1)}, bf16[4,256,1408]{2,1,0:T(8,128)(2,1)}) conditional(s32[]{:T(128)} %convert_element_type.128, () %tuple.102, (bf16[512,2048]{1,0:T(8,128)(2,1)S(1)}, bf16[256,2048]{1,0:T(8,128)(2,1)S(1)}, bf16[256,2048]{1,0:T(8,128)(2,1)}, ...), branch_computations={%region_2.0_spmd, %region_3.0_spmd} | conditional | flops 2099229 | bytes 54528536 | solution.py:524
  221.9 8.1 %branch_1_fun.31.refs_9_ = bf16[4,256,1408]{2,1,0:T(8,128)(2,1)} custom-call(s32[4]{0:T(128)S(1)} %get-tuple-element.982.refs_0_, bf16[512,2048]{1,0:T(8,128)(2,1)S(1)} %copy-done.7, bf16[512,2048]{1,0:T(8,128)(2,1)S(1)} %copy-done.7, bf16[512,2048]{1,0:T(8,128)(2,1)} %get-tuple-element.445.refs_3_.refs_4_, ...), custom_call_target="tpu_custom_call" | custom-call | flops 1024 | bytes 1024 | tf_op jit(solution)/shard_map/cond/branch_1_fun/pallas_call | solution.py:497
  236.8 9.0 %collective-permute-done.5 = bf16[256,2048]{1,0:T(8,128)(2,1)} collective-permute-done((bf16[256,2048]{1,0:T(8,128)(2,1)}, bf16[256,2048]{1,0:T(8,128)(2,1)}, u32[]{:S(2)}, u32[]{:S(2)}) %collective-permute-start.5) | collective-permute-done | bytes 1048608 | tf_op jit(solution)/shard_map/cond/branch_1_fun/ppermute | solution.py:515
  257.9 34.9 %conditional.13 = (bf16[256,2048]{1,0:T(8,128)(2,1)}, bf16[256,2048]{1,0:T(8,128)(2,1)}, bf16[512,512]{1,0:T(8,128)(2,1)}, bf16[512,512]{1,0:T(8,128)(2,1)}, f32...) conditional(s32[]{:T(128)} %convert_element_type.128, ...), branch_computations={%region_4.0_spmd, %region_5.0_spmd} | conditional | flops 3072 | bytes 31460644 | solution.py:524
  266.1 17.3 %collective-permute-done.1.refs_0_ = bf16[256,2048]{1,0:T(8,128)(2,1)} collective-permute-done((bf16[256,2048]{1,0:T(8,128)(2,1)}, bf16[256,2048]{1,0:T(8,128)(2,1)}, u32[]{:S(2)}, u32[]{:S(2)}) %collective-permute-start.1) | collective-permute-done | bytes 1048608 | tf_op jit(solution)/shard_map/cond/branch_1_fun/ppermute | solution.py:515
  292.8 71.1 %conditional.14 = (bf16[8,4,64,512]{3,2,1,0:T(8,128)(2,1)}, bf16[2,256,1408]{2,1,0:T(8,128)(2,1)}, bf16[4,256,512]{2,1,0:T(8,128)(2,1)}, bf16[4,256,512]{2,1,0:T...) conditional(s32[]{:T(128)} %convert_element_type.128, () %tuple.99, ...), branch_computations={%region_6.0_spmd, %region_7.0_spmd} | conditional | flops 2100247 | bytes 34606524 | solution.py:524
  320.3 7.5 %collective-permute-done.23 = bf16[256,2048]{1,0:T(8,128)(2,1)} collective-permute-done((bf16[256,2048]{1,0:T(8,128)(2,1)}, bf16[256,2048]{1,0:T(8,128)(2,1)}, u32[]{:S(2)}, u32[]{:S(2)}) %collective-permute-start.23) | collective-permute-done | bytes 1048608 | tf_op jit(solution)/shard_map/cond/branch_1_fun/ppermute | solution.py:515
  327.9 36.0 %all-to-all-done.2 = bf16[8,4,64,512]{3,2,1,0:T(8,128)(2,1)} async-done(((bf16[8,4,64,512]{3,2,1,0:T(8,128)(2,1)}), bf16[8,4,64,512]{3,2,1,0:T(8,128)(2,1)}, u32[]{:S(2)}, u32[]{:S(2)}) %all-to-all-start.2) | async-done | bytes 2097184 | tf_op jit(solution)/shard_map/cond/branch_1_fun/all_to_all | solution.py:554
  363.9 80.2 %conditional.15 = (bf16[8,4,64,512]{3,2,1,0:T(8,128)(2,1)}, bf16[2,256,1408]{2,1,0:T(8,128)(2,1)}, bf16[4,256,512]{2,1,0:T(8,128)(2,1)}, bf16[2,256,1408]{2,1,0:...) conditional(s32[]{:T(128)} %convert_element_type.128, () %tuple.98, ...), branch_computations={%region_8.0_spmd, %region_9.0_spmd} | conditional | flops 3673099 | bytes 30936432 | solution.py:524
  395.8 9.2 %collective-permute-done.8 = bf16[256,2048]{1,0:T(8,128)(2,1)} collective-permute-done((bf16[256,2048]{1,0:T(8,128)(2,1)}, bf16[256,2048]{1,0:T(8,128)(2,1)}, u32[]{:S(2)}, u32[]{:S(2)}) %collective-permute-start.8) | collective-permute-done | bytes 1048608 | tf_op jit(solution)/shard_map/cond/branch_1_fun/ppermute | solution.py:515
  405.0 17.3 %collective-permute-done.7 = bf16[4,256,512]{2,1,0:T(8,128)(2,1)} collective-permute-done((bf16[4,256,512]{2,1,0:T(8,128)(2,1)}, bf16[4,256,512]{2,1,0:T(8,128)(2,1)}, u32[]{:S(2)}, u32[]{:S(2)}) %collective-permute-start.7) | collective-permute-done | bytes 1048608 | tf_op jit(solution)/shard_map/cond/branch_1_fun/ppermute | solution.py:515
  422.3 21.8 %collective-permute-done.9 = bf16[4,256,512]{2,1,0:T(8,128)(2,1)} collective-permute-done((bf16[4,256,512]{2,1,0:T(8,128)(2,1)}, bf16[4,256,512]{2,1,0:T(8,128)(2,1)}, u32[]{:S(2)}, u32[]{:S(2)}) %collective-permute-start.9) | collective-permute-done | bytes 1048608 | tf_op jit(solution)/shard_map/cond/branch_1_fun/ppermute | solution.py:515
  448.4 64.3 %conditional.16 = (bf16[2,256,1408]{2,1,0:T(8,128)(2,1)}, bf16[1,256,1408]{2,1,0:T(8,128)(2,1)}, bf16[2,256,1408]{2,1,0:T(8,128)(2,1)}, bf16[2,256,512]{2,1,0:T(...) conditional(s32[]{:T(128)} %convert_element_type.128, () %tuple.97, ...), branch_computations={%region_10.0_spmd, %region_11.0_spmd} | conditional | flops 1056799 | bytes 97772736 | solution.py:524
  460.0 7.3 %branch_1_fun.43 = (bf16[512,512]{1,0:T(8,128)(2,1)}, bf16[512,512]{1,0:T(8,128)(2,1)}, bf16[512,512]{1,0:T(8,128)(2,1)}, f32[2,16,256]{2,1,0:T(8,128)S(1)}, f32...) custom-call(bf16[512,512]{1,0:T(8,128)(2,1)S(1)} %copy-done.77, bf16[512,512]{1,0:T(8,128)(2,1)S(1)} %copy-done.88, ...), custom_call_target="tpu_custom_call" | custom-call | flops 1024 | bytes 1024 | tf_op jit(solution)/shard_map/cond/branch_1_fun/pallas_call | solution.py:497
  467.4 7.6 %branch_1_fun.44 = (bf16[512,512]{1,0:T(8,128)(2,1)}, bf16[512,512]{1,0:T(8,128)(2,1)}, bf16[512,512]{1,0:T(8,128)(2,1)}, f32[2,16,256]{2,1,0:T(8,128)}, f32[2,16,512]{2,1,0:T(8,128)}, /*index=5*/f32[2,1,512]{2,1,0:T(1,128)}) custom-call(bf16[512,512]{1,0:T(8,128)(2,1)} %get-tuple-element.547.refs_0_, bf16[512,512]{1,0:T(8,128)(2,1)} %get-tuple-element.548.refs_1_, ...), custom_call_target="tpu_custom_call" | custom-call | flops 1024 | bytes 1024 | tf_op jit(solution)/shard_map/cond/branch_1_fun/pallas_call | solution.py:497
  482.4 7.4 %branch_1_fun.46 = (bf16[2,256,2048]{2,1,0:T(8,128)(2,1)}, bf16[2,256,2048]{2,1,0:T(8,128)(2,1)}) custom-call(bf16[512,512]{1,0:T(8,128)(2,1)} %get-tuple-element.1082.refs_0_.refs_5_.refs_6_, bf16[512,512]{1,0:T(8,128)(2,1)} %get-tuple-element.1083.refs_1_.refs_9_.refs_10_, ...), custom_call_target="tpu_custom_call", output_to_operand_aliasing={{0}: (8, {}), {1}: (9, {})} | custom-call | flops 1024 | bytes 1024 | tf_op jit(solution)/shard_map/cond/branch_1_fun/pallas_call | solution.py:497
  513.6 9.5 %conditional.17 = (bf16[2,256,2048]{2,1,0:T(8,128)(2,1)}, bf16[256,2048]{1,0:T(8,128)(2,1)}, bf16[1,256,512]{2,1,0:T(8,128)(2,1)S(1)}, bf16[1,256,1408]{2,1,0:T(8,128)(2,1)}) conditional(s32[]{:T(128)} %convert_element_type.128, () %tuple.108, (bf16[2,256,2048]{2,1,0:T(8,128)(2,1)}, bf16[2,256,2048]{2,1,0:T(8,128)(2,1)}, ...), branch_computations={%region_12.0_spmd, %region_13.0_spmd} | conditional | flops 2099204 | bytes 33556764 | solution.py:524
  523.1 48.3 %conditional.18 = (bf16[4,256,1024]{2,1,0:T(8,128)(2,1)}, bf16[4,256,512]{2,1,0:T(8,128)(2,1)}, bf16[1,256,512]{2,1,0:T(8,128)(2,1)}, bf16[1,256,1408]{2,1,0:T(8...) conditional(s32[]{:T(128)} %convert_element_type.128, () %tuple.96, ...), branch_computations={%region_14.0_spmd, %region_15.17_spmd} | conditional | flops 49192 | bytes 49692256 | solution.py:524
  552.4 17.3 %collective-permute-done.18 = bf16[1,256,512]{2,1,0:T(8,128)(2,1)} collective-permute-done((bf16[1,256,512]{2,1,0:T(8,128)(2,1)S(1)}, bf16[1,256,512]{2,1,0:T(8,128)(2,1)}, u32[]{:S(2)}, u32[]{:S(2)}) %collective-permute-start.18) | collective-permute-done | bytes 262176 | tf_op jit(solution)/shard_map/cond/branch_1_fun/ppermute | solution.py:515
  582.0 55.3 %conditional.19 = (bf16[2,256,1024]{2,1,0:T(8,128)(2,1)}, bf16[2,256,512]{2,1,0:T(8,128)(2,1)}, bf16[1,256,1408]{2,1,0:T(8,128)(2,1)}, bf16[2,256,512]{2,1,0:T(8...) conditional(s32[]{:T(128)} %convert_element_type.128, () %tuple.112, ...), branch_computations={%region_17.18_spmd, %region_18.20_spmd} | conditional | flops 205571 | bytes 33531278 | solution.py:524
  603.1 25.7 %all-to-all-done.3 = bf16[8,2,6784]{2,1,0:T(2,128)(2,1)S(1)} async-done(((bf16[8,2,6784]{2,1,0:T(2,128)(2,1)}), bf16[8,2,6784]{2,1,0:T(2,128)(2,1)S(1)}, u32[]{:S(2)}, u32[]{:S(2)}) %all-to-all-start.3) | async-done | bytes 217120 | tf_op jit(solution)/shard_map/cond/branch_1_fun/all_to_all | solution.py:1192
  629.5 7.9 %collective-permute-done.31 = bf16[2,256,512]{2,1,0:T(8,128)(2,1)} collective-permute-done((bf16[2,256,512]{2,1,0:T(8,128)(2,1)}, bf16[2,256,512]{2,1,0:T(8,128)(2,1)}, u32[]{:S(2)}, u32[]{:S(2)}) %collective-permute-start.31) | collective-permute-done | bytes 524320 | tf_op jit(solution)/shard_map/cond/branch_1_fun/ppermute | solution.py:515
  650.5 48.6 %conditional.20 = (bf16[256,2048]{1,0:T(8,128)(2,1)}, bf16[1,256,1024]{2,1,0:T(8,128)(2,1)}, bf16[1,256,512]{2,1,0:T(8,128)(2,1)}, bf16[1,256,512]{2,1,0:T(8,128...) conditional(s32[]{:T(128)} %convert_element_type.128, () %tuple.114, (bf16[256,2048]{1,0:T(8,128)(2,1)}, ...), branch_computations={%region_20.21_spmd, %region_21.23_spmd} | conditional | flops 6915 | bytes 8444182 | solution.py:524
  666.5 32.5 %all-to-all-done.4 = bf16[8,2,128]{2,1,0:T(2,128)(2,1)S(1)} async-done(((bf16[8,2,128]{2,1,0:T(2,128)(2,1)}), bf16[8,2,128]{2,1,0:T(2,128)(2,1)S(1)}, u32[]{:S(2)}, u32[]{:S(2)}) %all-to-all-start.4) | async-done | bytes 4128 | tf_op jit(solution)/shard_map/cond/branch_1_fun/all_to_all | solution.py:1192
  699.1 17.0 %conditional.21 = (bf16[4,256,2048]{2,1,0:T(8,128)(2,1)}, f32[256,1024]{1,0:T(8,128)}, f32[256,512]{1,0:T(8,128)}, f32[512,256]{1,0:T(8,128)}, f32[18,256]{1,0:T...) conditional(s32[]{:T(128)} %convert_element_type.128, () %tuple.111, (bf16[256,2048]{1,0:T(8,128)(2,1)}, ...), branch_computations={%region_23.24_spmd, %region_24.25_spmd} | conditional | flops 17923 | bytes 19245388 | solution.py:524
  (499 shorter events, 402.1 us)
Async XLA Ops:
  111.2 30.8 %collective-permute-start.53 = (bf16[256,2048]{1,0:T(8,128)(2,1)S(1)}, bf16[256,2048]{1,0:T(8,128)(2,1)S(1)}, u32[]{:S(2)}, u32[]{:S(2)}) collective-permute-start(bf16[256,2048]{1,0:T(8,128)(2,1)S(1)} %add_convert_fusion.4.refs_7_), channel_id=1, source_target_pairs={{0,2},{1,3},{2,0},{3,1},{4,6},{5,7},{6,4},{7,5},{8,10},{9,11},{10,... | collective-permute-start | bytes 3145736 | tf_op jit(solution)/shard_map/ppermute | solution.py:515
  145.5 28.5 %collective-permute-start.55 = (bf16[256,2048]{1,0:T(8,128)(2,1)S(1)}, bf16[256,2048]{1,0:T(8,128)(2,1)S(1)}, u32[]{:S(2)}, u32[]{:S(2)}) collective-permute-start(bf16[256,2048]{1,0:T(8,128)(2,1)S(1)} %get-tuple-element.874.refs_0_.refs_1_), channel_id=1, source_target_pairs={{0,2},{1,3},{2,0},{3,1},{4,6},{5,7},{6,4},{7,5},{8,10},{9,11},{10,... | collective-permute-start | bytes 3145736 | tf_op jit(solution)/shard_map/ppermute | solution.py:515
  214.6 78.2 %collective-permute-start.58 = (bf16[4,256,1408]{2,1,0:T(8,128)(2,1)}, bf16[4,256,1408]{2,1,0:T(8,128)(2,1)}, u32[]{:S(2)}, u32[]{:S(2)}) collective-permute-start(bf16[4,256,1408]{2,1,0:T(8,128)(2,1)} %shard_map.302), channel_id=1, source_target_pairs={{0,4},{4,0},{8,12},{12,8},{16,20},{20,16},{24,28},{28,24},{1,5},{5... | collective-permute-start | bytes 8650760 | tf_op jit(solution)/shard_map/ppermute | solution.py:515
  220.3 25.5 %collective-permute-start.5 = (bf16[256,2048]{1,0:T(8,128)(2,1)}, bf16[256,2048]{1,0:T(8,128)(2,1)}, u32[]{:S(2)}, u32[]{:S(2)}) collective-permute-start(bf16[256,2048]{1,0:T(8,128)(2,1)} %add_convert_fusion), channel_id=1, source_target_pairs={{0,2},{1,3},{2,0},{3,1},{4,6},{5,7},{6,4},{7,5},{8,10},{9,11},{10,... | collective-permute-start | bytes 3145736 | tf_op jit(solution)/shard_map/cond/branch_1_fun/ppermute | solution.py:515
  245.8 118.1 %collective-permute-start.59 = (bf16[4,256,1408]{2,1,0:T(8,128)(2,1)}, bf16[4,256,1408]{2,1,0:T(8,128)(2,1)}, u32[]{:S(2)}, u32[]{:S(2)}) collective-permute-start(bf16[4,256,1408]{2,1,0:T(8,128)(2,1)} %get-tuple-element.906), channel_id=1, source_target_pairs={{0,4},{4,0},{8,12},{12,8},{16,20},{20,16},{24,28},{28,24},{1,5},{5... | collective-permute-start | bytes 8650760 | tf_op jit(solution)/shard_map/ppermute | solution.py:515
  246.6 117.4 %collective-permute-start.60 = (bf16[4,256,1408]{2,1,0:T(8,128)(2,1)}, bf16[4,256,1408]{2,1,0:T(8,128)(2,1)}, u32[]{:S(2)}, u32[]{:S(2)}) collective-permute-start(bf16[4,256,1408]{2,1,0:T(8,128)(2,1)} %get-tuple-element.907), channel_id=1, source_target_pairs={{0,8},{4,12},{8,0},{12,4},{16,24},{20,28},{24,16},{28,20},{1,9},{5... | collective-permute-start | bytes 8650760 | tf_op jit(solution)/shard_map/ppermute | solution.py:515
  257.9 25.5 %collective-permute-start.1 = (bf16[256,2048]{1,0:T(8,128)(2,1)}, bf16[256,2048]{1,0:T(8,128)(2,1)}, u32[]{:S(2)}, u32[]{:S(2)}) collective-permute-start(bf16[256,2048]{1,0:T(8,128)(2,1)} %get-tuple-element.457.refs_0_), channel_id=1, source_target_pairs={{0,2},{1,3},{2,0},{3,1},{4,6},{5,7},{6,4},{7,5},{8,10},{9,11},{10,... | collective-permute-start | bytes 3145736 | tf_op jit(solution)/shard_map/cond/branch_1_fun/ppermute | solution.py:515
  292.8 71.1 %all-to-all-start.2 = ((bf16[8,4,64,512]{3,2,1,0:T(8,128)(2,1)}), bf16[8,4,64,512]{3,2,1,0:T(8,128)(2,1)}, u32[]{:S(2)}, u32[]{:S(2)}) async-start(bf16[8,4,64,512]{3,2,1,0:T(8,128)(2,1)} %get-tuple-element.477.refs_10_), calls=%async_computation.2 | async-start | bytes 4194304 | tf_op jit(solution)/shard_map/cond/branch_1_fun/all_to_all | solution.py:554
  368.1 76.0 %all-to-all-start = ((bf16[8,4,64,512]{3,2,1,0:T(8,128)(2,1)}), bf16[8,4,64,512]{3,2,1,0:T(8,128)(2,1)}, u32[]{:S(2)}, u32[]{:S(2)}) async-start(bf16[8,4,64,512]{3,2,1,0:T(8,128)(2,1)} %branch_1_fun.39), calls=%async_computation | async-start | bytes 4194304 | tf_op jit(solution)/shard_map/cond/branch_1_fun/all_to_all | solution.py:554
  374.0 70.1 %collective-permute-start.6 = (bf16[2,256,1408]{2,1,0:T(8,128)(2,1)}, bf16[2,256,1408]{2,1,0:T(8,128)(2,1)}, u32[]{:S(2)}, u32[]{:S(2)}) collective-permute-start(bf16[2,256,1408]{2,1,0:T(8,128)(2,1)} %get-tuple-element.501), channel_id=1, source_target_pairs={{0,8},{4,12},{8,0},{12,4},{16,24},{20,28},{24,16},{28,20},{1,9},{5... | collective-permute-start | bytes 4325384 | tf_op jit(solution)/shard_map/cond/branch_1_fun/ppermute | solution.py:515
  381.8 40.5 %collective-permute-start.7 = (bf16[4,256,512]{2,1,0:T(8,128)(2,1)}, bf16[4,256,512]{2,1,0:T(8,128)(2,1)}, u32[]{:S(2)}, u32[]{:S(2)}) collective-permute-start(bf16[4,256,512]{2,1,0:T(8,128)(2,1)} %get-tuple-element.502), channel_id=1, source_target_pairs={{0,4},{4,0},{8,12},{12,8},{16,20},{20,16},{24,28},{28,24},{1,5},{5... | collective-permute-start | bytes 3145736 | tf_op jit(solution)/shard_map/cond/branch_1_fun/ppermute | solution.py:515
  383.2 60.9 %collective-permute-start.9 = (bf16[4,256,512]{2,1,0:T(8,128)(2,1)}, bf16[4,256,512]{2,1,0:T(8,128)(2,1)}, u32[]{:S(2)}, u32[]{:S(2)}) collective-permute-start(bf16[4,256,512]{2,1,0:T(8,128)(2,1)} %get-tuple-element.521), channel_id=1, source_target_pairs={{0,4},{4,0},{8,12},{12,8},{16,20},{20,16},{24,28},{28,24},{1,5},{5... | collective-permute-start | bytes 3145736 | tf_op jit(solution)/shard_map/cond/branch_1_fun/ppermute | solution.py:515
  451.7 61.0 %collective-permute-start.14 = (bf16[2,256,2048]{2,1,0:T(8,128)(2,1)}, bf16[2,256,2048]{2,1,0:T(8,128)(2,1)}, u32[]{:S(2)}, u32[]{:S(2)}) collective-permute-start(bf16[2,256,2048]{2,1,0:T(8,128)(2,1)} %pad_maximum_fusion), channel_id=1, source_target_pairs={{0,1},{1,0},{2,3},{3,2},{4,5},{5,4},{6,7},{7,6},{8,9},{9,8},{10,11... | collective-permute-start | bytes 6291464 | tf_op jit(solution)/shard_map/cond/branch_1_fun/ppermute | solution.py:515
  451.7 61.0 %collective-permute-start.10 = (bf16[2,256,1408]{2,1,0:T(8,128)(2,1)}, bf16[2,256,1408]{2,1,0:T(8,128)(2,1)}, u32[]{:S(2)}, u32[]{:S(2)}) collective-permute-start(bf16[2,256,1408]{2,1,0:T(8,128)(2,1)} %get-tuple-element.522), channel_id=1, source_target_pairs={{0,8},{4,12},{8,0},{12,4},{16,24},{20,28},{24,16},{28,20},{1,9},{5... | collective-permute-start | bytes 4325384 | tf_op jit(solution)/shard_map/cond/branch_1_fun/ppermute | solution.py:515
  453.1 59.7 %collective-permute-start.12 = (bf16[2,256,1408]{2,1,0:T(8,128)(2,1)}, bf16[2,256,1408]{2,1,0:T(8,128)(2,1)}, u32[]{:S(2)}, u32[]{:S(2)}) collective-permute-start(bf16[2,256,1408]{2,1,0:T(8,128)(2,1)} %get-tuple-element.524), channel_id=1, source_target_pairs={{0,4},{4,0},{8,12},{12,8},{16,20},{20,16},{24,28},{28,24},{1,5},{5... | collective-permute-start | bytes 4325384 | tf_op jit(solution)/shard_map/cond/branch_1_fun/ppermute | solution.py:515
  453.9 58.8 %collective-permute-start.11 = (bf16[1,256,1408]{2,1,0:T(8,128)(2,1)}, bf16[1,256,1408]{2,1,0:T(8,128)(2,1)}, u32[]{:S(2)}, u32[]{:S(2)}) collective-permute-start(bf16[1,256,1408]{2,1,0:T(8,128)(2,1)} %get-tuple-element.523.refs_10_.refs_11_), channel_id=1, source_target_pairs={{0,16},{4,20},{8,24},{12,28},{16,0},{20,4},{24,8},{28,12},{1,17},{... | collective-permute-start | bytes 2162696 | tf_op jit(solution)/shard_map/cond/branch_1_fun/ppermute | solution.py:515
  459.0 53.7 %collective-permute-start.13 = (bf16[2,256,512]{2,1,0:T(8,128)(2,1)S(1)}, bf16[2,256,512]{2,1,0:T(8,128)(2,1)}, u32[]{:S(2)}, u32[]{:S(2)}) collective-permute-start(bf16[2,256,512]{2,1,0:T(8,128)(2,1)S(1)} %branch_1_fun.42), channel_id=1, source_target_pairs={{0,8},{4,12},{8,0},{12,4},{16,24},{20,28},{24,16},{28,20},{1,9},{5... | collective-permute-start | bytes 1572872 | tf_op jit(solution)/shard_map/cond/branch_1_fun/ppermute | solution.py:515
  523.1 48.3 %collective-permute-start.16 = (bf16[4,256,1024]{2,1,0:T(8,128)(2,1)}, bf16[4,256,1024]{2,1,0:T(8,128)(2,1)}, u32[]{:S(2)}, u32[]{:S(2)}) collective-permute-start(bf16[4,256,1024]{2,1,0:T(8,128)(2,1)} %get-tuple-element.593), channel_id=1, source_target_pairs={{0,4},{4,0},{8,12},{12,8},{16,20},{20,16},{24,28},{28,24},{1,5},{5... | collective-permute-start | bytes 6291464 | tf_op jit(solution)/shard_map/cond/branch_1_fun/ppermute | solution.py:515
  523.6 46.1 %collective-permute-start.19 = (bf16[1,256,1408]{2,1,0:T(8,128)(2,1)}, bf16[1,256,1408]{2,1,0:T(8,128)(2,1)}, u32[]{:S(2)}, u32[]{:S(2)}) collective-permute-start(bf16[1,256,1408]{2,1,0:T(8,128)(2,1)} %get-tuple-element.596.refs_5_), channel_id=1, source_target_pairs={{0,16},{4,20},{8,24},{12,28},{16,0},{20,4},{24,8},{28,12},{1,17},{... | collective-permute-start | bytes 2162696 | tf_op jit(solution)/shard_map/cond/branch_1_fun/ppermute | solution.py:515
  525.5 45.6 %collective-permute-start.17 = (bf16[4,256,512]{2,1,0:T(8,128)(2,1)}, bf16[4,256,512]{2,1,0:T(8,128)(2,1)}, u32[]{:S(2)}, u32[]{:S(2)}) collective-permute-start(bf16[4,256,512]{2,1,0:T(8,128)(2,1)} %get-tuple-element.594), channel_id=1, source_target_pairs={{0,8},{4,12},{8,0},{12,4},{16,24},{20,28},{24,16},{28,20},{1,9},{5... | collective-permute-start | bytes 3145736 | tf_op jit(solution)/shard_map/cond/branch_1_fun/ppermute | solution.py:515
  526.7 44.5 %collective-permute-start.20 = (bf16[256,2048]{1,0:T(8,128)(2,1)}, bf16[256,2048]{1,0:T(8,128)(2,1)}, u32[]{:S(2)}, u32[]{:S(2)}) collective-permute-start(bf16[256,2048]{1,0:T(8,128)(2,1)} %get-tuple-element.615), channel_id=1, source_target_pairs={{0,2},{1,3},{2,0},{3,1},{4,6},{5,7},{6,4},{7,5},{8,10},{9,11},{10,... | collective-permute-start | bytes 3145736 | tf_op jit(solution)/shard_map/cond/branch_1_fun/ppermute | solution.py:515
  532.8 36.9 %collective-permute-start.18 = (bf16[1,256,512]{2,1,0:T(8,128)(2,1)S(1)}, bf16[1,256,512]{2,1,0:T(8,128)(2,1)}, u32[]{:S(2)}, u32[]{:S(2)}) collective-permute-start(bf16[1,256,512]{2,1,0:T(8,128)(2,1)S(1)} %get-tuple-element.595), channel_id=1, source_target_pairs={{0,16},{4,20},{8,24},{12,28},{16,0},{20,4},{24,8},{28,12},{1,17},{... | collective-permute-start | bytes 786440 | tf_op jit(solution)/shard_map/cond/branch_1_fun/ppermute | solution.py:515
  582.0 55.3 %collective-permute-start.28 = (bf16[2,256,1024]{2,1,0:T(8,128)(2,1)}, bf16[2,256,1024]{2,1,0:T(8,128)(2,1)}, u32[]{:S(2)}, u32[]{:S(2)}) collective-permute-start(bf16[2,256,1024]{2,1,0:T(8,128)(2,1)} %get-tuple-element.619), channel_id=1, source_target_pairs={{0,8},{4,12},{8,0},{12,4},{16,24},{20,28},{24,16},{28,20},{1,9},{5... | collective-permute-start | bytes 3145736 | tf_op jit(solution)/shard_map/cond/branch_1_fun/ppermute | solution.py:515
  583.5 53.8 %collective-permute-start.30 = (bf16[1,256,1408]{2,1,0:T(8,128)(2,1)}, bf16[1,256,1408]{2,1,0:T(8,128)(2,1)}, u32[]{:S(2)}, u32[]{:S(2)}) collective-permute-start(bf16[1,256,1408]{2,1,0:T(8,128)(2,1)} %get-tuple-element.621), channel_id=1, source_target_pairs={{0,16},{4,20},{8,24},{12,28},{16,0},{20,4},{24,8},{28,12},{1,17},{... | collective-permute-start | bytes 2162696 | tf_op jit(solution)/shard_map/cond/branch_1_fun/ppermute | solution.py:515
  588.9 39.8 %all-to-all-start.3 = ((bf16[8,2,6784]{2,1,0:T(2,128)(2,1)}), bf16[8,2,6784]{2,1,0:T(2,128)(2,1)S(1)}, u32[]{:S(2)}, u32[]{:S(2)}) async-start(bf16[8,2,6784]{2,1,0:T(2,128)(2,1)} %reshape.223), calls=%async_computation.3 | async-start | bytes 434176 | tf_op jit(solution)/shard_map/cond/branch_1_fun/all_to_all | solution.py:1192
  592.6 36.9 %collective-permute-start.29 = (bf16[2,256,512]{2,1,0:T(8,128)(2,1)}, bf16[2,256,512]{2,1,0:T(8,128)(2,1)}, u32[]{:S(2)}, u32[]{:S(2)}) collective-permute-start(bf16[2,256,512]{2,1,0:T(8,128)(2,1)} %get-tuple-element.620), channel_id=1, source_target_pairs={{0,4},{4,0},{8,12},{12,8},{16,20},{20,16},{24,28},{28,24},{1,5},{5... | collective-permute-start | bytes 1572872 | tf_op jit(solution)/shard_map/cond/branch_1_fun/ppermute | solution.py:515
  594.6 42.7 %collective-permute-start.31 = (bf16[2,256,512]{2,1,0:T(8,128)(2,1)}, bf16[2,256,512]{2,1,0:T(8,128)(2,1)}, u32[]{:S(2)}, u32[]{:S(2)}) collective-permute-start(bf16[2,256,512]{2,1,0:T(8,128)(2,1)} %get-tuple-element.622), channel_id=1, source_target_pairs={{0,8},{4,12},{8,0},{12,4},{16,24},{20,28},{24,16},{28,20},{1,9},{5... | collective-permute-start | bytes 1572872 | tf_op jit(solution)/shard_map/cond/branch_1_fun/ppermute | solution.py:515
  650.5 48.6 %collective-permute-start.32 = (bf16[256,2048]{1,0:T(8,128)(2,1)}, bf16[256,2048]{1,0:T(8,128)(2,1)}, u32[]{:S(2)}, u32[]{:S(2)}) collective-permute-start(bf16[256,2048]{1,0:T(8,128)(2,1)} %get-tuple-element.639), channel_id=1, source_target_pairs={{0,2},{1,3},{2,0},{3,1},{4,6},{5,7},{6,4},{7,5},{8,10},{9,11},{10,... | collective-permute-start | bytes 3145736 | tf_op jit(solution)/shard_map/cond/branch_1_fun/ppermute | solution.py:515
  651.7 47.4 %collective-permute-start.33 = (bf16[1,256,1024]{2,1,0:T(8,128)(2,1)}, bf16[1,256,1024]{2,1,0:T(8,128)(2,1)}, u32[]{:S(2)}, u32[]{:S(2)}) collective-permute-start(bf16[1,256,1024]{2,1,0:T(8,128)(2,1)} %get-tuple-element.640), channel_id=1, source_target_pairs={{0,16},{4,20},{8,24},{12,28},{16,0},{20,4},{24,8},{28,12},{1,17},{... | collective-permute-start | bytes 1572872 | tf_op jit(solution)/shard_map/cond/branch_1_fun/ppermute | solution.py:515
  653.9 45.2 %collective-permute-start.34 = (bf16[1,256,512]{2,1,0:T(8,128)(2,1)}, bf16[1,256,512]{2,1,0:T(8,128)(2,1)}, u32[]{:S(2)}, u32[]{:S(2)}) collective-permute-start(bf16[1,256,512]{2,1,0:T(8,128)(2,1)} %get-tuple-element.641), channel_id=1, source_target_pairs={{0,16},{4,20},{8,24},{12,28},{16,0},{20,4},{24,8},{28,12},{1,17},{... | collective-permute-start | bytes 786440 | tf_op jit(solution)/shard_map/cond/branch_1_fun/ppermute | solution.py:515
  654.6 44.5 %collective-permute-start.35 = (bf16[1,256,512]{2,1,0:T(8,128)(2,1)}, bf16[1,256,512]{2,1,0:T(8,128)(2,1)}, u32[]{:S(2)}, u32[]{:S(2)}) collective-permute-start(bf16[1,256,512]{2,1,0:T(8,128)(2,1)} %get-tuple-element.642), channel_id=1, source_target_pairs={{0,16},{4,20},{8,24},{12,28},{16,0},{20,4},{24,8},{28,12},{1,17},{... | collective-permute-start | bytes 786440 | tf_op jit(solution)/shard_map/cond/branch_1_fun/ppermute | solution.py:515
  658.6 40.4 %all-to-all-start.4 = ((bf16[8,2,128]{2,1,0:T(2,128)(2,1)}), bf16[8,2,128]{2,1,0:T(2,128)(2,1)S(1)}, u32[]{:S(2)}, u32[]{:S(2)}) async-start(bf16[8,2,128]{2,1,0:T(2,128)(2,1)} %reshape.225), calls=%async_computation.4 | async-start | bytes 8192 | tf_op jit(solution)/shard_map/cond/branch_1_fun/all_to_all | solution.py:1192
  (156 other events, 2142.1 us)

commit v5 on v4

--- a/solution.py
+++ b/solution.py
@@ -620,40 +620,59 @@
             return swap(part, "seq", self.order[at])
         return part if at else lax.psum_scatter(part, "seq", scatter_dimension=0, tiled=True)
 
+    def whole(self):
+        return jnp.concatenate(
+            [
+                sum(
+                    across(a[i * ROWS : (i + 1) * ROWS], b[j * ROWS : (j + 1) * ROWS])
+                    for (a, i), (b, j) in zip(cuts, group)
+                ).astype(bf16)
+                for cuts, group in zip(
+                    self.cuts if len(self.cuts) > 1 else self.cuts * len(self.groups), self.groups
+                )
+            ],
+            axis=1,
+        )
+
     def away(self, after=()):
         if not self.split:
-            return jnp.concatenate(
-                [
-                    sum(
-                        across(a[i * ROWS : (i + 1) * ROWS], b[j * ROWS : (j + 1) * ROWS])
-                        for (a, i), (b, j) in zip(cuts, group)
-                    ).astype(bf16)
-                    for cuts, group in zip(
-                        self.cuts if len(self.cuts) > 1 else self.cuts * len(self.groups), self.groups
-                    )
-                ],
-                axis=1,
-            )
+            return self.whole()
         a, b, c = self.order
         return self.part([a ^ b, a ^ b ^ c, a ^ c, a], [], bf16, after=after)
 
+    def away_halves(self, after=()):
+        if not self.split:
+            return self.whole(), jnp.zeros((8, 128), bf16)
+        a, b, c = self.order
+        front = self.part([a ^ b, a ^ b ^ c], [], bf16, after=after)
+        return front, self.part([a ^ c, a], [], bf16, after=[front])
+
+    def hop_rest(self, part):
+        return swap(part, "seq", self.order[0]) if self.split else part
+
+    def arrived(self, at):
+        came = self.came[0]
+        if not isinstance(came, tuple):
+            return came, at
+        return (came[0], at) if at < 2 else (came[1], at - 2)
+
     def one(self, after=()):
         if not self.split:
-            return self.came[0]
+            return self.arrived(0)[0]
         a, b, c = self.order
-        return self.part([b, b ^ c], [(self.came[0], 0)], bf16, after=after)
+        return self.part([b, b ^ c], [self.arrived(0)], bf16, after=after)
 
     def two(self, after=()):
         if not self.split:
-            return self.came[0]
+            return self.arrived(0)[0]
         c = self.order[2]
-        return self.part([c], [(self.came[0], 2), (self.came[1], 1)], bf16, after=after)
+        return self.part([c], [self.arrived(2), (self.came[1], 1)], bf16, after=after)
 
     def last(self, after=()):
         if not self.split:
-            total = self.came[0].astype(f32)
+            total = self.arrived(0)[0].astype(f32)
             return total.T if self.turned else total
-        arrived = [(self.came[0], 3), (self.came[1], 0), (self.came[2], 0)]
+        arrived = [self.arrived(3), (self.came[1], 0), (self.came[2], 0)]
         total = self.part([0], arrived, f32, self.turned, after=after)
         return total if self.turned else total[0]
 
@@ -974,14 +993,14 @@
     def second_sum(near, far):
         parts, _ = tensor_reduce(near, far)
         down_away = down_grad.away([swish_away])
-        return parts[1:], down_away, up_grad.away([down_away])
+        return parts[1:], down_away, up_grad.away_halves([down_away])
 
     second_parts, down_away, up_away = region(
         second_sum, halves(feed_near[3]), (feed_two[3], feed_three[3])
     )
     second_parts = (feed_near[3], *second_parts)
     down_grad.came[0] = down_grad.hop(0, down_away)
-    up_grad.came[0] = up_grad.hop(0, up_away)
+    up_grad.came[0] = (up_grad.hop(0, up_away[0]), None)
 
     middle_grad, own_rows, mlp_norm_part = grid_call(
         middle_back_kernel,
@@ -1026,7 +1045,8 @@
     gate_back_far, mixed_back_far, gain_back_far = far
     norms = blocks(norm_near, norm_far)
 
-    out_grad = Scatter(rows, [blocks(branch_near, branch_far)], bits, True)
+    far_bits = [bits[0], *bits[2:], bits[1]]
+    out_grad = Scatter(rows, [blocks(branch_near, branch_far)], far_bits, True)
     gate_grad = Scatter(norms, [blocks(gate_back_near, gate_back_far)], bits)
 
     def states_back(state_back):
@@ -1044,11 +1064,12 @@
         own = sum((part.astype(f32) for part in output_parts), middle).astype(bf16)
         return (
             deal(carried(came, lines, True)), swish_grad.hop(1, swish_one), out_grad.hop(0, out_away),
-            up_one, down_grad.one([up_one]), own, swap(own, "tensor", 2), gate_grad.hop(0, gate_away),
+            up_one, down_grad.one([up_one]), [own, swap(own, "tensor", 1), swap(own, "tensor", 2)],
+            gate_grad.hop(0, gate_away),
         )
 
     (
-        outgoing, swish_grad.came[1], out_grad.came[0], up_one, down_one, output_own, output_second,
+        outgoing, swish_grad.came[1], out_grad.came[0], up_one, down_one, output_blocks,
         gate_grad.came[0],
     ) = region(states_out, came, swish_one, out_away, gate_away, output_parts)
     swish_two = swish_grad.two([outgoing])
@@ -1111,9 +1132,8 @@
         query_key = Scatter(norms, [blocks(near[0], far[0]), blocks(near[1], far[1])], bits)
         return query_key, Scatter(norms, [blocks(near[2], far[2])], late_bits)
 
-    def mixes_back(up_one, swish_two, down_one, output_own, output_second):
+    def mixes_back(up_one, swish_two, down_one):
         gate_one = gate_grad.one([swish_two])
-        output_pair = swap(jnp.stack([output_own, output_second]), "tensor", 1)
         near = mix_back(
             queries_near, keys_near, values_near, mixed_back_near, run_near, scores_near,
             incoming_near, half, rank_near, [swish_two],
@@ -1130,21 +1150,27 @@
         return (
             up_grad.hop(1, up_one), swish_grad.hop(2, swish_two), down_grad.hop(1, down_one),
             gate_grad.hop(1, gate_one), near, far, query_key_away, value_away,
-            keep, send, out_grad.one([value_away]), output_pair,
+            keep, send, up_grad.hop_rest(up_away[1]),
         )
 
     (
         up_grad.came[1], swish_grad.came[2], down_grad.came[1], gate_grad.came[1], near, far, query_key_away,
-        value_away, first_keep, first_send, out_one, output_pair,
-    ) = region(mixes_back, up_one, swish_two, down_one, output_own, output_second)
-
-    def first_sum(keep, send):
+        value_away, first_keep, first_send, up_rest,
+    ) = region(mixes_back, up_one, swish_two, down_one)
+    up_grad.came[0] = (up_grad.came[0][0], up_rest)
+
+    def first_sum(keep, send, output_second):
         came = swap(send, "tensor", 1)
+        output_third = swap(output_second, "tensor", 1)
         gate_two = gate_grad.two([send])
         down_two = down_grad.two([gate_two])
-        return came, (keep[1].astype(f32) + came[1].astype(f32)).astype(bf16), gate_two, down_two
-
-    first_came, first_second, gate_two, down_two = region(first_sum, first_keep, first_send)
+        second = (keep[1].astype(f32) + came[1].astype(f32)).astype(bf16)
+        return came, second, gate_two, down_two, output_third
+
+    first_came, first_second, gate_two, down_two, output_third = region(
+        first_sum, first_keep, first_send, output_blocks[2]
+    )
+    output_blocks.append(output_third)
     rank_part_near, up_part_near, bias_part_near = near[3:]
     rank_part_far, up_part_far, bias_part_far = far[3:]
     query_key_grad, value_grad = mixed_pair(near, far)
@@ -1156,51 +1182,15 @@
             query_key_grad.hop(0, query_key_away), value_grad.hop(0, value_away),
             gate_grad.hop(2, gate_two), down_grad.hop(2, down_two), up_grad.two(),
             swish_grad.last(), jnp.sum(rank_part, axis=0).astype(bf16), swap(first_second, "tensor", 2),
-            in_order([output_own, output_pair[0], output_second, output_pair[1]], [down_two]),
+            out_grad.one([down_two]), in_order(output_blocks, [down_two]),
         )
 
     (
         query_key_grad.came[0], value_grad.came[0], gate_grad.came[2], down_grad.came[2], up_two,
-        swish_share, rank_back, first_last, layer_output,
+        swish_share, rank_back, first_last, out_one, layer_output,
     ) = region(third_window, query_key_away, value_away, gate_two, down_two, first_second)
     query_key_one = query_key_grad.one()
     value_one = value_grad.one([query_key_one])
-
-    rank_down_part = contract(rank_back, norm_near[:length], 1, 0)
-    own_part = jnp.concatenate([rank_down_part, mlp_norm_part], axis=0)
-    shared = jnp.concatenate(
-        [
-            sum(up_part_near) + sum(up_part_far),
-            sum(bias_part_near) + sum(bias_part_far),
-            sum(gain_back_near) + sum(gain_back_far),
-        ],
-        axis=0,
-    )
-    column = width // devices
-    own_part = jnp.moveaxis(own_part.reshape(rank + 1, devices, column), 1, 0)
-    own_size = (rank + 1) * column
-    mail = jnp.concatenate(
-        [
-            own_part.reshape(devices, own_size),
-            jnp.broadcast_to(shared.reshape(1, -1), (devices, shared.size)),
-        ],
-        axis=1,
-    )
-
-    def summed(mail):
-        mail = mail.reshape(devices, 1, -1).astype(bf16)
-        return jnp.sum(lax.all_to_all(mail, "seq", 0, 0).astype(f32), axis=0)
-
-    def fourth_window(query_key_one, value_one, up_two, out_one, mail):
-        return (
-            query_key_grad.hop(1, query_key_one), value_grad.hop(1, value_one), up_grad.hop(2, up_two),
-            out_grad.hop(1, out_one), gate_grad.last(), down_grad.last(), summed(mail),
-        )
-
-    (
-        query_key_grad.came[1], value_grad.came[1], up_grad.came[2], out_grad.came[1], gate_share, down_share,
-        mail,
-    ) = region(fourth_window, query_key_one, value_one, up_two, out_one, mail)
 
     input_rows, attn_norm_part = grid_call(
         input_back_kernel,
@@ -1219,37 +1209,66 @@
             attn_norm.reshape(1, width),
         ],
         prefetch=1,
-        after=[gate_share],
-    )
-    out_two = out_grad.two([input_rows])
+        after=[value_one],
+    )
+    rank_down_part = contract(rank_back, norm_near[:length], 1, 0)
+    own_part = jnp.concatenate([rank_down_part, mlp_norm_part, attn_norm_part], axis=0)
+    shared = jnp.concatenate(
+        [
+            sum(up_part_near) + sum(up_part_far),
+            sum(bias_part_near) + sum(bias_part_far),
+            sum(gain_back_near) + sum(gain_back_far),
+        ],
+        axis=0,
+    )
+    column = width // devices
+    own_part = jnp.moveaxis(own_part.reshape(rank + 2, devices, column), 1, 0)
+    own_size = (rank + 2) * column
+    mail = jnp.concatenate(
+        [
+            own_part.reshape(devices, own_size),
+            jnp.broadcast_to(shared.reshape(1, -1), (devices, shared.size)),
+        ],
+        axis=1,
+    )
+
+    def summed(mail):
+        mail = mail.reshape(devices, 1, -1).astype(bf16)
+        return jnp.sum(lax.all_to_all(mail, "seq", 0, 0).astype(f32), axis=0)
+
+    def fourth_window(query_key_one, value_one, up_two, out_one, input_rows, mail):
+        return (
+            swap(input_rows, "tensor", 2),
+            query_key_grad.hop(1, query_key_one), value_grad.hop(1, value_one), up_grad.hop(2, up_two),
+            out_grad.hop(1, out_one), gate_grad.last(), down_grad.last(), summed(mail),
+        )
+
+    (
+        second_rows, query_key_grad.came[1], value_grad.came[1], up_grad.came[2], out_grad.came[1],
+        gate_share, down_share,
+        mail,
+    ) = region(fourth_window, query_key_one, value_one, up_two, out_one, input_rows, mail)
+
+    out_two = out_grad.two([mail])
     query_key_two = query_key_grad.two([out_two])
     value_two = value_grad.two([query_key_two])
 
-    def fifth_window(input_rows, query_key_two, value_two, out_two, attn_norm_part):
+    def fifth_window(query_key_two, value_two, out_two, input_rows, second_rows):
+        first_rows, third_rows = swap(input_rows, "tensor", 1), swap(second_rows, "tensor", 1)
         return (
-            swap(input_rows, "tensor", 2), query_key_grad.hop(2, query_key_two),
-            value_grad.hop(2, value_two), out_grad.hop(2, out_two),
-            summed(attn_norm_part), up_grad.last(),
-        )
-
-    (
-        second_rows, query_key_grad.came[2], value_grad.came[2], out_grad.came[2],
-        attn_norm_part, up_share,
-    ) = region(fifth_window, input_rows, query_key_two, value_two, out_two, attn_norm_part)
-
-    def sixth_window(input_rows, second_rows, mail, attn_norm_part):
-        first_rows = swap(input_rows, "tensor", 1)
-        third_rows = swap(second_rows, "tensor", 1)
-        parts = jnp.concatenate([mail.reshape(-1)[:own_size], attn_norm_part.reshape(-1)])
-        return (
-            in_order([input_rows, first_rows, second_rows, third_rows]), query_key_grad.last(),
-            value_grad.last(), out_grad.last(),
-            sum_over(parts.reshape(rank + 2, column), "tensor"),
-        )
-
-    input_grad, query_key_share, value_share, out_share, own_part = region(
-        sixth_window, input_rows, second_rows, mail, attn_norm_part
-    )
+            query_key_grad.hop(2, query_key_two), value_grad.hop(2, value_two), out_grad.hop(2, out_two),
+            in_order([input_rows, first_rows, second_rows, third_rows]), up_grad.last(),
+        )
+
+    query_key_grad.came[2], value_grad.came[2], out_grad.came[2], input_grad, up_share = region(
+        fifth_window, query_key_two, value_two, out_two, input_rows, second_rows
+    )
+
+    def sixth_window(mail):
+        parts = mail.reshape(-1)[:own_size].reshape(rank + 2, column)
+        return query_key_grad.last(), value_grad.last(), out_grad.last(), sum_over(parts, "tensor")
+
+    query_key_share, value_share, out_share, own_part = region(sixth_window, mail)
     shared = mail.reshape(-1)[own_size:].reshape(rank + 2, DK)
     return (
         layer_output,

time: 731 us -> 700 us (0.958)
  waiting for transfers between devices: 260 us -> 235 us
    all_to_all x2 -> x1, waiting for transfers between devices: 58.2 us -> 27.5 us  [summed(): return jnp.sum(lax.all_to_all(mail, 'seq', 0, 0).astype(f32), axis=0)]
    ppermute x61 -> x63, waiting for transfers between devices: 162 us -> 190 us  [swap(): return lax.ppermute(values, axis, [(i, i ^ distance) for i in range(count)])]
    all_to_all x2, waiting for transfers between devices: 36 us -> 17.8 us  [deal(): return lax.all_to_all(pieces, 'seq', 0, 0)]
    ppermute x61 -> x63, starting transfers between devices: 83.3 us -> 86.9 us  [swap(): return lax.ppermute(values, axis, [(i, i ^ distance) for i in range(count)])]
    pallas_call x63 -> x64, Pallas kernels: 271 us -> 273 us  [grid_call(): pl.pallas_call(run, grid_spec=pltpu.PrefetchScalarGridSpec(num_scalar_pre...]
  transfers between devices with their start and end apart: 66 -> 67, of which waited for: 25 -> 25; matrix products, arithmetic and copies ran while one was open for 6% -> 6% of each run, Pallas kernels for 28% -> 30%
where the time goes in v5:
time: 700 us; the launch traced here: 690 us
  Pallas kernels  273 us (39%)
  waiting for transfers between devices  235 us (34%)
  starting transfers between devices  103 us (15%)
  matrix products  32.8 us (5%)
  local copies, waits for them, and re-layouts  28.2 us (4%)
  other arithmetic  14.7 us (2%)
    pallas_call x64, Pallas kernels, grid_call(): pl.pallas_call(run, grid_spec=pltpu.PrefetchScalarGridSpec(num_scalar_pre...  273 us
    ppermute x63, waiting for transfers between devices, swap(): return lax.ppermute(values, axis, [(i, i ^ distance) for i in range(count)])  190 us
    ppermute x63, starting transfers between devices, swap(): return lax.ppermute(values, axis, [(i, i ^ distance) for i in range(count)])  86.9 us
    dot_general x13, matrix products, contract(): lax.dot_general(left, right, (((left_dim,), (right_dim,)), ((), ())), pre...  32.8 us
    all_to_all x1, waiting for transfers between devices, summed(): return jnp.sum(lax.all_to_all(mail, 'seq', 0, 0).astype(f32), axis=0)  27.5 us
    all_to_all x2, waiting for transfers between devices, deal(): return lax.all_to_all(pieces, 'seq', 0, 0)  17.8 us
  transfers between devices with their start and end apart: 67, of which 25 were waited for; matrix products, arithmetic and copies ran while one was open for 6% of the time, Pallas kernels for 30%

profile of v5, /device:TPU:0, one launch (start us, length us, event | category | flops | bytes accessed | tf_op | source)
XLA Modules:
  0.0 689.8 jit_solution(17573979155276632977)
XLA Ops:
  62.6 9.6 %collective-permute-start.49 = (bf16[2,64,512]{2,1,0:T(8,128)(2,1)S(1)}, bf16[2,64,512]{2,1,0:T(8,128)(2,1)S(1)}, u32[]{:S(2)}, u32[]{:S(2)}) collective-permute-start(bf16[2,64,512]{2,1,0:T(8,128)(2,1)S(1)} %get-tuple-element.864), channel_id=1, source_target_pairs={{0,8},{4,12},{8,0},{12,4},{16,24},{20,28},{24,16},{28,20},{1,9},{5... | collective-permute-start | bytes 393224 | tf_op jit(solution)/shard_map/ppermute | solution.py:515
  79.2 7.8 %collective-permute-done.50.refs_6_ = bf16[2,64,512]{2,1,0:T(8,128)(2,1)S(1)} collective-permute-done((bf16[2,64,512]{2,1,0:T(8,128)(2,1)S(1)}, bf16[2,64,512]{2,1,0:T(8,128)(2,1)S(1)}, u32[]{:S(2)}, u32[]{:S(2)}) %collective-permute-start.50) | collective-permute-done | bytes 131104 | tf_op jit(solution)/shard_map/ppermute | solution.py:515
  91.9 9.3 %collective-permute-done.53.refs_1_ = bf16[2,4,64,512]{3,2,1,0:T(8,128)(2,1)S(1)} collective-permute-done((bf16[2,4,64,512]{3,2,1,0:T(8,128)(2,1)S(1)}, bf16[2,4,64,512]{3,2,1,0:T(8,128)(2,1)S(1)}, u32[]{:S(2)}, u32[]{:S(2)}) %collective-permute-start.53) | collective-permute-done | bytes 524320 | tf_op jit(solution)/shard_map/ppermute | solution.py:515
  127.4 7.5 %collective-permute-done.52.refs_1_ = bf16[2,4,64,512]{3,2,1,0:T(8,128)(2,1)S(1)} collective-permute-done((bf16[2,4,64,512]{3,2,1,0:T(8,128)(2,1)S(1)}, bf16[2,4,64,512]{3,2,1,0:T(8,128)(2,1)S(1)}, u32[]{:S(2)}, u32[]{:S(2)}) %collective-permute-start.52) | collective-permute-done | bytes 524320 | tf_op jit(solution)/shard_map/ppermute | solution.py:515
  151.2 23.2 %shard_map.298 = (bf16[512,1408]{1,0:T(8,128)(2,1)}, bf16[512,1408]{1,0:T(8,128)(2,1)}, bf16[512,1408]{1,0:T(8,128)(2,1)}, bf16[512,2048]{1,0:T(8,128)(2,1)}, bf16[512,2048]{1,0:T(8,128)(2,1)S(1)}) custom-call(bf16[256,2048]{1,0:T(8,128)(2,1)S(1)} %get-tuple-element.873.refs_0_.refs_1_, bf16[256,2048]{1,0:T(8,128)(2,1)S(1)} %collective-permute-done.56.refs_1_.refs_2_, ...), custom_call_target="tpu_custom_call" | custom-call | flops 1024 | bytes 1024 | tf_op jit(solution)/shard_map/pallas_call | solution.py:497
  178.5 13.3 %shard_map.299 = (bf16[256,1408]{1,0:T(8,128)(2,1)}, bf16[256,1408]{1,0:T(8,128)(2,1)S(1)}, bf16[256,1408]{1,0:T(8,128)(2,1)}, bf16[256,2048]{1,0:T(8,128)(2,1)}, bf16[256,2048]{1,0:T(8,128)(2,1)S(1)}) custom-call(bf16[256,2048]{1,0:T(8,128)(2,1)S(1)} %collective-permute-done.57.refs_0_.refs_1_.refs_3_, ...), custom_call_target="tpu_custom_call" | custom-call | flops 1024 | bytes 1024 | tf_op jit(solution)/shard_map/pallas_call | solution.py:497
  191.9 15.6 %shard_map.301 = (bf16[256,1408]{1,0:T(8,128)(2,1)}, bf16[256,1408]{1,0:T(8,128)(2,1)S(1)}, bf16[256,1408]{1,0:T(8,128)(2,1)}, bf16[256,2048]{1,0:T(8,128)(2,1)}, bf16[256,2048]{1,0:T(8,128)(2,1)}) custom-call(bf16[256,2048]{1,0:T(8,128)(2,1)} %collective-permute-done.58.refs_0_.refs_1_.refs_4_, ...), custom_call_target="tpu_custom_call" | custom-call | flops 1024 | bytes 1024 | tf_op jit(solution)/shard_map/pallas_call | solution.py:497
  216.1 29.8 %conditional.12 = (bf16[256,2048]{1,0:T(8,128)(2,1)}, bf16[256,2048]{1,0:T(8,128)(2,1)}, bf16[4,256,1408]{2,1,0:T(8,128)(2,1)}, bf16[2,256,1408]{2,1,0:T(8,128)(2,1)}, bf16[2,256,1408]{2,1,0:T(8,128)(2,1)}) conditional(s32[]{:T(128)} %convert_element_type.111, () %tuple.102, (bf16[512,2048]{1,0:T(8,128)(2,1)S(1)}, bf16[256,2048]{1,0:T(8,128)(2,1)S(1)}, ...), branch_computations={%region_2.0_spmd, %region_3.0_spmd} | conditional | flops 2100249 | bytes 54529576 | solution.py:524
  222.0 7.8 %branch_1_fun.32.refs_9_ = bf16[4,256,1408]{2,1,0:T(8,128)(2,1)} custom-call(s32[4]{0:T(128)S(1)} %pad_add_fusion.refs_0_, bf16[512,2048]{1,0:T(8,128)(2,1)S(1)} %copy-done.7, bf16[512,2048]{1,0:T(8,128)(2,1)S(1)} %copy-done.7, bf16[512,2048]{1,0:T(8,128)(2,1)} %get-tuple-element.443.refs_3_.refs_4_, bf16[512,2048]{1,0:T(8,128)(2,1)} %get-tuple-element.443.refs_3_.refs_4_, ...), custom_call_target="tpu_custom_call" | custom-call | flops 1024 | bytes 1024 | tf_op jit(solution)/shard_map/cond/branch_1_fun/pallas_call | solution.py:497
  257.8 34.9 %conditional.13 = (bf16[256,2048]{1,0:T(8,128)(2,1)}, bf16[256,2048]{1,0:T(8,128)(2,1)}, bf16[512,512]{1,0:T(8,128)(2,1)}, bf16[512,512]{1,0:T(8,128)(2,1)}, f32...) conditional(s32[]{:T(128)} %convert_element_type.111, ...), branch_computations={%region_4.0_spmd, %region_5.0_spmd} | conditional | flops 3072 | bytes 31460644 | solution.py:524
  266.0 17.3 %collective-permute-done.1.refs_0_ = bf16[256,2048]{1,0:T(8,128)(2,1)} collective-permute-done((bf16[256,2048]{1,0:T(8,128)(2,1)}, bf16[256,2048]{1,0:T(8,128)(2,1)}, u32[]{:S(2)}, u32[]{:S(2)}) %collective-permute-start.1) | collective-permute-done | bytes 1048608 | tf_op jit(solution)/shard_map/cond/branch_1_fun/ppermute | solution.py:515
  292.7 52.8 %conditional.14 = (bf16[8,4,64,512]{3,2,1,0:T(8,128)(2,1)}, bf16[2,256,1408]{2,1,0:T(8,128)(2,1)}, bf16[4,256,512]{2,1,0:T(8,128)(2,1)}, bf16[4,256,512]{2,1,0:T...) conditional(s32[]{:T(128)} %convert_element_type.111, () %tuple.99, ...), branch_computations={%region_6.0_spmd, %region_7.0_spmd} | conditional | flops 2100259 | bytes 34606540 | solution.py:524
  320.1 7.5 %collective-permute-done.30 = bf16[256,2048]{1,0:T(8,128)(2,1)} collective-permute-done((bf16[256,2048]{1,0:T(8,128)(2,1)}, bf16[256,2048]{1,0:T(8,128)(2,1)}, u32[]{:S(2)}, u32[]{:S(2)}) %collective-permute-start.30) | collective-permute-done | bytes 1048608 | tf_op jit(solution)/shard_map/cond/branch_1_fun/ppermute | solution.py:515
  327.7 17.8 %all-to-all-done.2 = bf16[8,4,64,512]{3,2,1,0:T(8,128)(2,1)} async-done(((bf16[8,4,64,512]{3,2,1,0:T(8,128)(2,1)}), bf16[8,4,64,512]{3,2,1,0:T(8,128)(2,1)}, u32[]{:S(2)}, u32[]{:S(2)}) %all-to-all-start.2) | async-done | bytes 2097184 | tf_op jit(solution)/shard_map/cond/branch_1_fun/all_to_all | solution.py:554
  345.4 77.9 %conditional.15 = (bf16[8,4,64,512]{3,2,1,0:T(8,128)(2,1)}, bf16[2,256,1408]{2,1,0:T(8,128)(2,1)}, bf16[4,256,512]{2,1,0:T(8,128)(2,1)}, bf16[2,256,1408]{2,1,0:...) conditional(s32[]{:T(128)} %convert_element_type.111, () %tuple.98, ...), branch_computations={%region_8.0_spmd, %region_9.0_spmd} | conditional | flops 3673099 | bytes 35130784 | solution.py:524
  375.7 10.5 %collective-permute-done.14 = bf16[256,2048]{1,0:T(8,128)(2,1)} collective-permute-done((bf16[256,2048]{1,0:T(8,128)(2,1)}, bf16[256,2048]{1,0:T(8,128)(2,1)}, u32[]{:S(2)}, u32[]{:S(2)}) %collective-permute-start.14) | collective-permute-done | bytes 1048608 | tf_op jit(solution)/shard_map/cond/branch_1_fun/ppermute | solution.py:515
  386.2 14.9 %collective-permute-done.12 = bf16[4,256,512]{2,1,0:T(8,128)(2,1)} collective-permute-done((bf16[4,256,512]{2,1,0:T(8,128)(2,1)}, bf16[4,256,512]{2,1,0:T(8,128)(2,1)}, u32[]{:S(2)}, u32[]{:S(2)}) %collective-permute-start.12) | collective-permute-done | bytes 1048608 | tf_op jit(solution)/shard_map/cond/branch_1_fun/ppermute | solution.py:515
  401.1 22.3 %collective-permute-done.15 = bf16[4,256,512]{2,1,0:T(8,128)(2,1)} collective-permute-done((bf16[4,256,512]{2,1,0:T(8,128)(2,1)}, bf16[4,256,512]{2,1,0:T(8,128)(2,1)}, u32[]{:S(2)}, u32[]{:S(2)}) %collective-permute-start.15) | collective-permute-done | bytes 1048608 | tf_op jit(solution)/shard_map/cond/branch_1_fun/ppermute | solution.py:515
  427.7 64.8 %conditional.16 = (bf16[2,256,1408]{2,1,0:T(8,128)(2,1)}, bf16[1,256,1408]{2,1,0:T(8,128)(2,1)}, bf16[2,256,1408]{2,1,0:T(8,128)(2,1)}, bf16[2,256,512]{2,1,0:T(...) conditional(s32[]{:T(128)} %convert_element_type.111, () %tuple.97, ...), branch_computations={%region_10.0_spmd, %region_11.0_spmd} | conditional | flops 7199 | bytes 86630488 | solution.py:524
  438.8 7.3 %branch_1_fun.45 = (bf16[512,512]{1,0:T(8,128)(2,1)}, bf16[512,512]{1,0:T(8,128)(2,1)}, bf16[512,512]{1,0:T(8,128)(2,1)}, f32[2,16,256]{2,1,0:T(8,128)S(1)}, f32...) custom-call(bf16[512,512]{1,0:T(8,128)(2,1)S(1)} %copy-done.75, bf16[512,512]{1,0:T(8,128)(2,1)S(1)} %copy-done.86, ...), custom_call_target="tpu_custom_call" | custom-call | flops 1024 | bytes 1024 | tf_op jit(solution)/shard_map/cond/branch_1_fun/pallas_call | solution.py:497
  446.2 7.6 %branch_1_fun.46 = (bf16[512,512]{1,0:T(8,128)(2,1)}, bf16[512,512]{1,0:T(8,128)(2,1)}, bf16[512,512]{1,0:T(8,128)(2,1)}, f32[2,16,256]{2,1,0:T(8,128)}, f32[2,16,512]{2,1,0:T(8,128)}, /*index=5*/f32[2,1,512]{2,1,0:T(1,128)}) custom-call(bf16[512,512]{1,0:T(8,128)(2,1)} %get-tuple-element.545.refs_0_, bf16[512,512]{1,0:T(8,128)(2,1)} %get-tuple-element.546.refs_1_, ...), custom_call_target="tpu_custom_call" | custom-call | flops 1024 | bytes 1024 | tf_op jit(solution)/shard_map/cond/branch_1_fun/pallas_call | solution.py:497
  453.8 7.3 %branch_1_fun.47 = (bf16[2,256,2048]{2,1,0:T(8,128)(2,1)}, bf16[2,256,2048]{2,1,0:T(8,128)(2,1)}) custom-call(bf16[512,512]{1,0:T(8,128)(2,1)} %get-tuple-element.1090.refs_0_.refs_7_.refs_8_, bf16[512,512]{1,0:T(8,128)(2,1)} %get-tuple-element.1091.refs_1_.refs_11_.refs_12_, bf16[512,512]{1,0:T(8,128)(2,1)} %get-tuple-element.1092.refs_2_.refs_7_.refs_8_, ...), custom_call_target="tpu_custom_call" | custom-call | flops 1024 | bytes 1024 | tf_op jit(solution)/shard_map/cond/branch_1_fun/pallas_call | solution.py:497
  461.1 7.4 %branch_1_fun.48 = (bf16[2,256,2048]{2,1,0:T(8,128)(2,1)}, bf16[2,256,2048]{2,1,0:T(8,128)(2,1)}) custom-call(bf16[512,512]{1,0:T(8,128)(2,1)} %get-tuple-element.1084.refs_0_.refs_5_.refs_6_, bf16[512,512]{1,0:T(8,128)(2,1)} %get-tuple-element.1085.refs_1_.refs_9_.refs_10_, ...), custom_call_target="tpu_custom_call", output_to_operand_aliasing={{0}: (8, {}), {1}: (9, {})} | custom-call | flops 1024 | bytes 1024 | tf_op jit(solution)/shard_map/cond/branch_1_fun/pallas_call | solution.py:497
  493.9 10.0 %conditional.17 = (bf16[2,256,2048]{2,1,0:T(8,128)(2,1)}, bf16[256,2048]{1,0:T(8,128)(2,1)}, bf16[1,256,512]{2,1,0:T(8,128)(2,1)S(1)}, bf16[1,256,1408]{2,1,0:T(8,128)(2,1)}, bf16[256,2048]{1,0:T(8,128)(2,1)}) conditional(s32[]{:T(128)} %convert_element_type.111, () %tuple.108, (bf16[2,256,2048]{2,1,0:T(8,128)(2,1)}, ...), branch_computations={%region_12.0_spmd, %region_13.0_spmd} | conditional | flops 2099204 | bytes 37751116 | solution.py:524
  503.9 48.0 %conditional.18 = (bf16[4,256,1024]{2,1,0:T(8,128)(2,1)}, bf16[4,256,512]{2,1,0:T(8,128)(2,1)}, bf16[1,256,512]{2,1,0:T(8,128)(2,1)}, bf16[1,256,1408]{2,1,0:T(8...) conditional(s32[]{:T(128)} %convert_element_type.111, () %tuple.96, ...), branch_computations={%region_14.0_spmd, %region_15.17_spmd} | conditional | flops 50219 | bytes 59130612 | solution.py:524
  532.6 17.1 %collective-permute-done.25 = bf16[1,256,512]{2,1,0:T(8,128)(2,1)} collective-permute-done((bf16[1,256,512]{2,1,0:T(8,128)(2,1)S(1)}, bf16[1,256,512]{2,1,0:T(8,128)(2,1)}, u32[]{:S(2)}, u32[]{:S(2)}) %collective-permute-start.25) | collective-permute-done | bytes 262176 | tf_op jit(solution)/shard_map/cond/branch_1_fun/ppermute | solution.py:515
  566.4 64.2 %conditional.19 = (bf16[256,2048]{1,0:T(8,128)(2,1)}, bf16[2,256,1024]{2,1,0:T(8,128)(2,1)}, bf16[2,256,512]{2,1,0:T(8,128)(2,1)}, bf16[1,256,1408]{2,1,0:T(8,12...) conditional(s32[]{:T(128)} %convert_element_type.111, ...), branch_computations={%region_17.18_spmd, %region_18.20_spmd} | conditional | flops 209411 | bytes 37769664 | solution.py:524
  590.3 27.5 %all-to-all-done.3 = bf16[8,2,6912]{2,1,0:T(2,128)(2,1)} async-done(((bf16[8,2,6912]{2,1,0:T(2,128)(2,1)}), bf16[8,2,6912]{2,1,0:T(2,128)(2,1)}, u32[]{:S(2)}, u32[]{:S(2)}) %all-to-all-start.3) | async-done | bytes 221216 | tf_op jit(solution)/shard_map/cond/branch_1_fun/all_to_all | solution.py:1237
  620.0 10.6 %collective-permute-done.37 = bf16[2,256,512]{2,1,0:T(8,128)(2,1)} collective-permute-done((bf16[2,256,512]{2,1,0:T(8,128)(2,1)}, bf16[2,256,512]{2,1,0:T(8,128)(2,1)}, u32[]{:S(2)}, u32[]{:S(2)}) %collective-permute-start.37) | collective-permute-done | bytes 524320 | tf_op jit(solution)/shard_map/cond/branch_1_fun/ppermute | solution.py:515
  639.8 38.2 %conditional.20 = (bf16[1,256,1024]{2,1,0:T(8,128)(2,1)}, bf16[1,256,512]{2,1,0:T(8,128)(2,1)}, bf16[1,256,512]{2,1,0:T(8,128)(2,1)}, bf16[4,256,2048]{2,1,0:T(8,128)(2,1)}, f32[256,1408]{1,0:T(8,128)}) conditional(s32[]{:T(128)} %convert_element_type.111, () %tuple.111, (bf16[1,256,1024]{2,1,0:T(8,128)(2,1)}, bf16[1,256,512]{2,1,0:T(8,128)(2,1)}, ...), branch_computations={%region_20.21_spmd, %region_21.22_spmd} | conditional | flops 2051 | bytes 12585232 | solution.py:524
  653.3 24.7 %collective-permute-done.4 = bf16[1,256,512]{2,1,0:T(8,128)(2,1)} collective-permute-done((bf16[1,256,512]{2,1,0:T(8,128)(2,1)}, bf16[1,256,512]{2,1,0:T(8,128)(2,1)}, u32[]{:S(2)}, u32[]{:S(2)}) %collective-permute-start.4) | collective-permute-done | bytes 262176 | tf_op jit(solution)/shard_map/cond/branch_1_fun/ppermute | solution.py:515
  678.0 8.8 %conditional.21 = (f32[256,1024]{1,0:T(8,128)}, f32[256,512]{1,0:T(8,128)S(1)}, f32[512,256]{1,0:T(8,128)S(1)}, f32[18,256]{1,0:T(8,128)S(1)}, f32[256,512]{1,0:T(8,128)S(1)}, /*index=5*/f32[256,512]{1,0:T(8,128)S(1)}) conditional(s32[]{:T(128)} %convert_element_type.111, () %tuple.115, (bf16[512,2048]{1,0:T(8,128)(2,1)}, ...), branch_computations={%region_22.23_spmd, %region_23.24_spmd} | conditional | flops 12291 | bytes 10820852 | solution.py:524
  (504 shorter events, 396.0 us)
Async XLA Ops:
  111.4 30.8 %collective-permute-start.55 = (bf16[256,2048]{1,0:T(8,128)(2,1)S(1)}, bf16[256,2048]{1,0:T(8,128)(2,1)S(1)}, u32[]{:S(2)}, u32[]{:S(2)}) collective-permute-start(bf16[256,2048]{1,0:T(8,128)(2,1)S(1)} %add_convert_fusion.4.refs_7_), channel_id=1, source_target_pairs={{0,2},{1,3},{2,0},{3,1},{4,6},{5,7},{6,4},{7,5},{8,10},{9,11},{10,... | collective-permute-start | bytes 3145736 | tf_op jit(solution)/shard_map/ppermute | solution.py:515
  145.6 28.7 %collective-permute-start.57 = (bf16[256,2048]{1,0:T(8,128)(2,1)S(1)}, bf16[256,2048]{1,0:T(8,128)(2,1)S(1)}, u32[]{:S(2)}, u32[]{:S(2)}) collective-permute-start(bf16[256,2048]{1,0:T(8,128)(2,1)S(1)} %get-tuple-element.873.refs_0_.refs_1_), channel_id=1, source_target_pairs={{0,2},{1,3},{2,0},{3,1},{4,6},{5,7},{6,4},{7,5},{8,10},{9,11},{10,... | collective-permute-start | bytes 3145736 | tf_op jit(solution)/shard_map/ppermute | solution.py:515
  214.8 77.9 %collective-permute-start.60 = (bf16[4,256,1408]{2,1,0:T(8,128)(2,1)}, bf16[4,256,1408]{2,1,0:T(8,128)(2,1)}, u32[]{:S(2)}, u32[]{:S(2)}) collective-permute-start(bf16[4,256,1408]{2,1,0:T(8,128)(2,1)} %shard_map.302), channel_id=1, source_target_pairs={{0,4},{4,0},{8,12},{12,8},{16,20},{20,16},{24,28},{28,24},{1,5},{5... | collective-permute-start | bytes 8650760 | tf_op jit(solution)/shard_map/ppermute | solution.py:515
  220.4 25.5 %collective-permute-start.10 = (bf16[256,2048]{1,0:T(8,128)(2,1)}, bf16[256,2048]{1,0:T(8,128)(2,1)}, u32[]{:S(2)}, u32[]{:S(2)}) collective-permute-start(bf16[256,2048]{1,0:T(8,128)(2,1)} %add_convert_fusion), channel_id=1, source_target_pairs={{0,2},{1,3},{2,0},{3,1},{4,6},{5,7},{6,4},{7,5},{8,10},{9,11},{10,... | collective-permute-start | bytes 3145736 | tf_op jit(solution)/shard_map/cond/branch_1_fun/ppermute | solution.py:515
  245.9 99.5 %collective-permute-start.62 = (bf16[4,256,1408]{2,1,0:T(8,128)(2,1)}, bf16[4,256,1408]{2,1,0:T(8,128)(2,1)}, u32[]{:S(2)}, u32[]{:S(2)}) collective-permute-start(bf16[4,256,1408]{2,1,0:T(8,128)(2,1)} %get-tuple-element.906), channel_id=1, source_target_pairs={{0,8},{4,12},{8,0},{12,4},{16,24},{20,28},{24,16},{28,20},{1,9},{5... | collective-permute-start | bytes 8650760 | tf_op jit(solution)/shard_map/ppermute | solution.py:515
  249.3 96.2 %collective-permute-start.61 = (bf16[2,256,1408]{2,1,0:T(8,128)(2,1)}, bf16[2,256,1408]{2,1,0:T(8,128)(2,1)}, u32[]{:S(2)}, u32[]{:S(2)}) collective-permute-start(bf16[2,256,1408]{2,1,0:T(8,128)(2,1)} %get-tuple-element.905), channel_id=1, source_target_pairs={{0,4},{4,0},{8,12},{12,8},{16,20},{20,16},{24,28},{28,24},{1,5},{5... | collective-permute-start | bytes 4325384 | tf_op jit(solution)/shard_map/ppermute | solution.py:515
  257.8 25.5 %collective-permute-start.1 = (bf16[256,2048]{1,0:T(8,128)(2,1)}, bf16[256,2048]{1,0:T(8,128)(2,1)}, u32[]{:S(2)}, u32[]{:S(2)}) collective-permute-start(bf16[256,2048]{1,0:T(8,128)(2,1)} %get-tuple-element.455.refs_0_), channel_id=1, source_target_pairs={{0,2},{1,3},{2,0},{3,1},{4,6},{5,7},{6,4},{7,5},{8,10},{9,11},{10,... | collective-permute-start | bytes 3145736 | tf_op jit(solution)/shard_map/cond/branch_1_fun/ppermute | solution.py:515
  292.7 52.8 %all-to-all-start.2 = ((bf16[8,4,64,512]{3,2,1,0:T(8,128)(2,1)}), bf16[8,4,64,512]{3,2,1,0:T(8,128)(2,1)}, u32[]{:S(2)}, u32[]{:S(2)}) async-start(bf16[8,4,64,512]{3,2,1,0:T(8,128)(2,1)} %get-tuple-element.475.refs_10_), calls=%async_computation.2 | async-start | bytes 4194304 | tf_op jit(solution)/shard_map/cond/branch_1_fun/all_to_all | solution.py:554
  349.6 73.8 %all-to-all-start = ((bf16[8,4,64,512]{3,2,1,0:T(8,128)(2,1)}), bf16[8,4,64,512]{3,2,1,0:T(8,128)(2,1)}, u32[]{:S(2)}, u32[]{:S(2)}) async-start(bf16[8,4,64,512]{3,2,1,0:T(8,128)(2,1)} %branch_1_fun.41), calls=%async_computation | async-start | bytes 4194304 | tf_op jit(solution)/shard_map/cond/branch_1_fun/all_to_all | solution.py:554
  354.1 69.2 %collective-permute-start.11 = (bf16[2,256,1408]{2,1,0:T(8,128)(2,1)}, bf16[2,256,1408]{2,1,0:T(8,128)(2,1)}, u32[]{:S(2)}, u32[]{:S(2)}) collective-permute-start(bf16[2,256,1408]{2,1,0:T(8,128)(2,1)} %get-tuple-element.499), channel_id=1, source_target_pairs={{0,8},{4,12},{8,0},{12,4},{16,24},{20,28},{24,16},{28,20},{1,9},{5... | collective-permute-start | bytes 4325384 | tf_op jit(solution)/shard_map/cond/branch_1_fun/ppermute | solution.py:515
  360.3 25.9 %collective-permute-start.14 = (bf16[256,2048]{1,0:T(8,128)(2,1)}, bf16[256,2048]{1,0:T(8,128)(2,1)}, u32[]{:S(2)}, u32[]{:S(2)}) collective-permute-start(bf16[256,2048]{1,0:T(8,128)(2,1)} %add_convert_fusion.2), channel_id=1, source_target_pairs={{0,2},{1,3},{2,0},{3,1},{4,6},{5,7},{6,4},{7,5},{8,10},{9,11},{10,... | collective-permute-start | bytes 3145736 | tf_op jit(solution)/shard_map/cond/branch_1_fun/ppermute | solution.py:515
  361.8 39.3 %collective-permute-start.12 = (bf16[4,256,512]{2,1,0:T(8,128)(2,1)}, bf16[4,256,512]{2,1,0:T(8,128)(2,1)}, u32[]{:S(2)}, u32[]{:S(2)}) collective-permute-start(bf16[4,256,512]{2,1,0:T(8,128)(2,1)} %get-tuple-element.500), channel_id=1, source_target_pairs={{0,4},{4,0},{8,12},{12,8},{16,20},{20,16},{24,28},{28,24},{1,5},{5... | collective-permute-start | bytes 3145736 | tf_op jit(solution)/shard_map/cond/branch_1_fun/ppermute | solution.py:515
  363.2 60.1 %collective-permute-start.15 = (bf16[4,256,512]{2,1,0:T(8,128)(2,1)}, bf16[4,256,512]{2,1,0:T(8,128)(2,1)}, u32[]{:S(2)}, u32[]{:S(2)}) collective-permute-start(bf16[4,256,512]{2,1,0:T(8,128)(2,1)} %get-tuple-element.519), channel_id=1, source_target_pairs={{0,4},{4,0},{8,12},{12,8},{16,20},{20,16},{24,28},{28,24},{1,5},{5... | collective-permute-start | bytes 3145736 | tf_op jit(solution)/shard_map/cond/branch_1_fun/ppermute | solution.py:515
  427.7 60.5 %collective-permute-start.16 = (bf16[2,256,1408]{2,1,0:T(8,128)(2,1)}, bf16[2,256,1408]{2,1,0:T(8,128)(2,1)}, u32[]{:S(2)}, u32[]{:S(2)}) collective-permute-start(bf16[2,256,1408]{2,1,0:T(8,128)(2,1)} %get-tuple-element.520), channel_id=1, source_target_pairs={{0,8},{4,12},{8,0},{12,4},{16,24},{20,28},{24,16},{28,20},{1,9},{5... | collective-permute-start | bytes 4325384 | tf_op jit(solution)/shard_map/cond/branch_1_fun/ppermute | solution.py:515
  428.9 59.3 %collective-permute-start.18 = (bf16[2,256,1408]{2,1,0:T(8,128)(2,1)}, bf16[2,256,1408]{2,1,0:T(8,128)(2,1)}, u32[]{:S(2)}, u32[]{:S(2)}) collective-permute-start(bf16[2,256,1408]{2,1,0:T(8,128)(2,1)} %get-tuple-element.522), channel_id=1, source_target_pairs={{0,4},{4,0},{8,12},{12,8},{16,20},{20,16},{24,28},{28,24},{1,5},{5... | collective-permute-start | bytes 4325384 | tf_op jit(solution)/shard_map/cond/branch_1_fun/ppermute | solution.py:515
  429.5 63.0 %collective-permute-start.20 = (bf16[2,256,1408]{2,1,0:T(8,128)(2,1)}, bf16[2,256,1408]{2,1,0:T(8,128)(2,1)}, u32[]{:S(2)}, u32[]{:S(2)}) collective-permute-start(bf16[2,256,1408]{2,1,0:T(8,128)(2,1)} %get-tuple-element.567), channel_id=1, source_target_pairs={{0,4},{4,0},{8,12},{12,8},{16,20},{20,16},{24,28},{28,24},{1,5},{5... | collective-permute-start | bytes 4325384 | tf_op jit(solution)/shard_map/cond/branch_1_fun/ppermute | solution.py:515
  430.9 57.3 %collective-permute-start.17 = (bf16[1,256,1408]{2,1,0:T(8,128)(2,1)}, bf16[1,256,1408]{2,1,0:T(8,128)(2,1)}, u32[]{:S(2)}, u32[]{:S(2)}) collective-permute-start(bf16[1,256,1408]{2,1,0:T(8,128)(2,1)} %get-tuple-element.521.refs_10_.refs_11_), channel_id=1, source_target_pairs={{0,16},{4,20},{8,24},{12,28},{16,0},{20,4},{24,8},{28,12},{1,17},{... | collective-permute-start | bytes 2162696 | tf_op jit(solution)/shard_map/cond/branch_1_fun/ppermute | solution.py:515
  438.5 49.6 %collective-permute-start.19 = (bf16[2,256,512]{2,1,0:T(8,128)(2,1)S(1)}, bf16[2,256,512]{2,1,0:T(8,128)(2,1)}, u32[]{:S(2)}, u32[]{:S(2)}) collective-permute-start(bf16[2,256,512]{2,1,0:T(8,128)(2,1)S(1)} %branch_1_fun.44), channel_id=1, source_target_pairs={{0,8},{4,12},{8,0},{12,4},{16,24},{20,28},{24,16},{28,20},{1,9},{5... | collective-permute-start | bytes 1572872 | tf_op jit(solution)/shard_map/cond/branch_1_fun/ppermute | solution.py:515
  503.9 48.0 %collective-permute-start.23 = (bf16[4,256,1024]{2,1,0:T(8,128)(2,1)}, bf16[4,256,1024]{2,1,0:T(8,128)(2,1)}, u32[]{:S(2)}, u32[]{:S(2)}) collective-permute-start(bf16[4,256,1024]{2,1,0:T(8,128)(2,1)} %get-tuple-element.584), channel_id=1, source_target_pairs={{0,4},{4,0},{8,12},{12,8},{16,20},{20,16},{24,28},{28,24},{1,5},{5... | collective-permute-start | bytes 6291464 | tf_op jit(solution)/shard_map/cond/branch_1_fun/ppermute | solution.py:515
  504.5 46.2 %collective-permute-start.24 = (bf16[4,256,512]{2,1,0:T(8,128)(2,1)}, bf16[4,256,512]{2,1,0:T(8,128)(2,1)}, u32[]{:S(2)}, u32[]{:S(2)}) collective-permute-start(bf16[4,256,512]{2,1,0:T(8,128)(2,1)} %get-tuple-element.585), channel_id=1, source_target_pairs={{0,8},{4,12},{8,0},{12,4},{16,24},{20,28},{24,16},{28,20},{1,9},{5... | collective-permute-start | bytes 3145736 | tf_op jit(solution)/shard_map/cond/branch_1_fun/ppermute | solution.py:515
  505.9 44.8 %collective-permute-start.27 = (bf16[256,2048]{1,0:T(8,128)(2,1)}, bf16[256,2048]{1,0:T(8,128)(2,1)}, u32[]{:S(2)}, u32[]{:S(2)}) collective-permute-start(bf16[256,2048]{1,0:T(8,128)(2,1)} %get-tuple-element.606), channel_id=1, source_target_pairs={{0,2},{1,3},{2,0},{3,1},{4,6},{5,7},{6,4},{7,5},{8,10},{9,11},{10,... | collective-permute-start | bytes 3145736 | tf_op jit(solution)/shard_map/cond/branch_1_fun/ppermute | solution.py:515
  507.2 42.5 %collective-permute-start.26 = (bf16[1,256,1408]{2,1,0:T(8,128)(2,1)}, bf16[1,256,1408]{2,1,0:T(8,128)(2,1)}, u32[]{:S(2)}, u32[]{:S(2)}) collective-permute-start(bf16[1,256,1408]{2,1,0:T(8,128)(2,1)} %get-tuple-element.587.refs_10_.refs_5_), channel_id=1, source_target_pairs={{0,16},{4,20},{8,24},{12,28},{16,0},{20,4},{24,8},{28,12},{1,17},{... | collective-permute-start | bytes 2162696 | tf_op jit(solution)/shard_map/cond/branch_1_fun/ppermute | solution.py:515
  509.7 40.0 %collective-permute-start.25 = (bf16[1,256,512]{2,1,0:T(8,128)(2,1)S(1)}, bf16[1,256,512]{2,1,0:T(8,128)(2,1)}, u32[]{:S(2)}, u32[]{:S(2)}) collective-permute-start(bf16[1,256,512]{2,1,0:T(8,128)(2,1)S(1)} %get-tuple-element.586), channel_id=1, source_target_pairs={{0,16},{4,20},{8,24},{12,28},{16,0},{20,4},{24,8},{28,12},{1,17},{... | collective-permute-start | bytes 786440 | tf_op jit(solution)/shard_map/cond/branch_1_fun/ppermute | solution.py:515
  566.4 64.2 %collective-permute-start.33 = (bf16[256,2048]{1,0:T(8,128)(2,1)}, bf16[256,2048]{1,0:T(8,128)(2,1)}, u32[]{:S(2)}, u32[]{:S(2)}) collective-permute-start(bf16[256,2048]{1,0:T(8,128)(2,1)} %get-tuple-element.618), channel_id=1, source_target_pairs={{0,2},{1,3},{2,0},{3,1},{4,6},{5,7},{6,4},{7,5},{8,10},{9,11},{10,... | collective-permute-start | bytes 3145736 | tf_op jit(solution)/shard_map/cond/branch_1_fun/ppermute | solution.py:515
  567.7 62.9 %collective-permute-start.34 = (bf16[2,256,1024]{2,1,0:T(8,128)(2,1)}, bf16[2,256,1024]{2,1,0:T(8,128)(2,1)}, u32[]{:S(2)}, u32[]{:S(2)}) collective-permute-start(bf16[2,256,1024]{2,1,0:T(8,128)(2,1)} %get-tuple-element.619), channel_id=1, source_target_pairs={{0,8},{4,12},{8,0},{12,4},{16,24},{20,28},{24,16},{28,20},{1,9},{5... | collective-permute-start | bytes 3145736 | tf_op jit(solution)/shard_map/cond/branch_1_fun/ppermute | solution.py:515
  570.2 60.4 %collective-permute-start.36 = (bf16[1,256,1408]{2,1,0:T(8,128)(2,1)}, bf16[1,256,1408]{2,1,0:T(8,128)(2,1)}, u32[]{:S(2)}, u32[]{:S(2)}) collective-permute-start(bf16[1,256,1408]{2,1,0:T(8,128)(2,1)} %get-tuple-element.621), channel_id=1, source_target_pairs={{0,16},{4,20},{8,24},{12,28},{16,0},{20,4},{24,8},{28,12},{1,17},{... | collective-permute-start | bytes 2162696 | tf_op jit(solution)/shard_map/cond/branch_1_fun/ppermute | solution.py:515
  574.4 43.4 %all-to-all-start.3 = ((bf16[8,2,6912]{2,1,0:T(2,128)(2,1)}), bf16[8,2,6912]{2,1,0:T(2,128)(2,1)}, u32[]{:S(2)}, u32[]{:S(2)}) async-start(bf16[8,2,6912]{2,1,0:T(2,128)(2,1)} %reshape.206), calls=%async_computation.3 | async-start | bytes 442368 | tf_op jit(solution)/shard_map/cond/branch_1_fun/all_to_all | solution.py:1237
  578.7 41.3 %collective-permute-start.35 = (bf16[2,256,512]{2,1,0:T(8,128)(2,1)}, bf16[2,256,512]{2,1,0:T(8,128)(2,1)}, u32[]{:S(2)}, u32[]{:S(2)}) collective-permute-start(bf16[2,256,512]{2,1,0:T(8,128)(2,1)} %get-tuple-element.620), channel_id=1, source_target_pairs={{0,4},{4,0},{8,12},{12,8},{16,20},{20,16},{24,28},{28,24},{1,5},{5... | collective-permute-start | bytes 1572872 | tf_op jit(solution)/shard_map/cond/branch_1_fun/ppermute | solution.py:515
  580.7 49.9 %collective-permute-start.37 = (bf16[2,256,512]{2,1,0:T(8,128)(2,1)}, bf16[2,256,512]{2,1,0:T(8,128)(2,1)}, u32[]{:S(2)}, u32[]{:S(2)}) collective-permute-start(bf16[2,256,512]{2,1,0:T(8,128)(2,1)} %get-tuple-element.622), channel_id=1, source_target_pairs={{0,16},{4,20},{8,24},{12,28},{16,0},{20,4},{24,8},{28,12},{1,17},{... | collective-permute-start | bytes 1572872 | tf_op jit(solution)/shard_map/cond/branch_1_fun/ppermute | solution.py:515
  640.4 37.6 %collective-permute-start.3 = (bf16[1,256,1024]{2,1,0:T(8,128)(2,1)}, bf16[1,256,1024]{2,1,0:T(8,128)(2,1)}, u32[]{:S(2)}, u32[]{:S(2)}) collective-permute-start(bf16[1,256,1024]{2,1,0:T(8,128)(2,1)} %get-tuple-element.639), channel_id=1, source_target_pairs={{0,16},{4,20},{8,24},{12,28},{16,0},{20,4},{24,8},{28,12},{1,17},{... | collective-permute-start | bytes 1572872 | tf_op jit(solution)/shard_map/cond/branch_1_fun/ppermute | solution.py:515
  640.4 37.6 %collective-permute-start.4 = (bf16[1,256,512]{2,1,0:T(8,128)(2,1)}, bf16[1,256,512]{2,1,0:T(8,128)(2,1)}, u32[]{:S(2)}, u32[]{:S(2)}) collective-permute-start(bf16[1,256,512]{2,1,0:T(8,128)(2,1)} %get-tuple-element.640), channel_id=1, source_target_pairs={{0,16},{4,20},{8,24},{12,28},{16,0},{20,4},{24,8},{28,12},{1,17},{... | collective-permute-start | bytes 786440 | tf_op jit(solution)/shard_map/cond/branch_1_fun/ppermute | solution.py:515
  643.3 34.7 %collective-permute-start.5 = (bf16[1,256,512]{2,1,0:T(8,128)(2,1)S(1)}, bf16[1,256,512]{2,1,0:T(8,128)(2,1)}, u32[]{:S(2)}, u32[]{:S(2)}) collective-permute-start(bf16[1,256,512]{2,1,0:T(8,128)(2,1)S(1)} %get-tuple-element.641), channel_id=1, source_target_pairs={{0,8},{4,12},{8,0},{12,4},{16,24},{20,28},{24,16},{28,20},{1,9},{5... | collective-permute-start | bytes 786440 | tf_op jit(solution)/shard_map/cond/branch_1_fun/ppermute | solution.py:515
  (161 other events, 2117.6 us)

commit v6 on v5

--- a/solution.py
+++ b/solution.py
@@ -1072,7 +1072,6 @@
         outgoing, swish_grad.came[1], out_grad.came[0], up_one, down_one, output_blocks,
         gate_grad.came[0],
     ) = region(states_out, came, swish_one, out_away, gate_away, output_parts)
-    swish_two = swish_grad.two([outgoing])
 
     def mix_back(queries, keys, values, mixed_back, run, scores, incoming, at, rank_rows, after):
         return grid_call(
@@ -1132,7 +1131,8 @@
         query_key = Scatter(norms, [blocks(near[0], far[0]), blocks(near[1], far[1])], bits)
         return query_key, Scatter(norms, [blocks(near[2], far[2])], late_bits)
 
-    def mixes_back(up_one, swish_two, down_one):
+    def mixes_back(up_one, outgoing, down_one):
+        swish_two = swish_grad.two([outgoing])
         gate_one = gate_grad.one([swish_two])
         near = mix_back(
             queries_near, keys_near, values_near, mixed_back_near, run_near, scores_near,
@@ -1156,7 +1156,7 @@
     (
         up_grad.came[1], swish_grad.came[2], down_grad.came[1], gate_grad.came[1], near, far, query_key_away,
         value_away, first_keep, first_send, up_rest,
-    ) = region(mixes_back, up_one, swish_two, down_one)
+    ) = region(mixes_back, up_one, outgoing, down_one)
     up_grad.came[0] = (up_grad.came[0][0], up_rest)
 
     def first_sum(keep, send, output_second):
@@ -1236,32 +1236,31 @@
         mail = mail.reshape(devices, 1, -1).astype(bf16)
         return jnp.sum(lax.all_to_all(mail, "seq", 0, 0).astype(f32), axis=0)
 
-    def fourth_window(query_key_one, value_one, up_two, out_one, input_rows, mail):
+    def fourth_window(query_key_one, value_one, up_two, out_one, input_rows):
         return (
             swap(input_rows, "tensor", 2),
             query_key_grad.hop(1, query_key_one), value_grad.hop(1, value_one), up_grad.hop(2, up_two),
-            out_grad.hop(1, out_one), gate_grad.last(), down_grad.last(), summed(mail),
+            out_grad.hop(1, out_one), gate_grad.last(), down_grad.last(),
         )
 
     (
         second_rows, query_key_grad.came[1], value_grad.came[1], up_grad.came[2], out_grad.came[1],
         gate_share, down_share,
-        mail,
-    ) = region(fourth_window, query_key_one, value_one, up_two, out_one, input_rows, mail)
-
-    out_two = out_grad.two([mail])
-    query_key_two = query_key_grad.two([out_two])
-    value_two = value_grad.two([query_key_two])
-
-    def fifth_window(query_key_two, value_two, out_two, input_rows, second_rows):
+    ) = region(fourth_window, query_key_one, value_one, up_two, out_one, input_rows)
+
+
+    def fifth_window(input_rows, second_rows, mail):
+        query_key_two = query_key_grad.two([second_rows])
+        value_two = value_grad.two([query_key_two])
+        out_two = out_grad.two([value_two])
         first_rows, third_rows = swap(input_rows, "tensor", 1), swap(second_rows, "tensor", 1)
         return (
             query_key_grad.hop(2, query_key_two), value_grad.hop(2, value_two), out_grad.hop(2, out_two),
-            in_order([input_rows, first_rows, second_rows, third_rows]), up_grad.last(),
-        )
-
-    query_key_grad.came[2], value_grad.came[2], out_grad.came[2], input_grad, up_share = region(
-        fifth_window, query_key_two, value_two, out_two, input_rows, second_rows
+            in_order([input_rows, first_rows, second_rows, third_rows]), up_grad.last(), summed(mail),
+        )
+
+    query_key_grad.came[2], value_grad.came[2], out_grad.came[2], input_grad, up_share, mail = region(
+        fifth_window, input_rows, second_rows, mail
     )
 
     def sixth_window(mail):

time: 700 us -> 696 us (level)
    ppermute x63, waiting for transfers between devices: 190 us -> 215 us  [swap(): return lax.ppermute(values, axis, [(i, i ^ distance) for i in range(count)])]
    all_to_all x1, waiting for transfers between devices: 27.5 us -> 3.48 us  [summed(): return jnp.sum(lax.all_to_all(mail, 'seq', 0, 0).astype(f32), axis=0)]
  transfers between devices with their start and end apart: 67 -> 67, of which waited for: 25 -> 28; matrix products, arithmetic and copies ran while one was open for 6% -> 6% of each run, Pallas kernels for 30% -> 32%
where the time goes in v6:
time: 696 us; the launch traced here: 686 us
  Pallas kernels  273 us (39%)
  waiting for transfers between devices  237 us (34%)
  starting transfers between devices  100 us (14%)
  matrix products  28.6 us (4%)
  local copies, waits for them, and re-layouts  26.8 us (4%)
  other arithmetic  18.1 us (3%)
    pallas_call x64, Pallas kernels, grid_call(): pl.pallas_call(run, grid_spec=pltpu.PrefetchScalarGridSpec(num_scalar_pre...  273 us
    ppermute x63, waiting for transfers between devices, swap(): return lax.ppermute(values, axis, [(i, i ^ distance) for i in range(count)])  215 us
    ppermute x63, starting transfers between devices, swap(): return lax.ppermute(values, axis, [(i, i ^ distance) for i in range(count)])  82.9 us
    dot_general x13, matrix products, contract(): lax.dot_general(left, right, (((left_dim,), (right_dim,)), ((), ())), pre...  28.6 us
    all_to_all x2, waiting for transfers between devices, deal(): return lax.all_to_all(pieces, 'seq', 0, 0)  17.7 us
  transfers between devices with their start and end apart: 67, of which 28 were waited for; matrix products, arithmetic and copies ran while one was open for 6% of the time, Pallas kernels for 32%

profile of v6, /device:TPU:0, one launch (start us, length us, event | category | flops | bytes accessed | tf_op | source)
XLA Modules:
  0.0 685.8 jit_solution(12590786455259433434)
XLA Ops:
  58.2 11.2 %collective-permute-start.49 = (bf16[2,64,512]{2,1,0:T(8,128)(2,1)S(1)}, bf16[2,64,512]{2,1,0:T(8,128)(2,1)S(1)}, u32[]{:S(2)}, u32[]{:S(2)}) collective-permute-start(bf16[2,64,512]{2,1,0:T(8,128)(2,1)S(1)} %get-tuple-element.939), channel_id=1, source_target_pairs={{0,8},{4,12},{8,0},{12,4},{16,24},{20,28},{24,16},{28,20},{1,9},{5... | collective-permute-start | bytes 393224 | tf_op jit(solution)/shard_map/ppermute | solution.py:515
  73.3 10.5 %collective-permute-done.50.refs_6_ = bf16[2,64,512]{2,1,0:T(8,128)(2,1)S(1)} collective-permute-done((bf16[2,64,512]{2,1,0:T(8,128)(2,1)S(1)}, bf16[2,64,512]{2,1,0:T(8,128)(2,1)S(1)}, u32[]{:S(2)}, u32[]{:S(2)}) %collective-permute-start.50) | collective-permute-done | bytes 131104 | tf_op jit(solution)/shard_map/ppermute | solution.py:515
  123.6 8.3 %collective-permute-done.52.refs_1_ = bf16[2,4,64,512]{3,2,1,0:T(8,128)(2,1)S(1)} collective-permute-done((bf16[2,4,64,512]{3,2,1,0:T(8,128)(2,1)S(1)}, bf16[2,4,64,512]{3,2,1,0:T(8,128)(2,1)S(1)}, u32[]{:S(2)}, u32[]{:S(2)}) %collective-permute-start.52) | collective-permute-done | bytes 524320 | tf_op jit(solution)/shard_map/ppermute | solution.py:515
  148.1 22.9 %shard_map.298 = (bf16[512,1408]{1,0:T(8,128)(2,1)}, bf16[512,1408]{1,0:T(8,128)(2,1)}, bf16[512,1408]{1,0:T(8,128)(2,1)}, bf16[512,2048]{1,0:T(8,128)(2,1)}, bf16[512,2048]{1,0:T(8,128)(2,1)S(1)}) custom-call(bf16[256,2048]{1,0:T(8,128)(2,1)S(1)} %get-tuple-element.948.refs_0_.refs_1_, bf16[256,2048]{1,0:T(8,128)(2,1)S(1)} %collective-permute-done.56.refs_1_.refs_2_, ...), custom_call_target="tpu_custom_call" | custom-call | flops 1024 | bytes 1024 | tf_op jit(solution)/shard_map/pallas_call | solution.py:497
  175.3 13.6 %shard_map.299 = (bf16[256,1408]{1,0:T(8,128)(2,1)}, bf16[256,1408]{1,0:T(8,128)(2,1)S(1)}, bf16[256,1408]{1,0:T(8,128)(2,1)}, bf16[256,2048]{1,0:T(8,128)(2,1)}, bf16[256,2048]{1,0:T(8,128)(2,1)S(1)}) custom-call(bf16[256,2048]{1,0:T(8,128)(2,1)S(1)} %collective-permute-done.57.refs_0_.refs_1_.refs_3_, ...), custom_call_target="tpu_custom_call" | custom-call | flops 1024 | bytes 1024 | tf_op jit(solution)/shard_map/pallas_call | solution.py:497
  189.0 15.6 %shard_map.301 = (bf16[256,1408]{1,0:T(8,128)(2,1)}, bf16[256,1408]{1,0:T(8,128)(2,1)S(1)}, bf16[256,1408]{1,0:T(8,128)(2,1)}, bf16[256,2048]{1,0:T(8,128)(2,1)}, bf16[256,2048]{1,0:T(8,128)(2,1)}) custom-call(bf16[256,2048]{1,0:T(8,128)(2,1)} %collective-permute-done.58.refs_0_.refs_1_.refs_4_, ...), custom_call_target="tpu_custom_call" | custom-call | flops 1024 | bytes 1024 | tf_op jit(solution)/shard_map/pallas_call | solution.py:497
  204.6 7.2 %shard_map.302 = bf16[4,256,1408]{2,1,0:T(8,128)(2,1)} custom-call(s32[4]{0:T(128)S(1)} %pad_add_fusion.11.refs_0_, bf16[256,2048]{1,0:T(8,128)(2,1)S(1)} %copy-done.22, bf16[256,2048]{1,0:T(8,128)(2,1)S(1)} %copy-done.28, bf16[256,2048]{1,0:T(8,128)(2,1)S(1)} %collective-permute-done.57.refs_0_.refs_1_.refs_3_, ...), custom_call_target="tpu_custom_call" | custom-call | flops 1024 | bytes 1024 | tf_op jit(solution)/shard_map/pallas_call | solution.py:497
  213.4 29.8 %conditional.12 = (bf16[256,2048]{1,0:T(8,128)(2,1)}, bf16[256,2048]{1,0:T(8,128)(2,1)}, bf16[4,256,1408]{2,1,0:T(8,128)(2,1)}, bf16[2,256,1408]{2,1,0:T(8,128)(2,1)}, bf16[2,256,1408]{2,1,0:T(8,128)(2,1)}) conditional(s32[]{:T(128)} %convert_element_type.111, () %tuple.102, (bf16[512,2048]{1,0:T(8,128)(2,1)S(1)}, bf16[256,2048]{1,0:T(8,128)(2,1)S(1)}, ...), branch_computations={%region_2.0_spmd, %region_3.0_spmd} | conditional | flops 2100249 | bytes 54529576 | solution.py:524
  219.3 7.8 %branch_1_fun.36.refs_9_ = bf16[4,256,1408]{2,1,0:T(8,128)(2,1)} custom-call(s32[4]{0:T(128)S(1)} %pad_add_fusion.refs_0_, bf16[512,2048]{1,0:T(8,128)(2,1)S(1)} %copy-done.12, bf16[512,2048]{1,0:T(8,128)(2,1)S(1)} %copy-done.12, bf16[512,2048]{1,0:T(8,128)(2,1)} %get-tuple-element.493.refs_3_.refs_4_, bf16[512,2048]{1,0:T(8,128)(2,1)} %get-tuple-element.493.refs_3_.refs_4_, ...), custom_call_target="tpu_custom_call" | custom-call | flops 1024 | bytes 1024 | tf_op jit(solution)/shard_map/cond/branch_1_fun/pallas_call | solution.py:497
  255.1 34.9 %conditional.13 = (bf16[256,2048]{1,0:T(8,128)(2,1)}, bf16[256,2048]{1,0:T(8,128)(2,1)}, bf16[512,512]{1,0:T(8,128)(2,1)}, bf16[512,512]{1,0:T(8,128)(2,1)}, f32...) conditional(s32[]{:T(128)} %convert_element_type.111, ...), branch_computations={%region_4.0_spmd, %region_5.0_spmd} | conditional | flops 3072 | bytes 31460644 | solution.py:524
  262.8 17.8 %collective-permute-done.1.refs_0_ = bf16[256,2048]{1,0:T(8,128)(2,1)} collective-permute-done((bf16[256,2048]{1,0:T(8,128)(2,1)}, bf16[256,2048]{1,0:T(8,128)(2,1)}, u32[]{:S(2)}, u32[]{:S(2)}) %collective-permute-start.1) | collective-permute-done | bytes 1048608 | tf_op jit(solution)/shard_map/cond/branch_1_fun/ppermute | solution.py:515
  290.0 52.8 %conditional.14 = (bf16[8,4,64,512]{3,2,1,0:T(8,128)(2,1)}, bf16[2,256,1408]{2,1,0:T(8,128)(2,1)}, bf16[4,256,512]{2,1,0:T(8,128)(2,1)}, bf16[4,256,512]{2,1,0:T...) conditional(s32[]{:T(128)} %convert_element_type.111, () %tuple.99, ...), branch_computations={%region_6.0_spmd, %region_7.0_spmd} | conditional | flops 2100259 | bytes 34606540 | solution.py:524
  317.7 7.4 %collective-permute-done.30 = bf16[256,2048]{1,0:T(8,128)(2,1)} collective-permute-done((bf16[256,2048]{1,0:T(8,128)(2,1)}, bf16[256,2048]{1,0:T(8,128)(2,1)}, u32[]{:S(2)}, u32[]{:S(2)}) %collective-permute-start.30) | collective-permute-done | bytes 1048608 | tf_op jit(solution)/shard_map/cond/branch_1_fun/ppermute | solution.py:515
  325.0 17.7 %all-to-all-done.2 = bf16[8,4,64,512]{3,2,1,0:T(8,128)(2,1)} async-done(((bf16[8,4,64,512]{3,2,1,0:T(8,128)(2,1)}), bf16[8,4,64,512]{3,2,1,0:T(8,128)(2,1)}, u32[]{:S(2)}, u32[]{:S(2)}) %all-to-all-start.2) | async-done | bytes 2097184 | tf_op jit(solution)/shard_map/cond/branch_1_fun/all_to_all | solution.py:554
  342.8 78.4 %conditional.15 = (bf16[8,4,64,512]{3,2,1,0:T(8,128)(2,1)}, bf16[2,256,1408]{2,1,0:T(8,128)(2,1)}, bf16[4,256,512]{2,1,0:T(8,128)(2,1)}, bf16[2,256,1408]{2,1,0:...) conditional(s32[]{:T(128)} %convert_element_type.111, () %tuple.98, ...), branch_computations={%region_8.0_spmd, %region_9.0_spmd} | conditional | flops 3673099 | bytes 35130784 | solution.py:524
  374.1 10.4 %collective-permute-done.14 = bf16[256,2048]{1,0:T(8,128)(2,1)} collective-permute-done((bf16[256,2048]{1,0:T(8,128)(2,1)}, bf16[256,2048]{1,0:T(8,128)(2,1)}, u32[]{:S(2)}, u32[]{:S(2)}) %collective-permute-start.14) | collective-permute-done | bytes 1048608 | tf_op jit(solution)/shard_map/cond/branch_1_fun/ppermute | solution.py:515
  384.5 14.4 %collective-permute-done.12 = bf16[4,256,512]{2,1,0:T(8,128)(2,1)} collective-permute-done((bf16[4,256,512]{2,1,0:T(8,128)(2,1)}, bf16[4,256,512]{2,1,0:T(8,128)(2,1)}, u32[]{:S(2)}, u32[]{:S(2)}) %collective-permute-start.12) | collective-permute-done | bytes 1048608 | tf_op jit(solution)/shard_map/cond/branch_1_fun/ppermute | solution.py:515
  398.9 22.3 %collective-permute-done.15 = bf16[4,256,512]{2,1,0:T(8,128)(2,1)} collective-permute-done((bf16[4,256,512]{2,1,0:T(8,128)(2,1)}, bf16[4,256,512]{2,1,0:T(8,128)(2,1)}, u32[]{:S(2)}, u32[]{:S(2)}) %collective-permute-start.15) | collective-permute-done | bytes 1048608 | tf_op jit(solution)/shard_map/cond/branch_1_fun/ppermute | solution.py:515
  421.2 64.9 %conditional.16 = (bf16[2,256,1408]{2,1,0:T(8,128)(2,1)}, bf16[1,256,1408]{2,1,0:T(8,128)(2,1)}, bf16[2,256,1408]{2,1,0:T(8,128)(2,1)}, bf16[2,256,512]{2,1,0:T(...) conditional(s32[]{:T(128)} %convert_element_type.111, () %tuple.97, ...), branch_computations={%region_10.0_spmd, %region_11.0_spmd} | conditional | flops 8224 | bytes 97887368 | solution.py:524
  436.0 7.6 %branch_1_fun.50 = (bf16[512,512]{1,0:T(8,128)(2,1)}, bf16[512,512]{1,0:T(8,128)(2,1)}, bf16[512,512]{1,0:T(8,128)(2,1)}, f32[2,16,256]{2,1,0:T(8,128)S(1)}, f32...) custom-call(bf16[512,512]{1,0:T(8,128)(2,1)S(1)} %copy-done.84, bf16[512,512]{1,0:T(8,128)(2,1)S(1)} %copy-done.95, ...), custom_call_target="tpu_custom_call" | custom-call | flops 1024 | bytes 1024 | tf_op jit(solution)/shard_map/cond/branch_1_fun/pallas_call | solution.py:497
  443.7 7.8 %branch_1_fun.51 = (bf16[512,512]{1,0:T(8,128)(2,1)}, bf16[512,512]{1,0:T(8,128)(2,1)}, bf16[512,512]{1,0:T(8,128)(2,1)}, f32[2,16,256]{2,1,0:T(8,128)}, f32[2,1...) custom-call(bf16[512,512]{1,0:T(8,128)(2,1)S(1)} %copy-done.89, bf16[512,512]{1,0:T(8,128)(2,1)} %get-tuple-element.604.refs_1_, ...), custom_call_target="tpu_custom_call" | custom-call | flops 1024 | bytes 1024 | tf_op jit(solution)/shard_map/cond/branch_1_fun/pallas_call | solution.py:497
  451.6 7.6 %branch_1_fun.52 = (bf16[2,256,2048]{2,1,0:T(8,128)(2,1)}, bf16[2,256,2048]{2,1,0:T(8,128)(2,1)}) custom-call(bf16[512,512]{1,0:T(8,128)(2,1)} %get-tuple-element.1165.refs_0_.refs_7_.refs_8_, bf16[512,512]{1,0:T(8,128)(2,1)} %get-tuple-element.1166.refs_1_.refs_11_.refs_12_, bf16[512,512]{1,0:T(8,128)(2,1)} %get-tuple-element.1167.refs_2_.refs_7_.refs_8_, ...), custom_call_target="tpu_custom_call" | custom-call | flops 1024 | bytes 1024 | tf_op jit(solution)/shard_map/cond/branch_1_fun/pallas_call | solution.py:497
  459.2 7.5 %branch_1_fun.53 = (bf16[2,256,2048]{2,1,0:T(8,128)(2,1)}, bf16[2,256,2048]{2,1,0:T(8,128)(2,1)}) custom-call(bf16[512,512]{1,0:T(8,128)(2,1)} %get-tuple-element.1159.refs_0_.refs_5_.refs_6_, bf16[512,512]{1,0:T(8,128)(2,1)} %get-tuple-element.1160.refs_1_.refs_9_.refs_10_, ...), custom_call_target="tpu_custom_call", output_to_operand_aliasing={{0}: (8, {}), {1}: (9, {})} | custom-call | flops 1024 | bytes 1024 | tf_op jit(solution)/shard_map/cond/branch_1_fun/pallas_call | solution.py:497
  466.7 6.8 branch_1_fun.54.refs_9_
  487.7 10.0 %conditional.17 = (bf16[2,256,2048]{2,1,0:T(8,128)(2,1)}, bf16[256,2048]{1,0:T(8,128)(2,1)}, bf16[1,256,512]{2,1,0:T(8,128)(2,1)}, bf16[1,256,1408]{2,1,0:T(8,128)(2,1)}, bf16[256,2048]{1,0:T(8,128)(2,1)}) conditional(s32[]{:T(128)} %convert_element_type.111, () %tuple.108, (bf16[2,256,2048]{2,1,0:T(8,128)(2,1)}, bf16[2,256,2048]{2,1,0:T(8,128)(2,1)}, ...), branch_computations={%region_12.0_spmd, %region_13.0_spmd} | conditional | flops 2099204 | bytes 35653908 | solution.py:524
  497.7 48.1 %conditional.18 = (bf16[4,256,1024]{2,1,0:T(8,128)(2,1)}, bf16[4,256,512]{2,1,0:T(8,128)(2,1)}, bf16[1,256,512]{2,1,0:T(8,128)(2,1)}, bf16[1,256,1408]{2,1,0:T(8...) conditional(s32[]{:T(128)} %convert_element_type.111, () %tuple.96, ...), branch_computations={%region_14.0_spmd, %region_15.17_spmd} | conditional | flops 50219 | bytes 59130612 | solution.py:524
  525.8 17.9 %collective-permute-done.25 = bf16[1,256,512]{2,1,0:T(8,128)(2,1)} collective-permute-done((bf16[1,256,512]{2,1,0:T(8,128)(2,1)}, bf16[1,256,512]{2,1,0:T(8,128)(2,1)}, u32[]{:S(2)}, u32[]{:S(2)}) %collective-permute-start.25) | collective-permute-done | bytes 262176 | tf_op jit(solution)/shard_map/cond/branch_1_fun/ppermute | solution.py:515
  560.8 58.8 %conditional.19 = (bf16[256,2048]{1,0:T(8,128)(2,1)}, bf16[2,256,1024]{2,1,0:T(8,128)(2,1)}, bf16[2,256,512]{2,1,0:T(8,128)(2,1)}, bf16[1,256,1408]{2,1,0:T(8,12...) conditional(s32[]{:T(128)} %convert_element_type.111, () %tuple.112, ...), branch_computations={%region_17.18_spmd, %region_18.19_spmd} | conditional | flops 2051 | bytes 35391888 | solution.py:524
  578.2 41.5 %collective-permute-done.7 = bf16[2,256,512]{2,1,0:T(8,128)(2,1)} collective-permute-done((bf16[2,256,512]{2,1,0:T(8,128)(2,1)}, bf16[2,256,512]{2,1,0:T(8,128)(2,1)}, u32[]{:S(2)}, u32[]{:S(2)}) %collective-permute-start.7) | collective-permute-done | bytes 524320 | tf_op jit(solution)/shard_map/cond/branch_1_fun/ppermute | solution.py:515
  619.6 50.1 %conditional.20 = (bf16[1,256,1024]{2,1,0:T(8,128)(2,1)}, bf16[1,256,512]{2,1,0:T(8,128)(2,1)}, bf16[1,256,512]{2,1,0:T(8,128)(2,1)}, bf16[4,256,2048]{2,1,0:T(8...) conditional(s32[]{:T(128)} %convert_element_type.111, () %tuple.111, (bf16[512,2048]{1,0:T(8,128)(2,1)}, ...), branch_computations={%region_19.20_spmd, %region_20.22_spmd} | conditional | flops 212485 | bytes 47472152 | solution.py:524
  654.3 15.3 %collective-permute-done.34 = bf16[1,256,512]{2,1,0:T(8,128)(2,1)} collective-permute-done((bf16[1,256,512]{2,1,0:T(8,128)(2,1)S(1)}, bf16[1,256,512]{2,1,0:T(8,128)(2,1)}, u32[]{:S(2)}, u32[]{:S(2)}) %collective-permute-start.34) | collective-permute-done | bytes 262176 | tf_op jit(solution)/shard_map/cond/branch_1_fun/ppermute | solution.py:515
  669.7 13.4 %conditional.21 = (f32[256,1024]{1,0:T(8,128)}, f32[256,512]{1,0:T(8,128)}, f32[512,256]{1,0:T(8,128)}, f32[18,256]{1,0:T(8,128)S(1)}, f32[256,512]{1,0:T(8,128)}, /*index=5*/f32[256,512]{1,0:T(8,128)}) conditional(s32[]{:T(128)} %convert_element_type.111, () %tuple.115, (bf16[512,2048]{1,0:T(8,128)(2,1)}, bf16[512,2048]{1,0:T(8,128)(2,1)}, ...), branch_computations={%region_22.23_spmd, %region_23.24_spmd} | conditional | flops 12291 | bytes 15015156 | solution.py:524
  (502 shorter events, 386.9 us)
Async XLA Ops:
  108.6 30.5 %collective-permute-start.55 = (bf16[256,2048]{1,0:T(8,128)(2,1)S(1)}, bf16[256,2048]{1,0:T(8,128)(2,1)S(1)}, u32[]{:S(2)}, u32[]{:S(2)}) collective-permute-start(bf16[256,2048]{1,0:T(8,128)(2,1)S(1)} %add_convert_fusion.4.refs_7_), channel_id=1, source_target_pairs={{0,2},{1,3},{2,0},{3,1},{4,6},{5,7},{6,4},{7,5},{8,10},{9,11},{10,... | collective-permute-start | bytes 3145736 | tf_op jit(solution)/shard_map/ppermute | solution.py:515
  142.6 28.5 %collective-permute-start.57 = (bf16[256,2048]{1,0:T(8,128)(2,1)S(1)}, bf16[256,2048]{1,0:T(8,128)(2,1)S(1)}, u32[]{:S(2)}, u32[]{:S(2)}) collective-permute-start(bf16[256,2048]{1,0:T(8,128)(2,1)S(1)} %get-tuple-element.948.refs_0_.refs_1_), channel_id=1, source_target_pairs={{0,2},{1,3},{2,0},{3,1},{4,6},{5,7},{6,4},{7,5},{8,10},{9,11},{10,... | collective-permute-start | bytes 3145736 | tf_op jit(solution)/shard_map/ppermute | solution.py:515
  211.8 78.2 %collective-permute-start.60 = (bf16[4,256,1408]{2,1,0:T(8,128)(2,1)}, bf16[4,256,1408]{2,1,0:T(8,128)(2,1)}, u32[]{:S(2)}, u32[]{:S(2)}) collective-permute-start(bf16[4,256,1408]{2,1,0:T(8,128)(2,1)} %shard_map.302), channel_id=1, source_target_pairs={{0,4},{4,0},{8,12},{12,8},{16,20},{20,16},{24,28},{28,24},{1,5},{5... | collective-permute-start | bytes 8650760 | tf_op jit(solution)/shard_map/ppermute | solution.py:515
  217.7 25.5 %collective-permute-start.10 = (bf16[256,2048]{1,0:T(8,128)(2,1)}, bf16[256,2048]{1,0:T(8,128)(2,1)}, u32[]{:S(2)}, u32[]{:S(2)}) collective-permute-start(bf16[256,2048]{1,0:T(8,128)(2,1)} %add_convert_fusion), channel_id=1, source_target_pairs={{0,2},{1,3},{2,0},{3,1},{4,6},{5,7},{6,4},{7,5},{8,10},{9,11},{10,... | collective-permute-start | bytes 3145736 | tf_op jit(solution)/shard_map/cond/branch_1_fun/ppermute | solution.py:515
  243.2 99.6 %collective-permute-start.62 = (bf16[4,256,1408]{2,1,0:T(8,128)(2,1)}, bf16[4,256,1408]{2,1,0:T(8,128)(2,1)}, u32[]{:S(2)}, u32[]{:S(2)}) collective-permute-start(bf16[4,256,1408]{2,1,0:T(8,128)(2,1)} %get-tuple-element.981), channel_id=1, source_target_pairs={{0,8},{4,12},{8,0},{12,4},{16,24},{20,28},{24,16},{28,20},{1,9},{5... | collective-permute-start | bytes 8650760 | tf_op jit(solution)/shard_map/ppermute | solution.py:515
  245.8 97.0 %collective-permute-start.61 = (bf16[2,256,1408]{2,1,0:T(8,128)(2,1)}, bf16[2,256,1408]{2,1,0:T(8,128)(2,1)}, u32[]{:S(2)}, u32[]{:S(2)}) collective-permute-start(bf16[2,256,1408]{2,1,0:T(8,128)(2,1)} %get-tuple-element.980), channel_id=1, source_target_pairs={{0,4},{4,0},{8,12},{12,8},{16,20},{20,16},{24,28},{28,24},{1,5},{5... | collective-permute-start | bytes 4325384 | tf_op jit(solution)/shard_map/ppermute | solution.py:515
  255.1 25.5 %collective-permute-start.1 = (bf16[256,2048]{1,0:T(8,128)(2,1)}, bf16[256,2048]{1,0:T(8,128)(2,1)}, u32[]{:S(2)}, u32[]{:S(2)}) collective-permute-start(bf16[256,2048]{1,0:T(8,128)(2,1)} %get-tuple-element.505.refs_0_), channel_id=1, source_target_pairs={{0,2},{1,3},{2,0},{3,1},{4,6},{5,7},{6,4},{7,5},{8,10},{9,11},{10,... | collective-permute-start | bytes 3145736 | tf_op jit(solution)/shard_map/cond/branch_1_fun/ppermute | solution.py:515
  290.0 52.8 %all-to-all-start.2 = ((bf16[8,4,64,512]{3,2,1,0:T(8,128)(2,1)}), bf16[8,4,64,512]{3,2,1,0:T(8,128)(2,1)}, u32[]{:S(2)}, u32[]{:S(2)}) async-start(bf16[8,4,64,512]{3,2,1,0:T(8,128)(2,1)} %get-tuple-element.525.refs_10_), calls=%async_computation.2 | async-start | bytes 4194304 | tf_op jit(solution)/shard_map/cond/branch_1_fun/all_to_all | solution.py:554
  299.6 25.4 %collective-permute-start.30 = (bf16[256,2048]{1,0:T(8,128)(2,1)}, bf16[256,2048]{1,0:T(8,128)(2,1)}, u32[]{:S(2)}, u32[]{:S(2)}) collective-permute-start(bf16[256,2048]{1,0:T(8,128)(2,1)} %add_convert_fusion.1), channel_id=1, source_target_pairs={{0,2},{1,3},{2,0},{3,1},{4,6},{5,7},{6,4},{7,5},{8,10},{9,11},{10,... | collective-permute-start | bytes 3145736 | tf_op jit(solution)/shard_map/cond/branch_1_fun/ppermute | solution.py:515
  347.0 74.2 %all-to-all-start = ((bf16[8,4,64,512]{3,2,1,0:T(8,128)(2,1)}), bf16[8,4,64,512]{3,2,1,0:T(8,128)(2,1)}, u32[]{:S(2)}, u32[]{:S(2)}) async-start(bf16[8,4,64,512]{3,2,1,0:T(8,128)(2,1)} %branch_1_fun.45), calls=%async_computation | async-start | bytes 4194304 | tf_op jit(solution)/shard_map/cond/branch_1_fun/all_to_all | solution.py:554
  351.7 69.4 %collective-permute-start.11 = (bf16[2,256,1408]{2,1,0:T(8,128)(2,1)}, bf16[2,256,1408]{2,1,0:T(8,128)(2,1)}, u32[]{:S(2)}, u32[]{:S(2)}) collective-permute-start(bf16[2,256,1408]{2,1,0:T(8,128)(2,1)} %get-tuple-element.549), channel_id=1, source_target_pairs={{0,8},{4,12},{8,0},{12,4},{16,24},{20,28},{24,16},{28,20},{1,9},{5... | collective-permute-start | bytes 4325384 | tf_op jit(solution)/shard_map/cond/branch_1_fun/ppermute | solution.py:515
  358.6 25.9 %collective-permute-start.14 = (bf16[256,2048]{1,0:T(8,128)(2,1)}, bf16[256,2048]{1,0:T(8,128)(2,1)}, u32[]{:S(2)}, u32[]{:S(2)}) collective-permute-start(bf16[256,2048]{1,0:T(8,128)(2,1)} %add_convert_fusion.2), channel_id=1, source_target_pairs={{0,2},{1,3},{2,0},{3,1},{4,6},{5,7},{6,4},{7,5},{8,10},{9,11},{10,... | collective-permute-start | bytes 3145736 | tf_op jit(solution)/shard_map/cond/branch_1_fun/ppermute | solution.py:515
  360.2 38.7 %collective-permute-start.12 = (bf16[4,256,512]{2,1,0:T(8,128)(2,1)}, bf16[4,256,512]{2,1,0:T(8,128)(2,1)}, u32[]{:S(2)}, u32[]{:S(2)}) collective-permute-start(bf16[4,256,512]{2,1,0:T(8,128)(2,1)} %get-tuple-element.550), channel_id=1, source_target_pairs={{0,4},{4,0},{8,12},{12,8},{16,20},{20,16},{24,28},{28,24},{1,5},{5... | collective-permute-start | bytes 3145736 | tf_op jit(solution)/shard_map/cond/branch_1_fun/ppermute | solution.py:515
  360.7 60.5 %collective-permute-start.15 = (bf16[4,256,512]{2,1,0:T(8,128)(2,1)}, bf16[4,256,512]{2,1,0:T(8,128)(2,1)}, u32[]{:S(2)}, u32[]{:S(2)}) collective-permute-start(bf16[4,256,512]{2,1,0:T(8,128)(2,1)} %get-tuple-element.569), channel_id=1, source_target_pairs={{0,4},{4,0},{8,12},{12,8},{16,20},{20,16},{24,28},{28,24},{1,5},{5... | collective-permute-start | bytes 3145736 | tf_op jit(solution)/shard_map/cond/branch_1_fun/ppermute | solution.py:515
  421.2 60.5 %collective-permute-start.16 = (bf16[2,256,1408]{2,1,0:T(8,128)(2,1)}, bf16[2,256,1408]{2,1,0:T(8,128)(2,1)}, u32[]{:S(2)}, u32[]{:S(2)}) collective-permute-start(bf16[2,256,1408]{2,1,0:T(8,128)(2,1)} %get-tuple-element.570), channel_id=1, source_target_pairs={{0,8},{4,12},{8,0},{12,4},{16,24},{20,28},{24,16},{28,20},{1,9},{5... | collective-permute-start | bytes 4325384 | tf_op jit(solution)/shard_map/cond/branch_1_fun/ppermute | solution.py:515
  422.2 59.5 %collective-permute-start.18 = (bf16[2,256,1408]{2,1,0:T(8,128)(2,1)}, bf16[2,256,1408]{2,1,0:T(8,128)(2,1)}, u32[]{:S(2)}, u32[]{:S(2)}) collective-permute-start(bf16[2,256,1408]{2,1,0:T(8,128)(2,1)} %get-tuple-element.581), channel_id=1, source_target_pairs={{0,4},{4,0},{8,12},{12,8},{16,20},{20,16},{24,28},{28,24},{1,5},{5... | collective-permute-start | bytes 4325384 | tf_op jit(solution)/shard_map/cond/branch_1_fun/ppermute | solution.py:515
  423.5 62.6 %collective-permute-start.20 = (bf16[2,256,1408]{2,1,0:T(8,128)(2,1)}, bf16[2,256,1408]{2,1,0:T(8,128)(2,1)}, u32[]{:S(2)}, u32[]{:S(2)}) collective-permute-start(bf16[2,256,1408]{2,1,0:T(8,128)(2,1)} %get-tuple-element.625), channel_id=1, source_target_pairs={{0,4},{4,0},{8,12},{12,8},{16,20},{20,16},{24,28},{28,24},{1,5},{5... | collective-permute-start | bytes 4325384 | tf_op jit(solution)/shard_map/cond/branch_1_fun/ppermute | solution.py:515
  427.7 54.0 %collective-permute-start.17 = (bf16[1,256,1408]{2,1,0:T(8,128)(2,1)S(1)}, bf16[1,256,1408]{2,1,0:T(8,128)(2,1)}, u32[]{:S(2)}, u32[]{:S(2)}) collective-permute-start(bf16[1,256,1408]{2,1,0:T(8,128)(2,1)S(1)} %branch_1_fun.48.refs_10_.refs_11_), channel_id=1, source_target_pairs={{0,16},{4,20},{8,24},{12,28},{16,0},{20,4},{24,8},{28,12},{1,17},{... | collective-permute-start | bytes 2162696 | tf_op jit(solution)/shard_map/cond/branch_1_fun/ppermute | solution.py:515
  435.8 45.8 %collective-permute-start.19 = (bf16[2,256,512]{2,1,0:T(8,128)(2,1)}, bf16[2,256,512]{2,1,0:T(8,128)(2,1)}, u32[]{:S(2)}, u32[]{:S(2)}) collective-permute-start(bf16[2,256,512]{2,1,0:T(8,128)(2,1)} %branch_1_fun.49), channel_id=1, source_target_pairs={{0,8},{4,12},{8,0},{12,4},{16,24},{20,28},{24,16},{28,20},{1,9},{5... | collective-permute-start | bytes 1572872 | tf_op jit(solution)/shard_map/cond/branch_1_fun/ppermute | solution.py:515
  497.7 48.1 %collective-permute-start.23 = (bf16[4,256,1024]{2,1,0:T(8,128)(2,1)}, bf16[4,256,1024]{2,1,0:T(8,128)(2,1)}, u32[]{:S(2)}, u32[]{:S(2)}) collective-permute-start(bf16[4,256,1024]{2,1,0:T(8,128)(2,1)} %get-tuple-element.642), channel_id=1, source_target_pairs={{0,4},{4,0},{8,12},{12,8},{16,20},{20,16},{24,28},{28,24},{1,5},{5... | collective-permute-start | bytes 6291464 | tf_op jit(solution)/shard_map/cond/branch_1_fun/ppermute | solution.py:515
  499.5 46.2 %collective-permute-start.24 = (bf16[4,256,512]{2,1,0:T(8,128)(2,1)}, bf16[4,256,512]{2,1,0:T(8,128)(2,1)}, u32[]{:S(2)}, u32[]{:S(2)}) collective-permute-start(bf16[4,256,512]{2,1,0:T(8,128)(2,1)} %get-tuple-element.643), channel_id=1, source_target_pairs={{0,8},{4,12},{8,0},{12,4},{16,24},{20,28},{24,16},{28,20},{1,9},{5... | collective-permute-start | bytes 3145736 | tf_op jit(solution)/shard_map/cond/branch_1_fun/ppermute | solution.py:515
  499.9 45.9 %collective-permute-start.27 = (bf16[256,2048]{1,0:T(8,128)(2,1)}, bf16[256,2048]{1,0:T(8,128)(2,1)}, u32[]{:S(2)}, u32[]{:S(2)}) collective-permute-start(bf16[256,2048]{1,0:T(8,128)(2,1)} %get-tuple-element.664), channel_id=1, source_target_pairs={{0,2},{1,3},{2,0},{3,1},{4,6},{5,7},{6,4},{7,5},{8,10},{9,11},{10,... | collective-permute-start | bytes 3145736 | tf_op jit(solution)/shard_map/cond/branch_1_fun/ppermute | solution.py:515
  501.0 42.7 %collective-permute-start.26 = (bf16[1,256,1408]{2,1,0:T(8,128)(2,1)}, bf16[1,256,1408]{2,1,0:T(8,128)(2,1)}, u32[]{:S(2)}, u32[]{:S(2)}) collective-permute-start(bf16[1,256,1408]{2,1,0:T(8,128)(2,1)} %get-tuple-element.645.refs_10_.refs_5_), channel_id=1, source_target_pairs={{0,16},{4,20},{8,24},{12,28},{16,0},{20,4},{24,8},{28,12},{1,17},{... | collective-permute-start | bytes 2162696 | tf_op jit(solution)/shard_map/cond/branch_1_fun/ppermute | solution.py:515
  502.9 40.8 %collective-permute-start.25 = (bf16[1,256,512]{2,1,0:T(8,128)(2,1)}, bf16[1,256,512]{2,1,0:T(8,128)(2,1)}, u32[]{:S(2)}, u32[]{:S(2)}) collective-permute-start(bf16[1,256,512]{2,1,0:T(8,128)(2,1)} %get-tuple-element.644), channel_id=1, source_target_pairs={{0,16},{4,20},{8,24},{12,28},{16,0},{20,4},{24,8},{28,12},{1,17},{... | collective-permute-start | bytes 786440 | tf_op jit(solution)/shard_map/cond/branch_1_fun/ppermute | solution.py:515
  560.8 58.8 %collective-permute-start.3 = (bf16[256,2048]{1,0:T(8,128)(2,1)}, bf16[256,2048]{1,0:T(8,128)(2,1)}, u32[]{:S(2)}, u32[]{:S(2)}) collective-permute-start(bf16[256,2048]{1,0:T(8,128)(2,1)} %get-tuple-element.676), channel_id=1, source_target_pairs={{0,2},{1,3},{2,0},{3,1},{4,6},{5,7},{6,4},{7,5},{8,10},{9,11},{10,... | collective-permute-start | bytes 3145736 | tf_op jit(solution)/shard_map/cond/branch_1_fun/ppermute | solution.py:515
  562.0 57.7 %collective-permute-start.4 = (bf16[2,256,1024]{2,1,0:T(8,128)(2,1)}, bf16[2,256,1024]{2,1,0:T(8,128)(2,1)}, u32[]{:S(2)}, u32[]{:S(2)}) collective-permute-start(bf16[2,256,1024]{2,1,0:T(8,128)(2,1)} %get-tuple-element.677), channel_id=1, source_target_pairs={{0,8},{4,12},{8,0},{12,4},{16,24},{20,28},{24,16},{28,20},{1,9},{5... | collective-permute-start | bytes 3145736 | tf_op jit(solution)/shard_map/cond/branch_1_fun/ppermute | solution.py:515
  564.0 55.7 %collective-permute-start.6 = (bf16[1,256,1408]{2,1,0:T(8,128)(2,1)}, bf16[1,256,1408]{2,1,0:T(8,128)(2,1)}, u32[]{:S(2)}, u32[]{:S(2)}) collective-permute-start(bf16[1,256,1408]{2,1,0:T(8,128)(2,1)} %get-tuple-element.679), channel_id=1, source_target_pairs={{0,16},{4,20},{8,24},{12,28},{16,0},{20,4},{24,8},{28,12},{1,17},{... | collective-permute-start | bytes 2162696 | tf_op jit(solution)/shard_map/cond/branch_1_fun/ppermute | solution.py:515
  567.8 51.8 %collective-permute-start.7 = (bf16[2,256,512]{2,1,0:T(8,128)(2,1)}, bf16[2,256,512]{2,1,0:T(8,128)(2,1)}, u32[]{:S(2)}, u32[]{:S(2)}) collective-permute-start(bf16[2,256,512]{2,1,0:T(8,128)(2,1)} %get-tuple-element.680), channel_id=1, source_target_pairs={{0,16},{4,20},{8,24},{12,28},{16,0},{20,4},{24,8},{28,12},{1,17},{... | collective-permute-start | bytes 1572872 | tf_op jit(solution)/shard_map/cond/branch_1_fun/ppermute | solution.py:515
  619.6 30.1 %collective-permute-start.37 = (bf16[256,2048]{1,0:T(8,128)(2,1)}, bf16[256,2048]{1,0:T(8,128)(2,1)S(1)}, u32[]{:S(2)}, u32[]{:S(2)}) collective-permute-start(bf16[256,2048]{1,0:T(8,128)(2,1)} %get-tuple-element.704.refs_15_.refs_3_), channel_id=1, source_target_pairs={{0,1},{1,0},{2,3},{3,2},{4,5},{5,4},{6,7},{7,6},{8,9},{9,8},{10,11... | collective-permute-start | bytes 3145736 | tf_op jit(solution)/shard_map/cond/branch_1_fun/ppermute | solution.py:515
  619.7 30.1 %collective-permute-start.36 = (bf16[256,2048]{1,0:T(8,128)(2,1)}, bf16[256,2048]{1,0:T(8,128)(2,1)S(1)}, u32[]{:S(2)}, u32[]{:S(2)}) collective-permute-start(bf16[256,2048]{1,0:T(8,128)(2,1)} %get-tuple-element.718.refs_1_), channel_id=1, source_target_pairs={{0,1},{1,0},{2,3},{3,2},{4,5},{5,4},{6,7},{7,6},{8,9},{9,8},{10,11... | collective-permute-start | bytes 3145736 | tf_op jit(solution)/shard_map/cond/branch_1_fun/ppermute | solution.py:515
  630.7 39.0 %collective-permute-start.33 = (bf16[1,256,1024]{2,1,0:T(8,128)(2,1)S(1)}, bf16[1,256,1024]{2,1,0:T(8,128)(2,1)}, u32[]{:S(2)}, u32[]{:S(2)}) collective-permute-start(bf16[1,256,1024]{2,1,0:T(8,128)(2,1)S(1)} %branch_1_fun.64.refs_11_), channel_id=1, source_target_pairs={{0,16},{4,20},{8,24},{12,28},{16,0},{20,4},{24,8},{28,12},{1,17},{... | collective-permute-start | bytes 1572872 | tf_op jit(solution)/shard_map/cond/branch_1_fun/ppermute | solution.py:515
  639.4 30.3 %collective-permute-start.34 = (bf16[1,256,512]{2,1,0:T(8,128)(2,1)S(1)}, bf16[1,256,512]{2,1,0:T(8,128)(2,1)}, u32[]{:S(2)}, u32[]{:S(2)}) collective-permute-start(bf16[1,256,512]{2,1,0:T(8,128)(2,1)S(1)} %branch_1_fun.65.refs_11_), channel_id=1, source_target_pairs={{0,16},{4,20},{8,24},{12,28},{16,0},{20,4},{24,8},{28,12},{1,17},{... | collective-permute-start | bytes 786440 | tf_op jit(solution)/shard_map/cond/branch_1_fun/ppermute | solution.py:515
  (160 other events, 2004.9 us)

commit v7 on v6

--- a/solution.py
+++ b/solution.py
@@ -675,6 +675,15 @@
         arrived = [self.arrived(3), (self.came[1], 0), (self.came[2], 0)]
         total = self.part([0], arrived, f32, self.turned, after=after)
         return total if self.turned else total[0]
+
+    def most(self, after=()):
+        if not self.split:
+            return self.arrived(0)[0].astype(f32)
+        return self.part([0], [self.arrived(3), (self.came[1], 0)], f32, after=after)
+
+    def finish(self, most):
+        total = most[0] + self.came[2][0].astype(f32) if self.split else most
+        return total.T if self.turned else total
 
 
 def sum_over(values, axis):
@@ -1257,24 +1266,29 @@
         return (
             query_key_grad.hop(2, query_key_two), value_grad.hop(2, value_two), out_grad.hop(2, out_two),
             in_order([input_rows, first_rows, second_rows, third_rows]), up_grad.last(), summed(mail),
-        )
-
-    query_key_grad.came[2], value_grad.came[2], out_grad.came[2], input_grad, up_share, mail = region(
+            [query_key_grad.most([out_two]), value_grad.most([out_two]), out_grad.most([out_two])],
+        )
+
+    query_key_grad.came[2], value_grad.came[2], out_grad.came[2], input_grad, up_share, mail, mosts = region(
         fifth_window, input_rows, second_rows, mail
     )
 
     def sixth_window(mail):
         parts = mail.reshape(-1)[:own_size].reshape(rank + 2, column)
-        return query_key_grad.last(), value_grad.last(), out_grad.last(), sum_over(parts, "tensor")
-
-    query_key_share, value_share, out_share, own_part = region(sixth_window, mail)
+        query_key = query_key_grad.finish(mosts[0])
+        return (
+            query_key[:, :DK], query_key[:, DK:], value_grad.finish(mosts[1]), out_grad.finish(mosts[2]),
+            sum_over(parts, "tensor"),
+        )
+
+    query_share, key_share, value_share, out_share, own_part = region(sixth_window, mail)
     shared = mail.reshape(-1)[own_size:].reshape(rank + 2, DK)
     return (
         layer_output,
         input_grad,
         own_part[rank + 1],
-        query_key_share[:, :DK],
-        query_key_share[:, DK:],
+        query_share,
+        key_share,
         value_share,
         gate_share,
         own_part[:rank].T,

time: 696 us -> 690 us (level)
  waiting for transfers between devices: 237 us -> 229 us
where the time goes in v7:
time: 690 us; the launch traced here: 680 us
  Pallas kernels  272 us (39%)
  waiting for transfers between devices  229 us (33%)
  starting transfers between devices  100 us (14%)
  matrix products  28.6 us (4%)
  local copies, waits for them, and re-layouts  25.5 us (4%)
  other arithmetic  21.1 us (3%)
    pallas_call x64, Pallas kernels, grid_call(): pl.pallas_call(run, grid_spec=pltpu.PrefetchScalarGridSpec(num_scalar_pre...  272 us
    ppermute x63, waiting for transfers between devices, swap(): return lax.ppermute(values, axis, [(i, i ^ distance) for i in range(count)])  211 us
    ppermute x63, starting transfers between devices, swap(): return lax.ppermute(values, axis, [(i, i ^ distance) for i in range(count)])  83.3 us
    dot_general x13, matrix products, contract(): lax.dot_general(left, right, (((left_dim,), (right_dim,)), ((), ())), pre...  28.6 us
    all_to_all x2, waiting for transfers between devices, deal(): return lax.all_to_all(pieces, 'seq', 0, 0)  17.7 us
  transfers between devices with their start and end apart: 67, of which 28 were waited for; matrix products, arithmetic and copies ran while one was open for 6% of the time, Pallas kernels for 32%

profile of v7, /device:TPU:0, one launch (start us, length us, event | category | flops | bytes accessed | tf_op | source)
XLA Modules:
  0.0 679.5 jit_solution(11377258348490291202)
XLA Ops:
  58.2 11.2 %collective-permute-start.49 = (bf16[2,64,512]{2,1,0:T(8,128)(2,1)S(1)}, bf16[2,64,512]{2,1,0:T(8,128)(2,1)S(1)}, u32[]{:S(2)}, u32[]{:S(2)}) collective-permute-start(bf16[2,64,512]{2,1,0:T(8,128)(2,1)S(1)} %get-tuple-element.889), channel_id=1, source_target_pairs={{0,8},{4,12},{8,0},{12,4},{16,24},{20,28},{24,16},{28,20},{1,9},{5... | collective-permute-start | bytes 393224 | tf_op jit(solution)/shard_map/ppermute | solution.py:515
  73.3 10.5 %collective-permute-done.50.refs_6_ = bf16[2,64,512]{2,1,0:T(8,128)(2,1)S(1)} collective-permute-done((bf16[2,64,512]{2,1,0:T(8,128)(2,1)S(1)}, bf16[2,64,512]{2,1,0:T(8,128)(2,1)S(1)}, u32[]{:S(2)}, u32[]{:S(2)}) %collective-permute-start.50) | collective-permute-done | bytes 131104 | tf_op jit(solution)/shard_map/ppermute | solution.py:515
  123.6 8.3 %collective-permute-done.52.refs_1_ = bf16[2,4,64,512]{3,2,1,0:T(8,128)(2,1)S(1)} collective-permute-done((bf16[2,4,64,512]{3,2,1,0:T(8,128)(2,1)S(1)}, bf16[2,4,64,512]{3,2,1,0:T(8,128)(2,1)S(1)}, u32[]{:S(2)}, u32[]{:S(2)}) %collective-permute-start.52) | collective-permute-done | bytes 524320 | tf_op jit(solution)/shard_map/ppermute | solution.py:515
  148.2 23.1 %shard_map.298 = (bf16[512,1408]{1,0:T(8,128)(2,1)}, bf16[512,1408]{1,0:T(8,128)(2,1)}, bf16[512,1408]{1,0:T(8,128)(2,1)}, bf16[512,2048]{1,0:T(8,128)(2,1)}, bf16[512,2048]{1,0:T(8,128)(2,1)S(1)}) custom-call(bf16[256,2048]{1,0:T(8,128)(2,1)S(1)} %get-tuple-element.898.refs_0_.refs_1_, bf16[256,2048]{1,0:T(8,128)(2,1)S(1)} %collective-permute-done.56.refs_1_.refs_2_, ...), custom_call_target="tpu_custom_call" | custom-call | flops 1024 | bytes 1024 | tf_op jit(solution)/shard_map/pallas_call | solution.py:497
  175.5 13.3 %shard_map.299 = (bf16[256,1408]{1,0:T(8,128)(2,1)}, bf16[256,1408]{1,0:T(8,128)(2,1)S(1)}, bf16[256,1408]{1,0:T(8,128)(2,1)}, bf16[256,2048]{1,0:T(8,128)(2,1)}, bf16[256,2048]{1,0:T(8,128)(2,1)S(1)}) custom-call(bf16[256,2048]{1,0:T(8,128)(2,1)S(1)} %collective-permute-done.57.refs_0_.refs_1_.refs_3_, ...), custom_call_target="tpu_custom_call" | custom-call | flops 1024 | bytes 1024 | tf_op jit(solution)/shard_map/pallas_call | solution.py:497
  188.9 15.6 %shard_map.301 = (bf16[256,1408]{1,0:T(8,128)(2,1)}, bf16[256,1408]{1,0:T(8,128)(2,1)S(1)}, bf16[256,1408]{1,0:T(8,128)(2,1)}, bf16[256,2048]{1,0:T(8,128)(2,1)}, bf16[256,2048]{1,0:T(8,128)(2,1)}) custom-call(bf16[256,2048]{1,0:T(8,128)(2,1)} %collective-permute-done.58.refs_0_.refs_1_.refs_4_, ...), custom_call_target="tpu_custom_call" | custom-call | flops 1024 | bytes 1024 | tf_op jit(solution)/shard_map/pallas_call | solution.py:497
  204.6 7.2 %shard_map.302 = bf16[4,256,1408]{2,1,0:T(8,128)(2,1)} custom-call(s32[4]{0:T(128)S(1)} %pad_add_fusion.11.refs_0_, bf16[256,2048]{1,0:T(8,128)(2,1)S(1)} %copy-done.22, bf16[256,2048]{1,0:T(8,128)(2,1)S(1)} %copy-done.28, bf16[256,2048]{1,0:T(8,128)(2,1)S(1)} %collective-permute-done.57.refs_0_.refs_1_.refs_3_, ...), custom_call_target="tpu_custom_call" | custom-call | flops 1024 | bytes 1024 | tf_op jit(solution)/shard_map/pallas_call | solution.py:497
  213.3 29.8 %conditional.12 = (bf16[256,2048]{1,0:T(8,128)(2,1)}, bf16[256,2048]{1,0:T(8,128)(2,1)}, bf16[4,256,1408]{2,1,0:T(8,128)(2,1)}, bf16[2,256,1408]{2,1,0:T(8,128)(2,1)}, bf16[2,256,1408]{2,1,0:T(8,128)(2,1)}) conditional(s32[]{:T(128)} %convert_element_type.123, () %tuple.100, (bf16[512,2048]{1,0:T(8,128)(2,1)S(1)}, bf16[256,2048]{1,0:T(8,128)(2,1)S(1)}, ...), branch_computations={%region_2.0_spmd, %region_3.0_spmd} | conditional | flops 2100249 | bytes 54529576 | solution.py:524
  219.2 7.8 %branch_1_fun.36.refs_9_ = bf16[4,256,1408]{2,1,0:T(8,128)(2,1)} custom-call(s32[4]{0:T(128)S(1)} %pad_add_fusion.refs_0_, bf16[512,2048]{1,0:T(8,128)(2,1)S(1)} %copy-done.12, bf16[512,2048]{1,0:T(8,128)(2,1)S(1)} %copy-done.12, bf16[512,2048]{1,0:T(8,128)(2,1)} %get-tuple-element.457.refs_3_.refs_4_, bf16[512,2048]{1,0:T(8,128)(2,1)} %get-tuple-element.457.refs_3_.refs_4_, ...), custom_call_target="tpu_custom_call" | custom-call | flops 1024 | bytes 1024 | tf_op jit(solution)/shard_map/cond/branch_1_fun/pallas_call | solution.py:497
  255.0 34.9 %conditional.13 = (bf16[256,2048]{1,0:T(8,128)(2,1)}, bf16[256,2048]{1,0:T(8,128)(2,1)}, bf16[512,512]{1,0:T(8,128)(2,1)}, bf16[512,512]{1,0:T(8,128)(2,1)}, f32...) conditional(s32[]{:T(128)} %convert_element_type.123, () %tuple.98, ...), branch_computations={%region_4.0_spmd, %region_5.0_spmd} | conditional | flops 3072 | bytes 31460644 | solution.py:524
  262.8 17.8 %collective-permute-done.1.refs_0_ = bf16[256,2048]{1,0:T(8,128)(2,1)} collective-permute-done((bf16[256,2048]{1,0:T(8,128)(2,1)}, bf16[256,2048]{1,0:T(8,128)(2,1)}, u32[]{:S(2)}, u32[]{:S(2)}) %collective-permute-start.1) | collective-permute-done | bytes 1048608 | tf_op jit(solution)/shard_map/cond/branch_1_fun/ppermute | solution.py:515
  289.9 52.8 %conditional.14 = (bf16[8,4,64,512]{3,2,1,0:T(8,128)(2,1)}, bf16[2,256,1408]{2,1,0:T(8,128)(2,1)}, bf16[4,256,512]{2,1,0:T(8,128)(2,1)}, bf16[4,256,512]{2,1,0:T...) conditional(s32[]{:T(128)} %convert_element_type.123, () %tuple.97, ...), branch_computations={%region_6.0_spmd, %region_7.0_spmd} | conditional | flops 2100259 | bytes 34606540 | solution.py:524
  317.7 7.3 %collective-permute-done.30 = bf16[256,2048]{1,0:T(8,128)(2,1)} collective-permute-done((bf16[256,2048]{1,0:T(8,128)(2,1)}, bf16[256,2048]{1,0:T(8,128)(2,1)}, u32[]{:S(2)}, u32[]{:S(2)}) %collective-permute-start.30) | collective-permute-done | bytes 1048608 | tf_op jit(solution)/shard_map/cond/branch_1_fun/ppermute | solution.py:515
  324.9 17.7 %all-to-all-done.2 = bf16[8,4,64,512]{3,2,1,0:T(8,128)(2,1)} async-done(((bf16[8,4,64,512]{3,2,1,0:T(8,128)(2,1)}), bf16[8,4,64,512]{3,2,1,0:T(8,128)(2,1)}, u32[]{:S(2)}, u32[]{:S(2)}) %all-to-all-start.2) | async-done | bytes 2097184 | tf_op jit(solution)/shard_map/cond/branch_1_fun/all_to_all | solution.py:554
  342.7 78.1 %conditional.15 = (bf16[8,4,64,512]{3,2,1,0:T(8,128)(2,1)}, bf16[2,256,1408]{2,1,0:T(8,128)(2,1)}, bf16[4,256,512]{2,1,0:T(8,128)(2,1)}, bf16[2,256,1408]{2,1,0:...) conditional(s32[]{:T(128)} %convert_element_type.123, () %tuple.96, ...), branch_computations={%region_8.0_spmd, %region_9.0_spmd} | conditional | flops 3673099 | bytes 35130784 | solution.py:524
  373.8 10.3 %collective-permute-done.14 = bf16[256,2048]{1,0:T(8,128)(2,1)} collective-permute-done((bf16[256,2048]{1,0:T(8,128)(2,1)}, bf16[256,2048]{1,0:T(8,128)(2,1)}, u32[]{:S(2)}, u32[]{:S(2)}) %collective-permute-start.14) | collective-permute-done | bytes 1048608 | tf_op jit(solution)/shard_map/cond/branch_1_fun/ppermute | solution.py:515
  384.1 14.4 %collective-permute-done.12 = bf16[4,256,512]{2,1,0:T(8,128)(2,1)} collective-permute-done((bf16[4,256,512]{2,1,0:T(8,128)(2,1)}, bf16[4,256,512]{2,1,0:T(8,128)(2,1)}, u32[]{:S(2)}, u32[]{:S(2)}) %collective-permute-start.12) | collective-permute-done | bytes 1048608 | tf_op jit(solution)/shard_map/cond/branch_1_fun/ppermute | solution.py:515
  398.5 22.3 %collective-permute-done.15 = bf16[4,256,512]{2,1,0:T(8,128)(2,1)} collective-permute-done((bf16[4,256,512]{2,1,0:T(8,128)(2,1)}, bf16[4,256,512]{2,1,0:T(8,128)(2,1)}, u32[]{:S(2)}, u32[]{:S(2)}) %collective-permute-start.15) | collective-permute-done | bytes 1048608 | tf_op jit(solution)/shard_map/cond/branch_1_fun/ppermute | solution.py:515
  420.8 64.8 %conditional.16 = (bf16[2,256,1408]{2,1,0:T(8,128)(2,1)}, bf16[1,256,1408]{2,1,0:T(8,128)(2,1)}, bf16[2,256,1408]{2,1,0:T(8,128)(2,1)}, bf16[2,256,512]{2,1,0:T(...) conditional(s32[]{:T(128)} %convert_element_type.123, () %tuple.95, ...), branch_computations={%region_10.0_spmd, %region_11.0_spmd} | conditional | flops 8224 | bytes 97887368 | solution.py:524
  435.7 7.6 %branch_1_fun.50 = (bf16[512,512]{1,0:T(8,128)(2,1)}, bf16[512,512]{1,0:T(8,128)(2,1)}, bf16[512,512]{1,0:T(8,128)(2,1)}, f32[2,16,256]{2,1,0:T(8,128)S(1)}, f32...) custom-call(bf16[512,512]{1,0:T(8,128)(2,1)S(1)} %copy-done.84, bf16[512,512]{1,0:T(8,128)(2,1)S(1)} %copy-done.95, ...), custom_call_target="tpu_custom_call" | custom-call | flops 1024 | bytes 1024 | tf_op jit(solution)/shard_map/cond/branch_1_fun/pallas_call | solution.py:497
  443.4 7.8 %branch_1_fun.51 = (bf16[512,512]{1,0:T(8,128)(2,1)}, bf16[512,512]{1,0:T(8,128)(2,1)}, bf16[512,512]{1,0:T(8,128)(2,1)}, f32[2,16,256]{2,1,0:T(8,128)}, f32[2,1...) custom-call(bf16[512,512]{1,0:T(8,128)(2,1)S(1)} %copy-done.89, bf16[512,512]{1,0:T(8,128)(2,1)} %get-tuple-element.568.refs_1_, ...), custom_call_target="tpu_custom_call" | custom-call | flops 1024 | bytes 1024 | tf_op jit(solution)/shard_map/cond/branch_1_fun/pallas_call | solution.py:497
  451.2 7.6 %branch_1_fun.52 = (bf16[2,256,2048]{2,1,0:T(8,128)(2,1)}, bf16[2,256,2048]{2,1,0:T(8,128)(2,1)}) custom-call(bf16[512,512]{1,0:T(8,128)(2,1)} %get-tuple-element.1169.refs_0_.refs_7_.refs_8_, bf16[512,512]{1,0:T(8,128)(2,1)} %get-tuple-element.1170.refs_1_.refs_11_.refs_12_, bf16[512,512]{1,0:T(8,128)(2,1)} %get-tuple-element.1171.refs_2_.refs_7_.refs_8_, ...), custom_call_target="tpu_custom_call" | custom-call | flops 1024 | bytes 1024 | tf_op jit(solution)/shard_map/cond/branch_1_fun/pallas_call | solution.py:497
  458.8 7.5 %branch_1_fun.53 = (bf16[2,256,2048]{2,1,0:T(8,128)(2,1)}, bf16[2,256,2048]{2,1,0:T(8,128)(2,1)}) custom-call(bf16[512,512]{1,0:T(8,128)(2,1)} %get-tuple-element.1163.refs_0_.refs_5_.refs_6_, bf16[512,512]{1,0:T(8,128)(2,1)} %get-tuple-element.1164.refs_1_.refs_9_.refs_10_, ...), custom_call_target="tpu_custom_call", output_to_operand_aliasing={{0}: (8, {}), {1}: (9, {})} | custom-call | flops 1024 | bytes 1024 | tf_op jit(solution)/shard_map/cond/branch_1_fun/pallas_call | solution.py:497
  466.4 6.8 %branch_1_fun.54.refs_9_ = bf16[4,256,1024]{2,1,0:T(8,128)(2,1)} custom-call(s32[4]{0:T(128)S(1)} %get-tuple-element.1064.refs_0_, bf16[512,2048]{1,0:T(8,128)(2,1)} %get-tuple-element.546.refs_1_.refs_2_, bf16[512,2048]{1,0:T(8,128)(2,1)} %get-tuple-element.546.refs_1_.refs_2_, bf16[512,2048]{1,0:T(8,128)(2,1)} %get-tuple-element.547.refs_3_.refs_4_, ...), custom_call_target="tpu_custom_call" | custom-call | flops 1024 | bytes 1024 | tf_op jit(solution)/shard_map/cond/branch_1_fun/pallas_call | solution.py:497
  487.3 10.0 %conditional.17 = (bf16[2,256,2048]{2,1,0:T(8,128)(2,1)}, bf16[256,2048]{1,0:T(8,128)(2,1)}, bf16[1,256,512]{2,1,0:T(8,128)(2,1)}, bf16[1,256,1408]{2,1,0:T(8,128)(2,1)}, bf16[256,2048]{1,0:T(8,128)(2,1)}) conditional(s32[]{:T(128)} %convert_element_type.123, () %tuple.106, (bf16[2,256,2048]{2,1,0:T(8,128)(2,1)}, bf16[2,256,2048]{2,1,0:T(8,128)(2,1)}, ...), branch_computations={%region_12.0_spmd, %region_13.0_spmd} | conditional | flops 2099204 | bytes 35653908 | solution.py:524
  497.3 48.1 %conditional.18 = (bf16[4,256,1024]{2,1,0:T(8,128)(2,1)}, bf16[4,256,512]{2,1,0:T(8,128)(2,1)}, bf16[1,256,512]{2,1,0:T(8,128)(2,1)}, bf16[1,256,1408]{2,1,0:T(8...) conditional(s32[]{:T(128)} %convert_element_type.123, () %tuple.94, ...), branch_computations={%region_14.0_spmd, %region_15.17_spmd} | conditional | flops 50219 | bytes 59130612 | solution.py:524
  525.5 17.8 %collective-permute-done.25 = bf16[1,256,512]{2,1,0:T(8,128)(2,1)} collective-permute-done((bf16[1,256,512]{2,1,0:T(8,128)(2,1)}, bf16[1,256,512]{2,1,0:T(8,128)(2,1)}, u32[]{:S(2)}, u32[]{:S(2)}) %collective-permute-start.25) | collective-permute-done | bytes 262176 | tf_op jit(solution)/shard_map/cond/branch_1_fun/ppermute | solution.py:515
  560.4 58.9 %conditional.19 = (bf16[256,2048]{1,0:T(8,128)(2,1)}, bf16[2,256,1024]{2,1,0:T(8,128)(2,1)}, bf16[2,256,512]{2,1,0:T(8,128)(2,1)}, bf16[1,256,1408]{2,1,0:T(8,12...) conditional(s32[]{:T(128)} %convert_element_type.123, () %tuple.110, ...), branch_computations={%region_17.18_spmd, %region_18.19_spmd} | conditional | flops 2051 | bytes 35391888 | solution.py:524
  577.8 41.5 %collective-permute-done.7 = bf16[2,256,512]{2,1,0:T(8,128)(2,1)} collective-permute-done((bf16[2,256,512]{2,1,0:T(8,128)(2,1)}, bf16[2,256,512]{2,1,0:T(8,128)(2,1)}, u32[]{:S(2)}, u32[]{:S(2)}) %collective-permute-start.7) | collective-permute-done | bytes 524320 | tf_op jit(solution)/shard_map/cond/branch_1_fun/ppermute | solution.py:515
  619.3 50.1 %conditional.20 = (bf16[1,256,1024]{2,1,0:T(8,128)(2,1)}, bf16[1,256,512]{2,1,0:T(8,128)(2,1)}, bf16[1,256,512]{2,1,0:T(8,128)(2,1)}, bf16[4,256,2048]{2,1,0:T(8...) conditional(s32[]{:T(128)} %convert_element_type.123, ...), branch_computations={%region_19.20_spmd, %region_20.22_spmd} | conditional | flops 215557 | bytes 60058244 | solution.py:524
  660.2 9.1 %collective-permute-done.34 = bf16[1,256,512]{2,1,0:T(8,128)(2,1)} collective-permute-done((bf16[1,256,512]{2,1,0:T(8,128)(2,1)S(1)}, bf16[1,256,512]{2,1,0:T(8,128)(2,1)}, u32[]{:S(2)}, u32[]{:S(2)}) %collective-permute-start.34) | collective-permute-done | bytes 262176 | tf_op jit(solution)/shard_map/cond/branch_1_fun/ppermute | solution.py:515
  669.4 7.1 %conditional.21 = (f32[256,512]{1,0:T(8,128)S(1)}, f32[256,512]{1,0:T(8,128)S(1)}, f32[256,512]{1,0:T(8,128)S(1)}, f32[18,256]{1,0:T(8,128)S(1)}, f32[512,256]{1,0:T(8,128)S(1)}) conditional(s32[]{:T(128)} %convert_element_type.123, () %tuple.113, (bf16[1,256,1024]{2,1,0:T(8,128)(2,1)}, f32[1,256,1024]{2,1,0:T(8,128)}, ...), branch_computations={%region_22.23_spmd, %region_23.24_spmd} | conditional | flops 1057792 | bytes 8720504 | solution.py:524
  (513 shorter events, 387.0 us)
Async XLA Ops:
  108.6 30.5 %collective-permute-start.55 = (bf16[256,2048]{1,0:T(8,128)(2,1)S(1)}, bf16[256,2048]{1,0:T(8,128)(2,1)S(1)}, u32[]{:S(2)}, u32[]{:S(2)}) collective-permute-start(bf16[256,2048]{1,0:T(8,128)(2,1)S(1)} %add_convert_fusion.4.refs_7_), channel_id=1, source_target_pairs={{0,2},{1,3},{2,0},{3,1},{4,6},{5,7},{6,4},{7,5},{8,10},{9,11},{10,... | collective-permute-start | bytes 3145736 | tf_op jit(solution)/shard_map/ppermute | solution.py:515
  142.6 28.7 %collective-permute-start.57 = (bf16[256,2048]{1,0:T(8,128)(2,1)S(1)}, bf16[256,2048]{1,0:T(8,128)(2,1)S(1)}, u32[]{:S(2)}, u32[]{:S(2)}) collective-permute-start(bf16[256,2048]{1,0:T(8,128)(2,1)S(1)} %get-tuple-element.898.refs_0_.refs_1_), channel_id=1, source_target_pairs={{0,2},{1,3},{2,0},{3,1},{4,6},{5,7},{6,4},{7,5},{8,10},{9,11},{10,... | collective-permute-start | bytes 3145736 | tf_op jit(solution)/shard_map/ppermute | solution.py:515
  211.8 78.2 %collective-permute-start.60 = (bf16[4,256,1408]{2,1,0:T(8,128)(2,1)}, bf16[4,256,1408]{2,1,0:T(8,128)(2,1)}, u32[]{:S(2)}, u32[]{:S(2)}) collective-permute-start(bf16[4,256,1408]{2,1,0:T(8,128)(2,1)} %shard_map.302), channel_id=1, source_target_pairs={{0,4},{4,0},{8,12},{12,8},{16,20},{20,16},{24,28},{28,24},{1,5},{5... | collective-permute-start | bytes 8650760 | tf_op jit(solution)/shard_map/ppermute | solution.py:515
  217.6 25.5 %collective-permute-start.10 = (bf16[256,2048]{1,0:T(8,128)(2,1)}, bf16[256,2048]{1,0:T(8,128)(2,1)}, u32[]{:S(2)}, u32[]{:S(2)}) collective-permute-start(bf16[256,2048]{1,0:T(8,128)(2,1)} %add_convert_fusion), channel_id=1, source_target_pairs={{0,2},{1,3},{2,0},{3,1},{4,6},{5,7},{6,4},{7,5},{8,10},{9,11},{10,... | collective-permute-start | bytes 3145736 | tf_op jit(solution)/shard_map/cond/branch_1_fun/ppermute | solution.py:515
  243.1 99.6 %collective-permute-start.62 = (bf16[4,256,1408]{2,1,0:T(8,128)(2,1)}, bf16[4,256,1408]{2,1,0:T(8,128)(2,1)}, u32[]{:S(2)}, u32[]{:S(2)}) collective-permute-start(bf16[4,256,1408]{2,1,0:T(8,128)(2,1)} %get-tuple-element.931), channel_id=1, source_target_pairs={{0,8},{4,12},{8,0},{12,4},{16,24},{20,28},{24,16},{28,20},{1,9},{5... | collective-permute-start | bytes 8650760 | tf_op jit(solution)/shard_map/ppermute | solution.py:515
  245.7 97.0 %collective-permute-start.61 = (bf16[2,256,1408]{2,1,0:T(8,128)(2,1)}, bf16[2,256,1408]{2,1,0:T(8,128)(2,1)}, u32[]{:S(2)}, u32[]{:S(2)}) collective-permute-start(bf16[2,256,1408]{2,1,0:T(8,128)(2,1)} %get-tuple-element.930), channel_id=1, source_target_pairs={{0,4},{4,0},{8,12},{12,8},{16,20},{20,16},{24,28},{28,24},{1,5},{5... | collective-permute-start | bytes 4325384 | tf_op jit(solution)/shard_map/ppermute | solution.py:515
  255.0 25.5 %collective-permute-start.1 = (bf16[256,2048]{1,0:T(8,128)(2,1)}, bf16[256,2048]{1,0:T(8,128)(2,1)}, u32[]{:S(2)}, u32[]{:S(2)}) collective-permute-start(bf16[256,2048]{1,0:T(8,128)(2,1)} %get-tuple-element.469.refs_0_), channel_id=1, source_target_pairs={{0,2},{1,3},{2,0},{3,1},{4,6},{5,7},{6,4},{7,5},{8,10},{9,11},{10,... | collective-permute-start | bytes 3145736 | tf_op jit(solution)/shard_map/cond/branch_1_fun/ppermute | solution.py:515
  289.9 52.7 %all-to-all-start.2 = ((bf16[8,4,64,512]{3,2,1,0:T(8,128)(2,1)}), bf16[8,4,64,512]{3,2,1,0:T(8,128)(2,1)}, u32[]{:S(2)}, u32[]{:S(2)}) async-start(bf16[8,4,64,512]{3,2,1,0:T(8,128)(2,1)} %get-tuple-element.489.refs_10_), calls=%async_computation.2 | async-start | bytes 4194304 | tf_op jit(solution)/shard_map/cond/branch_1_fun/all_to_all | solution.py:554
  346.9 74.0 %all-to-all-start = ((bf16[8,4,64,512]{3,2,1,0:T(8,128)(2,1)}), bf16[8,4,64,512]{3,2,1,0:T(8,128)(2,1)}, u32[]{:S(2)}, u32[]{:S(2)}) async-start(bf16[8,4,64,512]{3,2,1,0:T(8,128)(2,1)} %branch_1_fun.45), calls=%async_computation | async-start | bytes 4194304 | tf_op jit(solution)/shard_map/cond/branch_1_fun/all_to_all | solution.py:554
  351.4 69.4 %collective-permute-start.11 = (bf16[2,256,1408]{2,1,0:T(8,128)(2,1)}, bf16[2,256,1408]{2,1,0:T(8,128)(2,1)}, u32[]{:S(2)}, u32[]{:S(2)}) collective-permute-start(bf16[2,256,1408]{2,1,0:T(8,128)(2,1)} %get-tuple-element.513), channel_id=1, source_target_pairs={{0,8},{4,12},{8,0},{12,4},{16,24},{20,28},{24,16},{28,20},{1,9},{5... | collective-permute-start | bytes 4325384 | tf_op jit(solution)/shard_map/cond/branch_1_fun/ppermute | solution.py:515
  358.2 25.9 %collective-permute-start.14 = (bf16[256,2048]{1,0:T(8,128)(2,1)}, bf16[256,2048]{1,0:T(8,128)(2,1)}, u32[]{:S(2)}, u32[]{:S(2)}) collective-permute-start(bf16[256,2048]{1,0:T(8,128)(2,1)} %add_convert_fusion.2), channel_id=1, source_target_pairs={{0,2},{1,3},{2,0},{3,1},{4,6},{5,7},{6,4},{7,5},{8,10},{9,11},{10,... | collective-permute-start | bytes 3145736 | tf_op jit(solution)/shard_map/cond/branch_1_fun/ppermute | solution.py:515
  359.8 38.7 %collective-permute-start.12 = (bf16[4,256,512]{2,1,0:T(8,128)(2,1)}, bf16[4,256,512]{2,1,0:T(8,128)(2,1)}, u32[]{:S(2)}, u32[]{:S(2)}) collective-permute-start(bf16[4,256,512]{2,1,0:T(8,128)(2,1)} %get-tuple-element.514), channel_id=1, source_target_pairs={{0,4},{4,0},{8,12},{12,8},{16,20},{20,16},{24,28},{28,24},{1,5},{5... | collective-permute-start | bytes 3145736 | tf_op jit(solution)/shard_map/cond/branch_1_fun/ppermute | solution.py:515
  360.4 60.5 %collective-permute-start.15 = (bf16[4,256,512]{2,1,0:T(8,128)(2,1)}, bf16[4,256,512]{2,1,0:T(8,128)(2,1)}, u32[]{:S(2)}, u32[]{:S(2)}) collective-permute-start(bf16[4,256,512]{2,1,0:T(8,128)(2,1)} %get-tuple-element.533), channel_id=1, source_target_pairs={{0,4},{4,0},{8,12},{12,8},{16,20},{20,16},{24,28},{28,24},{1,5},{5... | collective-permute-start | bytes 3145736 | tf_op jit(solution)/shard_map/cond/branch_1_fun/ppermute | solution.py:515
  420.9 60.5 %collective-permute-start.16 = (bf16[2,256,1408]{2,1,0:T(8,128)(2,1)}, bf16[2,256,1408]{2,1,0:T(8,128)(2,1)}, u32[]{:S(2)}, u32[]{:S(2)}) collective-permute-start(bf16[2,256,1408]{2,1,0:T(8,128)(2,1)} %get-tuple-element.534), channel_id=1, source_target_pairs={{0,8},{4,12},{8,0},{12,4},{16,24},{20,28},{24,16},{28,20},{1,9},{5... | collective-permute-start | bytes 4325384 | tf_op jit(solution)/shard_map/cond/branch_1_fun/ppermute | solution.py:515
  421.8 59.5 %collective-permute-start.18 = (bf16[2,256,1408]{2,1,0:T(8,128)(2,1)}, bf16[2,256,1408]{2,1,0:T(8,128)(2,1)}, u32[]{:S(2)}, u32[]{:S(2)}) collective-permute-start(bf16[2,256,1408]{2,1,0:T(8,128)(2,1)} %get-tuple-element.545), channel_id=1, source_target_pairs={{0,4},{4,0},{8,12},{12,8},{16,20},{20,16},{24,28},{28,24},{1,5},{5... | collective-permute-start | bytes 4325384 | tf_op jit(solution)/shard_map/cond/branch_1_fun/ppermute | solution.py:515
  423.1 62.5 %collective-permute-start.20 = (bf16[2,256,1408]{2,1,0:T(8,128)(2,1)}, bf16[2,256,1408]{2,1,0:T(8,128)(2,1)}, u32[]{:S(2)}, u32[]{:S(2)}) collective-permute-start(bf16[2,256,1408]{2,1,0:T(8,128)(2,1)} %get-tuple-element.589), channel_id=1, source_target_pairs={{0,4},{4,0},{8,12},{12,8},{16,20},{20,16},{24,28},{28,24},{1,5},{5... | collective-permute-start | bytes 4325384 | tf_op jit(solution)/shard_map/cond/branch_1_fun/ppermute | solution.py:515
  427.3 54.0 %collective-permute-start.17 = (bf16[1,256,1408]{2,1,0:T(8,128)(2,1)S(1)}, bf16[1,256,1408]{2,1,0:T(8,128)(2,1)}, u32[]{:S(2)}, u32[]{:S(2)}) collective-permute-start(bf16[1,256,1408]{2,1,0:T(8,128)(2,1)S(1)} %branch_1_fun.48.refs_10_.refs_11_), channel_id=1, source_target_pairs={{0,16},{4,20},{8,24},{12,28},{16,0},{20,4},{24,8},{28,12},{1,17},{... | collective-permute-start | bytes 2162696 | tf_op jit(solution)/shard_map/cond/branch_1_fun/ppermute | solution.py:515
  435.5 45.8 %collective-permute-start.19 = (bf16[2,256,512]{2,1,0:T(8,128)(2,1)}, bf16[2,256,512]{2,1,0:T(8,128)(2,1)}, u32[]{:S(2)}, u32[]{:S(2)}) collective-permute-start(bf16[2,256,512]{2,1,0:T(8,128)(2,1)} %branch_1_fun.49), channel_id=1, source_target_pairs={{0,8},{4,12},{8,0},{12,4},{16,24},{20,28},{24,16},{28,20},{1,9},{5... | collective-permute-start | bytes 1572872 | tf_op jit(solution)/shard_map/cond/branch_1_fun/ppermute | solution.py:515
  497.3 48.1 %collective-permute-start.23 = (bf16[4,256,1024]{2,1,0:T(8,128)(2,1)}, bf16[4,256,1024]{2,1,0:T(8,128)(2,1)}, u32[]{:S(2)}, u32[]{:S(2)}) collective-permute-start(bf16[4,256,1024]{2,1,0:T(8,128)(2,1)} %get-tuple-element.606), channel_id=1, source_target_pairs={{0,4},{4,0},{8,12},{12,8},{16,20},{20,16},{24,28},{28,24},{1,5},{5... | collective-permute-start | bytes 6291464 | tf_op jit(solution)/shard_map/cond/branch_1_fun/ppermute | solution.py:515
  499.1 46.2 %collective-permute-start.24 = (bf16[4,256,512]{2,1,0:T(8,128)(2,1)}, bf16[4,256,512]{2,1,0:T(8,128)(2,1)}, u32[]{:S(2)}, u32[]{:S(2)}) collective-permute-start(bf16[4,256,512]{2,1,0:T(8,128)(2,1)} %get-tuple-element.607), channel_id=1, source_target_pairs={{0,8},{4,12},{8,0},{12,4},{16,24},{20,28},{24,16},{28,20},{1,9},{5... | collective-permute-start | bytes 3145736 | tf_op jit(solution)/shard_map/cond/branch_1_fun/ppermute | solution.py:515
  499.5 45.9 %collective-permute-start.27 = (bf16[256,2048]{1,0:T(8,128)(2,1)}, bf16[256,2048]{1,0:T(8,128)(2,1)}, u32[]{:S(2)}, u32[]{:S(2)}) collective-permute-start(bf16[256,2048]{1,0:T(8,128)(2,1)} %get-tuple-element.628), channel_id=1, source_target_pairs={{0,2},{1,3},{2,0},{3,1},{4,6},{5,7},{6,4},{7,5},{8,10},{9,11},{10,... | collective-permute-start | bytes 3145736 | tf_op jit(solution)/shard_map/cond/branch_1_fun/ppermute | solution.py:515
  500.7 42.5 %collective-permute-start.26 = (bf16[1,256,1408]{2,1,0:T(8,128)(2,1)}, bf16[1,256,1408]{2,1,0:T(8,128)(2,1)}, u32[]{:S(2)}, u32[]{:S(2)}) collective-permute-start(bf16[1,256,1408]{2,1,0:T(8,128)(2,1)} %get-tuple-element.609.refs_10_.refs_5_), channel_id=1, source_target_pairs={{0,16},{4,20},{8,24},{12,28},{16,0},{20,4},{24,8},{28,12},{1,17},{... | collective-permute-start | bytes 2162696 | tf_op jit(solution)/shard_map/cond/branch_1_fun/ppermute | solution.py:515
  502.6 40.7 %collective-permute-start.25 = (bf16[1,256,512]{2,1,0:T(8,128)(2,1)}, bf16[1,256,512]{2,1,0:T(8,128)(2,1)}, u32[]{:S(2)}, u32[]{:S(2)}) collective-permute-start(bf16[1,256,512]{2,1,0:T(8,128)(2,1)} %get-tuple-element.608), channel_id=1, source_target_pairs={{0,16},{4,20},{8,24},{12,28},{16,0},{20,4},{24,8},{28,12},{1,17},{... | collective-permute-start | bytes 786440 | tf_op jit(solution)/shard_map/cond/branch_1_fun/ppermute | solution.py:515
  560.4 58.9 %collective-permute-start.3 = (bf16[256,2048]{1,0:T(8,128)(2,1)}, bf16[256,2048]{1,0:T(8,128)(2,1)}, u32[]{:S(2)}, u32[]{:S(2)}) collective-permute-start(bf16[256,2048]{1,0:T(8,128)(2,1)} %get-tuple-element.640), channel_id=1, source_target_pairs={{0,2},{1,3},{2,0},{3,1},{4,6},{5,7},{6,4},{7,5},{8,10},{9,11},{10,... | collective-permute-start | bytes 3145736 | tf_op jit(solution)/shard_map/cond/branch_1_fun/ppermute | solution.py:515
  561.7 57.6 %collective-permute-start.4 = (bf16[2,256,1024]{2,1,0:T(8,128)(2,1)}, bf16[2,256,1024]{2,1,0:T(8,128)(2,1)}, u32[]{:S(2)}, u32[]{:S(2)}) collective-permute-start(bf16[2,256,1024]{2,1,0:T(8,128)(2,1)} %get-tuple-element.641), channel_id=1, source_target_pairs={{0,8},{4,12},{8,0},{12,4},{16,24},{20,28},{24,16},{28,20},{1,9},{5... | collective-permute-start | bytes 3145736 | tf_op jit(solution)/shard_map/cond/branch_1_fun/ppermute | solution.py:515
  563.6 55.7 %collective-permute-start.6 = (bf16[1,256,1408]{2,1,0:T(8,128)(2,1)}, bf16[1,256,1408]{2,1,0:T(8,128)(2,1)}, u32[]{:S(2)}, u32[]{:S(2)}) collective-permute-start(bf16[1,256,1408]{2,1,0:T(8,128)(2,1)} %get-tuple-element.643), channel_id=1, source_target_pairs={{0,16},{4,20},{8,24},{12,28},{16,0},{20,4},{24,8},{28,12},{1,17},{... | collective-permute-start | bytes 2162696 | tf_op jit(solution)/shard_map/cond/branch_1_fun/ppermute | solution.py:515
  567.5 51.8 %collective-permute-start.7 = (bf16[2,256,512]{2,1,0:T(8,128)(2,1)}, bf16[2,256,512]{2,1,0:T(8,128)(2,1)}, u32[]{:S(2)}, u32[]{:S(2)}) collective-permute-start(bf16[2,256,512]{2,1,0:T(8,128)(2,1)} %get-tuple-element.644), channel_id=1, source_target_pairs={{0,16},{4,20},{8,24},{12,28},{16,0},{20,4},{24,8},{28,12},{1,17},{... | collective-permute-start | bytes 1572872 | tf_op jit(solution)/shard_map/cond/branch_1_fun/ppermute | solution.py:515
  619.3 36.4 %collective-permute-start.37 = (bf16[256,2048]{1,0:T(8,128)(2,1)}, bf16[256,2048]{1,0:T(8,128)(2,1)S(1)}, u32[]{:S(2)}, u32[]{:S(2)}) collective-permute-start(bf16[256,2048]{1,0:T(8,128)(2,1)} %get-tuple-element.668.refs_15_.refs_3_), channel_id=1, source_target_pairs={{0,1},{1,0},{2,3},{3,2},{4,5},{5,4},{6,7},{7,6},{8,9},{9,8},{10,11... | collective-permute-start | bytes 3145736 | tf_op jit(solution)/shard_map/cond/branch_1_fun/ppermute | solution.py:515
  619.4 36.3 %collective-permute-start.36 = (bf16[256,2048]{1,0:T(8,128)(2,1)}, bf16[256,2048]{1,0:T(8,128)(2,1)S(1)}, u32[]{:S(2)}, u32[]{:S(2)}) collective-permute-start(bf16[256,2048]{1,0:T(8,128)(2,1)} %get-tuple-element.682.refs_1_), channel_id=1, source_target_pairs={{0,1},{1,0},{2,3},{3,2},{4,5},{5,4},{6,7},{7,6},{8,9},{9,8},{10,11... | collective-permute-start | bytes 3145736 | tf_op jit(solution)/shard_map/cond/branch_1_fun/ppermute | solution.py:515
  622.8 30.4 %all-to-all-start.3 = ((bf16[8,2,6912]{2,1,0:T(2,128)(2,1)}), bf16[8,2,6912]{2,1,0:T(2,128)(2,1)S(1)}, u32[]{:S(2)}, u32[]{:S(2)}) async-start(bf16[8,2,6912]{2,1,0:T(2,128)(2,1)} %reshape.212), calls=%async_computation.3 | async-start | bytes 442368 | tf_op jit(solution)/shard_map/cond/branch_1_fun/all_to_all | solution.py:1246
  630.3 39.0 %collective-permute-start.33 = (bf16[1,256,1024]{2,1,0:T(8,128)(2,1)S(1)}, bf16[1,256,1024]{2,1,0:T(8,128)(2,1)}, u32[]{:S(2)}, u32[]{:S(2)}) collective-permute-start(bf16[1,256,1024]{2,1,0:T(8,128)(2,1)S(1)} %branch_1_fun.64.refs_11_), channel_id=1, source_target_pairs={{0,16},{4,20},{8,24},{12,28},{16,0},{20,4},{24,8},{28,12},{1,17},{... | collective-permute-start | bytes 1572872 | tf_op jit(solution)/shard_map/cond/branch_1_fun/ppermute | solution.py:515
  639.0 30.3 %collective-permute-start.34 = (bf16[1,256,512]{2,1,0:T(8,128)(2,1)S(1)}, bf16[1,256,512]{2,1,0:T(8,128)(2,1)}, u32[]{:S(2)}, u32[]{:S(2)}) collective-permute-start(bf16[1,256,512]{2,1,0:T(8,128)(2,1)S(1)} %branch_1_fun.65.refs_11_), channel_id=1, source_target_pairs={{0,16},{4,20},{8,24},{12,28},{16,0},{20,4},{24,8},{28,12},{1,17},{... | collective-permute-start | bytes 786440 | tf_op jit(solution)/shard_map/cond/branch_1_fun/ppermute | solution.py:515
  (164 other events, 2007.4 us)
